TPU v7x, 32 devices: a whole 2x2x4 slice. The times are simulated.
32 devices in a mesh: dp: 8 (over z, y), tensor: 4 (over x, core).
Axes of the slice: x: 2, y: 2, z: 4, core: 2. Of those that a mesh axis runs over, the one named last changes fastest.
Arguments:
- inputs: bfloat16 [16, 1024, 1280], P('dp', 'tensor'), may hold values from -6 to 6
- cotangent: bfloat16 [16, 1024, 1280], P('dp', 'tensor'), may hold values from -6 to 6
- lengths: int32 [16], P('dp'), may hold values from 128 to 1024, as said below
- adapter_pick: int32 [16, 6], P('dp'), may hold values from 0 to 7
- first_gain: float32 [1280], replicated, may hold values from 0.5 to 1.5
- first_bias: float32 [1280], replicated, may hold values from -1.5 to 1.5
- query_weight: bfloat16 [1280, 1280], P(None, 'tensor'), may hold values from -0.15625 to 0.15625
- key_weight: bfloat16 [1280, 1280], P(None, 'tensor'), may hold values from -0.15625 to 0.15625
- value_weight: bfloat16 [1280, 1280], P(None, 'tensor'), may hold values from -0.15625 to 0.15625
- output_weight: bfloat16 [1280, 1280], P('tensor'), may hold values from -0.625 to 0.625
- second_gain: float32 [1280], replicated, may hold values from 0.5 to 1.5
- second_bias: float32 [1280], replicated, may hold values from -1.5 to 1.5
- widen_weight: bfloat16 [1280, 5120], P(None, 'tensor'), may hold values from -0.15625 to 0.15625
- narrow_weight: bfloat16 [5120, 1280], P('tensor'), may hold values from -0.078125 to 0.078125
- query_inner: bfloat16 [8, 1280, 16], replicated, may hold values from -0.15625 to 0.15625
- query_outer: bfloat16 [8, 16, 1280], P(None, None, 'tensor'), may hold values from -1.5 to 1.5
- key_inner: bfloat16 [8, 1280, 16], replicated, may hold values from -0.15625 to 0.15625
- key_outer: bfloat16 [8, 16, 1280], P(None, None, 'tensor'), may hold values from -1.5 to 1.5
- value_inner: bfloat16 [8, 1280, 16], replicated, may hold values from -0.15625 to 0.15625
- value_outer: bfloat16 [8, 16, 1280], P(None, None, 'tensor'), may hold values from -1.5 to 1.5
- output_inner: bfloat16 [8, 1280, 16], P(None, 'tensor'), may hold values from -0.625 to 0.625
- output_outer: bfloat16 [8, 16, 1280], replicated, may hold values from -1.5 to 1.5
- widen_inner: bfloat16 [8, 1280, 16], replicated, may hold values from -0.15625 to 0.15625
- widen_outer: bfloat16 [8, 16, 5120], P(None, None, 'tensor'), may hold values from -1.5 to 1.5
- narrow_inner: bfloat16 [8, 5120, 16], P(None, 'tensor'), may hold values from -0.078125 to 0.078125
- narrow_outer: bfloat16 [8, 16, 1280], replicated, may hold values from -1.5 to 1.5
Outputs:
- output: bfloat16 [16, 1024, 1280], P('dp', 'tensor')
- input_grad: float32 [16, 1024, 1280], P('dp', 'tensor')
- query_inner_gradient: float32 [8, 1280, 16], replicated
- query_outer_gradient: float32 [8, 16, 1280], P(None, None, 'tensor')
- key_inner_gradient: float32 [8, 1280, 16], replicated
- key_outer_gradient: float32 [8, 16, 1280], P(None, None, 'tensor')
- value_inner_gradient: float32 [8, 1280, 16], replicated
- value_outer_gradient: float32 [8, 16, 1280], P(None, None, 'tensor')
- output_inner_gradient: float32 [8, 1280, 16], P(None, 'tensor')
- output_outer_gradient: float32 [8, 16, 1280], replicated
- widen_inner_gradient: float32 [8, 1280, 16], replicated
- widen_outer_gradient: float32 [8, 16, 5120], P(None, None, 'tensor')
- narrow_inner_gradient: float32 [8, 5120, 16], P(None, 'tensor')
- narrow_outer_gradient: float32 [8, 16, 1280], replicated
Inputs may be any that keep to these rules, and one draw needn't show every extreme that they name: `lengths`: of the 2 clips that share an index of dp, one has all 1024 tokens; some clip has 128 tokens.
All inputs are finite; a program needn't handle non-finite values.
Results may differ from a plain program's by a relative error of at most 0.015.
The roundings to bfloat16 on the way count: a program that leaves them out, or rounds other values in their place, can miss the bound.
Values may be sent and summed in bfloat16 or wider, within the bound.
No kernel may reach another device: no remote copies, remote signals or barrier semaphores. Data moves between devices by JAX's collectives and lax.ppermute only.
A program may use at most 192 MiB of HBM per device.

v0:
```python
import math

import jax
import jax.numpy as jnp
from jax import lax
from jax.sharding import PartitionSpec as P

HEAD_DIM = 80


highest = lax.Precision.HIGHEST
neg_fill = -1000000000.0


def normalize(states, norm_gain, norm_shift):
    centre = states - jnp.mean(states, axis=-1, keepdims=True)
    scaled = lax.rsqrt(jnp.mean(centre * centre, axis=-1, keepdims=True) + 1e-05)
    unit_rows = centre * scaled
    return (unit_rows * norm_gain + norm_shift, unit_rows, scaled)


def normalize_back(grad_rows, unit_rows, scaled, norm_gain):
    grad_unit = grad_rows * norm_gain
    return scaled * (
        grad_unit
        - jnp.mean(grad_unit, axis=-1, keepdims=True)
        - unit_rows * jnp.mean(grad_unit * unit_rows, axis=-1, keepdims=True)
    )


def pick_pair(picked_hot, inner_factor, outer_factor):
    chosen_inner = jnp.einsum(
        "ce,eir->cir", picked_hot, inner_factor.astype(jnp.float32), precision=highest
    )
    chosen_outer = jnp.einsum(
        "ce,ero->cro", picked_hot, outer_factor.astype(jnp.float32), precision=highest
    )
    return (chosen_inner.astype(jnp.bfloat16), chosen_outer.astype(jnp.bfloat16))


def project(source, weight, chosen_inner, chosen_outer):
    lowrank = jnp.einsum("csi,cir->csr", source, chosen_inner, preferred_element_type=jnp.float32)
    main_term = jnp.einsum("csi,io->cso", source, weight, preferred_element_type=jnp.float32)
    return (
        main_term
        + jnp.einsum("csr,cro->cso", lowrank, chosen_outer.astype(jnp.float32), precision=highest),
        lowrank,
    )


def project_back(source, lowrank, grad_rows, weight, chosen_inner, chosen_outer, picked_hot):
    grad_low = jnp.einsum(
        "cso,cro->csr", grad_rows, chosen_outer, preferred_element_type=jnp.float32
    )
    grad_source = jnp.einsum("cso,io->csi", grad_rows, weight, preferred_element_type=jnp.float32)
    grad_source = grad_source + jnp.einsum(
        "csr,cir->csi", grad_low, chosen_inner.astype(jnp.float32), precision=highest
    )
    outer_clip = jnp.einsum(
        "csr,cso->cro", lowrank, grad_rows.astype(jnp.float32), precision=highest
    )
    inner_clip = jnp.einsum("csi,csr->cir", source.astype(jnp.float32), grad_low, precision=highest)
    grad_inner = jnp.einsum("ce,cir->eir", picked_hot, inner_clip, precision=highest)
    grad_outer = jnp.einsum("ce,cro->ero", picked_hot, outer_clip, precision=highest)
    return (grad_source, grad_inner, grad_outer)


def block_layout(clip_slots, features):
    head_count = features // HEAD_DIM
    block_rows = min(512, clip_slots)
    return (head_count, block_rows, clip_slots // block_rows)


def attend_clip(queries, key_rows, values, length):
    clip_slots, features = queries.shape
    head_count, block_rows, block_count = block_layout(clip_slots, features)
    score_scale = 1.0 / math.sqrt(HEAD_DIM)
    query_blocks = queries.reshape(block_count, block_rows, head_count, HEAD_DIM)
    key_heads = key_rows.reshape(clip_slots, head_count, HEAD_DIM)
    value_heads = values.reshape(clip_slots, head_count, HEAD_DIM)
    key_live = jnp.arange(clip_slots, dtype=jnp.int32) < length

    def one_block(query_block):
        scores = (
            jnp.einsum("qhd,khd->hqk", query_block, key_heads, preferred_element_type=jnp.float32)
            * score_scale
        )
        scores = jnp.where(key_live[None, None, :], scores, neg_fill)
        row_top = jnp.max(scores, axis=-1, keepdims=True)
        log_total = jnp.log(jnp.sum(jnp.exp(scores - row_top), axis=-1, keepdims=True)) + row_top
        soft_weights = jnp.exp(scores - log_total).astype(jnp.bfloat16)
        context = jnp.einsum(
            "hqk,khd->qhd", soft_weights, value_heads, preferred_element_type=jnp.float32
        )
        return (context.astype(jnp.bfloat16).reshape(block_rows, features), log_total[..., 0])

    context, log_totals = lax.map(one_block, query_blocks)
    return (context.reshape(clip_slots, features), log_totals)


def attend_back(queries, key_rows, values, length, log_totals, grad_context):
    clip_slots, features = queries.shape
    head_count, block_rows, block_count = block_layout(clip_slots, features)
    score_scale = 1.0 / math.sqrt(HEAD_DIM)
    query_blocks = queries.reshape(block_count, block_rows, head_count, HEAD_DIM)
    grad_blocks = grad_context.reshape(block_count, block_rows, head_count, HEAD_DIM)
    key_heads = key_rows.reshape(clip_slots, head_count, HEAD_DIM)
    value_heads = values.reshape(clip_slots, head_count, HEAD_DIM)
    key_live = jnp.arange(clip_slots, dtype=jnp.int32) < length

    def one_block(carried, block_items):
        grad_keys, grad_values = carried
        query_block, grad_block, total_block = block_items
        scores = (
            jnp.einsum("qhd,khd->hqk", query_block, key_heads, preferred_element_type=jnp.float32)
            * score_scale
        )
        scores = jnp.where(key_live[None, None, :], scores, neg_fill)
        soft_full = jnp.exp(scores - total_block[..., None])
        soft_weights = soft_full.astype(jnp.bfloat16)
        grad_soft = jnp.einsum(
            "qhd,khd->hqk", grad_block, value_heads, preferred_element_type=jnp.float32
        )
        weighted = jnp.sum(grad_soft * soft_full, axis=-1, keepdims=True)
        grad_scores = (soft_full * (grad_soft - weighted)).astype(jnp.bfloat16)
        grad_query = (
            jnp.einsum("hqk,khd->qhd", grad_scores, key_heads, preferred_element_type=jnp.float32)
            * score_scale
        )
        grad_keys = (
            grad_keys
            + jnp.einsum(
                "hqk,qhd->khd", grad_scores, query_block, preferred_element_type=jnp.float32
            )
            * score_scale
        )
        grad_values = grad_values + jnp.einsum(
            "hqk,qhd->khd", soft_weights, grad_block, preferred_element_type=jnp.float32
        )
        return (
            (grad_keys, grad_values),
            grad_query.astype(jnp.bfloat16).reshape(block_rows, features),
        )

    zeros_heads = jnp.zeros((clip_slots, head_count, HEAD_DIM), jnp.float32)
    (grad_keys, grad_values), grad_queries = lax.scan(
        one_block, (zeros_heads, zeros_heads), (query_blocks, grad_blocks, log_totals)
    )
    return (
        grad_queries.reshape(clip_slots, features),
        grad_keys.reshape(clip_slots, features).astype(jnp.bfloat16),
        grad_values.reshape(clip_slots, features).astype(jnp.bfloat16),
    )


def body(
    inputs,
    cotangent,
    lengths,
    adapter_pick,
    first_gain,
    first_bias,
    query_weight,
    key_weight,
    value_weight,
    output_weight,
    second_gain,
    second_bias,
    widen_weight,
    narrow_weight,
    query_inner,
    query_outer,
    key_inner,
    key_outer,
    value_inner,
    value_outer,
    output_inner,
    output_outer,
    widen_inner,
    widen_outer,
    narrow_inner,
    narrow_outer,
):
    clip_count, rows_local, features = inputs.shape
    row_start = lax.axis_index("tensor") * rows_local
    position = row_start + jnp.arange(rows_local, dtype=jnp.int32)
    row_mask = (position[None, :] < lengths[:, None]).astype(jnp.float32)[:, :, None]
    picked_hot = (
        adapter_pick[:, :, None] == jnp.arange(query_inner.shape[0], dtype=jnp.int32)
    ).astype(jnp.float32)
    factor_pairs = (
        (query_inner, query_outer),
        (key_inner, key_outer),
        (value_inner, value_outer),
        (output_inner, output_outer),
        (widen_inner, widen_outer),
        (narrow_inner, narrow_outer),
    )
    pairs = [
        pick_pair(picked_hot[:, number], factor_pairs[number][0], factor_pairs[number][1])
        for number in range(6)
    ]
    states = inputs.astype(jnp.float32)
    first_normed, first_unit, first_scaled = normalize(states, first_gain, first_bias)
    first_local = first_normed.astype(jnp.bfloat16)
    first_rows = lax.all_gather(first_local, "tensor", axis=1, tiled=True)
    queries, query_low = project(first_rows, query_weight, pairs[0][0], pairs[0][1])
    key_rows, key_low = project(first_rows, key_weight, pairs[1][0], pairs[1][1])
    values, value_low = project(first_rows, value_weight, pairs[2][0], pairs[2][1])
    queries = queries.astype(jnp.bfloat16)
    key_rows = key_rows.astype(jnp.bfloat16)
    values = values.astype(jnp.bfloat16)
    context_list = []
    total_list = []
    for clip_number in range(clip_count):
        context_clip, total_clip = attend_clip(
            queries[clip_number], key_rows[clip_number], values[clip_number], lengths[clip_number]
        )
        context_list.append(context_clip)
        total_list.append(total_clip)
    context = jnp.stack(context_list)
    attended_part, output_low = project(context, output_weight, pairs[3][0], pairs[3][1])
    attended = lax.psum_scatter(attended_part, "tensor", scatter_dimension=1, tiled=True)
    hidden = states + row_mask * attended
    second_normed, second_unit, second_scaled = normalize(hidden, second_gain, second_bias)
    second_rows = lax.all_gather(second_normed.astype(jnp.bfloat16), "tensor", axis=1, tiled=True)
    widened, widen_low = project(second_rows, widen_weight, pairs[4][0], pairs[4][1])
    activated = jax.nn.gelu(widened).astype(jnp.bfloat16)
    branch_part, narrow_low = project(activated, narrow_weight, pairs[5][0], pairs[5][1])
    branch = lax.psum_scatter(
        branch_part.astype(jnp.bfloat16), "tensor", scatter_dimension=1, tiled=True
    ).astype(jnp.float32)
    output = (hidden + row_mask * branch).astype(jnp.bfloat16)
    grad_output = cotangent.astype(jnp.float32)
    grad_branch = lax.all_gather(
        (row_mask * grad_output).astype(jnp.bfloat16), "tensor", axis=1, tiled=True
    )
    grad_activated, narrow_inner_part, narrow_outer_part = project_back(
        activated,
        narrow_low,
        grad_branch,
        narrow_weight,
        pairs[5][0],
        pairs[5][1],
        picked_hot[:, 5],
    )
    grad_widened = jax.vjp(jax.nn.gelu, widened)[1](grad_activated)[0].astype(jnp.bfloat16)
    grad_second, widen_inner_part, widen_outer_part = project_back(
        second_rows,
        widen_low,
        grad_widened,
        widen_weight,
        pairs[4][0],
        pairs[4][1],
        picked_hot[:, 4],
    )
    grad_second_local = lax.psum_scatter(grad_second, "tensor", scatter_dimension=1, tiled=True)
    grad_hidden = grad_output + normalize_back(
        grad_second_local, second_unit, second_scaled, second_gain
    )
    grad_attended = lax.all_gather(
        (row_mask * grad_hidden).astype(jnp.bfloat16), "tensor", axis=1, tiled=True
    )
    grad_context, output_inner_part, output_outer_part = project_back(
        context,
        output_low,
        grad_attended,
        output_weight,
        pairs[3][0],
        pairs[3][1],
        picked_hot[:, 3],
    )
    grad_context = grad_context.astype(jnp.bfloat16)
    grad_query_list = []
    grad_key_list = []
    grad_value_list = []
    for clip_number in range(clip_count):
        grad_query_clip, grad_key_clip, grad_value_clip = attend_back(
            queries[clip_number],
            key_rows[clip_number],
            values[clip_number],
            lengths[clip_number],
            total_list[clip_number],
            grad_context[clip_number],
        )
        grad_query_list.append(grad_query_clip)
        grad_key_list.append(grad_key_clip)
        grad_value_list.append(grad_value_clip)
    grad_first_query, query_inner_part, query_outer_part = project_back(
        first_rows,
        query_low,
        jnp.stack(grad_query_list),
        query_weight,
        pairs[0][0],
        pairs[0][1],
        picked_hot[:, 0],
    )
    grad_first_key, key_inner_part, key_outer_part = project_back(
        first_rows,
        key_low,
        jnp.stack(grad_key_list),
        key_weight,
        pairs[1][0],
        pairs[1][1],
        picked_hot[:, 1],
    )
    grad_first_value, value_inner_part, value_outer_part = project_back(
        first_rows,
        value_low,
        jnp.stack(grad_value_list),
        value_weight,
        pairs[2][0],
        pairs[2][1],
        picked_hot[:, 2],
    )
    grad_first_local = lax.psum_scatter(
        (grad_first_query + grad_first_key + grad_first_value).astype(jnp.bfloat16),
        "tensor",
        scatter_dimension=1,
        tiled=True,
    ).astype(jnp.float32)
    input_grad = grad_hidden + normalize_back(
        grad_first_local, first_unit, first_scaled, first_gain
    )
    sharded = lax.psum(
        (
            query_outer_part,
            key_outer_part,
            value_outer_part,
            output_inner_part,
            widen_outer_part,
            narrow_inner_part,
        ),
        "dp",
    )
    shared = lax.psum(
        (
            query_inner_part,
            key_inner_part,
            value_inner_part,
            output_outer_part,
            widen_inner_part,
            narrow_outer_part,
        ),
        ("dp", "tensor"),
    )
    return (
        output,
        input_grad,
        shared[0],
        sharded[0],
        shared[1],
        sharded[1],
        shared[2],
        sharded[2],
        sharded[3],
        shared[3],
        shared[4],
        sharded[4],
        sharded[5],
        shared[5],
    )


def solution(mesh):
    placed = (
        P("dp", "tensor", None),
        P("dp", "tensor", None),
        P("dp"),
        P("dp", None),
        P(),
        P(),
        P(None, "tensor"),
        P(None, "tensor"),
        P(None, "tensor"),
        P("tensor", None),
        P(),
        P(),
        P(None, "tensor"),
        P("tensor", None),
        P(),
        P(None, None, "tensor"),
        P(),
        P(None, None, "tensor"),
        P(),
        P(None, None, "tensor"),
        P(None, "tensor", None),
        P(),
        P(),
        P(None, None, "tensor"),
        P(None, "tensor", None),
        P(),
    )
    return jax.shard_map(
        body,
        mesh=mesh,
        in_specs=placed,
        out_specs=(
            P("dp", "tensor", None),
            P("dp", "tensor", None),
            P(),
            P(None, None, "tensor"),
            P(),
            P(None, None, "tensor"),
            P(),
            P(None, None, "tensor"),
            P(None, "tensor", None),
            P(),
            P(),
            P(None, None, "tensor"),
            P(None, "tensor", None),
            P(),
        ),
        check_vma=False,
    )
```

profile of v0, /device:TPU:0, one launch (start us, length us, event | category | flops | bytes accessed | tf_op | source)
XLA Modules:
  0.0 1010.7 jit_solution(18220473539681796085)
XLA Ops:
  25.1 32.5 %all-gather.5.cloned.1.call-done = bf16[2,1024,1280]{2,1,0:T(8,128)(2,1)} async-done(((bf16[2,256,1280]{2,1,0:T(8,128)(2,1)}), bf16[2,1024,1280]{2,1,0:T(8,128)(2,1)}) %all-gather.5.cloned.1.call-update) | async-done | bytes 5242896 | tf_op jit(solution)/shard_map/all_gather | solution.py:206
  85.5 17.0 %while.57 = (s32[]{:T(128)}, bf16[2,512,320]{1,2,0:T(8,128)(2,1)}, f32[2,4,512]{2,1,0:T(4,128)S(1)}, bf16[2,512,4,80]{1,3,2,0:T(8,128)(2,1)}, bf16[1024,4,80]{0,...) while((s32[]{:T(128)}, bf16[2,512,320]{1,2,0:T(8,128)(2,1)}, ...), condition=%wide.region_9.10_spmd.clone, body=%wide.region_6.9_spmd.clone.sunk | while | flops 694320128 | bytes 35721408 | solution.py:97
  114.6 18.3 %while.56 = (s32[]{:T(128)}, bf16[2,512,320]{1,2,0:T(8,128)(2,1)}, f32[2,4,512]{2,1,0:T(4,128)}, bf16[2,512,4,80]{1,3,2,0:T(8,128)(2,1)}, bf16[1024,4,80]{0,2,1:...) while((s32[]{:T(128)}, bf16[2,512,320]{1,2,0:T(8,128)(2,1)}, ...), condition=%wide.region_5.6_spmd.clone, body=%wide.region_2.5_spmd.clone.sunk | while | flops 694320128 | bytes 35721408 | solution.py:97
  144.8 7.1 convolution_add_fusion.2
  152.1 85.3 %reduce-scatter.5.cloned.1.call-done = f32[2,256,1280]{2,1,0:T(8,128)} async-done(((f32[2,1024,1280]{2,1,0:T(8,128)}), f32[2,256,1280]{2,1,0:T(8,128)}) %reduce-scatter.5.cloned.1.call-update) | async-done | bytes 2621456 | tf_op jit(solution)/shard_map/reduce_scatter | solution.py:223
  252.9 32.9 %all-gather.7.cloned.1.call-done = bf16[2,1024,1280]{2,1,0:T(8,128)(2,1)} async-done(((bf16[2,256,1280]{2,1,0:T(8,128)(2,1)}), bf16[2,1024,1280]{2,1,0:T(8,128)(2,1)}) %all-gather.7.cloned.1.call-update) | async-done | bytes 5242896 | tf_op jit(solution)/shard_map/all_gather | solution.py:226
  289.9 7.0 fusion.99
  297.0 11.1 %multiply_convert_fusion.2 = (bf16[2,1024,1280]{2,1,0:T(8,128)(2,1)}, f32[2,1024,1280]{2,1,0:T(8,128)}) fusion(f32[2,1024,1280]{2,1,0:T(8,128)S(1)} %fusion.99, f32[2,1024,16]{1,2,0:T(8,128)S(1)} %fusion.173, bf16[2,16,1280]{2,0,1:T(2,128)(2,1)S(1)} %copy-done.72), kind=kOutput, calls=%fused_computation.113 | convolution fusion | flops 529530880 | bytes 26427392 | tf_op jit(solution)/shard_map/csr,cro->cso/dot_general | solution.py:46
  308.1 20.2 %all-gather.9.cloned.1.call-done = bf16[2,1024,1280]{2,1,0:T(8,128)(2,1)} async-done(((bf16[2,256,1280]{2,1,0:T(8,128)(2,1)}), bf16[2,1024,1280]{2,1,0:T(8,128)(2,1)}) %all-gather.9.cloned.1.call-update) | async-done | bytes 5242896 | tf_op jit(solution)/shard_map/all_gather | solution.py:235
  332.4 11.7 %fusion.93 = f32[2,1024,1280]{2,1,0:T(8,128)} fusion(bf16[2,1024,1280]{2,1,0:T(8,128)(2,1)S(1)} %copy-done.18, bf16[1280,1280]{1,0:T(8,128)(2,1)} %param.47), kind=kOutput, calls=%fused_computation.120 | convolution fusion | flops 6710886400 | bytes 19005440 | tf_op jit(solution)/shard_map/cso,io->csi/dot_general | solution.py:55
  344.1 13.9 %fusion.92 = bf16[2,1024,1280]{2,1,0:T(8,128)(2,1)S(1)} fusion(f32[2,1024,1280]{2,1,0:T(8,128)S(1)} %bitcast.341, f32[2,1024,1280]{2,1,0:T(8,128)} %fusion.93, f32[2,1024,16]{1,2,0:T(8,128)S(1)} %fusion.163, bf16[2,1280,16]{1,0,2:T(2,128)(2,1)S(1)} %copy-done.70), kind=kOutput, calls=%fused_computation.110 | convolution fusion | flops 558366720 | bytes 26427392 | tf_op jit(solution)/shard_map/csr,cir->csi/dot_general | solution.py:56
  359.5 7.1 fusion.97
  366.6 7.1 convolution_add_fusion
  378.7 9.4 fusion.95
  394.7 64.5 %reduce-scatter.9.cloned.1.call-done = f32[2,256,1280]{2,1,0:T(8,128)} async-done(((f32[2,1024,1280]{2,1,0:T(8,128)}), f32[2,256,1280]{2,1,0:T(8,128)}) %reduce-scatter.9.cloned.1.call-update) | async-done | bytes 2621456 | tf_op jit(solution)/shard_map/reduce_scatter | solution.py:257
  461.7 51.4 %reduce-scatter.7.cloned.1.call-done = bf16[2,256,1280]{2,1,0:T(8,128)(2,1)} async-done(((bf16[2,1024,1280]{2,1,0:T(8,128)(2,1)}), bf16[2,256,1280]{2,1,0:T(8,128)(2,1)}) %reduce-scatter.7.cloned.1.call-update) | async-done | bytes 1310736 | tf_op jit(solution)/shard_map/reduce_scatter | solution.py:230
  540.3 17.8 %all-gather.11.cloned.1.call-done = bf16[2,1024,1280]{2,1,0:T(8,128)(2,1)} async-done(((bf16[2,256,1280]{2,1,0:T(8,128)(2,1)}), bf16[2,1024,1280]{2,1,0:T(8,128)(2,1)}) %all-gather.11.cloned.1.call-update) | async-done | bytes 5242896 | tf_op jit(solution)/shard_map/all_gather | solution.py:261
  577.1 28.7 %while.58 = (s32[]{:T(128)}, f32[1024,4,80]{0,2,1:T(8,128)S(1)}, f32[1024,4,80]{0,2,1:T(8,128)}, bf16[2,512,320]{1,2,0:T(8,128)(2,1)}, bf16[2,512,4,80]{1,3,2,0:...) while((s32[]{:T(128)}, f32[1024,4,80]{0,2,1:T(8,128)S(1)}, ...), condition=%wide.region_19.20_spmd.clone, body=%wide.region_17.19_spmd.clone.sunk | while | flops 1711143936 | bytes 96072048 | solution.py:146
  619.3 27.4 %while.59 = (s32[]{:T(128)}, f32[1024,4,80]{0,2,1:T(8,128)S(1)}, f32[1024,4,80]{0,2,1:T(8,128)}, bf16[2,512,320]{1,2,0:T(8,128)(2,1)}, bf16[2,512,4,80]{1,3,2,0:...) while((s32[]{:T(128)}, f32[1024,4,80]{0,2,1:T(8,128)S(1)}, ...), condition=%wide.region_22.23_spmd.clone, body=%wide.region_20.22_spmd.clone.sunk | while | flops 1711143936 | bytes 96072048 | solution.py:146
  670.2 7.2 fusion.181
  711.7 20.9 %add_convert_fusion = bf16[2,1024,1280]{2,1,0:T(8,128)(2,1)} fusion(f32[2,1024,1280]{2,1,0:T(8,128)} %fusion.119, f32[2,1024,1280]{2,1,0:T(8,128)} %fusion.123, f32[2,1024,1280]{2,1,0:T(8,128)} %fusion.181, f32[2,1024,1280]{2,1,0:T(8,128)} %fusion.127, f32[2,1024,1280]{2,1,0:T(8,128)} %fusion.185, f32[2,1024,16]{1,2,0:T(8,128)S(1)} %fusion.132, ...), kind=kOutput, calls=%fused_computation.111 | convolution fusion | flops 519045120 | bytes 57884672 | tf_op jit(solution)/shard_map/csr,cir->csi/dot_general | solution.py:56
  732.5 60.3 %all-reduce.7.cloned.1.call-done = (f32[8,16,320]{2,0,1:T(8,128)}, f32[8,16,320]{2,0,1:T(8,128)}, f32[8,16,320]{2,0,1:T(8,128)}, f32[8,320,16]{1,0,2:T(8,128)}, ...) async-done(((f32[8,16,320]{2,0,1:T(8,128)}, f32[8,16,320]{2,0,1:T(8,128)}, f32[8,16,320]{2,0,1:T(8,128)}, f32[8,320,16]{1,0,2:T(8,128)}, f32[8,16,1280]{2,0,1:T(8,128)}, ...) | async-done | bytes 1966096 | tf_op jit(solution)/shard_map/psum | solution.py:325
  799.4 143.7 %all-reduce.5.cloned.1.call-done = (f32[8,1280,16]{1,0,2:T(8,128)}, f32[8,1280,16]{1,0,2:T(8,128)}, f32[8,1280,16]{1,0,2:T(8,128)}, f32[8,16,1280]{2,0,1:T(8,128...) async-done(((f32[8,1280,16]{1,0,2:T(8,128)}, f32[8,1280,16]{1,0,2:T(8,128)}, f32[8,1280,16]{1,0,2:T(8,128)}, f32[8,16,1280]{2,0,1:T(8,128)}, f32[8,1280,16]{1,0,2:T(8,128)}, ...) | async-done | bytes 3932176 | tf_op jit(solution)/shard_map/psum | solution.py:336
  955.1 41.1 %reduce-scatter.11.cloned.1.call-done = bf16[2,256,1280]{2,1,0:T(8,128)(2,1)} async-done(((bf16[2,1024,1280]{2,1,0:T(8,128)(2,1)}), bf16[2,256,1280]{2,1,0:T(8,128)(2,1)}) %reduce-scatter.11.cloned.1.call-update) | async-done | bytes 1310736 | tf_op jit(solution)/shard_map/reduce_scatter | solution.py:316
  (493 shorter events, 342.2 us)
Async XLA Ops:
  7.2 282.7 %copy-start = (bf16[1280,1280]{1,0:T(8,128)(2,1)S(1)}, bf16[1280,1280]{1,0:T(8,128)(2,1)}, u32[]{:S(2)}) copy-start(bf16[1280,1280]{1,0:T(8,128)(2,1)} %param.46) | copy-start | bytes 9830404
  7.2 50.4 %all-gather.5.cloned.1.call-start = ((), (), s32[]{:S(2)}) async-start(), calls=%async_computation.4 | async-start | bytes 6553600 | tf_op jit(solution)/shard_map/all_gather | solution.py:206
  14.4 223.0 %reduce-scatter.5.cloned.1.call-start = ((), (), s32[]{:S(2)}) async-start(), calls=%async_computation.5 | async-start | bytes 13107200 | tf_op jit(solution)/shard_map/reduce_scatter | solution.py:223
  15.3 523.6 %copy-start.89 = (pred[2,6,8]{2,0,1:T(4,128)(4,1)}, pred[2,6,8]{2,0,1:T(4,128)(4,1)S(1)}, u32[]{:S(2)}) copy-start(pred[2,6,8]{2,0,1:T(4,128)(4,1)S(1)} %iota_compare_fusion.4) | copy-start | bytes 292
  17.8 58.9 %copy-start.74 = (bf16[2,16,320]{2,0,1:T(2,128)(2,1)}, bf16[2,16,320]{2,0,1:T(2,128)(2,1)S(1)}, u32[]{:S(2)}) copy-start(bf16[2,16,320]{2,0,1:T(2,128)(2,1)S(1)} %convolution_convert_fusion.11) | copy-start | bytes 61444
  151.9 133.9 %all-gather.7.cloned.1.call-start = ((), (), s32[]{:S(2)}) async-start(), calls=%async_computation.6 | async-start | bytes 6553600 | tf_op jit(solution)/shard_map/all_gather | solution.py:226
  152.1 89.5 %copy-start.105 = (f32[2,256]{1,0:T(2,128)}, f32[2,256]{1,0:T(2,128)S(1)}, u32[]{:S(2)}) copy-start(f32[2,256]{1,0:T(2,128)S(1)} %compare_convert_fusion) | copy-start | bytes 6148
  152.1 91.6 %copy-start.81 = (f32[1280]{0:T(1024)S(1)}, f32[1280]{0:T(1024)}, u32[]{:S(2)}) copy-start(f32[1280]{0:T(1024)} %param.44) | copy-start | bytes 15364
  152.1 91.6 %copy-start.107 = (f32[1280]{0:T(1024)S(1)}, f32[1280]{0:T(1024)}, u32[]{:S(2)}) copy-start(f32[1280]{0:T(1024)} %param.45) | copy-start | bytes 15364
  241.6 271.5 %copy-start.92 = (f32[2,256]{1,0:T(2,128)}, f32[2,256]{1,0:T(2,128)S(1)}, u32[]{:S(2)}) copy-start(f32[2,256]{1,0:T(2,128)S(1)} %broadcast_multiply_fusion.4) | copy-start | bytes 6148
  245.2 83.1 %all-gather.9.cloned.1.call-start = ((), (), s32[]{:S(2)}) async-start(), calls=%async_computation.8 | async-start | bytes 6553600 | tf_op jit(solution)/shard_map/all_gather | solution.py:235
  245.8 213.5 %reduce-scatter.9.cloned.1.call-start = ((), (), s32[]{:S(2)}) async-start(), calls=%async_computation.9 | async-start | bytes 13107200 | tf_op jit(solution)/shard_map/reduce_scatter | solution.py:257
  247.3 81.0 %copy-start.54 = (bf16[2,16,1280]{2,0,1:T(2,128)(2,1)}, bf16[2,16,1280]{2,0,1:T(2,128)(2,1)S(1)}, u32[]{:S(2)}) copy-start(bf16[2,16,1280]{2,0,1:T(2,128)(2,1)S(1)} %convolution_convert_fusion) | copy-start | bytes 245764
  373.8 139.3 %reduce-scatter.7.cloned.1.call-start = ((), (), s32[]{:S(2)}) async-start(), calls=%async_computation.7 | async-start | bytes 6553600 | tf_op jit(solution)/shard_map/reduce_scatter | solution.py:230
  394.6 64.6 %copy-start.4 = (f32[2,256,1280]{2,1,0:T(8,128)S(1)}, f32[2,256,1280]{2,1,0:T(8,128)}, u32[]{:S(2)}) copy-start(f32[2,256,1280]{2,1,0:T(8,128)} %copy-done.3) | copy-start | bytes 7864324
  394.6 64.6 %copy-start.97 = (f32[2,256]{1,0:T(2,128)S(1)}, f32[2,256]{1,0:T(2,128)}, u32[]{:S(2)}) copy-start(f32[2,256]{1,0:T(2,128)} %copy-done.96) | copy-start | bytes 6148
  394.6 118.4 %copy-start.106 = (f32[2,256]{1,0:T(2,128)S(1)}, f32[2,256]{1,0:T(2,128)}, u32[]{:S(2)}) copy-start(f32[2,256]{1,0:T(2,128)} %copy-done.105) | copy-start | bytes 6148
  394.7 163.3 %all-gather.11.cloned.1.call-start = ((), (), s32[]{:S(2)}) async-start(), calls=%async_computation.10 | async-start | bytes 6553600 | tf_op jit(solution)/shard_map/all_gather | solution.py:261
  461.7 55.7 %copy-start.101 = (f32[2,256]{1,0:T(2,128)}, f32[2,256]{1,0:T(2,128)S(1)}, u32[]{:S(2)}) copy-start(f32[2,256]{1,0:T(2,128)S(1)} %get-tuple-element.475) | copy-start | bytes 6148
  461.7 55.7 %copy-start.103 = (f32[2,256]{1,0:T(2,128)}, f32[2,256]{1,0:T(2,128)S(1)}, u32[]{:S(2)}) copy-start(f32[2,256]{1,0:T(2,128)S(1)} %get-tuple-element.476) | copy-start | bytes 6148
  517.4 275.4 %all-reduce.7.cloned.1.call-start = ((), (), s32[]{:S(2)}) async-start(), calls=%async_computation.13 | async-start | bytes 4194304 | tf_op jit(solution)/shard_map/psum | solution.py:325
  688.0 255.2 %all-reduce.5.cloned.1.call-start = ((), (), s32[]{:S(2)}) async-start(), calls=%async_computation.12 | async-start | bytes 7864320 | tf_op jit(solution)/shard_map/psum | solution.py:336
  711.6 284.6 %reduce-scatter.11.cloned.1.call-start = ((), (), s32[]{:S(2)}) async-start(), calls=%async_computation.11 | async-start | bytes 6553600 | tf_op jit(solution)/shard_map/reduce_scatter | solution.py:316
  797.7 155.3 %copy-start.60 = (f32[8,16,1280]{2,0,1:T(8,128)S(1)}, f32[8,16,1280]{2,0,1:T(8,128)}, u32[]{:S(2)}) copy-start(f32[8,16,1280]{2,0,1:T(8,128)} %get-tuple-element.444) | copy-start | bytes 1966084
  (124 other events, 1119.2 us)
Sparse Core Ops, SparseCore 0:
  14.5 43.1 all-gather.4
  152.1 85.2 reduce-scatter.4
  245.3 40.4 all-gather.6
  287.8 40.4 all-gather.8
  373.9 85.3 reduce-scatter.8
  461.6 51.3 reduce-scatter.6
  517.5 40.4 all-gather.10
  688.1 104.6 all-reduce.6
  801.0 142.1 all-reduce.4
  945.5 50.6 reduce-scatter.10
where the time goes:
time: 1020 us; the launch traced here: 1010 us
  waiting for transfers between devices  550 us (54%)
  matrix products  304 us (30%)
  local copies, waits for them, and re-layouts  88.3 us (9%)
  other arithmetic  51 us (5%)
  between operations  15.4 us (2%)
    psum x1, waiting for transfers between devices, body(): lax.psum((query_inner_part, key_inner_part, value_inner_part, output_oute...  144 us
    reduce_scatter x1, waiting for transfers between devices, body(): lax.psum_scatter(attended_part, 'tensor', scatter_dimension=1, tiled=True)  85.3 us
    reduce_scatter x1, waiting for transfers between devices, body(): lax.psum_scatter(grad_second, 'tensor', scatter_dimension=1, tiled=True)  64.5 us
    psum x1, waiting for transfers between devices, body(): lax.psum((query_outer_part, key_outer_part, value_outer_part, output_inne...  60.3 us
    dot_general x6, matrix products, project_back(): jnp.einsum('csr,cir->csi', grad_low, chosen_inner.astype(jnp.float32), pr...  57.2 us
    reduce_scatter x1, waiting for transfers between devices, body(): lax.psum_scatter(branch_part.astype(jnp.bfloat16), 'tensor', scatter_dime...  51.4 us
    reduce_scatter x1, waiting for transfers between devices, body(): lax.psum_scatter((grad_first_query + grad_first_key + grad_first_value).a...  41.1 us
    dot_general x6, matrix products, project_back(): jnp.einsum('cso,io->csi', grad_rows, weight, preferred_element_type=jnp.f...  38.9 us
  transfers between devices with their start and end apart: 10, of which 10 were waited for; matrix products, arithmetic and copies ran while one was open for 15% of the time, Pallas kernels for 0%

commit v1 on v0

v1 whole, which is shorter than its diff:
```python
import functools
import math

import jax
import jax.numpy as jnp
from jax import lax
from jax.experimental import pallas as pl
from jax.experimental.pallas import tpu as pltpu
from jax.sharding import PartitionSpec as P

HEAD_DIM = 80
f32 = jnp.float32
bf16 = jnp.bfloat16
neg_fill = -1000000000.0
score_scale = 1.0 / math.sqrt(HEAD_DIM)
log2_e = math.log2(math.e)


def swap(array, axis, bits, size):
    return lax.ppermute(array, axis, [(i, i ^ bits) for i in range(size)])


def nn(a, b):
    return jnp.dot(a, b, preferred_element_type=f32)


def nt(a, b):
    return lax.dot_general(a, b, (((1,), (1,)), ((), ())), preferred_element_type=f32)


def tn(a, b):
    return lax.dot_general(a, b, (((0,), (0,)), ((), ())), preferred_element_type=f32)


def halves(low):
    top = low.astype(bf16)
    return jnp.concatenate([top, (low - top.astype(f32)).astype(bf16)], axis=0)


def twice(factor):
    return jnp.concatenate([factor, factor], axis=0)


def folded(pair):
    count = pair.shape[0] // 2
    return pair[:count] + pair[count:]


def normalize(states, gain, shift):
    centre = states - jnp.mean(states, axis=-1, keepdims=True)
    scaled = lax.rsqrt(jnp.mean(centre * centre, axis=-1, keepdims=True) + 1e-05)
    unit = centre * scaled
    return unit * gain + shift, unit, scaled


def normalize_back(grad_rows, unit, scaled, gain):
    grad_unit = grad_rows * gain
    return scaled * (
        grad_unit
        - jnp.mean(grad_unit, axis=-1, keepdims=True)
        - unit * jnp.mean(grad_unit * unit, axis=-1, keepdims=True)
    )


def live_column(spot_ref, length_ref, rows, bits):
    iota = lax.broadcasted_iota(jnp.int32, (2 * rows, 1), 0)
    place = spot_ref[3]
    first, second = place ^ bits[0], place ^ bits[1]
    position = jnp.where(iota < rows, first * rows + iota, second * rows + iota - rows)
    return position < length_ref[spot_ref[0]]


def whole(shape):
    return pl.BlockSpec(shape, lambda *_: (0,) * len(shape), pipeline_mode=pl.Buffered(1))


def placed_block(shape, index):
    return pl.BlockSpec(shape, index, pipeline_mode=pl.Buffered(1))


def call(body, scalars, operands, specs, outs, out_specs, grid=(1,), scratch=(), cost=(0, 0, 0), limit=58):
    return pl.pallas_call(
        body,
        grid_spec=pltpu.PrefetchScalarGridSpec(
            num_scalar_prefetch=len(scalars),
            grid=grid,
            in_specs=specs,
            out_specs=out_specs,
            scratch_shapes=list(scratch),
        ),
        out_shape=outs,
        cost_estimate=pl.CostEstimate(
            flops=int(cost[0]), bytes_accessed=int(cost[1]), transcendentals=int(cost[2])
        ),
        compiler_params=pltpu.CompilerParams(vmem_limit_bytes=limit * 2**20),
    )(*scalars, *operands)


def shaped(shape, dtype):
    return jax.ShapeDtypeStruct(shape, dtype)


def of_mine(number):
    return lambda i, spot, pick, *_: (pick[spot[0], number], 0, 0)


def of_other(number):
    return lambda i, spot, pick, *_: (pick[spot[1], number], 0, 0)


def stage(spot, pick, inputs, factors):
    rows, features = inputs.shape[1:]
    rank = factors[0].shape[1]

    def body(spot_ref, pick_ref, inputs_ref, *refs):
        send_ref, pack_ref = refs[12:]
        send_ref[:rows] = inputs_ref[0]
        for group, ref, base in ((refs[:6], pack_ref, 0), (refs[6:12], send_ref, rows)):
            ref[base : base + rank] = jnp.concatenate([r[0] for r in group[:4]], axis=1)
            ref[base + rank : base + 2 * rank] = group[4][0]
            ref[base + 2 * rank : base + 3 * rank] = group[5][0]

    specs = [placed_block((1, rows, features), lambda i, spot, *_: (spot[1], 0, 0))]
    for of in (of_mine, of_other):
        specs += [placed_block((1,) + f.shape[1:], of(n)) for n, f in enumerate(factors)]
    outs = [shaped((rows + 3 * rank, features), bf16), shaped((3 * rank, features), bf16)]
    return call(
        body, (spot, pick), [inputs] + factors * 2, specs, outs, [whole(o.shape) for o in outs],
        cost=(0, 4e6, 0),
    )


def stage_weights(spot, pick, heads, dense, cotangent):
    features = heads[0].shape[1]
    head_rows = heads[0].shape[0] // 4
    dense_rows = dense[0].shape[0] // 4
    rows = cotangent.shape[1]

    def body(spot_ref, pick_ref, *refs):
        ins, (heads_ref, wide_ref, thin_ref, cot_ref) = refs[:7], refs[7:]
        for n in range(4):
            heads_ref[n] = ins[n][...]
        wide_ref[...] = ins[4][...]
        thin_ref[...] = ins[5][...]
        cot_ref[...] = ins[6][0]

    part = lambda i, spot, *_: (spot[2], 0)
    specs = [placed_block((head_rows, features), part)] * 4
    specs += [placed_block((dense_rows, features), part)] * 2
    specs += [placed_block((1, rows, features), lambda i, spot, *_: (spot[1], 0, 0))]
    outs = [
        shaped((4, head_rows, features), bf16),
        shaped((dense_rows, features), bf16),
        shaped((dense_rows, features), bf16),
        shaped((rows, features), bf16),
    ]
    return call(
        body, (spot, pick), heads + dense + [cotangent], specs, outs, [whole(o.shape) for o in outs],
        cost=(0, 6e6, 0),
    )


def project_rows(weight, rows_in, outer, low):
    return (nt(weight, rows_in) + tn(twice(outer), halves(low))).astype(bf16)


def project_near(spot, pick, inputs, received, gain, shift, inners, pack, side, weights):
    rows, features = inputs.shape[1:]
    tokens = 2 * rows
    width = weights[0].shape[0]
    rank = inners[0].shape[1]

    def body(spot_ref, pick_ref, xa, xb, gain_ref, shift_ref, iq, ik, iv, pack_ref, side_ref, *refs):
        ws, (z_ref, low_ref, q_ref, kv_ref) = refs[:6], refs[6:]
        states = jnp.concatenate([xa[0], xb[...]], axis=0).astype(f32)
        z = normalize(states, gain_ref[...], shift_ref[...])[0].astype(bf16)
        z_ref[...] = z
        low = nt(jnp.concatenate([iq[0], ik[0], iv[0]], axis=0), z)
        low_ref[...] = low
        for i, packs in enumerate((pack_ref, side_ref)):
            for n in range(3):
                outer = packs[:rank, n * width : (n + 1) * width]
                y = project_rows(
                    ws[3 * i + n][...], z_ref[...], outer, low[n * rank : (n + 1) * rank]
                )
                if n == 0:
                    q_ref[i] = y
                else:
                    kv_ref[i, n - 1] = y

    specs = [
        placed_block((1, rows, features), lambda i, spot, *_: (spot[0], 0, 0)),
        whole((rows, features)),
        whole((1, features)),
        whole((1, features)),
    ]
    specs += [placed_block((1, rank, features), of_mine(n)) for n in range(3)]
    specs += [whole(pack.shape), whole(side.shape)] + [whole((width, features))] * 6
    outs = [
        shaped((tokens, features), bf16),
        shaped((3 * rank, tokens), f32),
        shaped((2, width, tokens), bf16),
        shaped((2, 2, width, tokens), bf16),
    ]
    return call(
        body,
        (spot, pick),
        [inputs, received, gain, shift] + inners + [pack, side] + weights,
        specs,
        outs,
        [whole(o.shape) for o in outs],
        cost=(2 * tokens * features * width * 6, 1e7, tokens),
    )


def project_far(spot, pick, z, low, received, side, parts):
    tokens, features = z.shape
    head_rows = parts[0][0].shape[1]
    width = 4 * head_rows
    rank = low.shape[0] // 3
    base = received.shape[0] - 3 * rank
    flat = [p for group in parts for p in group]

    def body(spot_ref, pick_ref, z_ref, low_ref, received_ref, side_ref, *refs):
        ins, (weight_ref, q_ref, kv_ref) = refs[:10], refs[10:]
        for i in range(2):
            group = ins[5 * i : 5 * i + 5]
            for n in range(4):
                for r in range(4):
                    at = pl.ds(pl.multiple_of((spot_ref[2] ^ r) * head_rows, 16), head_rows)
                    if r < 3:
                        weight_ref[i, n, at] = group[r][n]
                    else:
                        weight_ref[i, n, at] = group[3 + n // 2][n % 2]
        for i in range(2):
            for n in range(3):
                lanes = slice(n * width, (n + 1) * width)
                if i == 0:
                    outer = received_ref[base : base + rank, lanes]
                else:
                    outer = side_ref[3 * rank : 4 * rank, lanes]
                y = project_rows(
                    weight_ref[i, n], z_ref[...], outer, low_ref[n * rank : (n + 1) * rank]
                )
                if n == 0:
                    q_ref[i] = y
                else:
                    kv_ref[i, n - 1] = y

    operands = [z, low, received, side] + flat
    outs = [
        shaped((2, 4, width, features), bf16),
        shaped((2, width, tokens), bf16),
        shaped((2, 2, width, tokens), bf16),
    ]
    return call(
        body,
        (spot, pick),
        operands,
        [whole(o.shape) for o in operands],
        outs,
        [whole(o.shape) for o in outs],
        cost=(2 * tokens * features * width * 6, 2e7, 0),
    )


def attend(spot, lengths, q, kv, kv_side):
    _, width, tokens = q.shape
    rows = tokens // 2
    pair = 2 * HEAD_DIM
    steps = width // pair

    def body(spot_ref, length_ref, q_ref, k1, k2, v1, v2, ctx_ref, total_ref):
        bias1 = jnp.where(live_column(spot_ref, length_ref, rows, (0, 2)), 0.0, neg_fill * log2_e)
        bias2 = jnp.where(live_column(spot_ref, length_ref, rows, (1, 3)), 0.0, neg_fill * log2_e)
        for h in range(2):
            at = slice(h * HEAD_DIM, (h + 1) * HEAD_DIM)
            query = q_ref[0, at]
            s1 = tn(k1[0, 0, at], query) * (score_scale * log2_e) + bias1
            s2 = tn(k2[0, 0, at], query) * (score_scale * log2_e) + bias2
            top = jnp.maximum(jnp.max(s1, axis=0, keepdims=True), jnp.max(s2, axis=0, keepdims=True))
            p1 = jnp.exp2(s1 - top)
            p2 = jnp.exp2(s2 - top)
            total = jnp.sum(p1, axis=0, keepdims=True) + jnp.sum(p2, axis=0, keepdims=True)
            context = nn(v1[0, 0, at], p1.astype(bf16)) + nn(v2[0, 0, at], p2.astype(bf16))
            ctx_ref[0, at] = (context * (1.0 / total)).astype(bf16)
            total_ref[h] = top + jnp.log2(total)

    def own(n):
        return pl.BlockSpec((1, 1, pair, tokens), lambda h, *_: (h // steps, n, h % steps, 0))

    def beside(n):
        return pl.BlockSpec((1, 1, pair, tokens), lambda h, *_: (1 - h // steps, n, h % steps, 0))

    rows_spec = pl.BlockSpec((1, pair, tokens), lambda h, *_: (h // steps, h % steps, 0))
    return call(
        body,
        (spot, lengths),
        [q, kv, kv_side, kv, kv_side],
        [rows_spec, own(0), beside(0), own(1), beside(1)],
        [shaped(q.shape, bf16), shaped((4 * steps, 1, tokens), f32)],
        [rows_spec, pl.BlockSpec((2, 1, tokens), lambda h, *_: (h, 0, 0))],
        grid=(2 * steps,),
        cost=(2 * 2 * 2 * width * 256 // HEAD_DIM * tokens * 2 * tokens, 6e6, 0),
    )


def attend_back(spot, lengths, q, kv, kv_side, grad_context, totals, deltas, which):
    _, width, tokens = q.shape
    rows = tokens // 2
    pair = 2 * HEAD_DIM
    steps = width // pair

    def body(spot_ref, length_ref, q_ref, k1, k2, v1, v2, g_ref, total_ref, delta_ref, gq, own_ref, other_ref):
        bias1 = jnp.where(live_column(spot_ref, length_ref, rows, (0, 2)), 0.0, neg_fill * log2_e)
        bias2 = jnp.where(live_column(spot_ref, length_ref, rows, (1, 3)), 0.0, neg_fill * log2_e)
        for h in range(2):
            at = slice(h * HEAD_DIM, (h + 1) * HEAD_DIM)
            query = q_ref[0, at]
            grad = g_ref[0, at]
            grad_query = None
            for k, v, bias, out in ((k1, v1, bias1, own_ref), (k2, v2, bias2, other_ref)):
                s = tn(k[0, 0, at], query) * (score_scale * log2_e) + bias
                soft = jnp.exp2(s - total_ref[h])
                grad_soft = tn(v[0, 0, at], grad)
                grad_scores = (soft * (grad_soft - delta_ref[h])).astype(bf16)
                part = nn(k[0, 0, at], grad_scores)
                grad_query = part if grad_query is None else grad_query + part
                out[0, 0, at] = nt(query, grad_scores) * score_scale
                out[0, 1, at] = nt(grad, soft.astype(bf16))
            gq[0, at] = (grad_query * score_scale).astype(bf16)

    def own(n):
        return pl.BlockSpec((1, 1, pair, tokens), lambda h, *_: (h // steps, n, h % steps, 0))

    def beside(n):
        return pl.BlockSpec((1, 1, pair, tokens), lambda h, *_: (1 - h // steps, n, h % steps, 0))

    rows_spec = pl.BlockSpec((1, pair, tokens), lambda h, *_: (h // steps, h % steps, 0))
    grads_spec = pl.BlockSpec((1, pair, tokens), lambda h, *_: (2 * which + h // steps, h % steps, 0))
    line = pl.BlockSpec((2, 1, tokens), lambda h, *_: (h, 0, 0))
    line_at = pl.BlockSpec((2, 1, tokens), lambda h, *_: (2 * steps * which + h, 0, 0))
    both = pl.BlockSpec((1, 2, pair, tokens), lambda h, *_: (h // steps, 0, h % steps, 0))
    return call(
        body,
        (spot, lengths),
        [q, kv, kv_side, kv, kv_side, grad_context, totals, deltas],
        [rows_spec, own(0), beside(0), own(1), beside(1), grads_spec, line, line_at],
        [shaped(q.shape, bf16), shaped(kv.shape, f32), shaped(kv.shape, f32)],
        [rows_spec, both, both],
        grid=(2 * steps,),
        cost=(5 * 2 * 2 * width * 256 // HEAD_DIM * tokens * 2 * tokens, 2e7, 0),
    )


cubic = 0.044715
root = math.sqrt(2.0 / math.pi)


def feed_quarter(z_ref, gy_ref, wide_ref, thin_ref, outer_ref, inner_ref, rows_at, low_w, low_n, act_ref, grad_ref):
    features = wide_ref.shape[0]
    units = wide_ref.shape[1]
    block = 256
    outer_at, inner_at, rank = rows_at
    low_w2, low_n2 = halves(low_w), halves(low_n)

    def step(b, carry):
        at = pl.ds(pl.multiple_of(b * block, block), block)
        widened = nn(z_ref[...], wide_ref[:, at]) + tn(low_w2, twice(outer_ref[pl.ds(outer_at, rank), at]))
        grad = nt(gy_ref[...], thin_ref[at, :]) + tn(low_n2, twice(inner_ref[pl.ds(inner_at, rank), at]))
        square = widened * widened
        bend = jnp.tanh(root * widened * (1.0 + cubic * square))
        up = 0.5 * (1.0 + bend)
        act_ref[:, at] = (widened * up).astype(bf16)
        slope = up + widened * (0.5 * root) * (1.0 - bend * bend) * (1.0 + 3.0 * cubic * square)
        grad_ref[:, at] = (grad * slope).astype(bf16)
        return carry

    lax.fori_loop(0, units // block, step, 0)


def feed_sums(wide_ref, thin_ref, outer, inner, low_w, low_n, act_ref, grad_ref, sums_ref):
    branch = nn(act_ref[...], thin_ref[...])
    grad_second = nt(grad_ref[...], wide_ref[...])
    low_next = nt(inner, act_ref[...])
    grad_low = nt(outer, grad_ref[...])
    rank = outer.shape[0]
    sums_ref[:rank] = folded(nn(halves(low_w), grad_ref[...]))
    sums_ref[rank:] = folded(nn(halves(low_n), act_ref[...]))
    return branch, grad_second, low_next, grad_low


def feed_near(spot, pick, lengths, contexts, outs_w, far, packs, tables, inputs, received, cotangent, cot_side, gain, shift, dense):
    rows, features = inputs.shape[1:]
    tokens = 2 * rows
    width = contexts[0].shape[1]
    rank = tables[0].shape[1]
    pack, side = packs
    base = received.shape[0] - 3 * rank
    units = dense[0].shape[1]

    def body(spot_ref, pick_ref, length_ref, c01, c23, wo0, wo1, far_ref, pack_ref, side_ref, received_ref, oo, wi, no, xa, ca, cb, gain_ref, shift_ref, *refs):
        hbm, (hidden_ref, z_ref, gy_ref, branch_ref, second_ref, lows_ref, sums_ref) = refs[:4], refs[4:11]
        wide0, thin0, wide1, thin1, act_ref, grad_ref, sems = refs[11:]
        local = (wide0, thin0, wide1, thin1)
        copies = [pltpu.make_async_copy(hbm[n], local[n], sems.at[n]) for n in range(4)]
        for c in copies:
            c.start()
        states = jnp.concatenate([xa[0], received_ref[:rows]], axis=0).astype(f32)
        mask = live_column(spot_ref, length_ref, rows, (0, 2)).astype(f32)
        low_o = jnp.zeros((rank, tokens), f32)
        attended = jnp.zeros((tokens, features), f32)
        inner_lanes = slice(3 * width, 4 * width)
        inner_o = [
            pack_ref[:rank, inner_lanes],
            side_ref[:rank, inner_lanes],
            received_ref[base : base + rank, inner_lanes],
            side_ref[3 * rank : 4 * rank, inner_lanes],
        ]
        contexts_all = [c01[0], c01[1], c23[0], c23[1]]
        weights_all = [wo0[...], wo1[...], far_ref[0, 0], far_ref[1, 0]]
        attended = tn(jnp.concatenate(contexts_all, axis=0), jnp.concatenate(weights_all, axis=0))
        for i in range(4):
            low_o = low_o + nn(inner_o[i], contexts_all[i])
        attended = attended + tn(halves(low_o), twice(oo[0]))
        hidden = states + mask * attended
        hidden_ref[...] = hidden
        z_ref[...] = normalize(hidden, gain_ref[...], shift_ref[...])[0].astype(bf16)
        grad_in = jnp.concatenate([ca[0], cb[...]], axis=0).astype(f32)
        gy_ref[...] = (mask * grad_in).astype(bf16)
        low_w = nt(wi[0], z_ref[...])
        low_n = nt(no[0], gy_ref[...])
        lows_ref[:rank] = low_o
        lows_ref[rank : 2 * rank] = low_w
        lows_ref[2 * rank : 3 * rank] = low_n
        for i, ref in enumerate((pack_ref, side_ref)):
            wide, thin = local[2 * i], local[2 * i + 1]
            copies[2 * i].wait()
            copies[2 * i + 1].wait()
            feed_quarter(z_ref, gy_ref, wide, thin, ref, ref, (rank, 2 * rank, rank), low_w, low_n, act_ref, grad_ref)
            sums = feed_sums(
                wide, thin, ref[rank : 2 * rank], ref[2 * rank : 3 * rank], low_w, low_n, act_ref, grad_ref, sums_ref.at[i]
            )
            if i == 0:
                branch_ref[...], second_ref[...], low_next, grad_low = sums
            else:
                branch_ref[...] += sums[0]
                second_ref[...] += sums[1]
                low_next += sums[2]
                grad_low += sums[3]
        lows_ref[3 * rank : 4 * rank] = low_next
        lows_ref[4 * rank :] = grad_low

    operands = contexts + outs_w + [far, pack, side, received] + tables
    specs = [whole(c.shape) for c in contexts] + [whole(w.shape) for w in outs_w]
    specs += [placed_block((2, 1, width, features), lambda *_: (0, 3, 0, 0))]
    specs += [whole(pack.shape), whole(side.shape), whole(received.shape)]
    specs += [placed_block((1, rank, features), of_mine(n)) for n in (3, 4, 5)]
    operands += [inputs, cotangent, cot_side, gain, shift] + dense
    specs += [placed_block((1, rows, features), lambda i, spot, *_: (spot[0], 0, 0))] * 2
    specs += [whole(cot_side.shape), whole(gain.shape), whole(shift.shape)]
    specs += [pl.BlockSpec(memory_space=pl.ANY)] * 4
    outs = [
        shaped((tokens, features), f32),
        shaped((tokens, features), bf16),
        shaped((tokens, features), bf16),
        shaped((tokens, features), f32),
        shaped((tokens, features), f32),
        shaped((5 * rank, tokens), f32),
        shaped((2, 2 * rank, units), f32),
    ]
    scratch = [pltpu.VMEM(d.shape, bf16) for d in dense]
    scratch += [pltpu.VMEM((tokens, units), bf16)] * 2 + [pltpu.SemaphoreType.DMA((4,))]
    return call(
        body,
        (spot, pick, lengths),
        operands,
        specs,
        outs,
        [whole(o.shape) for o in outs],
        scratch=scratch,
        cost=(2 * tokens * features * (4 * width + 8 * units), 4e7, tokens * units * 2),
    )


def feed_far(spot, pick, lengths, near, contexts, outs_w, far, packs, tables, received, cotangent, cot_side, gain, parts):
    hidden, z, gy, branch, second, lows = near
    tokens, features = hidden.shape
    rows = tokens // 2
    width = contexts[0].shape[1]
    rank = tables[0].shape[1]
    pack, side = packs
    base = received.shape[0] - 3 * rank
    part_rows = parts[0][0].shape[0]
    units = features
    flat = [p for group in parts for p in group]
    heads = width // HEAD_DIM

    def body(spot_ref, pick_ref, length_ref, hidden_ref, z_ref, gy_ref, branch_in, second_in, lows_ref, c01, c23, wo0, wo1, far_ref, pack_ref, side_ref, received_ref, oo, wi, no, ca, cb, gain_ref, *refs):
        hbm = refs[:16]
        outa_ref, outb_ref, gh_ref, gc_ref, delta_ref, sums_ref, shared_ref, inner_ref = refs[16:24]
        wide0, thin0, wide1, thin1, act_ref, grad_ref, sems = refs[24:]
        local = (wide0, thin0, wide1, thin1)
        copies = []
        for n in range(4):
            for r in range(4):
                at = pl.ds(pl.multiple_of((spot_ref[2] ^ r) * part_rows, 16), part_rows)
                copies.append(pltpu.make_async_copy(hbm[4 * n + r], local[n].at[at], sems.at[4 * n + r]))
        for c in copies:
            c.start()
        low_w = lows_ref[rank : 2 * rank]
        low_n = lows_ref[2 * rank : 3 * rank]
        low_next = lows_ref[3 * rank : 4 * rank]
        grad_low = lows_ref[4 * rank :]
        branch, grad_second = branch_in[...], second_in[...]
        places = ((received_ref, base), (side_ref, 3 * rank))
        for i, (ref, start) in enumerate(places):
            wide, thin = local[2 * i], local[2 * i + 1]
            for c in copies[8 * i : 8 * i + 8]:
                c.wait()
            at = (start + rank, start + 2 * rank, rank)
            feed_quarter(z_ref, gy_ref, wide, thin, ref, ref, at, low_w, low_n, act_ref, grad_ref)
            sums = feed_sums(
                wide, thin, ref[start + rank : start + 2 * rank], ref[start + 2 * rank : start + 3 * rank],
                low_w, low_n, act_ref, grad_ref, sums_ref.at[i],
            )
            branch = branch + sums[0]
            grad_second = grad_second + sums[1]
            low_next = low_next + sums[2]
            grad_low = grad_low + sums[3]
        mask = live_column(spot_ref, length_ref, rows, (0, 2)).astype(f32)
        branch = branch + tn(halves(low_next), twice(no[0]))
        grad_second = grad_second + tn(halves(grad_low), twice(wi[0]))
        hidden_now = hidden_ref[...]
        output = (hidden_now + mask * branch).astype(bf16)
        outa_ref[...] = output[:rows]
        outb_ref[...] = output[rows:]
        _, unit, scaled = normalize(hidden_now, gain_ref[...], gain_ref[...])
        grad_in = jnp.concatenate([ca[0], cb[...]], axis=0).astype(f32)
        grad_hidden = grad_in + normalize_back(grad_second, unit, scaled, gain_ref[...])
        gh_ref[...] = grad_hidden
        grad_attended = (mask * grad_hidden).astype(bf16)
        act_ref[...] = grad_attended
        grad_low_o = nt(oo[0], act_ref[...])
        shared_ref[:rank] = folded(nn(halves(grad_low), z_ref[...]))
        shared_ref[rank : 2 * rank] = folded(nn(halves(lows_ref[:rank]), act_ref[...]))
        shared_ref[2 * rank :] = folded(nn(halves(low_next), gy_ref[...]))
        inner_lanes = slice(3 * width, 4 * width)
        inner_o = [
            pack_ref[:rank, inner_lanes],
            side_ref[:rank, inner_lanes],
            received_ref[base : base + rank, inner_lanes],
            side_ref[3 * rank : 4 * rank, inner_lanes],
        ]
        contexts_all = [c01[0], c01[1], c23[0], c23[1]]
        weights_all = [wo0, wo1, far_ref.at[0, 0], far_ref.at[1, 0]]
        low_o2 = halves(grad_low_o)
        for i in range(4):
            grad = (nt(weights_all[i][...], act_ref[...]) + tn(twice(inner_o[i]), low_o2)).astype(bf16)
            gc_ref[i] = grad
            product = grad.astype(f32) * contexts_all[i].astype(f32)
            for h in range(heads):
                delta_ref[heads * i + h] = jnp.sum(
                    product[h * HEAD_DIM : (h + 1) * HEAD_DIM], axis=0, keepdims=True
                )
            inner_ref[i] = folded(nt(low_o2, contexts_all[i]))

    operands = [hidden, z, gy, branch, second, lows] + contexts + outs_w + [far, pack, side, received] + tables
    specs = [whole(o.shape) for o in operands[:10]]
    specs += [placed_block((2, 1, width, features), lambda *_: (0, 3, 0, 0))]
    specs += [whole(pack.shape), whole(side.shape), whole(received.shape)]
    specs += [placed_block((1, rank, features), of_mine(n)) for n in (3, 4, 5)]
    operands += [cotangent, cot_side, gain] + flat
    specs += [placed_block((1, rows, features), lambda i, spot, *_: (spot[0], 0, 0))]
    specs += [whole(cot_side.shape), whole(gain.shape)]
    specs += [pl.BlockSpec(memory_space=pl.ANY)] * 16
    outs = [
        shaped((rows, features), bf16),
        shaped((rows, features), bf16),
        shaped((tokens, features), f32),
        shaped((4, width, tokens), bf16),
        shaped((4 * heads, 1, tokens), f32),
        shaped((2, 2 * rank, units), f32),
        shaped((3 * rank, features), f32),
        shaped((4, rank, width), f32),
    ]
    scratch = [pltpu.VMEM((features, units), bf16), pltpu.VMEM((units, features), bf16)] * 2
    scratch += [pltpu.VMEM((tokens, units), bf16)] * 2 + [pltpu.SemaphoreType.DMA((16,))]
    return call(
        body,
        (spot, pick, lengths),
        operands,
        specs,
        outs,
        [whole(o.shape) for o in outs],
        scratch=scratch,
        cost=(2 * tokens * features * (4 * width + 8 * units), 5e7, tokens * units * 2),
    )


def gather_grads(near, far, z, low, packs, received):
    tokens, features = z.shape
    rank = low.shape[0] // 3
    width = near[0].shape[1]
    pack, side = packs
    base = received.shape[0] - 3 * rank

    def body(q01, own01, side01, q23, own23, side23, z_ref, low_ref, pack_ref, side_ref, received_ref, g_ref, gl_ref, outer_ref, inner_ref):
        groups = ((q01, own01, side01), (q23, own23, side23))
        places = ((pack_ref, 0), (side_ref, 0), (received_ref, base), (side_ref, 3 * rank))
        lows = [halves(low_ref[n * rank : (n + 1) * rank]) for n in range(3)]
        total = [jnp.zeros((rank, tokens), f32) for _ in range(3)]
        for i in range(4):
            q, own, other = groups[i // 2]
            ref, start = places[i]
            for n in range(3):
                if n == 0:
                    g = q[i % 2]
                else:
                    g = (own[i % 2, n - 1] + other[1 - i % 2, n - 1]).astype(bf16)
                g_ref[i, n] = g
                lanes = slice(n * width, (n + 1) * width)
                total[n] = total[n] + nn(ref[start : start + rank, lanes], g)
                outer_ref[i, n] = folded(nt(lows[n], g))
        for n in range(3):
            gl_ref[n * rank : (n + 1) * rank] = total[n]
            inner_ref[n * rank : (n + 1) * rank] = folded(nn(halves(total[n]), z_ref[...]))

    operands = list(near) + list(far) + [z, low, pack, side, received]
    outs = [
        shaped((4, 3, width, tokens), bf16),
        shaped((3 * rank, tokens), f32),
        shaped((4, 3, rank, width), f32),
        shaped((3 * rank, features), f32),
    ]
    return call(
        body, (), operands, [whole(o.shape) for o in operands], outs, [whole(o.shape) for o in outs],
        cost=(2 * tokens * features * 3 * 256, 2e7, 0),
    )


def finish(spot, pick, g, gl, inners, weights, far, inputs, received, grad_hidden, gain):
    rows, features = inputs.shape[1:]
    tokens = 2 * rows
    width = g.shape[2]
    rank = gl.shape[0] // 3

    def body(spot_ref, pick_ref, g_ref, gl_ref, iq, ik, iv, *refs):
        ws, (far_ref, xa, xb, gh_ref, gain_ref, grada_ref, gradb_ref) = refs[:6], refs[6:]
        low = [halves(gl_ref[n * rank : (n + 1) * rank]) for n in range(3)]
        total = tn(
            jnp.concatenate(low, axis=0),
            jnp.concatenate([twice(iq[0]), twice(ik[0]), twice(iv[0])], axis=0),
        )
        for i in range(4):
            for n in range(3):
                weight = ws[3 * i + n][...] if i < 2 else far_ref[i - 2, n]
                total = total + tn(g_ref[i, n], weight)
        states = jnp.concatenate([xa[0], xb[...]], axis=0).astype(f32)
        _, unit, scaled = normalize(states, gain_ref[...], gain_ref[...])
        grad = gh_ref[...] + normalize_back(total, unit, scaled, gain_ref[...])
        grada_ref[...] = grad[:rows]
        gradb_ref[...] = grad[rows:].astype(bf16)

    operands = [g, gl] + inners + weights + [far, inputs, received, grad_hidden, gain]
    specs = [whole(g.shape), whole(gl.shape)]
    specs += [placed_block((1, rank, features), of_mine(n)) for n in range(3)]
    specs += [whole(w.shape) for w in weights]
    specs += [placed_block((2, 3, width, features), lambda *_: (0, 0, 0, 0))]
    specs += [placed_block((1, rows, features), lambda i, spot, *_: (spot[0], 0, 0))]
    specs += [whole((rows, features)), whole(grad_hidden.shape), whole(gain.shape)]
    outs = [shaped((rows, features), f32), shaped((rows, features), bf16)]
    return call(
        body, (spot, pick), operands, specs, outs, [whole(o.shape) for o in outs],
        cost=(2 * tokens * features * 12 * width, 3e7, tokens),
    )


def make_body(dp_size, tensor_size):
    def across(array):
        return swap(array, "tensor", 2, tensor_size)

    def beside(array):
        return swap(array, "tensor", 1, tensor_size)

    def along(array, bits):
        return swap(array, "dp", bits, dp_size)

    def body(
        inputs,
        cotangent,
        lengths,
        adapter_pick,
        first_gain,
        first_bias,
        query_weight,
        key_weight,
        value_weight,
        output_weight,
        second_gain,
        second_bias,
        widen_weight,
        narrow_weight,
        query_inner,
        query_outer,
        key_inner,
        key_outer,
        value_inner,
        value_outer,
        output_inner,
        output_outer,
        widen_inner,
        widen_outer,
        narrow_inner,
        narrow_outer,
    ):
        rows, features = inputs.shape[1:]
        place = lax.axis_index("tensor")
        quad = lax.axis_index("dp") & 3
        mine = place >> 1
        spot = jnp.stack([mine, 1 - mine, quad, place]).astype(jnp.int32)
        pick = adapter_pick

        def flip(array):
            return jnp.swapaxes(array, 1, 2)

        small = [query_outer, key_outer, value_outer, flip(output_inner), widen_outer, flip(narrow_inner)]
        inners = [flip(query_inner), flip(key_inner), flip(value_inner)]
        tables = [output_outer, flip(widen_inner), narrow_outer]
        gains = [v.reshape(1, -1) for v in (first_gain, first_bias, second_gain, second_bias)]
        rank = query_outer.shape[1]
        heads = [query_weight.T, key_weight.T, value_weight.T, output_weight]
        dense = [widen_weight, narrow_weight]

        send, pack = stage(spot, pick, inputs, small)
        received = across(send)
        part_heads, part_wide, part_thin, cot_send = stage_weights(spot, pick, heads, dense, cotangent)
        near_heads = [beside(w) for w in heads]
        side = beside(jnp.concatenate([pack, received[rows:]], axis=0))
        near_dense = [beside(w) for w in dense]

        far_heads = [across(part_heads)]
        far_heads += [along(far_heads[0], 1), along(far_heads[0], 2)]
        far_heads += [along(far_heads[2][:2], 1), along(far_heads[1][2:], 2)]
        far_wide = [across(part_wide)]
        far_thin = [across(part_thin)]
        cot_side = across(cot_send)
        for far, bits in ((far_wide, 1), (far_thin, 2)):
            far += [along(far[0], 1), along(far[0], 2)]
            far += [along(far[3 - bits], bits)]
        side_heads = [beside(p) for p in far_heads]
        side_wide = [beside(p) for p in far_wide]
        side_thin = [beside(p) for p in far_thin]

        z, low, q01, kv01 = project_near(
            spot, pick, inputs, received, gains[0], gains[1], inners, pack, side, heads[:3] + near_heads[:3]
        )
        kv01_side = beside(kv01)
        c01, total01 = attend(spot, lengths, q01, kv01, kv01_side)
        far, q23, kv23 = project_far(spot, pick, z, low, received, side, [far_heads, side_heads])
        kv23_side = beside(kv23)
        c23, total23 = attend(spot, lengths, q23, kv23, kv23_side)
        *near, near_sums = feed_near(
            spot, pick, lengths, [c01, c23], [heads[3], near_heads[3]], far, [pack, side], tables,
            inputs, received, cotangent, cot_side, gains[2], gains[3], dense + near_dense,
        )
        outa, outb, grad_hidden, grad_context, deltas, far_sums, shared_early, inner_sums = feed_far(
            spot, pick, lengths, near, [c01, c23], [heads[3], near_heads[3]], far, [pack, side], tables,
            received, cotangent, cot_side, gains[2], [far_wide, far_thin, side_wide, side_thin],
        )
        out_side = across(outb)
        gq01, own01, other01 = attend_back(
            spot, lengths, q01, kv01, kv01_side, grad_context, total01, deltas, 0
        )
        side01 = beside(other01)
        gq23, own23, other23 = attend_back(
            spot, lengths, q23, kv23, kv23_side, grad_context, total23, deltas, 1
        )
        side23 = beside(other23)
        g, gl, outer_sums, shared_late = gather_grads(
            (gq01, own01, side01), (gq23, own23, side23), z, low, (pack, side), received
        )
        grada, gradb = finish(
            spot, pick, g, gl, inners, heads[:3] + near_heads[:3], far, inputs, received, grad_hidden, gains[0]
        )
        grad_side = across(gradb)

        def pair_up(first, second):
            pair = jnp.stack([first, second.astype(first.dtype)])
            return jnp.where(mine == 0, pair, pair[::-1])

        output = pair_up(outa, out_side)
        input_grad = pair_up(grada, grad_side)

        core = place & 1
        half = features // 2
        picks = jnp.zeros((8, features), f32).at[0, :6].set(pick[mine].astype(f32))

        def reduce(quarters, shared):
            count = quarters[0].shape[0]
            keep = lax.dynamic_slice_in_dim(shared, core * half, half, 1)
            give = lax.dynamic_slice_in_dim(shared, (1 - core) * half, half, 1)

            def packed(a, b, s):
                s = jnp.concatenate([s[: s.shape[0] // 2], s[s.shape[0] // 2 :]], axis=1)
                return jnp.concatenate([a, b, s], axis=0)

            moved = beside(packed(quarters[1], quarters[3], give))
            kept = packed(quarters[0], quarters[2], keep) + moved
            here = jnp.concatenate([kept[:count], kept[2 * count :], picks], axis=0).astype(bf16)
            there = jnp.concatenate([kept[count:], picks], axis=0).astype(bf16)
            every = jnp.stack([here, across(there)])
            bits = 1
            while bits < min(dp_size, 8):
                every = jnp.concatenate([every, along(every, bits)], axis=0)
                bits *= 2
            hot = (
                every[:, -8, :6, None].astype(jnp.int32) == jnp.arange(query_inner.shape[0])
            ).astype(bf16)
            s = every[:, count:-8]
            return every[:, :count], jnp.concatenate([s[..., :half], s[..., half:]], axis=1), hot

        def spread(hot, number, values):
            table = jnp.einsum("ce,crw->erw", hot[:, number], values, preferred_element_type=f32)
            bits = 8
            while bits < dp_size:
                table = table + along(table, bits)
                bits *= 2
            return table

        sums = [near_sums[0], near_sums[1], far_sums[0], far_sums[1]]
        wide, shared, hot = reduce(sums, shared_early)
        widen_outer_grad = spread(hot, 4, wide[:, :rank])
        narrow_inner_grad = spread(hot, 5, wide[:, rank:])
        early = [
            spread(hot, 4, shared[:, :rank]),
            spread(hot, 3, shared[:, rank : 2 * rank]),
            spread(hot, 5, shared[:, 2 * rank :]),
        ]
        quarters = [
            jnp.concatenate([outer_sums[i, 0], outer_sums[i, 1], outer_sums[i, 2], inner_sums[i]], axis=1)
            for i in range(4)
        ]
        thin, shared, hot = reduce(quarters, shared_late)
        width = query_outer.shape[2]
        heads_grads = [spread(hot, n, thin[:, :, n * width : (n + 1) * width]) for n in range(4)]
        late = [spread(hot, n, shared[:, n * rank : (n + 1) * rank]) for n in range(3)]

        def complete(group):
            group = jnp.stack(group)
            moved = beside(group)
            first = jnp.where(core == 0, group, moved)
            second = jnp.where(core == 0, moved, group)
            return jnp.concatenate([first, second], axis=-1)

        early = complete(early)
        late = complete(late)
        return (
            output,
            input_grad,
            flip(late[0]),
            heads_grads[0],
            flip(late[1]),
            heads_grads[1],
            flip(late[2]),
            heads_grads[2],
            flip(heads_grads[3]),
            early[1],
            flip(early[0]),
            widen_outer_grad,
            flip(narrow_inner_grad),
            early[2],
        )

    return body


def solution(mesh):
    placed = (
        P("dp", "tensor", None),
        P("dp", "tensor", None),
        P("dp"),
        P("dp", None),
        P(),
        P(),
        P(None, "tensor"),
        P(None, "tensor"),
        P(None, "tensor"),
        P("tensor", None),
        P(),
        P(),
        P(None, "tensor"),
        P("tensor", None),
        P(),
        P(None, None, "tensor"),
        P(),
        P(None, None, "tensor"),
        P(),
        P(None, None, "tensor"),
        P(None, "tensor", None),
        P(),
        P(),
        P(None, None, "tensor"),
        P(None, "tensor", None),
        P(),
    )
    return jax.shard_map(
        make_body(mesh.shape["dp"], mesh.shape["tensor"]),
        mesh=mesh,
        in_specs=placed,
        out_specs=(
            P("dp", "tensor", None),
            P("dp", "tensor", None),
            P(),
            P(None, None, "tensor"),
            P(),
            P(None, None, "tensor"),
            P(),
            P(None, None, "tensor"),
            P(None, "tensor", None),
            P(),
            P(),
            P(None, None, "tensor"),
            P(None, "tensor", None),
            P(),
        ),
        check_vma=False,
    )
```

time: 1020 us -> 484 us (0.47)
  waiting for transfers between devices: 550 us -> 214 us
  matrix products: 304 us -> 4.35 us
  Pallas kernels: 0 us -> 173 us
  local copies, waits for them, and re-layouts: 88.3 us -> 30.6 us
  starting transfers between devices: 0.84 us -> 42.9 us
  other arithmetic: 51 us -> 9.06 us
  between operations: 15.4 us -> 2 us
    dot_general x100 -> x12, matrix products: 304 us -> 4.35 us  [spread(): jnp.einsum('ce,crw->erw', hot[:, number], values, preferred_element_type=...]
    reduce_scatter x4 -> x0, waiting for transfers between devices: 242 us -> none  [the longest x1 85.3 us: body(): lax.psum_scatter(attended_part, 'tensor', scatter_dimension=1, tiled=True)]
    ppermute x0 -> x53, waiting for transfers between devices: none -> 214 us  [swap(): return lax.ppermute(array, axis, [(i, i ^ bits) for i in range(size)])]
    psum x2 -> x0, waiting for transfers between devices: 204 us -> none  [the longest x1 144 us: body(): lax.psum((query_inner_part, key_inner_part, value_inner_part, output_oute...]
    pallas_call x0 -> x12, Pallas kernels: none -> 173 us  [call(): pl.pallas_call(body, grid_spec=pltpu.PrefetchScalarGridSpec(num_scalar_pr...]
    all_gather x4 -> x0, waiting for transfers between devices: 103 us -> none  [the longest x1 32.9 us: body(): lax.all_gather(second_normed.astype(jnp.bfloat16), 'tensor', axis=1, tile...]
    ppermute x0 -> x53, starting transfers between devices: none -> 42.9 us  [swap(): return lax.ppermute(array, axis, [(i, i ^ bits) for i in range(size)])]
    another operation x16 -> x1, local copies, waits for them, and re-layouts: 29.9 us -> 0.01 us  [the longest x3 7.01 us: body(): context = jnp.stack(context_list)]
  transfers between devices with their start and end apart: 10 -> 53, of which waited for: 10 -> 16; matrix products, arithmetic and copies ran while one was open for 15% -> 6% of each run, Pallas kernels for 0% -> 28%
where the time goes in v1:
time: 484 us; the launch traced here: 476 us
  waiting for transfers between devices  214 us (44%)
  Pallas kernels  173 us (36%)
  starting transfers between devices  42.9 us (9%)
  local copies, waits for them, and re-layouts  30.6 us (6%)
  other arithmetic  9.06 us (2%)
    ppermute x53, waiting for transfers between devices, swap(): return lax.ppermute(array, axis, [(i, i ^ bits) for i in range(size)])  214 us
    pallas_call x12, Pallas kernels, call(): pl.pallas_call(body, grid_spec=pltpu.PrefetchScalarGridSpec(num_scalar_pr...  173 us
    ppermute x53, starting transfers between devices, swap(): return lax.ppermute(array, axis, [(i, i ^ bits) for i in range(size)])  42.9 us
    unnamed x112, local copies, waits for them, and re-layouts  17 us
  transfers between devices with their start and end apart: 53, of which 16 were waited for; matrix products, arithmetic and copies ran while one was open for 6% of the time, Pallas kernels for 28%

profile of v1, /device:TPU:0, one launch (start us, length us, event | category | flops | bytes accessed | tf_op | source)
XLA Modules:
  0.0 476.0 jit_solution(10376564937753822824)
XLA Ops:
  7.2 4.6 shard_map.356
  14.0 25.7 %collective-permute-done.18.cb = bf16[256,1280]{1,0:T(8,128)(2,1)} collective-permute-done((bf16[256,1280]{1,0:T(8,128)(2,1)}, bf16[256,1280]{1,0:T(8,128)(2,1)}, u32[]{:S(2)}, u32[]{:S(2)}) %collective-permute-start.18) | collective-permute-done | bytes 655392 | tf_op jit(solution)/shard_map/ppermute | solution.py:20
  42.3 14.8 %collective-permute-done.6.refs_0_ = bf16[4,80,1280]{2,1,0:T(8,128)(2,1)S(1)} collective-permute-done((bf16[4,80,1280]{2,1,0:T(8,128)(2,1)}, bf16[4,80,1280]{2,1,0:T(8,128)(2,1)S(1)}, u32[]{:S(2)}, u32[]{:S(2)}) %collective-permute-start.6) | collective-permute-done | bytes 819232 | tf_op jit(solution)/shard_map/ppermute | solution.py:20
  63.2 11.6 %collective-permute-done.21.refs_0_ = bf16[320,1280]{1,0:T(8,128)(2,1)} collective-permute-done((bf16[320,1280]{1,0:T(8,128)(2,1)}, bf16[320,1280]{1,0:T(8,128)(2,1)}, u32[]{:S(2)}, u32[]{:S(2)}) %collective-permute-start.21) | collective-permute-done | bytes 819232 | tf_op jit(solution)/shard_map/ppermute | solution.py:20
  77.1 14.4 %collective-permute-done.25.refs_4_ = bf16[320,1280]{1,0:T(8,128)(2,1)} collective-permute-done((bf16[320,1280]{1,0:T(8,128)(2,1)}, bf16[320,1280]{1,0:T(8,128)(2,1)}, u32[]{:S(2)}, u32[]{:S(2)}) %collective-permute-start.25) | collective-permute-done | bytes 819232 | tf_op jit(solution)/shard_map/ppermute | solution.py:20
  95.5 24.4 %collective-permute-done.9.refs_3_ = bf16[2,80,1280]{2,1,0:T(8,128)(2,1)S(1)} collective-permute-done((bf16[2,80,1280]{2,1,0:T(8,128)(2,1)S(1)}, bf16[2,80,1280]{2,1,0:T(8,128)(2,1)S(1)}, u32[]{:S(2)}, u32[]{:S(2)}) %collective-permute-start.9) | collective-permute-done | bytes 409632 | tf_op jit(solution)/shard_map/ppermute | solution.py:20
  130.1 9.1 %shard_map.354 = (bf16[512,1280]{1,0:T(8,128)(2,1)}, f32[48,512]{1,0:T(8,128)}, bf16[2,320,512]{2,1,0:T(8,128)(2,1)}, bf16[2,2,320,512]{3,2,1,0:T(8,128)(2,1)}) custom-call(s32[4]{0:T(128)} %pad_add_fusion.spot_ref, s32[2,6]{1,0:T(2,128)} %pick_ref.13, bf16[2,256,1280]{2,1,0:T(8,128)(2,1)} %refs_7_.3, bf16[304,1280]{1,0:T(8,128)(2,1)} %copy-done, ...), custom_call_target="tpu_custom_call" | custom-call | flops 2516582400 | bytes 10000000 | tf_op jit(solution)/shard_map/pallas_call | solution.py:82
  139.3 9.1 %shard_map.357 = (bf16[2,4,320,1280]{3,2,1,0:T(8,128)(2,1)}, bf16[2,320,512]{2,1,0:T(8,128)(2,1)}, bf16[2,2,320,512]{3,2,1,0:T(8,128)(2,1)}) custom-call(s32[4]{0:T(128)} %pad_add_fusion.spot_ref, s32[2,6]{1,0:T(2,128)} %pick_ref.13, bf16[512,1280]{1,0:T(8,128)(2,1)} %get-tuple-element.75.z_ref, f32[48,512]{1,0:T(8,128)} %get-tuple-element.76.low_ref, ...), custom_call_target="tpu_custom_call" | custom-call | flops 2516582400 | bytes 20000000 | tf_op jit(solution)/shard_map/pallas_call | solution.py:82
  149.1 5.8 %collective-permute-done.33.refs_12_ = bf16[320,1280]{1,0:T(8,128)(2,1)} collective-permute-done((bf16[320,1280]{1,0:T(8,128)(2,1)}, bf16[320,1280]{1,0:T(8,128)(2,1)}, u32[]{:S(2)}, u32[]{:S(2)}) %collective-permute-start.33) | collective-permute-done | bytes 819232 | tf_op jit(solution)/shard_map/ppermute | solution.py:20
  157.2 10.6 %shard_map.355 = (bf16[2,320,512]{2,1,0:T(8,128)(2,1)}, f32[8,1,512]{2,1,0:T(1,128)}) custom-call(s32[4]{0:T(128)} %pad_add_fusion.spot_ref, s32[2]{0:T(128)} %length_ref.11, bf16[2,320,512]{2,1,0:T(8,128)(2,1)} %get-tuple-element.72.q_ref, bf16[2,2,320,512]{3,2,1,0:T(8,128)(2,1)} %get-tuple-element.73.k1.v1, bf16[2,2,320,512]{3,2,1,0:T(8,128)(2,1)} %copy-done.29, ...), custom_call_target="tpu_custom_call" | custom-call | flops 4294967296 | bytes 6000000 | tf_op jit(solution)/shard_map/pallas_call | solution.py:82
  167.8 10.5 %shard_map.358 = (bf16[2,320,512]{2,1,0:T(8,128)(2,1)}, f32[8,1,512]{2,1,0:T(1,128)}) custom-call(s32[4]{0:T(128)} %pad_add_fusion.spot_ref, s32[2]{0:T(128)} %length_ref.11, bf16[2,320,512]{2,1,0:T(8,128)(2,1)} %get-tuple-element.78.q_ref, bf16[2,2,320,512]{3,2,1,0:T(8,128)(2,1)} %get-tuple-element.79.k1.v1, ...), custom_call_target="tpu_custom_call" | custom-call | flops 4294967296 | bytes 6000000 | tf_op jit(solution)/shard_map/pallas_call | solution.py:82
  179.5 30.6 %shard_map.359 = (f32[512,1280]{1,0:T(8,128)}, bf16[512,1280]{1,0:T(8,128)(2,1)}, bf16[512,1280]{1,0:T(8,128)(2,1)}, f32[512,1280]{1,0:T(8,128)}, f32[512,1280]{...) custom-call(s32[4]{0:T(128)} %pad_add_fusion.spot_ref, s32[2,6]{1,0:T(2,128)} %pick_ref.13, s32[2]{0:T(128)} %length_ref.11, ...), custom_call_target="tpu_custom_call" | custom-call | flops 15099494400 | bytes 40000000 | tf_op jit(solution)/shard_map/pallas_call | solution.py:82
  211.7 37.8 %shard_map.360 = (bf16[256,1280]{1,0:T(8,128)(2,1)}, bf16[256,1280]{1,0:T(8,128)(2,1)}, f32[512,1280]{1,0:T(8,128)}, bf16[4,320,512]{2,1,0:T(8,128)(2,1)}, f32[1...) custom-call(s32[4]{0:T(128)} %pad_add_fusion.spot_ref, ...), custom_call_target="tpu_custom_call" | custom-call | flops 15099494400 | bytes 50000000 | tf_op jit(solution)/shard_map/pallas_call | solution.py:82
  252.0 15.6 %shard_map.362 = (bf16[2,320,512]{2,1,0:T(8,128)(2,1)}, f32[2,2,320,512]{3,2,1,0:T(8,128)}, f32[2,2,320,512]{3,2,1,0:T(8,128)}) custom-call(s32[4]{0:T(128)} %pad_add_fusion.spot_ref, s32[2]{0:T(128)} %length_ref.11, bf16[2,320,512]{2,1,0:T(8,128)(2,1)} %get-tuple-element.78.q_ref, bf16[2,2,320,512]{3,2,1,0:T(8,128)(2,1)} %get-tuple-element.79.k1.v1, ...), custom_call_target="tpu_custom_call" | custom-call | flops 10737418240 | bytes 20000000 | tf_op jit(solution)/shard_map/pallas_call | solution.py:82
  267.8 15.9 %shard_map.361 = (bf16[2,320,512]{2,1,0:T(8,128)(2,1)}, f32[2,2,320,512]{3,2,1,0:T(8,128)}, f32[2,2,320,512]{3,2,1,0:T(8,128)}) custom-call(s32[4]{0:T(128)} %pad_add_fusion.spot_ref, s32[2]{0:T(128)} %length_ref.11, bf16[2,320,512]{2,1,0:T(8,128)(2,1)} %get-tuple-element.72.q_ref, bf16[2,2,320,512]{3,2,1,0:T(8,128)(2,1)} %get-tuple-element.73.k1.v1, ...), custom_call_target="tpu_custom_call" | custom-call | flops 10737418240 | bytes 20000000 | tf_op jit(solution)/shard_map/pallas_call | solution.py:82
  286.3 18.3 %collective-permute-done.48 = bf16[64,1280]{1,0:T(8,128)(2,1)S(1)} collective-permute-done((bf16[64,1280]{1,0:T(8,128)(2,1)S(1)}, bf16[64,1280]{1,0:T(8,128)(2,1)S(1)}, u32[]{:S(2)}, u32[]{:S(2)}) %collective-permute-start.48) | collective-permute-done | bytes 163872 | tf_op jit(solution)/shard_map/ppermute | solution.py:20
  306.3 7.3 %collective-permute-done.49 = bf16[2,64,1280]{2,1,0:T(8,128)(2,1)S(1)} collective-permute-done((bf16[2,64,1280]{2,1,0:T(8,128)(2,1)S(1)}, bf16[2,64,1280]{2,1,0:T(8,128)(2,1)S(1)}, u32[]{:S(2)}, u32[]{:S(2)}) %collective-permute-start.49) | collective-permute-done | bytes 327712 | tf_op jit(solution)/shard_map/ppermute | solution.py:20
  316.6 12.3 %collective-permute-done.50 = bf16[4,64,1280]{2,1,0:T(8,128)(2,1)S(1)} collective-permute-done((bf16[4,64,1280]{2,1,0:T(8,128)(2,1)S(1)}, bf16[4,64,1280]{2,1,0:T(8,128)(2,1)S(1)}, u32[]{:S(2)}, u32[]{:S(2)}) %collective-permute-start.50) | collective-permute-done | bytes 655392 | tf_op jit(solution)/shard_map/ppermute | solution.py:20
  334.1 8.7 %shard_map.363 = (bf16[4,3,320,512]{3,2,1,0:T(8,128)(2,1)}, f32[48,512]{1,0:T(8,128)}, f32[4,3,16,320]{3,2,1,0:T(8,128)}, f32[48,1280]{1,0:T(8,128)}) custom-call(bf16[2,320,512]{2,1,0:T(8,128)(2,1)} %get-tuple-element.96.q01, f32[2,2,320,512]{3,2,1,0:T(8,128)} %get-tuple-element.97.own01, f32[2,2,320,512]{3,2,1,0:T(8,128)} %collective-permute-done.38.side01, ...), custom_call_target="tpu_custom_call" | custom-call | flops 1006632960 | bytes 20000000 | tf_op jit(solution)/shard_map/pallas_call | solution.py:82
  346.2 17.9 %shard_map.364 = (f32[256,1280]{1,0:T(8,128)}, bf16[256,1280]{1,0:T(8,128)(2,1)}) custom-call(s32[4]{0:T(128)} %pad_add_fusion.spot_ref, s32[2,6]{1,0:T(2,128)} %pick_ref.13, bf16[4,3,320,512]{3,2,1,0:T(8,128)(2,1)} %get-tuple-element.103.g_ref, f32[48,512]{1,0:T(8,128)} %get-tuple-element.104.gl_ref, bf16[8,16,1280]{2,1,0:T(8,128)(2,1)} %bitcast.170, ...), custom_call_target="tpu_custom_call" | custom-call | flops 5033164800 | bytes 30000000 | tf_op jit(solution)/shard_map/pallas_call | solution.py:82
  365.8 21.6 %collective-permute-done.51 = bf16[8,64,1280]{2,1,0:T(8,128)(2,1)} collective-permute-done((bf16[8,64,1280]{2,1,0:T(8,128)(2,1)}, bf16[8,64,1280]{2,1,0:T(8,128)(2,1)}, u32[]{:S(2)}, u32[]{:S(2)}) %collective-permute-start.51) | collective-permute-done | bytes 1310752 | tf_op jit(solution)/shard_map/ppermute | solution.py:20
  405.1 5.7 %collective-permute-done.43 = bf16[2,48,1280]{2,1,0:T(8,128)(2,1)S(1)} collective-permute-done((bf16[2,48,1280]{2,1,0:T(8,128)(2,1)S(1)}, bf16[2,48,1280]{2,1,0:T(8,128)(2,1)S(1)}, u32[]{:S(2)}, u32[]{:S(2)}) %collective-permute-start.43) | collective-permute-done | bytes 245792 | tf_op jit(solution)/shard_map/ppermute | solution.py:20
  414.5 7.9 %collective-permute-done.44 = bf16[4,48,1280]{2,1,0:T(8,128)(2,1)S(1)} collective-permute-done((bf16[4,48,1280]{2,1,0:T(8,128)(2,1)S(1)}, bf16[4,48,1280]{2,1,0:T(8,128)(2,1)S(1)}, u32[]{:S(2)}, u32[]{:S(2)}) %collective-permute-start.44) | collective-permute-done | bytes 491552 | tf_op jit(solution)/shard_map/ppermute | solution.py:20
  428.3 37.4 %collective-permute-done.45 = bf16[8,48,1280]{2,1,0:T(8,128)(2,1)S(1)} collective-permute-done((bf16[8,48,1280]{2,1,0:T(8,128)(2,1)S(1)}, bf16[8,48,1280]{2,1,0:T(8,128)(2,1)S(1)}, u32[]{:S(2)}, u32[]{:S(2)}) %collective-permute-start.45) | collective-permute-done | bytes 983072 | tf_op jit(solution)/shard_map/ppermute | solution.py:20
  (287 shorter events, 96.6 us)
Async XLA Ops:
  4.2 35.5 %collective-permute-start = (bf16[304,1280]{1,0:T(8,128)(2,1)}, bf16[304,1280]{1,0:T(8,128)(2,1)S(1)}, u32[]{:S(2)}, u32[]{:S(2)}) collective-permute-start(bf16[304,1280]{1,0:T(8,128)(2,1)} %get-tuple-element.70), channel_id=1, source_target_pairs={{0,2},{1,3},{2,0},{3,1},{4,6},{5,7},{6,4},{7,5},{8,10},{9,11},{10,... | collective-permute-start | bytes 2334728 | tf_op jit(solution)/shard_map/ppermute | solution.py:20
  11.9 45.3 %collective-permute-start.6 = (bf16[4,80,1280]{2,1,0:T(8,128)(2,1)}, bf16[4,80,1280]{2,1,0:T(8,128)(2,1)S(1)}, u32[]{:S(2)}, u32[]{:S(2)}) collective-permute-start(bf16[4,80,1280]{2,1,0:T(8,128)(2,1)} %get-tuple-element.77), channel_id=1, source_target_pairs={{0,2},{1,3},{2,0},{3,1},{4,6},{5,7},{6,4},{7,5},{8,10},{9,11},{10,... | collective-permute-start | bytes 2457608 | tf_op jit(solution)/shard_map/ppermute | solution.py:20
  13.8 45.5 %collective-permute-start.3 = (bf16[320,1280]{1,0:T(8,128)(2,1)S(1)}, bf16[320,1280]{1,0:T(8,128)(2,1)S(1)}, u32[]{:S(2)}, u32[]{:S(2)}) collective-permute-start(bf16[320,1280]{1,0:T(8,128)(2,1)S(1)} %bitcast.151), channel_id=1, source_target_pairs={{0,1},{1,0},{2,3},{3,2},{4,5},{5,4},{6,7},{7,6},{8,9},{9,8},{10,11... | collective-permute-start | bytes 2457608 | tf_op jit(solution)/shard_map/ppermute | solution.py:20
  40.3 34.5 %collective-permute-start.21 = (bf16[320,1280]{1,0:T(8,128)(2,1)}, bf16[320,1280]{1,0:T(8,128)(2,1)}, u32[]{:S(2)}, u32[]{:S(2)}) collective-permute-start(bf16[320,1280]{1,0:T(8,128)(2,1)} %get-tuple-element.89), channel_id=1, source_target_pairs={{0,2},{1,3},{2,0},{3,1},{4,6},{5,7},{6,4},{7,5},{8,10},{9,11},{10,... | collective-permute-start | bytes 2457608 | tf_op jit(solution)/shard_map/ppermute | solution.py:20
  59.3 32.2 %collective-permute-start.25 = (bf16[320,1280]{1,0:T(8,128)(2,1)}, bf16[320,1280]{1,0:T(8,128)(2,1)}, u32[]{:S(2)}, u32[]{:S(2)}) collective-permute-start(bf16[320,1280]{1,0:T(8,128)(2,1)} %get-tuple-element.90), channel_id=1, source_target_pairs={{0,2},{1,3},{2,0},{3,1},{4,6},{5,7},{6,4},{7,5},{8,10},{9,11},{10,... | collective-permute-start | bytes 2457608 | tf_op jit(solution)/shard_map/ppermute | solution.py:20
  60.8 32.5 %collective-permute-start.7 = (bf16[4,80,1280]{2,1,0:T(8,128)(2,1)S(1)}, bf16[4,80,1280]{2,1,0:T(8,128)(2,1)S(1)}, u32[]{:S(2)}, u32[]{:S(2)}) collective-permute-start(bf16[4,80,1280]{2,1,0:T(8,128)(2,1)S(1)} %collective-permute-done.6.refs_0_), channel_id=1, source_target_pairs={{0,4},{4,0},{8,12},{12,8},{16,20},{20,16},{24,28},{28,24},{1,5},{5... | collective-permute-start | bytes 2457608 | tf_op jit(solution)/shard_map/ppermute | solution.py:20
  63.2 32.3 %collective-permute-start.11 = (bf16[4,80,1280]{2,1,0:T(8,128)(2,1)S(1)}, bf16[4,80,1280]{2,1,0:T(8,128)(2,1)S(1)}, u32[]{:S(2)}, u32[]{:S(2)}) collective-permute-start(bf16[4,80,1280]{2,1,0:T(8,128)(2,1)S(1)} %collective-permute-done.6.refs_0_), channel_id=1, source_target_pairs={{0,1},{1,0},{2,3},{3,2},{4,5},{5,4},{6,7},{7,6},{8,9},{9,8},{10,11... | collective-permute-start | bytes 2457608 | tf_op jit(solution)/shard_map/ppermute | solution.py:20
  74.8 45.2 %collective-permute-start.23 = (bf16[320,1280]{1,0:T(8,128)(2,1)}, bf16[320,1280]{1,0:T(8,128)(2,1)S(1)}, u32[]{:S(2)}, u32[]{:S(2)}) collective-permute-start(bf16[320,1280]{1,0:T(8,128)(2,1)} %collective-permute-done.21.refs_0_), channel_id=1, source_target_pairs={{0,8},{4,12},{8,0},{12,4},{16,24},{20,28},{24,16},{28,20},{1,9},{5... | collective-permute-start | bytes 2457608 | tf_op jit(solution)/shard_map/ppermute | solution.py:20
  91.5 29.1 %collective-permute-start.26 = (bf16[320,1280]{1,0:T(8,128)(2,1)}, bf16[320,1280]{1,0:T(8,128)(2,1)S(1)}, u32[]{:S(2)}, u32[]{:S(2)}) collective-permute-start(bf16[320,1280]{1,0:T(8,128)(2,1)} %collective-permute-done.25.refs_4_), channel_id=1, source_target_pairs={{0,4},{4,0},{8,12},{12,8},{16,20},{20,16},{24,28},{28,24},{1,5},{5... | collective-permute-start | bytes 2457608 | tf_op jit(solution)/shard_map/ppermute | solution.py:20
  95.5 30.0 %collective-permute-start.12 = (bf16[4,80,1280]{2,1,0:T(8,128)(2,1)S(1)}, bf16[4,80,1280]{2,1,0:T(8,128)(2,1)S(1)}, u32[]{:S(2)}, u32[]{:S(2)}) collective-permute-start(bf16[4,80,1280]{2,1,0:T(8,128)(2,1)S(1)} %collective-permute-done.7.refs_1_), channel_id=1, source_target_pairs={{0,1},{1,0},{2,3},{3,2},{4,5},{5,4},{6,7},{7,6},{8,9},{9,8},{10,11... | collective-permute-start | bytes 2457608 | tf_op jit(solution)/shard_map/ppermute | solution.py:20
  120.6 58.4 %collective-permute-start.19 = (bf16[1280,1280]{1,0:T(8,128)(2,1)}, bf16[1280,1280]{1,0:T(8,128)(2,1)}, u32[]{:S(2)}, u32[]{:S(2)}) collective-permute-start(bf16[1280,1280]{1,0:T(8,128)(2,1)} %refs_0_.3), channel_id=1, source_target_pairs={{0,1},{1,0},{2,3},{3,2},{4,5},{5,4},{6,7},{7,6},{8,9},{9,8},{10,11... | collective-permute-start | bytes 9830408 | tf_op jit(solution)/shard_map/ppermute | solution.py:20
  121.7 57.7 %collective-permute-start.20 = (bf16[1280,1280]{1,0:T(8,128)(2,1)}, bf16[1280,1280]{1,0:T(8,128)(2,1)}, u32[]{:S(2)}, u32[]{:S(2)}) collective-permute-start(bf16[1280,1280]{1,0:T(8,128)(2,1)} %refs_1_.3), channel_id=1, source_target_pairs={{0,1},{1,0},{2,3},{3,2},{4,5},{5,4},{6,7},{7,6},{8,9},{9,8},{10,11... | collective-permute-start | bytes 9830408 | tf_op jit(solution)/shard_map/ppermute | solution.py:20
  178.3 31.9 %collective-permute-start.34 = (bf16[320,1280]{1,0:T(8,128)(2,1)S(1)}, bf16[320,1280]{1,0:T(8,128)(2,1)S(1)}, u32[]{:S(2)}, u32[]{:S(2)}) collective-permute-start(bf16[320,1280]{1,0:T(8,128)(2,1)S(1)} %copy-done.33), channel_id=1, source_target_pairs={{0,1},{1,0},{2,3},{3,2},{4,5},{5,4},{6,7},{7,6},{8,9},{9,8},{10,11... | collective-permute-start | bytes 2457608 | tf_op jit(solution)/shard_map/ppermute | solution.py:20
  178.5 31.7 %collective-permute-start.30 = (bf16[320,1280]{1,0:T(8,128)(2,1)}, bf16[320,1280]{1,0:T(8,128)(2,1)S(1)}, u32[]{:S(2)}, u32[]{:S(2)}) collective-permute-start(bf16[320,1280]{1,0:T(8,128)(2,1)} %collective-permute-done.22.refs_1_), channel_id=1, source_target_pairs={{0,1},{1,0},{2,3},{3,2},{4,5},{5,4},{6,7},{7,6},{8,9},{9,8},{10,11... | collective-permute-start | bytes 2457608 | tf_op jit(solution)/shard_map/ppermute | solution.py:20
  178.9 31.4 %collective-permute-start.35 = (bf16[320,1280]{1,0:T(8,128)(2,1)}, bf16[320,1280]{1,0:T(8,128)(2,1)S(1)}, u32[]{:S(2)}, u32[]{:S(2)}) collective-permute-start(bf16[320,1280]{1,0:T(8,128)(2,1)} %collective-permute-done.27.refs_6_), channel_id=1, source_target_pairs={{0,1},{1,0},{2,3},{3,2},{4,5},{5,4},{6,7},{7,6},{8,9},{9,8},{10,11... | collective-permute-start | bytes 2457608 | tf_op jit(solution)/shard_map/ppermute | solution.py:20
  179.0 31.2 %collective-permute-start.32 = (bf16[320,1280]{1,0:T(8,128)(2,1)}, bf16[320,1280]{1,0:T(8,128)(2,1)}, u32[]{:S(2)}, u32[]{:S(2)}) collective-permute-start(bf16[320,1280]{1,0:T(8,128)(2,1)} %collective-permute-done.24.refs_3_), channel_id=1, source_target_pairs={{0,1},{1,0},{2,3},{3,2},{4,5},{5,4},{6,7},{7,6},{8,9},{9,8},{10,11... | collective-permute-start | bytes 2457608 | tf_op jit(solution)/shard_map/ppermute | solution.py:20
  179.4 30.9 %collective-permute-start.36 = (bf16[320,1280]{1,0:T(8,128)(2,1)S(1)}, bf16[320,1280]{1,0:T(8,128)(2,1)}, u32[]{:S(2)}, u32[]{:S(2)}) collective-permute-start(bf16[320,1280]{1,0:T(8,128)(2,1)S(1)} %collective-permute-done.28.refs_7_), channel_id=1, source_target_pairs={{0,1},{1,0},{2,3},{3,2},{4,5},{5,4},{6,7},{7,6},{8,9},{9,8},{10,11... | collective-permute-start | bytes 2457608 | tf_op jit(solution)/shard_map/ppermute | solution.py:20
  251.6 34.0 %collective-permute-start.47 = (f32[88,1280]{1,0:T(8,128)S(1)}, f32[88,1280]{1,0:T(8,128)S(1)}, u32[]{:S(2)}, u32[]{:S(2)}) collective-permute-start(f32[88,1280]{1,0:T(8,128)S(1)} %maximum_maximum_fusion), channel_id=1, source_target_pairs={{0,1},{1,0},{2,3},{3,2},{4,5},{5,4},{6,7},{7,6},{8,9},{9,8},{10,11... | collective-permute-start | bytes 1351688 | tf_op jit(solution)/shard_map/ppermute | solution.py:20
  267.6 64.9 %collective-permute-start.39 = (f32[2,2,320,512]{3,2,1,0:T(8,128)}, f32[2,2,320,512]{3,2,1,0:T(8,128)S(1)}, u32[]{:S(2)}, u32[]{:S(2)}) collective-permute-start(f32[2,2,320,512]{3,2,1,0:T(8,128)} %get-tuple-element.102), channel_id=1, source_target_pairs={{0,1},{1,0},{2,3},{3,2},{4,5},{5,4},{6,7},{7,6},{8,9},{9,8},{10,11... | collective-permute-start | bytes 7864328 | tf_op jit(solution)/shard_map/ppermute | solution.py:20
  283.6 48.9 %collective-permute-start.38 = (f32[2,2,320,512]{3,2,1,0:T(8,128)}, f32[2,2,320,512]{3,2,1,0:T(8,128)}, u32[]{:S(2)}, u32[]{:S(2)}) collective-permute-start(f32[2,2,320,512]{3,2,1,0:T(8,128)} %get-tuple-element.98), channel_id=1, source_target_pairs={{0,1},{1,0},{2,3},{3,2},{4,5},{5,4},{6,7},{7,6},{8,9},{9,8},{10,11... | collective-permute-start | bytes 7864328 | tf_op jit(solution)/shard_map/ppermute | solution.py:20
  330.0 57.5 %collective-permute-start.51 = (bf16[8,64,1280]{2,1,0:T(8,128)(2,1)}, bf16[8,64,1280]{2,1,0:T(8,128)(2,1)}, u32[]{:S(2)}, u32[]{:S(2)}) collective-permute-start(bf16[8,64,1280]{2,1,0:T(8,128)(2,1)} %pad_maximum_fusion.2), channel_id=1, source_target_pairs={{0,16},{4,20},{8,24},{12,28},{16,0},{20,4},{24,8},{28,12},{1,17},{... | collective-permute-start | bytes 3932168 | tf_op jit(solution)/shard_map/ppermute | solution.py:20
  346.2 45.8 %collective-permute-start.41 = (f32[56,1280]{1,0:T(8,128)}, f32[56,1280]{1,0:T(8,128)}, u32[]{:S(2)}, u32[]{:S(2)}) collective-permute-start(f32[56,1280]{1,0:T(8,128)} %maximum_maximum_fusion.1), channel_id=1, source_target_pairs={{0,1},{1,0},{2,3},{3,2},{4,5},{5,4},{6,7},{7,6},{8,9},{9,8},{10,11... | collective-permute-start | bytes 860168 | tf_op jit(solution)/shard_map/ppermute | solution.py:20
  364.2 47.3 %collective-permute-start.40 = (bf16[256,1280]{1,0:T(8,128)(2,1)}, bf16[256,1280]{1,0:T(8,128)(2,1)}, u32[]{:S(2)}, u32[]{:S(2)}) collective-permute-start(bf16[256,1280]{1,0:T(8,128)(2,1)} %get-tuple-element.107), channel_id=1, source_target_pairs={{0,2},{1,3},{2,0},{3,1},{4,6},{5,7},{6,4},{7,5},{8,10},{9,11},{10,... | collective-permute-start | bytes 1966088 | tf_op jit(solution)/shard_map/ppermute | solution.py:20
  422.5 43.2 %collective-permute-start.45 = (bf16[8,48,1280]{2,1,0:T(8,128)(2,1)S(1)}, bf16[8,48,1280]{2,1,0:T(8,128)(2,1)S(1)}, u32[]{:S(2)}, u32[]{:S(2)}) collective-permute-start(bf16[8,48,1280]{2,1,0:T(8,128)(2,1)S(1)} %pad_maximum_fusion.3), channel_id=1, source_target_pairs={{0,16},{4,20},{8,24},{12,28},{16,0},{20,4},{24,8},{28,12},{1,17},{... | collective-permute-start | bytes 2949128 | tf_op jit(solution)/shard_map/ppermute | solution.py:20
  (77 other events, 1675.8 us)

commit v2 on v1

v2 whole, which is shorter than its diff:
```python
import functools
import math

import jax
import jax.numpy as jnp
from jax import lax
from jax.experimental import pallas as pl
from jax.experimental.pallas import tpu as pltpu
from jax.sharding import PartitionSpec as P

HEAD_DIM = 80
f32 = jnp.float32
bf16 = jnp.bfloat16
neg_fill = -1000000000.0
score_scale = 1.0 / math.sqrt(HEAD_DIM)
log2_e = math.log2(math.e)
LIMIT = 26
KEEP = pl.BlockSpec(memory_space=pltpu.VMEM)
remain = pl.BlockSpec(memory_space=pl.ANY)


def swap(array, axis, bits, size):
    return lax.ppermute(array, axis, [(i, i ^ bits) for i in range(size)])


def nn(a, b):
    return jnp.dot(a, b, preferred_element_type=f32)


def nt(a, b):
    return lax.dot_general(a, b, (((1,), (1,)), ((), ())), preferred_element_type=f32)


def tn(a, b):
    return lax.dot_general(a, b, (((0,), (0,)), ((), ())), preferred_element_type=f32)


def halves(low):
    top = low.astype(bf16)
    return jnp.concatenate([top, (low - top.astype(f32)).astype(bf16)], axis=0)


def twice(factor):
    return jnp.concatenate([factor, factor], axis=0)


def folded(pair):
    count = pair.shape[0] // 2
    return pair[:count] + pair[count:]


def normalize(states, gain, shift):
    centre = states - jnp.mean(states, axis=-1, keepdims=True)
    scaled = lax.rsqrt(jnp.mean(centre * centre, axis=-1, keepdims=True) + 1e-05)
    unit = centre * scaled
    return unit * gain + shift, unit, scaled


def normalize_back(grad_rows, unit, scaled, gain):
    grad_unit = grad_rows * gain
    return scaled * (
        grad_unit
        - jnp.mean(grad_unit, axis=-1, keepdims=True)
        - unit * jnp.mean(grad_unit * unit, axis=-1, keepdims=True)
    )


def live_column(spot_ref, length_ref, rows, bits):
    iota = lax.broadcasted_iota(jnp.int32, (2 * rows, 1), 0)
    place = spot_ref[3]
    first, second = place ^ bits[0], place ^ bits[1]
    position = jnp.where(iota < rows, first * rows + iota, second * rows + iota - rows)
    return position < length_ref[spot_ref[0]]


def whole(shape):
    return KEEP


def placed_block(shape, index):
    return pl.BlockSpec(shape, index, pipeline_mode=pl.Buffered(1))


def call(body, scalars, operands, specs, outs, out_specs, grid=(1,), scratch=(), limit=LIMIT, aliases=None, weight=100):
    return pl.pallas_call(
        body,
        grid_spec=pltpu.PrefetchScalarGridSpec(
            num_scalar_prefetch=len(scalars),
            grid=grid,
            in_specs=specs,
            out_specs=out_specs,
            scratch_shapes=list(scratch),
        ),
        out_shape=outs,
        cost_estimate=pl.CostEstimate(flops=weight * 10**9, bytes_accessed=100000, transcendentals=0),
        input_output_aliases=aliases or {},
        compiler_params=pltpu.CompilerParams(vmem_limit_bytes=limit * 2**20),
    )(*scalars, *operands)


def shaped(shape, dtype):
    return jax.ShapeDtypeStruct(shape, dtype)


def of_mine(number):
    return lambda i, spot, pick, *_: (pick[spot[0], number], 0, 0)


def of_other(number):
    return lambda i, spot, pick, *_: (pick[spot[1], number], 0, 0)


def after(values, *others):
    return lax.optimization_barrier((values, others))[0]


def shuffled(array, quad):
    count = array.shape[1] // 4
    blocks = [array[:, n * count : (n + 1) * count] for n in range(4)]
    for bits in (1, 2):
        on = ((quad >> (bits - 1)) & 1) == 1
        blocks = [jnp.where(on, blocks[n ^ bits], blocks[n]) for n in range(4)]
    return jnp.concatenate(blocks, axis=1)


def stage(spot, pick, inputs, factors):
    rows, features = inputs.shape[1:]
    rank = factors[0].shape[1]

    def body(spot_ref, pick_ref, inputs_ref, *refs):
        send_ref, pack_ref = refs[12:]
        send_ref[:rows] = inputs_ref[0]
        quad = spot_ref[2]
        for group, ref, base in ((refs[:6], pack_ref, 0), (refs[6:12], send_ref, rows)):
            ref[base : base + rank] = jnp.concatenate([r[0] for r in group[:4]], axis=1)
            wide, thin = group[4][0], group[5][0]
            if base:
                wide, thin = shuffled(wide, quad), shuffled(thin, quad)
            ref[base + rank : base + 2 * rank] = wide
            ref[base + 2 * rank : base + 3 * rank] = thin

    specs = [placed_block((1, rows, features), lambda i, spot, *_: (spot[1], 0, 0))]
    for of in (of_mine, of_other):
        specs += [placed_block((1,) + f.shape[1:], of(n)) for n, f in enumerate(factors)]
    outs = [shaped((rows + 3 * rank, features), bf16), shaped((3 * rank, features), bf16)]
    return call(body, (spot, pick), [inputs] + factors * 2, specs, outs, [whole(o.shape) for o in outs])


def stage_heads(spot, heads):
    features = heads[0].shape[1]
    head_rows = heads[0].shape[0] // 4

    def body(spot_ref, *refs):
        out, sems = refs[4:]
        at = pl.ds(pl.multiple_of(spot_ref[2] * head_rows, 16), head_rows)
        copies = [pltpu.make_async_copy(refs[n].at[at], out.at[n], sems.at[n]) for n in range(4)]
        for c in copies:
            c.start()
        for c in copies:
            c.wait()

    out = shaped((4, head_rows, features), bf16)
    return call(body, (spot,), heads, [remain] * 4, out, KEEP, scratch=[pltpu.SemaphoreType.DMA((4,))])


def stage_dense(spot, wide, thin, cotangent):
    features, units = wide.shape
    part = units // 4
    rows = cotangent.shape[1]

    def body(spot_ref, wide_ref, thin_ref, cot_ref, wide_out, thin_out, cot_out):
        for r in range(4):

            @pl.when(spot_ref[2] == r)
            def _():
                wide_out[...] = wide_ref[:, r * part : (r + 1) * part].T

        thin_out[...] = thin_ref[...]
        cot_out[...] = cot_ref[0]

    specs = [
        whole(wide.shape),
        placed_block((part, features), lambda i, spot: (spot[2], 0)),
        placed_block((1, rows, features), lambda i, spot: (spot[1], 0, 0)),
    ]
    outs = [shaped((part, features), bf16), shaped((part, features), bf16), shaped((rows, features), bf16)]
    return call(body, (spot,), [wide, thin, cotangent], specs, outs, [whole(o.shape) for o in outs])


def project_rows(weight, rows_in, outer, low):
    return (nt(weight, rows_in) + tn(twice(outer), halves(low))).astype(bf16)


def project_near(spot, pick, inputs, received, gain, shift, inners, pack, side, weights):
    rows, features = inputs.shape[1:]
    tokens = 2 * rows
    width = weights[0].shape[0]
    rank = inners[0].shape[1]

    def body(spot_ref, pick_ref, xa, xb, gain_ref, shift_ref, iq, ik, iv, pack_ref, side_ref, *refs):
        ws, (z_ref, low_ref, kv_ref) = refs[:4], refs[4:]
        states = jnp.concatenate([xa[0], xb[...]], axis=0).astype(f32)
        z_ref[...] = normalize(states, gain_ref[...], shift_ref[...])[0].astype(bf16)
        low = nt(jnp.concatenate([iq[0], ik[0], iv[0]], axis=0), z_ref[...])
        low_ref[...] = low
        for i, packs in enumerate((pack_ref, side_ref)):
            for n in (1, 2):
                outer = packs[:rank, n * width : (n + 1) * width]
                kv_ref[i, n - 1] = project_rows(
                    ws[2 * i + n - 1][...], z_ref[...], outer, low[n * rank : (n + 1) * rank]
                )

    specs = [
        placed_block((1, rows, features), lambda i, spot, *_: (spot[0], 0, 0)),
        placed_block((rows, features), lambda *_: (0, 0)),
        whole((1, features)),
        whole((1, features)),
    ]
    specs += [placed_block((1, rank, features), of_mine(n)) for n in range(3)]
    specs += [whole(pack.shape), whole(side.shape)] + [whole((width, features))] * 4
    outs = [
        shaped((tokens, features), bf16),
        shaped((3 * rank, tokens), f32),
        shaped((2, 2, width, tokens), bf16),
    ]
    return call(
        body,
        (spot, pick),
        [inputs, received, gain, shift] + inners + [pack, side] + weights,
        specs,
        outs,
        [whole(o.shape) for o in outs],
    )


def queries_near(z, low, pack, side, weights):
    tokens, features = z.shape
    width = weights[0].shape[0]
    rank = low.shape[0] // 3

    def body(z_ref, low_ref, pack_ref, side_ref, w0, w1, q_ref):
        for i, (packs, w) in enumerate(((pack_ref, w0), (side_ref, w1))):
            q_ref[i] = project_rows(w[...], z_ref[...], packs[:rank, :width], low_ref[:rank])

    operands = [z, low, pack, side] + weights
    out = shaped((2, width, tokens), bf16)
    return call(body, (), operands, [whole(o.shape) for o in operands], out, whole(out.shape))


def project_far(spot, z, low, received, side, parts):
    tokens, features = z.shape
    head_rows = parts[0][0].shape[1]
    width = 4 * head_rows
    rank = low.shape[0] // 3
    base = received.shape[0] - 3 * rank
    flat = [p for group in parts for p in group]

    def body(spot_ref, z_ref, low_ref, received_ref, side_ref, *refs):
        ins, (weight_ref, kv_ref) = refs[:10], refs[10:]
        for i in range(2):
            group = ins[5 * i : 5 * i + 5]
            for n in range(4):
                for r in range(4):
                    at = pl.ds(pl.multiple_of((spot_ref[0] ^ r) * head_rows, 16), head_rows)
                    if r < 3:
                        weight_ref[i, n, at] = group[r][n]
                    else:
                        weight_ref[i, n, at] = group[3 + n // 2][n % 2]
        for i, (ref, start) in enumerate(((received_ref, base), (side_ref, 0))):
            for n in (1, 2):
                outer = ref[start : start + rank, n * width : (n + 1) * width]
                kv_ref[i, n - 1] = project_rows(
                    weight_ref[i, n], z_ref[...], outer, low_ref[n * rank : (n + 1) * rank]
                )

    operands = [z, low, received, side] + flat
    outs = [shaped((2, 4, width, features), bf16), shaped((2, 2, width, tokens), bf16)]
    return call(
        body, (spot[2:3],), operands, [whole(o.shape) for o in operands], outs, [whole(o.shape) for o in outs]
    )


def queries_far(z, low, received, side, far):
    tokens, features = z.shape
    width = far.shape[2]
    rank = low.shape[0] // 3
    base = received.shape[0] - 3 * rank

    def body(z_ref, low_ref, received_ref, side_ref, far_ref, q_ref):
        for i, (ref, start) in enumerate(((received_ref, base), (side_ref, 0))):
            outer = ref[start : start + rank, :width]
            q_ref[i] = project_rows(far_ref[i, 0], z_ref[...], outer, low_ref[:rank])

    operands = [z, low, received, side, far]
    specs = [whole(o.shape) for o in operands[:4]] + [placed_block((2, 1, width, features), lambda *_: (0, 0, 0, 0))]
    out = shaped((2, width, tokens), bf16)
    return call(body, (), operands, specs, out, whole(out.shape))


def attend(spot, lengths, q, kv, kv_side):
    _, width, tokens = q.shape
    rows = tokens // 2
    pair = 2 * HEAD_DIM
    steps = width // pair

    def body(spot_ref, length_ref, q_ref, k1, k2, v1, v2, ctx_ref, total_ref):
        bias1 = jnp.where(live_column(spot_ref, length_ref, rows, (0, 2)), 0.0, neg_fill * log2_e)
        bias2 = jnp.where(live_column(spot_ref, length_ref, rows, (1, 3)), 0.0, neg_fill * log2_e)
        for h in range(2):
            at = slice(h * HEAD_DIM, (h + 1) * HEAD_DIM)
            query = q_ref[0, at]
            s1 = tn(k1[0, 0, at], query) * (score_scale * log2_e) + bias1
            s2 = tn(k2[0, 0, at], query) * (score_scale * log2_e) + bias2
            top = jnp.maximum(jnp.max(s1, axis=0, keepdims=True), jnp.max(s2, axis=0, keepdims=True))
            p1 = jnp.exp2(s1 - top)
            p2 = jnp.exp2(s2 - top)
            total = jnp.sum(p1, axis=0, keepdims=True) + jnp.sum(p2, axis=0, keepdims=True)
            context = nn(v1[0, 0, at], p1.astype(bf16)) + nn(v2[0, 0, at], p2.astype(bf16))
            ctx_ref[0, at] = (context * (1.0 / total)).astype(bf16)
            total_ref[h] = top + jnp.log2(total)

    def own(n):
        return pl.BlockSpec((1, 1, pair, tokens), lambda h, *_: (h // steps, n, h % steps, 0))

    def beside(n):
        return pl.BlockSpec((1, 1, pair, tokens), lambda h, *_: (1 - h // steps, n, h % steps, 0))

    rows_spec = pl.BlockSpec((1, pair, tokens), lambda h, *_: (h // steps, h % steps, 0))
    return call(
        body,
        (spot, lengths),
        [q, kv, kv_side, kv, kv_side],
        [rows_spec, own(0), beside(0), own(1), beside(1)],
        [shaped(q.shape, bf16), shaped((4 * steps, 1, tokens), f32)],
        [rows_spec, pl.BlockSpec((2, 1, tokens), lambda h, *_: (h, 0, 0))],
        grid=(2 * steps,),
    )


def attend_back(spot, lengths, q, kv, kv_side, grad_context, totals, deltas, which):
    _, width, tokens = q.shape
    rows = tokens // 2
    pair = 2 * HEAD_DIM
    steps = width // pair

    def body(spot_ref, length_ref, q_ref, k1, k2, v1, v2, g_ref, total_ref, delta_ref, gq, own_ref, other_ref):
        bias1 = jnp.where(live_column(spot_ref, length_ref, rows, (0, 2)), 0.0, neg_fill * log2_e)
        bias2 = jnp.where(live_column(spot_ref, length_ref, rows, (1, 3)), 0.0, neg_fill * log2_e)
        for h in range(2):
            at = slice(h * HEAD_DIM, (h + 1) * HEAD_DIM)
            query = q_ref[0, at]
            grad = g_ref[0, at]
            grad_query = None
            for k, v, bias, out in ((k1, v1, bias1, own_ref), (k2, v2, bias2, other_ref)):
                s = tn(k[0, 0, at], query) * (score_scale * log2_e) + bias
                soft = jnp.exp2(s - total_ref[h])
                grad_soft = tn(v[0, 0, at], grad)
                grad_scores = (soft * (grad_soft - delta_ref[h])).astype(bf16)
                part = nn(k[0, 0, at], grad_scores)
                grad_query = part if grad_query is None else grad_query + part
                out[0, 0, at] = nt(query, grad_scores) * score_scale
                out[0, 1, at] = nt(grad, soft.astype(bf16))
            gq[0, at] = (grad_query * score_scale).astype(bf16)

    def own(n):
        return pl.BlockSpec((1, 1, pair, tokens), lambda h, *_: (h // steps, n, h % steps, 0))

    def beside(n):
        return pl.BlockSpec((1, 1, pair, tokens), lambda h, *_: (1 - h // steps, n, h % steps, 0))

    rows_spec = pl.BlockSpec((1, pair, tokens), lambda h, *_: (h // steps, h % steps, 0))
    grads_spec = pl.BlockSpec((1, pair, tokens), lambda h, *_: (2 * which + h // steps, h % steps, 0))
    line = pl.BlockSpec((2, 1, tokens), lambda h, *_: (h, 0, 0))
    line_at = pl.BlockSpec((2, 1, tokens), lambda h, *_: (2 * steps * which + h, 0, 0))
    both = pl.BlockSpec((1, 2, pair, tokens), lambda h, *_: (h // steps, 0, h % steps, 0))
    return call(
        body,
        (spot, lengths),
        [q, kv, kv_side, kv, kv_side, grad_context, totals, deltas],
        [rows_spec, own(0), beside(0), own(1), beside(1), grads_spec, line, line_at],
        [shaped(q.shape, bf16), shaped(kv.shape, f32), shaped(kv.shape, f32)],
        [rows_spec, both, both],
        grid=(2 * steps,),
    )


cubic = 0.044715
root = math.sqrt(2.0 / math.pi)


def bend_of(widened, grad):
    square = widened * widened
    bend = jnp.tanh(root * widened * (1.0 + cubic * square))
    up = 0.5 * (1.0 + bend)
    slope = up + widened * (0.5 * root) * (1.0 - bend * bend) * (1.0 + 3.0 * cubic * square)
    return (widened * up).astype(bf16), (grad * slope).astype(bf16)


def feed_quarter(z_ref, gy_ref, wide_ref, thin_ref, pack_ref, rank, low_w, low_n, act_ref, grad_ref, sums_ref):
    units = wide_ref.shape[1]
    block = 256
    low_w2, low_n2 = halves(low_w), halves(low_n)

    def step(b, carry):
        at = pl.ds(pl.multiple_of(b * block, block), block)
        widened = nn(z_ref[...], wide_ref[:, at]) + tn(low_w2, twice(pack_ref[rank : 2 * rank, at]))
        grad = nt(gy_ref[...], thin_ref[at, :]) + tn(low_n2, twice(pack_ref[2 * rank : 3 * rank, at]))
        act_ref[:, at], grad_ref[:, at] = bend_of(widened, grad)
        return carry

    lax.fori_loop(0, units // block, step, 0)
    sums_ref[:rank] = folded(nn(low_w2, grad_ref[...]))
    sums_ref[rank:] = folded(nn(low_n2, act_ref[...]))
    return (
        nn(act_ref[...], thin_ref[...]),
        nt(grad_ref[...], wide_ref[...]),
        nt(pack_ref[2 * rank : 3 * rank], act_ref[...]),
        nt(pack_ref[rank : 2 * rank], grad_ref[...]),
    )


def feed_units(z_ref, gy_ref, wide_ref, thin_ref, outer, inner, low_w, low_n, act_ref, grad_ref):
    units = wide_ref.shape[0]
    block = 256
    low_w2, low_n2 = halves(low_w), halves(low_n)
    for start in range(0, units, block):
        at = slice(start, min(start + block, units))
        widened = nt(z_ref[...], wide_ref[at]) + tn(low_w2, twice(outer[:, at]))
        grad = nt(gy_ref[...], thin_ref[at]) + tn(low_n2, twice(inner[:, at]))
        act_ref[:, at], grad_ref[:, at] = bend_of(widened, grad)
    sums = jnp.concatenate(
        [folded(nn(low_w2, grad_ref[...])), folded(nn(low_n2, act_ref[...]))], axis=0
    )
    return (
        nn(act_ref[...], thin_ref[...]),
        nn(grad_ref[...], wide_ref[...]),
        nt(inner, act_ref[...]),
        nt(outer, grad_ref[...]),
        sums,
    )


def output_inner_rows(pack_ref, side_ref, received_ref, far_side_ref, rank, base, width):
    lanes = slice(3 * width, 4 * width)
    return [
        pack_ref[:rank, lanes],
        side_ref[:rank, lanes],
        received_ref[base : base + rank, lanes],
        far_side_ref[:rank, lanes],
    ]


def feed_open(spot, pick, lengths, contexts, outs_w, far, packs, tables, inputs, received, gain, shift):
    rows, features = inputs.shape[1:]
    tokens = 2 * rows
    width = contexts[0].shape[1]
    rank = tables[0].shape[1]
    pack, side, far_side = packs
    base = received.shape[0] - 3 * rank

    def body(spot_ref, pick_ref, length_ref, c01, c23, wo0, wo1, far_ref, pack_ref, side_ref, far_side_ref, received_ref, oo, wi, xa, gain_ref, shift_ref, hidden_ref, z_ref, lows_ref):
        states = jnp.concatenate([xa[0], received_ref[:rows]], axis=0).astype(f32)
        mask = live_column(spot_ref, length_ref, rows, (0, 2)).astype(f32)
        inner_o = output_inner_rows(pack_ref, side_ref, received_ref, far_side_ref, rank, base, width)
        contexts_all = [c01[0], c01[1], c23[0], c23[1]]
        weights_all = [wo0[...], wo1[...], far_ref[0, 0], far_ref[1, 0]]
        joined = jnp.concatenate(contexts_all, axis=0)
        attended = tn(joined, jnp.concatenate(weights_all, axis=0))
        low_o = nn(jnp.concatenate(inner_o, axis=1), joined)
        attended = attended + tn(halves(low_o), twice(oo[0]))
        hidden = states + mask * attended
        hidden_ref[...] = hidden
        z_ref[...] = normalize(hidden, gain_ref[...], shift_ref[...])[0].astype(bf16)
        lows_ref[:rank] = low_o
        lows_ref[rank:] = nt(wi[0], z_ref[...])

    operands = contexts + outs_w + [far, pack, side, far_side, received] + tables[:2]
    specs = [whole(c.shape) for c in contexts] + [whole(w.shape) for w in outs_w]
    specs += [placed_block((2, 1, width, features), lambda *_: (0, 3, 0, 0))]
    specs += [whole(p.shape) for p in packs] + [whole(received.shape)]
    specs += [placed_block((1, rank, features), of_mine(n)) for n in (3, 4)]
    operands += [inputs, gain, shift]
    specs += [placed_block((1, rows, features), lambda i, spot, *_: (spot[0], 0, 0))]
    specs += [whole(gain.shape), whole(shift.shape)]
    outs = [shaped((tokens, features), f32), shaped((tokens, features), bf16), shaped((2 * rank, tokens), f32)]
    return call(body, (spot, pick, lengths), operands, specs, outs, [KEEP] * 3)


def feed_first(spot, pick, lengths, z, lows, table, cotangent, cot_side, pack, dense):
    tokens, features = z.shape
    rows = tokens // 2
    rank = table.shape[1]
    units = dense[0].shape[1]

    def body(spot_ref, pick_ref, length_ref, z_ref, lows_in, no, ca, cb, pack_ref, wide, thin, gy_ref, branch_ref, second_ref, lows_ref, sums_ref, act_ref, grad_ref):
        mask = live_column(spot_ref, length_ref, rows, (0, 2)).astype(f32)
        grad_in = jnp.concatenate([ca[0], cb[...]], axis=0).astype(f32)
        gy_ref[...] = (mask * grad_in).astype(bf16)
        low_n = nt(no[0], gy_ref[...])
        lows_ref[: 2 * rank] = lows_in[...]
        lows_ref[2 * rank : 3 * rank] = low_n
        branch_ref[...], second_ref[...], lows_ref[3 * rank : 4 * rank], lows_ref[4 * rank :] = feed_quarter(
            z_ref, gy_ref, wide, thin, pack_ref, rank, lows_in[rank:], low_n, act_ref, grad_ref, sums_ref
        )

    operands = [z, lows, table, cotangent, cot_side, pack] + dense
    specs = [KEEP, KEEP, placed_block((1, rank, features), of_mine(5))]
    specs += [placed_block((1, rows, features), lambda i, spot, *_: (spot[0], 0, 0))] + [KEEP] * 4
    outs = [
        shaped((tokens, features), bf16),
        shaped((tokens, features), f32),
        shaped((tokens, features), f32),
        shaped((5 * rank, tokens), f32),
        shaped((2 * rank, units), f32),
    ]
    scratch = [pltpu.VMEM((tokens, units), bf16)] * 2
    return call(body, (spot, pick, lengths), operands, specs, outs, [KEEP] * 5, scratch=scratch)


def feed_near(z, gy, branch, second, lows, pack, dense):
    tokens, features = z.shape
    units = dense[0].shape[1]
    rank = lows.shape[0] // 5

    def body(z_ref, gy_ref, branch_in, second_in, lows_in, pack_ref, wide, thin, branch_ref, second_ref, lows_ref, sums_ref, act_ref, grad_ref):
        sums = feed_quarter(
            z_ref, gy_ref, wide, thin, pack_ref, rank, lows_in[rank : 2 * rank], lows_in[2 * rank : 3 * rank],
            act_ref, grad_ref, sums_ref,
        )
        branch_ref[...] = branch_in[...] + sums[0]
        second_ref[...] = second_in[...] + sums[1]
        lows_ref[: 3 * rank] = lows_in[: 3 * rank]
        lows_ref[3 * rank : 4 * rank] = lows_in[3 * rank : 4 * rank] + sums[2]
        lows_ref[4 * rank :] = lows_in[4 * rank :] + sums[3]

    operands = [z, gy, branch, second, lows, pack] + dense
    outs = [shaped(branch.shape, f32), shaped(second.shape, f32), shaped(lows.shape, f32), shaped((2 * rank, units), f32)]
    scratch = [pltpu.VMEM((tokens, units), bf16)] * 2
    return call(body, (), operands, [KEEP] * len(operands), outs, [KEEP] * 4, scratch=scratch, aliases={2: 0, 3: 1})


def far_parts(parts, z_ref, gy_ref, ins, wide, thin, received_ref, far_side_ref, rank, base, low_w, low_n, act_ref, grad_ref, sums_ref):
    count = wide.shape[0] // 2
    total = None
    for n, r in enumerate(parts):
        lanes = slice(r * count, (r + 1) * count)
        outer = jnp.concatenate(
            [received_ref[base + rank : base + 2 * rank, lanes], far_side_ref[rank : 2 * rank, lanes]], axis=1
        )
        inner = jnp.concatenate(
            [received_ref[base + 2 * rank : base + 3 * rank, lanes], far_side_ref[2 * rank : 3 * rank, lanes]], axis=1
        )
        for q in range(2):
            at = slice(q * count, (q + 1) * count)
            wide[at] = ins[4 * n + q][...]
            thin[at] = ins[4 * n + 2 + q][...]
        found = feed_units(z_ref, gy_ref, wide, thin, outer, inner, low_w, low_n, act_ref, grad_ref)
        sums_ref[n] = found[4]
        total = found[:4] if total is None else [a + b for a, b in zip(total, found[:4])]
    return total


def far_scratch(part, features, tokens):
    return [pltpu.VMEM((2 * part, features), bf16)] * 2 + [pltpu.VMEM((tokens, 2 * part), bf16)] * 2


def feed_far(parts, z, gy, branch, second, lows, received, far_side, weights):
    tokens, features = z.shape
    part = weights[0].shape[0]
    rank = lows.shape[0] // 5
    base = received.shape[0] - 3 * rank
    count = len(weights)

    def body(z_ref, gy_ref, branch_in, second_in, lows_in, received_ref, far_side_ref, *refs):
        ins, (branch_ref, second_ref, lows_ref, sums_ref) = refs[:count], refs[count : count + 4]
        wide, thin, act_ref, grad_ref = refs[count + 4 :]
        total = far_parts(
            parts, z_ref, gy_ref, ins, wide, thin, received_ref, far_side_ref, rank, base,
            lows_in[rank : 2 * rank], lows_in[2 * rank : 3 * rank], act_ref, grad_ref, sums_ref,
        )
        branch_ref[...] = branch_in[...] + total[0]
        second_ref[...] = second_in[...] + total[1]
        lows_ref[: 3 * rank] = lows_in[: 3 * rank]
        lows_ref[3 * rank : 4 * rank] = lows_in[3 * rank : 4 * rank] + total[2]
        lows_ref[4 * rank :] = lows_in[4 * rank :] + total[3]

    operands = [z, gy, branch, second, lows, received, far_side] + weights
    outs = [
        shaped(branch.shape, f32),
        shaped(second.shape, f32),
        shaped(lows.shape, f32),
        shaped((len(parts), 2 * rank, 2 * part), f32),
    ]
    return call(
        body, (), operands, [KEEP] * len(operands), outs, [KEEP] * 4,
        scratch=far_scratch(part, features, tokens), aliases={2: 0, 3: 1},
    )


def shares(array, core):
    half = array.shape[1] // 2
    low, high = array[:, :half], array[:, half:]
    return jnp.where(core == 0, low, high), jnp.where(core == 0, high, low)


def padded(array, count):
    return jnp.concatenate([array, jnp.zeros((array.shape[0], count - array.shape[1]), array.dtype)], axis=1)


def lanes_up(count):
    return (count + 127) // 128 * 128


def feed_close(parts, spot, pick, lengths, hidden, z, gy, branch, second, lows, near_sums, far_sums, contexts, outs_w, far, packs, tables, received, cotangent, cot_side, gain, weights):
    tokens, features = hidden.shape
    rows = tokens // 2
    width = contexts[0].shape[1]
    rank = tables[0].shape[1]
    pack, side, far_side = packs
    base = received.shape[0] - 3 * rank
    part = weights[0].shape[0]
    units = 4 * part
    heads = width // HEAD_DIM
    half = features // 2
    tail = lanes_up(width)
    total_lanes = 3 * half + 2 * (2 * units + tail)

    def body(spot_ref, pick_ref, length_ref, hidden_ref, z_ref, gy_ref, branch_in, second_in, lows_ref, near0, near1, far0, far12, c01, c23, wo0, wo1, far_ref, pack_ref, side_ref, far_side_ref, received_ref, oo, wi, no, ca, cb, gain_ref, *refs):
        hbm, (outa_ref, outb_ref, gh_ref, gc_ref, delta_ref, keep_ref, give_ref) = refs[:4], refs[4:11]
        wide, thin, act_ref, grad_ref, far3, ga_ref = refs[11:]
        low_w = lows_ref[rank : 2 * rank]
        low_n = lows_ref[2 * rank : 3 * rank]
        found = far_parts(
            parts, z_ref, gy_ref, hbm, wide, thin, received_ref, far_side_ref, rank, base,
            low_w, low_n, act_ref, grad_ref, far3,
        )
        branch = branch_in[...] + found[0]
        grad_second = second_in[...] + found[1]
        low_next = lows_ref[3 * rank : 4 * rank] + found[2]
        grad_low = lows_ref[4 * rank :] + found[3]
        mask = live_column(spot_ref, length_ref, rows, (0, 2)).astype(f32)
        branch = branch + tn(halves(low_next), twice(no[0]))
        grad_second = grad_second + tn(halves(grad_low), twice(wi[0]))
        hidden_now = hidden_ref[...]
        output = (hidden_now + mask * branch).astype(bf16)
        outa_ref[...] = output[:rows]
        outb_ref[...] = output[rows:]
        _, unit, scaled = normalize(hidden_now, gain_ref[...], gain_ref[...])
        grad_in = jnp.concatenate([ca[0], cb[...]], axis=0).astype(f32)
        grad_hidden = grad_in + normalize_back(grad_second, unit, scaled, gain_ref[...])
        gh_ref[...] = grad_hidden
        ga_ref[...] = (mask * grad_hidden).astype(bf16)
        grad_low_o = nt(oo[0], ga_ref[...])
        low_o2 = halves(grad_low_o)
        inner_o = output_inner_rows(pack_ref, side_ref, received_ref, far_side_ref, rank, base, width)
        contexts_all = [c01[0], c01[1], c23[0], c23[1]]
        weights_all = [wo0, wo1, far_ref.at[0, 0], far_ref.at[1, 0]]
        inner_sums = []
        for i in range(4):
            grad = (nt(weights_all[i][...], ga_ref[...]) + tn(twice(inner_o[i]), low_o2)).astype(bf16)
            gc_ref[i] = grad
            product = grad.astype(f32) * contexts_all[i].astype(f32)
            for h in range(heads):
                delta_ref[heads * i + h] = jnp.sum(
                    product[h * HEAD_DIM : (h + 1) * HEAD_DIM], axis=0, keepdims=True
                )
            inner_sums.append(folded(nt(low_o2, contexts_all[i])))
        core = spot_ref[3] & 1
        quad = spot_ref[2]
        shared = (
            folded(nn(halves(grad_low), z_ref[...])),
            folded(nn(halves(lows_ref[:rank]), ga_ref[...])),
            folded(nn(halves(low_next), gy_ref[...])),
        )
        for n in range(3):
            keep_ref[:, n * half : (n + 1) * half], give_ref[:, n * half : (n + 1) * half] = shares(shared[n], core)
        quarters = []
        for near in (near0, near1):
            quarters.append((near[:rank], near[rank:]))
        for q in range(2):
            lanes = slice(q * part, (q + 1) * part)
            pieces = [far0[0, :, lanes], far12[0, :, lanes], far12[1, :, lanes], far3[0, :, lanes]]
            joined = shuffled(jnp.concatenate(pieces, axis=1), quad)
            quarters.append((joined[:rank], joined[rank:]))
        for i in range(4):
            ref = (keep_ref, give_ref)[i % 2]
            at = 3 * half + (i // 2) * (2 * units + tail)
            ref[:, at : at + units] = quarters[i][0]
            ref[:, at + units : at + 2 * units] = quarters[i][1]
            ref[:, at + 2 * units : at + 2 * units + tail] = padded(inner_sums[i], tail)

    operands = [hidden, z, gy, branch, second, lows] + near_sums + far_sums + contexts + outs_w
    specs = [whole(hidden.shape), KEEP, KEEP, KEEP, KEEP] + [whole(o.shape) for o in operands[5:]]
    operands += [far, pack, side, far_side, received] + tables
    specs += [placed_block((2, 1, width, features), lambda *_: (0, 3, 0, 0))]
    specs += [whole(p.shape) for p in packs] + [whole(received.shape)]
    specs += [placed_block((1, rank, features), of_mine(n)) for n in (3, 4, 5)]
    operands += [cotangent, cot_side, gain] + weights
    specs += [placed_block((1, rows, features), lambda i, spot, *_: (spot[0], 0, 0))]
    specs += [whole(cot_side.shape), whole(gain.shape)] + [KEEP] * 4
    outs = [
        shaped((rows, features), bf16),
        shaped((rows, features), bf16),
        shaped((tokens, features), f32),
        shaped((4, width, tokens), bf16),
        shaped((4 * heads, 1, tokens), f32),
        shaped((rank, total_lanes), f32),
        shaped((rank, total_lanes), f32),
    ]
    scratch = far_scratch(part, features, tokens)
    scratch += [pltpu.VMEM((1, 2 * rank, 2 * part), f32), pltpu.VMEM((tokens, features), bf16)]
    return call(
        body, (spot, pick, lengths), operands, specs, outs, [whole(o.shape) for o in outs], scratch=scratch
    )


def gather_grads(spot, near, far, z, low, packs, received):
    tokens, features = z.shape
    rank = low.shape[0] // 3
    width = near[0].shape[1]
    pack, side, far_side = packs
    base = received.shape[0] - 3 * rank
    half = features // 2
    tail = lanes_up(3 * width)
    total_lanes = 3 * half + 2 * tail

    def body(spot_ref, q01, own01, side01, q23, own23, side23, z_ref, low_ref, pack_ref, side_ref, far_side_ref, received_ref, g_ref, gl_ref, keep_ref, give_ref):
        groups = ((q01, own01, side01), (q23, own23, side23))
        places = ((pack_ref, 0), (side_ref, 0), (received_ref, base), (far_side_ref, 0))
        lows = [halves(low_ref[n * rank : (n + 1) * rank]) for n in range(3)]
        total = [jnp.zeros((rank, tokens), f32) for _ in range(3)]
        core = spot_ref[3] & 1
        for i in range(4):
            q, own, other = groups[i // 2]
            ref, start = places[i]
            outers = []
            for n in range(3):
                if n == 0:
                    g = q[i % 2]
                else:
                    g = (own[i % 2, n - 1] + other[1 - i % 2, n - 1]).astype(bf16)
                g_ref[i, n] = g
                lanes = slice(n * width, (n + 1) * width)
                total[n] = total[n] + nn(ref[start : start + rank, lanes], g)
                outers.append(folded(nt(lows[n], g)))
            at = 3 * half + (i // 2) * tail
            (keep_ref, give_ref)[i % 2][:, at : at + tail] = padded(jnp.concatenate(outers, axis=1), tail)
        for n in range(3):
            gl_ref[n * rank : (n + 1) * rank] = total[n]
            inner = folded(nn(halves(total[n]), z_ref[...]))
            keep_ref[:, n * half : (n + 1) * half], give_ref[:, n * half : (n + 1) * half] = shares(inner, core)

    operands = list(near) + list(far) + [z, low] + list(packs) + [received]
    outs = [
        shaped((4, 3, width, tokens), bf16),
        shaped((3 * rank, tokens), f32),
        shaped((rank, total_lanes), f32),
        shaped((rank, total_lanes), f32),
    ]
    return call(
        body, (spot,), operands, [whole(o.shape) for o in operands], outs, [whole(o.shape) for o in outs]
    )


def settle(spot, pick, keep, moved, common, with_picks):
    rank, lanes = keep.shape
    own = (lanes - common) // 2
    extra = 128 if with_picks else 0

    def body(spot_ref, pick_ref, keep_ref, moved_ref, here_ref, there_ref):
        total = (keep_ref[...] + moved_ref[...]).astype(bf16)
        here_ref[:, : common + own] = total[:, : common + own]
        there_ref[:, :common] = total[:, :common]
        there_ref[:, common : common + own] = total[:, common + own :]
        if with_picks:
            iota = lax.broadcasted_iota(jnp.int32, (rank, 128), 1)
            line = jnp.zeros((rank, 128), f32)
            for n in range(6):
                line = jnp.where(iota == n, pick_ref[spot_ref[0], n].astype(f32), line)
            here_ref[:, common + own :] = line.astype(bf16)
            there_ref[:, common + own :] = line.astype(bf16)

    out = shaped((rank, common + own + extra), bf16)
    return call(body, (spot, pick), [keep, moved], [whole(keep.shape)] * 2, [out, out], [whole(out.shape)] * 2)


def combine(picks, arrays, groups, rows_of_table):
    per, rank = arrays[0].shape[:2]

    def body(pick_ref, *refs):
        ins, outs = refs[: len(arrays)], refs[len(arrays) :]
        outs = [outs[0].at[n] for n in range(3)] + list(outs[1:])
        for out in outs:
            out[...] = jnp.zeros(out.shape, f32)
        for a, ref in enumerate(ins):
            for c in range(per):
                for (start, count, number), out in zip(groups, outs):
                    row = pick_ref[a * per + c, number]
                    out[row] += ref[c, :, start : start + count].astype(f32)

    outs = [shaped((3, rows_of_table, rank, groups[0][1]), f32)]
    outs += [shaped((rows_of_table, rank, count), f32) for _, count, _ in groups[3:]]
    return call(body, (picks,), list(arrays), [whole(a.shape) for a in arrays], outs, [whole(o.shape) for o in outs])


def complete(spot, own, moved):
    _, count, rank, half = own.shape

    def body(spot_ref, own_ref, moved_ref, *outs):
        core = spot_ref[3] & 1
        for n in range(3):
            mine, theirs = own_ref[n], moved_ref[n]
            outs[n][:, :, :half] = jnp.where(core == 0, mine, theirs)
            outs[n][:, :, half:] = jnp.where(core == 0, theirs, mine)

    out = shaped((count, rank, 2 * half), f32)
    return call(body, (spot,), [own, moved], [whole(own.shape)] * 2, [out] * 3, [whole(out.shape)] * 3)


def pair_up(spot, first, second):
    rows, features = first.shape

    def body(spot_ref, first_ref, second_ref, out_ref):
        out_ref[spot_ref[0]] = first_ref[...]
        out_ref[spot_ref[1]] = second_ref[...].astype(first.dtype)

    out = shaped((2, rows, features), first.dtype)
    return call(body, (spot,), [first, second], [whole(first.shape)] * 2, out, whole(out.shape))


def finish(spot, pick, g, gl, inners, weights, far, inputs, received, grad_hidden, gain):
    rows, features = inputs.shape[1:]
    tokens = 2 * rows
    width = g.shape[2]
    rank = gl.shape[0] // 3

    def body(spot_ref, pick_ref, g_ref, gl_ref, iq, ik, iv, *refs):
        ws, (far_ref, xa, xb, gh_ref, gain_ref, grada_ref, gradb_ref) = refs[:6], refs[6:]
        low = [halves(gl_ref[n * rank : (n + 1) * rank]) for n in range(3)]
        total = tn(
            jnp.concatenate(low, axis=0),
            jnp.concatenate([twice(iq[0]), twice(ik[0]), twice(iv[0])], axis=0),
        )
        for i in range(4):
            for n in range(3):
                weight = ws[3 * i + n][...] if i < 2 else far_ref[i - 2, n]
                total = total + tn(g_ref[i, n], weight)
        states = jnp.concatenate([xa[0], xb[...]], axis=0).astype(f32)
        _, unit, scaled = normalize(states, gain_ref[...], gain_ref[...])
        grad = gh_ref[...] + normalize_back(total, unit, scaled, gain_ref[...])
        grada_ref[...] = grad[:rows]
        gradb_ref[...] = grad[rows:].astype(bf16)

    operands = [g, gl] + inners + weights + [far, inputs, received, grad_hidden, gain]
    specs = [whole(g.shape), whole(gl.shape)]
    specs += [placed_block((1, rank, features), of_mine(n)) for n in range(3)]
    specs += [whole(w.shape) for w in weights]
    specs += [placed_block((2, 3, width, features), lambda *_: (0, 0, 0, 0))]
    specs += [placed_block((1, rows, features), lambda i, spot, *_: (spot[0], 0, 0))]
    specs += [placed_block((rows, features), lambda *_: (0, 0)), whole(grad_hidden.shape), whole(gain.shape)]
    outs = [shaped((rows, features), f32), shaped((rows, features), bf16)]
    return call(
        body, (spot, pick), operands, specs, outs, [whole(o.shape) for o in outs],
    )


def make_body(dp_size, tensor_size):
    def across(array):
        return swap(array, "tensor", 2, tensor_size)

    def beside(array):
        return swap(array, "tensor", 1, tensor_size)

    def along(array, bits):
        return swap(array, "dp", bits, dp_size)

    def body(
        inputs,
        cotangent,
        lengths,
        adapter_pick,
        first_gain,
        first_bias,
        query_weight,
        key_weight,
        value_weight,
        output_weight,
        second_gain,
        second_bias,
        widen_weight,
        narrow_weight,
        query_inner,
        query_outer,
        key_inner,
        key_outer,
        value_inner,
        value_outer,
        output_inner,
        output_outer,
        widen_inner,
        widen_outer,
        narrow_inner,
        narrow_outer,
    ):
        rows, features = inputs.shape[1:]
        place = lax.axis_index("tensor")
        quad = lax.axis_index("dp") & 3
        mine = place >> 1
        spot = jnp.stack([mine, 1 - mine, quad, place]).astype(jnp.int32)
        pick = adapter_pick

        def flip(array):
            return jnp.swapaxes(array, 1, 2)

        small = [query_outer, key_outer, value_outer, flip(output_inner), widen_outer, flip(narrow_inner)]
        inners = [flip(query_inner), flip(key_inner), flip(value_inner)]
        tables = [output_outer, flip(widen_inner), narrow_outer]
        gains = [v.reshape(1, -1) for v in (first_gain, first_bias, second_gain, second_bias)]
        heads = [query_weight.T, key_weight.T, value_weight.T, output_weight]
        dense = [widen_weight, narrow_weight]
        width = query_outer.shape[2]
        half = features // 2

        part_heads = stage_heads(spot, heads)
        far0 = across(part_heads)
        near_heads = [beside(w) for w in after(heads, part_heads)]
        send, pack = stage(after(spot, part_heads), pick, inputs, small)
        side = beside(pack)
        part_wide, part_thin, cot_send = stage_dense(after(spot, pack), widen_weight, narrow_weight, cotangent)
        near_dense = [beside(w) for w in after(dense, near_heads)]
        received = across(after(send, far0))
        far1, far2 = along(far0, 1), along(far0, 2)
        side0 = beside(after(far0, side, near_dense, part_wide))
        wide0 = across(after(part_wide, received))
        far3, far4 = along(far2[:2], 1), along(far1[2:], 2)
        side1 = beside(far1)
        z, low, kv01 = project_near(
            after(spot, part_wide, far1, far2, side0), pick, inputs, received, gains[0], gains[1], inners, pack, side,
            [heads[1], heads[2], near_heads[1], near_heads[2]],
        )
        kv01_side = beside(kv01)
        side2 = beside(after(far2, kv01, side1))
        q01 = queries_near(after(z, kv01), low, pack, side, [heads[0], near_heads[0]])
        far_side = beside(after(received[rows:], q01))
        side3, side4 = beside(after(far3, q01, side2)), beside(after(far4, q01, side2))
        c01, total01 = attend(after(spot, side2), lengths, q01, kv01, kv01_side)
        wide1, wide2 = along(after(wide0, c01), 1), along(after(wide0, c01), 2)
        cot_side = across(after(cot_send, c01, wide0))
        far, kv23 = project_far(
            after(spot, c01, wide0), z, low, received, far_side,
            [[far0, far1, far2, far3, far4], [side0, side1, side2, side3, side4]],
        )
        kv23_side = beside(kv23)
        q23 = queries_far(after(z, kv23), low, received, far_side, far)
        c23, total23 = attend(spot, lengths, q23, kv23, kv23_side)
        thin0 = across(after(part_thin, c23))
        packs = [pack, side, far_side]
        outs_w = [heads[3], near_heads[3]]
        hidden, z2, lows = feed_open(
            spot, pick, lengths, [c01, c23], outs_w, far, packs, tables, inputs, received, gains[2], gains[3]
        )
        wide3 = along(after(wide2, lows), 1)
        wide_sides = [beside(after(w, lows, wide1, wide2)) for w in (wide0, wide1, wide2)]
        gy, branch, second, lows, sums0 = feed_first(
            spot, pick, lengths, z2, lows, tables[2], cotangent, cot_side, pack, dense
        )
        wide_sides.append(beside(after(wide3, lows)))
        thin1, thin2 = along(after(thin0, lows), 1), along(after(thin0, lows), 2)
        thin_sides = [beside(after(thin0, lows))]
        branch, second, lows, sums1 = feed_near(
            z2, gy, branch, second, after(lows, wide_sides[:3], thin0, wide3), side, near_dense
        )
        thin3 = along(after(thin1, sums1), 2)
        thin_sides += [beside(after(t, sums1)) for t in (thin1, thin2)]
        branch, second, lows, sums2 = feed_far(
            (0,), z2, gy, branch, second, after(lows, thin1, thin2), received, far_side,
            [wide0, wide_sides[0], thin0, thin_sides[0]],
        )
        thin_sides.append(beside(after(thin3, sums2)))
        branch, second, lows, sums3 = feed_far(
            (1, 2), z2, gy, branch, second, after(lows, thin3), received, far_side,
            [wide1, wide_sides[1], thin1, thin_sides[1], wide2, wide_sides[2], thin2, thin_sides[2]],
        )
        outa, outb, grad_hidden, grad_context, deltas, keep, give = feed_close(
            (3,), spot, pick, lengths, hidden, z2, gy, branch, second, lows, [sums0, sums1], [sums2, sums3],
            [c01, c23], outs_w, far, packs, tables, received, cotangent, cot_side, gains[2],
            [wide3, wide_sides[3], thin3, thin_sides[3]],
        )

        def crossing(here, other):
            both = jnp.stack([here, other])
            return along(both, 4)

        def first_turn(here, other, crossed):
            one = jnp.stack([here, crossed[0]])
            two = jnp.stack([other, crossed[1]])
            return [(one, along(one, 1)), (two, along(two, 2))]

        def second_turn(turns):
            one, two = [jnp.concatenate(t) for t in turns]
            return [one, along(one, 2), two, along(two, 1)]

        def whole_sum(table):
            bits = 8
            while bits < dp_size:
                table = table + along(table, bits)
                bits *= 2
            return table

        moved = beside(give)
        here, there = settle(spot, pick, keep, moved, 3 * half, True)
        other = across(there)
        gq01, own01, other01 = attend_back(
            after(spot, here), lengths, q01, kv01, kv01_side, grad_context, total01, deltas, 0
        )
        side01 = beside(other01)
        crossed = crossing(here, after(other, gq01))
        out_side = across(after(outb, other, gq01))
        gq23, own23, other23 = attend_back(
            after(spot, gq01, other), lengths, q23, kv23, kv23_side, grad_context, total23, deltas, 1
        )
        side23 = beside(other23)
        turns = first_turn(here, other, after(crossed, gq23))
        output = pair_up(after(spot, gq23), outa, out_side)
        g, gl, keep, give = gather_grads(
            after(spot, output), (gq01, own01, side01), (gq23, own23, side23), z, low, packs, received
        )
        moved = beside(give)
        early = second_turn(after(turns, g))
        here, there = settle(spot, pick, keep, moved, 3 * half, False)
        other = across(there)
        crossed = crossing(here, other)
        grada, gradb = finish(
            after(spot, other), pick, g, gl, inners, heads[:3] + near_heads[:3], far, inputs, received, grad_hidden,
            gains[0],
        )
        grad_side = across(after(gradb, crossed))
        turns = first_turn(here, other, after(crossed, grada))
        picks = jnp.concatenate([a[:, 0, -128:-122] for a in early]).astype(jnp.int32)
        adapters = query_inner.shape[0]
        units = widen_weight.shape[1]
        base = 3 * half
        early = combine(
            after(picks, grada),
            early,
            [
                (0, half, 4),
                (half, half, 3),
                (2 * half, half, 5),
                (base, units, 4),
                (base + units, units, 5),
                (base + 2 * units, width, 3),
            ],
            adapters,
        )
        early = [whole_sum(t) for t in early]
        early_shared = complete(spot, early[0], beside(early[0]))
        late = second_turn(turns)
        input_grad = pair_up(spot, grada, grad_side)
        late = combine(
            picks,
            late,
            [(n * half, half, n) for n in range(3)] + [(base + n * width, width, n) for n in range(3)],
            adapters,
        )
        late = [whole_sum(t) for t in late]
        late_shared = complete(spot, late[0], beside(late[0]))
        return (
            output,
            input_grad,
            flip(late_shared[0]),
            late[1],
            flip(late_shared[1]),
            late[2],
            flip(late_shared[2]),
            late[3],
            flip(early[3]),
            early_shared[1],
            flip(early_shared[0]),
            early[1],
            flip(early[2]),
            early_shared[2],
        )

    return body


def solution(mesh):
    placed = (
        P("dp", "tensor", None),
        P("dp", "tensor", None),
        P("dp"),
        P("dp", None),
        P(),
        P(),
        P(None, "tensor"),
        P(None, "tensor"),
        P(None, "tensor"),
        P("tensor", None),
        P(),
        P(),
        P(None, "tensor"),
        P("tensor", None),
        P(),
        P(None, None, "tensor"),
        P(),
        P(None, None, "tensor"),
        P(),
        P(None, None, "tensor"),
        P(None, "tensor", None),
        P(),
        P(),
        P(None, None, "tensor"),
        P(None, "tensor", None),
        P(),
    )
    return jax.shard_map(
        make_body(mesh.shape["dp"], mesh.shape["tensor"]),
        mesh=mesh,
        in_specs=placed,
        out_specs=(
            P("dp", "tensor", None),
            P("dp", "tensor", None),
            P(),
            P(None, None, "tensor"),
            P(),
            P(None, None, "tensor"),
            P(),
            P(None, None, "tensor"),
            P(None, "tensor", None),
            P(),
            P(),
            P(None, None, "tensor"),
            P(None, "tensor", None),
            P(),
        ),
        check_vma=False,
    )
```

time: 484 us -> 321 us (0.66)
  waiting for transfers between devices: 214 us -> 70.3 us
  other arithmetic: 9.06 us -> 1.81 us
  Pallas kernels: 173 us -> 166 us
    ppermute x53 -> x58, waiting for transfers between devices: 214 us -> 70.3 us  [swap(): return lax.ppermute(array, axis, [(i, i ^ bits) for i in range(size)])]
    unnamed x112 -> x217, local copies, waits for them, and re-layouts: 17 us -> 25 us
    pallas_call x12 -> x27, Pallas kernels: 173 us -> 166 us  [call(): pl.pallas_call(body, grid_spec=pltpu.PrefetchScalarGridSpec(num_scalar_pr...]
    ppermute x53 -> x58, starting transfers between devices: 42.9 us -> 40.3 us  [swap(): return lax.ppermute(array, axis, [(i, i ^ bits) for i in range(size)])]
  transfers between devices with their start and end apart: 53 -> 58, of which waited for: 16 -> 17; matrix products, arithmetic and copies ran while one was open for 6% -> 3% of each run, Pallas kernels for 28% -> 46%
where the time goes in v2:
time: 321 us; the launch traced here: 315 us
  Pallas kernels  166 us (52%)
  waiting for transfers between devices  70.3 us (22%)
  starting transfers between devices  40.3 us (13%)
  local copies, waits for them, and re-layouts  34.1 us (11%)
    pallas_call x27, Pallas kernels, call(): pl.pallas_call(body, grid_spec=pltpu.PrefetchScalarGridSpec(num_scalar_pr...  166 us
    ppermute x58, waiting for transfers between devices, swap(): return lax.ppermute(array, axis, [(i, i ^ bits) for i in range(size)])  70.3 us
    ppermute x58, starting transfers between devices, swap(): return lax.ppermute(array, axis, [(i, i ^ bits) for i in range(size)])  40.3 us
    unnamed x217, local copies, waits for them, and re-layouts  25 us
  transfers between devices with their start and end apart: 58, of which 17 were waited for; matrix products, arithmetic and copies ran while one was open for 3% of the time, Pallas kernels for 46%

profile of v2, /device:TPU:0, one launch (start us, length us, event | category | flops | bytes accessed | tf_op | source)
XLA Modules:
  0.0 314.7 jit_solution(16753646487423535968)
XLA Ops:
  15.7 9.5 %collective-permute-done.refs_0_ = bf16[4,80,1280]{2,1,0:T(8,128)(2,1)} collective-permute-done((bf16[4,80,1280]{2,1,0:T(8,128)(2,1)}, bf16[4,80,1280]{2,1,0:T(8,128)(2,1)}, u32[]{:S(2)}, u32[]{:S(2)}) %collective-permute-start) | collective-permute-done | bytes 819232 | tf_op jit(solution)/shard_map/ppermute | solution.py:23
  33.5 18.2 %collective-permute-done.11.xb.received_ref.refs_8_ = bf16[304,1280]{1,0:T(8,128)(2,1)S(1)} collective-permute-done((bf16[304,1280]{1,0:T(8,128)(2,1)S(1)}, bf16[304,1280]{1,0:T(8,128)(2,1)S(1)}, u32[]{:S(2)}, u32[]{:S(2)}) %collective-permute-start.11) | collective-permute-done | bytes 778272 | tf_op jit(solution)/shard_map/ppermute | solution.py:23
  57.4 5.2 %shard_map.356 = (bf16[512,1280]{1,0:T(8,128)(2,1)S(1)}, f32[48,512]{1,0:T(8,128)S(1)}, bf16[2,2,320,512]{3,2,1,0:T(8,128)(2,1)S(1)}) custom-call(s32[4]{0:T(128)S(1)} %pad_add_fusion.spot_ref, s32[2,6]{1,0:T(2,128)S(1)} %copy-done.77, bf16[2,256,1280]{2,1,0:T(8,128)(2,1)S(1)} %copy-done.22, ...), custom_call_target="tpu_custom_call" | custom-call | flops 99999997952 | bytes 100000 | tf_op jit(solution)/shard_map/pallas_call | solution.py:85
  69.0 8.4 %shard_map.358 = (bf16[2,320,512]{2,1,0:T(8,128)(2,1)S(1)}, f32[8,1,512]{2,1,0:T(1,128)S(1)}) custom-call(s32[4]{0:T(128)S(1)} %pad_add_fusion.spot_ref, s32[2]{0:T(128)S(1)} %copy-done.79, bf16[2,320,512]{2,1,0:T(8,128)(2,1)S(1)} %shard_map.357.q_ref, bf16[2,2,320,512]{3,2,1,0:T(8,128)(2,1)S(1)} %get-tuple-element.149.k1.v1, ...), custom_call_target="tpu_custom_call" | custom-call | flops 99999997952 | bytes 100000 | tf_op jit(solution)/shard_map/pallas_call | solution.py:85
  81.2 4.7 %shard_map.359 = (bf16[2,4,320,1280]{3,2,1,0:T(8,128)(2,1)S(1)}, bf16[2,2,320,512]{3,2,1,0:T(8,128)(2,1)S(1)}) custom-call(s32[1]{0:T(128)} %slice.36.spot_ref, bf16[512,1280]{1,0:T(8,128)(2,1)S(1)} %get-tuple-element.162.z_ref, f32[48,512]{1,0:T(8,128)S(1)} %get-tuple-element.154.low_ref, bf16[304,1280]{1,0:T(8,128)(2,1)S(1)} %copy-done.3, ...), custom_call_target="tpu_custom_call" | custom-call | flops 99999997952 | bytes 100000 | tf_op jit(solution)/shard_map/pallas_call | solution.py:85
  92.4 8.2 %shard_map.361 = (bf16[2,320,512]{2,1,0:T(8,128)(2,1)S(1)}, f32[8,1,512]{2,1,0:T(1,128)S(1)}) custom-call(s32[4]{0:T(128)S(1)} %copy-done.10, s32[2]{0:T(128)S(1)} %copy-done.80, bf16[2,320,512]{2,1,0:T(8,128)(2,1)S(1)} %shard_map.360.q_ref, bf16[2,2,320,512]{3,2,1,0:T(8,128)(2,1)S(1)} %get-tuple-element.161.k1.v1, ...), custom_call_target="tpu_custom_call" | custom-call | flops 99999997952 | bytes 100000 | tf_op jit(solution)/shard_map/pallas_call | solution.py:85
  105.1 6.0 %shard_map.362 = (f32[512,1280]{1,0:T(8,128)S(1)}, bf16[512,1280]{1,0:T(8,128)(2,1)S(1)}, f32[32,512]{1,0:T(8,128)S(1)}) custom-call(s32[4]{0:T(128)S(1)} %copy-done.10, s32[2,6]{1,0:T(2,128)S(1)} %copy-done.78, s32[2]{0:T(128)S(1)} %copy-done.80, bf16[2,320,512]{2,1,0:T(8,128)(2,1)S(1)} %get-tuple-element.155.c01, ...), custom_call_target="tpu_custom_call" | custom-call | flops 99999997952 | bytes 100000 | tf_op jit(solution)/shard_map/pallas_call | solution.py:85
  113.8 13.0 %shard_map.363 = (bf16[512,1280]{1,0:T(8,128)(2,1)S(1)}, f32[512,1280]{1,0:T(8,128)S(1)}, f32[512,1280]{1,0:T(8,128)S(1)}, f32[80,512]{1,0:T(8,128)S(1)}, f32[32,1280]{1,0:T(8,128)S(1)}) custom-call(s32[4]{0:T(128)S(1)} %copy-done.10, s32[2,6]{1,0:T(2,128)S(1)} %copy-done.78, s32[2]{0:T(128)S(1)} %copy-done.80, ...), custom_call_target="tpu_custom_call" | custom-call | flops 99999997952 | bytes 100000 | tf_op jit(solution)/shard_map/pallas_call | solution.py:85
  127.0 7.2 %collective-permute-done.29.refs_0_ = bf16[320,1280]{1,0:T(8,128)(2,1)} collective-permute-done((bf16[320,1280]{1,0:T(8,128)(2,1)}, bf16[320,1280]{1,0:T(8,128)(2,1)}, u32[]{:S(2)}, u32[]{:S(2)}) %collective-permute-start.29) | collective-permute-done | bytes 819232 | tf_op jit(solution)/shard_map/ppermute | solution.py:23
  136.1 11.2 %shard_map.364 = (f32[512,1280]{1,0:T(8,128)S(1)}, f32[512,1280]{1,0:T(8,128)S(1)}, f32[80,512]{1,0:T(8,128)S(1)}, f32[32,1280]{1,0:T(8,128)S(1)}) custom-call(bf16[512,1280]{1,0:T(8,128)(2,1)S(1)} %get-tuple-element.166.z_ref, bf16[512,1280]{1,0:T(8,128)(2,1)S(1)} %get-tuple-element.170.gy_ref, ...), custom_call_target="tpu_custom_call", output_to_operand_aliasing={{0}: (2, {}), {1}: (3, {})} | custom-call | flops 99999997952 | bytes 100000 | tf_op jit(solution)/shard_map/pallas_call | solution.py:85
  147.3 7.0 %collective-permute-done.30.refs_2_ = bf16[320,1280]{1,0:T(8,128)(2,1)S(1)} collective-permute-done((bf16[320,1280]{1,0:T(8,128)(2,1)}, bf16[320,1280]{1,0:T(8,128)(2,1)S(1)}, u32[]{:S(2)}, u32[]{:S(2)}) %collective-permute-start.30) | collective-permute-done | bytes 819232 | tf_op jit(solution)/shard_map/ppermute | solution.py:23
  156.2 7.4 %shard_map.365 = (f32[512,1280]{1,0:T(8,128)S(1)}, f32[512,1280]{1,0:T(8,128)S(1)}, f32[80,512]{1,0:T(8,128)S(1)}, f32[1,32,640]{2,1,0:T(8,128)S(1)}) custom-call(bf16[512,1280]{1,0:T(8,128)(2,1)S(1)} %get-tuple-element.166.z_ref, bf16[512,1280]{1,0:T(8,128)(2,1)S(1)} %get-tuple-element.170.gy_ref, ...), custom_call_target="tpu_custom_call", output_to_operand_aliasing={{0}: (2, {}), {1}: (3, {})} | custom-call | flops 99999997952 | bytes 100000 | tf_op jit(solution)/shard_map/pallas_call | solution.py:85
  163.5 11.5 %collective-permute-done.33.refs_2_ = bf16[320,1280]{1,0:T(8,128)(2,1)S(1)} collective-permute-done((bf16[320,1280]{1,0:T(8,128)(2,1)S(1)}, bf16[320,1280]{1,0:T(8,128)(2,1)S(1)}, u32[]{:S(2)}, u32[]{:S(2)}) %collective-permute-start.33) | collective-permute-done | bytes 819232 | tf_op jit(solution)/shard_map/ppermute | solution.py:23
  175.2 12.9 %shard_map.366 = (f32[512,1280]{1,0:T(8,128)S(1)}, f32[512,1280]{1,0:T(8,128)S(1)}, f32[80,512]{1,0:T(8,128)S(1)}, f32[2,32,640]{2,1,0:T(8,128)S(1)}) custom-call(bf16[512,1280]{1,0:T(8,128)(2,1)S(1)} %get-tuple-element.166.z_ref, bf16[512,1280]{1,0:T(8,128)(2,1)S(1)} %get-tuple-element.170.gy_ref, ...), custom_call_target="tpu_custom_call", output_to_operand_aliasing={{0}: (2, {}), {1}: (3, {})} | custom-call | flops 99999997952 | bytes 100000 | tf_op jit(solution)/shard_map/pallas_call | solution.py:85
  191.5 14.6 %shard_map.367 = (bf16[256,1280]{1,0:T(8,128)(2,1)S(1)}, bf16[256,1280]{1,0:T(8,128)(2,1)S(1)}, f32[512,1280]{1,0:T(8,128)S(1)}, bf16[4,320,512]{2,1,0:T(8,128)(...) custom-call(s32[4]{0:T(128)S(1)} %copy-done.11, s32[2,6]{1,0:T(2,128)S(1)} %copy-done.78, ...), custom_call_target="tpu_custom_call" | custom-call | flops 99999997952 | bytes 100000 | tf_op jit(solution)/shard_map/pallas_call | solution.py:85
  210.0 13.9 %shard_map.369 = (bf16[2,320,512]{2,1,0:T(8,128)(2,1)S(1)}, f32[2,2,320,512]{3,2,1,0:T(8,128)S(1)}, f32[2,2,320,512]{3,2,1,0:T(8,128)}) custom-call(s32[4]{0:T(128)S(1)} %copy-done.11, s32[2]{0:T(128)S(1)} %copy-done.81, bf16[2,320,512]{2,1,0:T(8,128)(2,1)S(1)} %copy-done.98, bf16[2,2,320,512]{3,2,1,0:T(8,128)(2,1)S(1)} %copy-done.26, ...), custom_call_target="tpu_custom_call" | custom-call | flops 99999997952 | bytes 100000 | tf_op jit(solution)/shard_map/pallas_call | solution.py:85
  227.5 13.5 %shard_map.370 = (bf16[2,320,512]{2,1,0:T(8,128)(2,1)S(1)}, f32[2,2,320,512]{3,2,1,0:T(8,128)S(1)}, f32[2,2,320,512]{3,2,1,0:T(8,128)S(1)}) custom-call(s32[4]{0:T(128)S(1)} %copy-done.11, s32[2]{0:T(128)S(1)} %copy-done.81, bf16[2,320,512]{2,1,0:T(8,128)(2,1)S(1)} %copy-done.96, bf16[2,2,320,512]{3,2,1,0:T(8,128)(2,1)S(1)} %copy-done.30, ...), custom_call_target="tpu_custom_call" | custom-call | flops 99999997952 | bytes 100000 | tf_op jit(solution)/shard_map/pallas_call | solution.py:85
  246.6 4.8 %shard_map.372 = (bf16[4,3,320,512]{3,2,1,0:T(8,128)(2,1)S(1)}, f32[48,512]{1,0:T(8,128)S(1)}, f32[16,3968]{1,0:T(8,128)S(1)}, f32[16,3968]{1,0:T(8,128)S(1)}) custom-call(s32[4]{0:T(128)S(1)} %copy-done.11, bf16[2,320,512]{2,1,0:T(8,128)(2,1)S(1)} %get-tuple-element.209.q01, f32[2,2,320,512]{3,2,1,0:T(8,128)S(1)} %get-tuple-element.219.own01, ...), custom_call_target="tpu_custom_call" | custom-call | flops 99999997952 | bytes 100000 | tf_op jit(solution)/shard_map/pallas_call | solution.py:85
  266.7 3.4 %collective-permute-done.44 = bf16[16,2944]{1,0:T(8,128)(2,1)S(1)} collective-permute-done((bf16[16,2944]{1,0:T(8,128)(2,1)S(1)}, bf16[16,2944]{1,0:T(8,128)(2,1)S(1)}, u32[]{:S(2)}, u32[]{:S(2)}) %collective-permute-start.44) | collective-permute-done | bytes 94240 | tf_op jit(solution)/shard_map/ppermute | solution.py:23
  272.8 13.3 %shard_map.374 = (f32[256,1280]{1,0:T(8,128)S(1)}, bf16[256,1280]{1,0:T(8,128)(2,1)}) custom-call(s32[4]{0:T(128)S(1)} %copy-done.11, s32[2,6]{1,0:T(2,128)S(1)} %copy-done.78, bf16[4,3,320,512]{3,2,1,0:T(8,128)(2,1)S(1)} %get-tuple-element.227.g_ref, f32[48,512]{1,0:T(8,128)S(1)} %get-tuple-element.228.gl_ref, bf16[8,16,1280]{2,1,0:T(8,128)(2,1)S(1)} %bitcast.44, ...), custom_call_target="tpu_custom_call" | custom-call | flops 99999997952 | bytes 100000 | tf_op jit(solution)/shard_map/pallas_call | solution.py:85
  294.0 4.2 %shard_map.378 = (f32[3,8,16,640]{3,2,1,0:T(8,128)}, f32[8,16,1280]{2,1,0:T(8,128)}, f32[8,16,1280]{2,1,0:T(8,128)}, f32[8,16,320]{2,1,0:T(8,128)}) custom-call(s32[16,6]{1,0:T(8,128)S(1)} %maximum_convert_fusion.pick_ref, bf16[4,16,4992]{2,1,0:T(8,128)(2,1)} %constant_dynamic-update-slice_fusion.refs_0_, ...), custom_call_target="tpu_custom_call" | custom-call | flops 99999997952 | bytes 100000 | tf_op jit(solution)/shard_map/pallas_call | solution.py:85
  304.1 3.3 %shard_map.375 = f32[2,256,1280]{2,1,0:T(8,128)} custom-call(s32[4]{0:T(128)S(1)} %copy-done.11, f32[256,1280]{1,0:T(8,128)S(1)} %get-tuple-element.230.first_ref, bf16[256,1280]{1,0:T(8,128)(2,1)} %collective-permute-done.46.second_ref), custom_call_target="tpu_custom_call" | custom-call | flops 99999997952 | bytes 100000 | tf_op jit(solution)/shard_map/pallas_call | solution.py:85
  307.4 3.4 %shard_map.379 = (f32[8,16,1280]{2,1,0:T(8,128)}, f32[8,16,1280]{2,1,0:T(8,128)}, f32[8,16,1280]{2,1,0:T(8,128)}) custom-call(s32[4]{0:T(128)S(1)} %copy-done.11, f32[3,8,16,640]{3,2,1,0:T(8,128)} %get-tuple-element.250.own_ref, f32[3,8,16,640]{3,2,1,0:T(8,128)} %collective-permute-done.57.moved_ref), custom_call_target="tpu_custom_call" | custom-call | flops 99999997952 | bytes 100000 | tf_op jit(solution)/shard_map/pallas_call | solution.py:85
  310.8 3.4 %shard_map.377 = (f32[8,16,1280]{2,1,0:T(8,128)}, f32[8,16,1280]{2,1,0:T(8,128)}, f32[8,16,1280]{2,1,0:T(8,128)}) custom-call(s32[4]{0:T(128)S(1)} %copy-done.11, f32[3,8,16,640]{3,2,1,0:T(8,128)} %get-tuple-element.241.own_ref, f32[3,8,16,640]{3,2,1,0:T(8,128)} %collective-permute-done.56.moved_ref), custom_call_target="tpu_custom_call" | custom-call | flops 99999997952 | bytes 100000 | tf_op jit(solution)/shard_map/pallas_call | solution.py:85
  (362 shorter events, 104.3 us)
Async XLA Ops:
  3.6 21.6 %collective-permute-start = (bf16[4,80,1280]{2,1,0:T(8,128)(2,1)}, bf16[4,80,1280]{2,1,0:T(8,128)(2,1)}, u32[]{:S(2)}, u32[]{:S(2)}) collective-permute-start(bf16[4,80,1280]{2,1,0:T(8,128)(2,1)} %shard_map.353), channel_id=1, source_target_pairs={{0,2},{1,3},{2,0},{3,1},{4,6},{5,7},{6,4},{7,5},{8,10},{9,11},{10,... | collective-permute-start | bytes 2457608 | tf_op jit(solution)/shard_map/ppermute | solution.py:23
  25.2 28.7 %collective-permute-start.2 = (bf16[4,80,1280]{2,1,0:T(8,128)(2,1)}, bf16[4,80,1280]{2,1,0:T(8,128)(2,1)S(1)}, u32[]{:S(2)}, u32[]{:S(2)}) collective-permute-start(bf16[4,80,1280]{2,1,0:T(8,128)(2,1)} %collective-permute-done.refs_0_), channel_id=1, source_target_pairs={{0,4},{4,0},{8,12},{12,8},{16,20},{20,16},{24,28},{28,24},{1,5},{5... | collective-permute-start | bytes 2457608 | tf_op jit(solution)/shard_map/ppermute | solution.py:23
  26.9 28.2 %collective-permute-start.1 = (bf16[4,80,1280]{2,1,0:T(8,128)(2,1)}, bf16[4,80,1280]{2,1,0:T(8,128)(2,1)S(1)}, u32[]{:S(2)}, u32[]{:S(2)}) collective-permute-start(bf16[4,80,1280]{2,1,0:T(8,128)(2,1)} %collective-permute-done.refs_0_), channel_id=1, source_target_pairs={{0,8},{4,12},{8,0},{12,4},{16,24},{20,28},{24,16},{28,20},{1,9},{5... | collective-permute-start | bytes 2457608 | tf_op jit(solution)/shard_map/ppermute | solution.py:23
  31.9 24.5 %collective-permute-start.10 = (bf16[4,80,1280]{2,1,0:T(8,128)(2,1)}, bf16[4,80,1280]{2,1,0:T(8,128)(2,1)S(1)}, u32[]{:S(2)}, u32[]{:S(2)}) collective-permute-start(bf16[4,80,1280]{2,1,0:T(8,128)(2,1)} %collective-permute-done.refs_0_), channel_id=1, source_target_pairs={{0,1},{1,0},{2,3},{3,2},{4,5},{5,4},{6,7},{7,6},{8,9},{9,8},{10,11... | collective-permute-start | bytes 2457608 | tf_op jit(solution)/shard_map/ppermute | solution.py:23
  31.9 19.8 %collective-permute-start.11 = (bf16[304,1280]{1,0:T(8,128)(2,1)S(1)}, bf16[304,1280]{1,0:T(8,128)(2,1)S(1)}, u32[]{:S(2)}, u32[]{:S(2)}) collective-permute-start(bf16[304,1280]{1,0:T(8,128)(2,1)S(1)} %get-tuple-element.148), channel_id=1, source_target_pairs={{0,2},{1,3},{2,0},{3,1},{4,6},{5,7},{6,4},{7,5},{8,10},{9,11},{10,... | collective-permute-start | bytes 2334728 | tf_op jit(solution)/shard_map/ppermute | solution.py:23
  51.7 25.7 %collective-permute-start.15 = (bf16[320,1280]{1,0:T(8,128)(2,1)}, bf16[320,1280]{1,0:T(8,128)(2,1)}, u32[]{:S(2)}, u32[]{:S(2)}) collective-permute-start(bf16[320,1280]{1,0:T(8,128)(2,1)} %get-tuple-element.156), channel_id=1, source_target_pairs={{0,2},{1,3},{2,0},{3,1},{4,6},{5,7},{6,4},{7,5},{8,10},{9,11},{10,... | collective-permute-start | bytes 2457608 | tf_op jit(solution)/shard_map/ppermute | solution.py:23
  77.4 35.3 %collective-permute-start.24 = (bf16[320,1280]{1,0:T(8,128)(2,1)}, bf16[320,1280]{1,0:T(8,128)(2,1)}, u32[]{:S(2)}, u32[]{:S(2)}) collective-permute-start(bf16[320,1280]{1,0:T(8,128)(2,1)} %collective-permute-done.15.refs_0_), channel_id=1, source_target_pairs={{0,8},{4,12},{8,0},{12,4},{16,24},{20,28},{24,16},{28,20},{1,9},{5... | collective-permute-start | bytes 2457608 | tf_op jit(solution)/shard_map/ppermute | solution.py:23
  79.0 33.6 %collective-permute-start.23 = (bf16[320,1280]{1,0:T(8,128)(2,1)}, bf16[320,1280]{1,0:T(8,128)(2,1)}, u32[]{:S(2)}, u32[]{:S(2)}) collective-permute-start(bf16[320,1280]{1,0:T(8,128)(2,1)} %collective-permute-done.15.refs_0_), channel_id=1, source_target_pairs={{0,4},{4,0},{8,12},{12,8},{16,20},{20,16},{24,28},{28,24},{1,5},{5... | collective-permute-start | bytes 2457608 | tf_op jit(solution)/shard_map/ppermute | solution.py:23
  86.0 27.3 %collective-permute-start.22 = (bf16[256,1280]{1,0:T(8,128)(2,1)}, bf16[256,1280]{1,0:T(8,128)(2,1)}, u32[]{:S(2)}, u32[]{:S(2)}) collective-permute-start(bf16[256,1280]{1,0:T(8,128)(2,1)} %get-tuple-element.169), channel_id=1, source_target_pairs={{0,2},{1,3},{2,0},{3,1},{4,6},{5,7},{6,4},{7,5},{8,10},{9,11},{10,... | collective-permute-start | bytes 1966088 | tf_op jit(solution)/shard_map/ppermute | solution.py:23
  100.6 26.2 %collective-permute-start.28 = (bf16[320,1280]{1,0:T(8,128)(2,1)}, bf16[320,1280]{1,0:T(8,128)(2,1)}, u32[]{:S(2)}, u32[]{:S(2)}) collective-permute-start(bf16[320,1280]{1,0:T(8,128)(2,1)} %get-tuple-element.179), channel_id=1, source_target_pairs={{0,2},{1,3},{2,0},{3,1},{4,6},{5,7},{6,4},{7,5},{8,10},{9,11},{10,... | collective-permute-start | bytes 2457608 | tf_op jit(solution)/shard_map/ppermute | solution.py:23
  112.7 22.0 %collective-permute-start.25 = (bf16[320,1280]{1,0:T(8,128)(2,1)}, bf16[320,1280]{1,0:T(8,128)(2,1)S(1)}, u32[]{:S(2)}, u32[]{:S(2)}) collective-permute-start(bf16[320,1280]{1,0:T(8,128)(2,1)} %collective-permute-done.15.refs_0_), channel_id=1, source_target_pairs={{0,1},{1,0},{2,3},{3,2},{4,5},{5,4},{6,7},{7,6},{8,9},{9,8},{10,11... | collective-permute-start | bytes 2457608 | tf_op jit(solution)/shard_map/ppermute | solution.py:23
  112.7 22.4 %collective-permute-start.26 = (bf16[320,1280]{1,0:T(8,128)(2,1)}, bf16[320,1280]{1,0:T(8,128)(2,1)S(1)}, u32[]{:S(2)}, u32[]{:S(2)}) collective-permute-start(bf16[320,1280]{1,0:T(8,128)(2,1)} %collective-permute-done.23.refs_0_), channel_id=1, source_target_pairs={{0,1},{1,0},{2,3},{3,2},{4,5},{5,4},{6,7},{7,6},{8,9},{9,8},{10,11... | collective-permute-start | bytes 2457608 | tf_op jit(solution)/shard_map/ppermute | solution.py:23
  113.2 21.9 %collective-permute-start.27 = (bf16[320,1280]{1,0:T(8,128)(2,1)}, bf16[320,1280]{1,0:T(8,128)(2,1)S(1)}, u32[]{:S(2)}, u32[]{:S(2)}) collective-permute-start(bf16[320,1280]{1,0:T(8,128)(2,1)} %collective-permute-done.24.refs_4_), channel_id=1, source_target_pairs={{0,1},{1,0},{2,3},{3,2},{4,5},{5,4},{6,7},{7,6},{8,9},{9,8},{10,11... | collective-permute-start | bytes 2457608 | tf_op jit(solution)/shard_map/ppermute | solution.py:23
  113.3 20.9 %collective-permute-start.29 = (bf16[320,1280]{1,0:T(8,128)(2,1)}, bf16[320,1280]{1,0:T(8,128)(2,1)}, u32[]{:S(2)}, u32[]{:S(2)}) collective-permute-start(bf16[320,1280]{1,0:T(8,128)(2,1)} %collective-permute-done.24.refs_4_), channel_id=1, source_target_pairs={{0,4},{4,0},{8,12},{12,8},{16,20},{20,16},{24,28},{28,24},{1,5},{5... | collective-permute-start | bytes 2457608 | tf_op jit(solution)/shard_map/ppermute | solution.py:23
  126.8 29.3 %collective-permute-start.32 = (bf16[320,1280]{1,0:T(8,128)(2,1)}, bf16[320,1280]{1,0:T(8,128)(2,1)S(1)}, u32[]{:S(2)}, u32[]{:S(2)}) collective-permute-start(bf16[320,1280]{1,0:T(8,128)(2,1)} %collective-permute-done.28.refs_2_), channel_id=1, source_target_pairs={{0,1},{1,0},{2,3},{3,2},{4,5},{5,4},{6,7},{7,6},{8,9},{9,8},{10,11... | collective-permute-start | bytes 2457608 | tf_op jit(solution)/shard_map/ppermute | solution.py:23
  134.2 21.8 %collective-permute-start.31 = (bf16[320,1280]{1,0:T(8,128)(2,1)}, bf16[320,1280]{1,0:T(8,128)(2,1)S(1)}, u32[]{:S(2)}, u32[]{:S(2)}) collective-permute-start(bf16[320,1280]{1,0:T(8,128)(2,1)} %collective-permute-done.28.refs_2_), channel_id=1, source_target_pairs={{0,8},{4,12},{8,0},{12,4},{16,24},{20,28},{24,16},{28,20},{1,9},{5... | collective-permute-start | bytes 2457608 | tf_op jit(solution)/shard_map/ppermute | solution.py:23
  134.6 19.7 %collective-permute-start.30 = (bf16[320,1280]{1,0:T(8,128)(2,1)}, bf16[320,1280]{1,0:T(8,128)(2,1)S(1)}, u32[]{:S(2)}, u32[]{:S(2)}) collective-permute-start(bf16[320,1280]{1,0:T(8,128)(2,1)} %collective-permute-done.28.refs_2_), channel_id=1, source_target_pairs={{0,4},{4,0},{8,12},{12,8},{16,20},{20,16},{24,28},{28,24},{1,5},{5... | collective-permute-start | bytes 2457608 | tf_op jit(solution)/shard_map/ppermute | solution.py:23
  136.1 53.5 %collective-permute-start.36 = (bf16[320,1280]{1,0:T(8,128)(2,1)}, bf16[320,1280]{1,0:T(8,128)(2,1)}, u32[]{:S(2)}, u32[]{:S(2)}) collective-permute-start(bf16[320,1280]{1,0:T(8,128)(2,1)} %collective-permute-done.29.refs_0_), channel_id=1, source_target_pairs={{0,1},{1,0},{2,3},{3,2},{4,5},{5,4},{6,7},{7,6},{8,9},{9,8},{10,11... | collective-permute-start | bytes 2457608 | tf_op jit(solution)/shard_map/ppermute | solution.py:23
  154.4 20.7 %collective-permute-start.34 = (bf16[320,1280]{1,0:T(8,128)(2,1)S(1)}, bf16[320,1280]{1,0:T(8,128)(2,1)S(1)}, u32[]{:S(2)}, u32[]{:S(2)}) collective-permute-start(bf16[320,1280]{1,0:T(8,128)(2,1)S(1)} %collective-permute-done.30.refs_2_), channel_id=1, source_target_pairs={{0,1},{1,0},{2,3},{3,2},{4,5},{5,4},{6,7},{7,6},{8,9},{9,8},{10,11... | collective-permute-start | bytes 2457608 | tf_op jit(solution)/shard_map/ppermute | solution.py:23
  154.4 20.7 %collective-permute-start.33 = (bf16[320,1280]{1,0:T(8,128)(2,1)S(1)}, bf16[320,1280]{1,0:T(8,128)(2,1)S(1)}, u32[]{:S(2)}, u32[]{:S(2)}) collective-permute-start(bf16[320,1280]{1,0:T(8,128)(2,1)S(1)} %collective-permute-done.30.refs_2_), channel_id=1, source_target_pairs={{0,8},{4,12},{8,0},{12,4},{16,24},{20,28},{24,16},{28,20},{1,9},{5... | collective-permute-start | bytes 2457608 | tf_op jit(solution)/shard_map/ppermute | solution.py:23
  155.9 19.1 %collective-permute-start.35 = (bf16[320,1280]{1,0:T(8,128)(2,1)S(1)}, bf16[320,1280]{1,0:T(8,128)(2,1)S(1)}, u32[]{:S(2)}, u32[]{:S(2)}) collective-permute-start(bf16[320,1280]{1,0:T(8,128)(2,1)S(1)} %collective-permute-done.31.refs_6_), channel_id=1, source_target_pairs={{0,1},{1,0},{2,3},{3,2},{4,5},{5,4},{6,7},{7,6},{8,9},{9,8},{10,11... | collective-permute-start | bytes 2457608 | tf_op jit(solution)/shard_map/ppermute | solution.py:23
  223.9 22.7 %collective-permute-start.41 = (f32[2,2,320,512]{3,2,1,0:T(8,128)}, f32[2,2,320,512]{3,2,1,0:T(8,128)}, u32[]{:S(2)}, u32[]{:S(2)}) collective-permute-start(f32[2,2,320,512]{3,2,1,0:T(8,128)} %get-tuple-element.220), channel_id=1, source_target_pairs={{0,1},{1,0},{2,3},{3,2},{4,5},{5,4},{6,7},{7,6},{8,9},{9,8},{10,11... | collective-permute-start | bytes 7864328 | tf_op jit(solution)/shard_map/ppermute | solution.py:23
  257.3 30.7 %collective-permute-start.51 = (bf16[4,16,4992]{2,1,0:T(8,128)(2,1)}, bf16[4,16,4992]{2,1,0:T(8,128)(2,1)}, u32[]{:S(2)}, u32[]{:S(2)}) collective-permute-start(bf16[4,16,4992]{2,1,0:T(8,128)(2,1)} %constant_dynamic-update-slice_fusion.2.refs_2_), channel_id=1, source_target_pairs={{0,4},{4,0},{8,12},{12,8},{16,20},{20,16},{24,28},{28,24},{1,5},{5... | collective-permute-start | bytes 1916936 | tf_op jit(solution)/shard_map/ppermute | solution.py:23
  262.9 25.8 %collective-permute-start.50 = (bf16[4,16,4992]{2,1,0:T(8,128)(2,1)}, bf16[4,16,4992]{2,1,0:T(8,128)(2,1)}, u32[]{:S(2)}, u32[]{:S(2)}) collective-permute-start(bf16[4,16,4992]{2,1,0:T(8,128)(2,1)} %constant_dynamic-update-slice_fusion.refs_0_), channel_id=1, source_target_pairs={{0,8},{4,12},{8,0},{12,4},{16,24},{20,28},{24,16},{28,20},{1,9},{5... | collective-permute-start | bytes 1916936 | tf_op jit(solution)/shard_map/ppermute | solution.py:23
  (140 other events, 1654.5 us)

commit v3 on v2

--- a/solution.py
+++ b/solution.py
@@ -14,7 +14,7 @@
 neg_fill = -1000000000.0
 score_scale = 1.0 / math.sqrt(HEAD_DIM)
 log2_e = math.log2(math.e)
-LIMIT = 26
+LIMIT = 16
 KEEP = pl.BlockSpec(memory_space=pltpu.VMEM)
 remain = pl.BlockSpec(memory_space=pl.ANY)
 
@@ -168,7 +168,7 @@
     part = units // 4
     rows = cotangent.shape[1]
 
-    def body(spot_ref, wide_ref, thin_ref, cot_ref, wide_out, thin_out, cot_out):
+    def body(spot_ref, wide_ref, thin_ref, last_ref, cot_ref, wide_out, thin_out, last_out, cot_out):
         for r in range(4):
 
             @pl.when(spot_ref[2] == r)
@@ -176,15 +176,17 @@
                 wide_out[...] = wide_ref[:, r * part : (r + 1) * part].T
 
         thin_out[...] = thin_ref[...]
+        last_out[...] = last_ref[...]
         cot_out[...] = cot_ref[0]
 
     specs = [
         whole(wide.shape),
         placed_block((part, features), lambda i, spot: (spot[2], 0)),
+        placed_block((part, features), lambda i, spot: (spot[2] ^ 3, 0)),
         placed_block((1, rows, features), lambda i, spot: (spot[1], 0, 0)),
     ]
-    outs = [shaped((part, features), bf16), shaped((part, features), bf16), shaped((rows, features), bf16)]
-    return call(body, (spot,), [wide, thin, cotangent], specs, outs, [whole(o.shape) for o in outs])
+    outs = [shaped((part, features), bf16)] * 3 + [shaped((rows, features), bf16)]
+    return call(body, (spot,), [wide, thin, thin, cotangent], specs, outs, [whole(o.shape) for o in outs])
 
 
 def project_rows(weight, rows_in, outer, low):
@@ -256,7 +258,7 @@
     flat = [p for group in parts for p in group]
 
     def body(spot_ref, z_ref, low_ref, received_ref, side_ref, *refs):
-        ins, (weight_ref, kv_ref) = refs[:10], refs[10:]
+        ins, (out_ref, kv_ref, weight_ref, sems) = refs[:10], refs[10:]
         for i in range(2):
             group = ins[5 * i : 5 * i + 5]
             for n in range(4):
@@ -266,17 +268,23 @@
                         weight_ref[i, n, at] = group[r][n]
                     else:
                         weight_ref[i, n, at] = group[3 + n // 2][n % 2]
+        copies = [pltpu.make_async_copy(weight_ref.at[i], out_ref.at[i], sems.at[i]) for i in range(2)]
+        for c in copies:
+            c.start()
         for i, (ref, start) in enumerate(((received_ref, base), (side_ref, 0))):
             for n in (1, 2):
                 outer = ref[start : start + rank, n * width : (n + 1) * width]
                 kv_ref[i, n - 1] = project_rows(
                     weight_ref[i, n], z_ref[...], outer, low_ref[n * rank : (n + 1) * rank]
                 )
+        for c in copies:
+            c.wait()
 
     operands = [z, low, received, side] + flat
     outs = [shaped((2, 4, width, features), bf16), shaped((2, 2, width, tokens), bf16)]
     return call(
-        body, (spot[2:3],), operands, [whole(o.shape) for o in operands], outs, [whole(o.shape) for o in outs]
+        body, (spot[2:3],), operands, [KEEP] * len(operands), outs, [remain, KEEP],
+        scratch=[pltpu.VMEM((2, 4, width, features), bf16), pltpu.SemaphoreType.DMA((2,))],
     )
 
 
@@ -337,11 +345,12 @@
     )
 
 
-def attend_back(spot, lengths, q, kv, kv_side, grad_context, totals, deltas, which):
+def attend_back(spot, lengths, q, kv, kv_side, grad_context, totals, deltas, number):
     _, width, tokens = q.shape
     rows = tokens // 2
     pair = 2 * HEAD_DIM
     steps = width // pair
+    at_hand = number % 2
 
     def body(spot_ref, length_ref, q_ref, k1, k2, v1, v2, g_ref, total_ref, delta_ref, gq, own_ref, other_ref):
         bias1 = jnp.where(live_column(spot_ref, length_ref, rows, (0, 2)), 0.0, neg_fill * log2_e)
@@ -358,30 +367,29 @@
                 grad_scores = (soft * (grad_soft - delta_ref[h])).astype(bf16)
                 part = nn(k[0, 0, at], grad_scores)
                 grad_query = part if grad_query is None else grad_query + part
-                out[0, 0, at] = nt(query, grad_scores) * score_scale
-                out[0, 1, at] = nt(grad, soft.astype(bf16))
-            gq[0, at] = (grad_query * score_scale).astype(bf16)
+                out[0, at] = (nt(query, grad_scores) * score_scale).astype(out.dtype)
+                out[1, at] = nt(grad, soft.astype(bf16)).astype(out.dtype)
+            gq[at] = (grad_query * score_scale).astype(bf16)
 
     def own(n):
-        return pl.BlockSpec((1, 1, pair, tokens), lambda h, *_: (h // steps, n, h % steps, 0))
+        return pl.BlockSpec((1, 1, pair, tokens), lambda h, *_: (at_hand, n, h, 0))
 
     def beside(n):
-        return pl.BlockSpec((1, 1, pair, tokens), lambda h, *_: (1 - h // steps, n, h % steps, 0))
-
-    rows_spec = pl.BlockSpec((1, pair, tokens), lambda h, *_: (h // steps, h % steps, 0))
-    grads_spec = pl.BlockSpec((1, pair, tokens), lambda h, *_: (2 * which + h // steps, h % steps, 0))
-    line = pl.BlockSpec((2, 1, tokens), lambda h, *_: (h, 0, 0))
-    line_at = pl.BlockSpec((2, 1, tokens), lambda h, *_: (2 * steps * which + h, 0, 0))
-    both = pl.BlockSpec((1, 2, pair, tokens), lambda h, *_: (h // steps, 0, h % steps, 0))
+        return pl.BlockSpec((1, 1, pair, tokens), lambda h, *_: (1 - at_hand, n, h, 0))
+
+    rows_spec = pl.BlockSpec((1, pair, tokens), lambda h, *_: (at_hand, h, 0))
+    grads_spec = pl.BlockSpec((1, pair, tokens), lambda h, *_: (number, h, 0))
+    line = pl.BlockSpec((2, 1, tokens), lambda h, *_: (steps * at_hand + h, 0, 0))
+    line_at = pl.BlockSpec((2, 1, tokens), lambda h, *_: (steps * number + h, 0, 0))
+    both = pl.BlockSpec((2, pair, tokens), lambda h, *_: (0, h, 0))
     return call(
         body,
         (spot, lengths),
         [q, kv, kv_side, kv, kv_side, grad_context, totals, deltas],
         [rows_spec, own(0), beside(0), own(1), beside(1), grads_spec, line, line_at],
-        [shaped(q.shape, bf16), shaped(kv.shape, f32), shaped(kv.shape, f32)],
-        [rows_spec, both, both],
-        grid=(2 * steps,),
-    )
+        [shaped(q.shape[1:], bf16), shaped(kv.shape[1:], f32), shaped(kv.shape[1:], bf16)],
+        [pl.BlockSpec((pair, tokens), lambda h, *_: (h, 0)), both, both],
+        grid=(steps,), weight=8)
 
 
 cubic = 0.044715
@@ -396,12 +404,14 @@
     return (widened * up).astype(bf16), (grad * slope).astype(bf16)
 
 
-def feed_quarter(z_ref, gy_ref, wide_ref, thin_ref, pack_ref, rank, low_w, low_n, act_ref, grad_ref, sums_ref):
+def feed_quarter(z_ref, gy_ref, wide_ref, thin_ref, pack_ref, rank, low_w, low_n, act_ref, grad_ref, sums_ref, ready=None):
     units = wide_ref.shape[1]
     block = 256
     low_w2, low_n2 = halves(low_w), halves(low_n)
 
     def step(b, carry):
+        if ready is not None:
+            ready(b)
         at = pl.ds(pl.multiple_of(b * block, block), block)
         widened = nn(z_ref[...], wide_ref[:, at]) + tn(low_w2, twice(pack_ref[rank : 2 * rank, at]))
         grad = nt(gy_ref[...], thin_ref[at, :]) + tn(low_n2, twice(pack_ref[2 * rank : 3 * rank, at]))
@@ -419,11 +429,12 @@
     )
 
 
-def feed_units(z_ref, gy_ref, wide_ref, thin_ref, outer, inner, low_w, low_n, act_ref, grad_ref):
+def feed_units(z_ref, gy_ref, wide_ref, thin_ref, outer, inner, low_w, low_n, act_ref, grad_ref, ready):
     units = wide_ref.shape[0]
     block = 256
     low_w2, low_n2 = halves(low_w), halves(low_n)
     for start in range(0, units, block):
+        ready(start // block)
         at = slice(start, min(start + block, units))
         widened = nt(z_ref[...], wide_ref[at]) + tn(low_w2, twice(outer[:, at]))
         grad = nt(gy_ref[...], thin_ref[at]) + tn(low_n2, twice(inner[:, at]))
@@ -521,11 +532,27 @@
     tokens, features = z.shape
     units = dense[0].shape[1]
     rank = lows.shape[0] // 5
-
-    def body(z_ref, gy_ref, branch_in, second_in, lows_in, pack_ref, wide, thin, branch_ref, second_ref, lows_ref, sums_ref, act_ref, grad_ref):
+    blocks = units // 256
+
+    def body(z_ref, gy_ref, branch_in, second_in, lows_in, pack_ref, wide_hbm, thin_hbm, branch_ref, second_ref, lows_ref, sums_ref, wide, thin, act_ref, grad_ref, sems):
+        def copies(b):
+            at = pl.ds(pl.multiple_of(b * 256, 256), 256)
+            return (
+                pltpu.make_async_copy(wide_hbm.at[:, at], wide.at[:, at], sems.at[0, b]),
+                pltpu.make_async_copy(thin_hbm.at[at], thin.at[at], sems.at[1, b]),
+            )
+
+        for b in range(blocks):
+            for c in copies(b):
+                c.start()
+
+        def ready(b):
+            for c in copies(b):
+                c.wait()
+
         sums = feed_quarter(
             z_ref, gy_ref, wide, thin, pack_ref, rank, lows_in[rank : 2 * rank], lows_in[2 * rank : 3 * rank],
-            act_ref, grad_ref, sums_ref,
+            act_ref, grad_ref, sums_ref, ready,
         )
         branch_ref[...] = branch_in[...] + sums[0]
         second_ref[...] = second_in[...] + sums[1]
@@ -535,12 +562,28 @@
 
     operands = [z, gy, branch, second, lows, pack] + dense
     outs = [shaped(branch.shape, f32), shaped(second.shape, f32), shaped(lows.shape, f32), shaped((2 * rank, units), f32)]
-    scratch = [pltpu.VMEM((tokens, units), bf16)] * 2
-    return call(body, (), operands, [KEEP] * len(operands), outs, [KEEP] * 4, scratch=scratch, aliases={2: 0, 3: 1})
-
-
-def far_parts(parts, z_ref, gy_ref, ins, wide, thin, received_ref, far_side_ref, rank, base, low_w, low_n, act_ref, grad_ref, sums_ref):
-    count = wide.shape[0] // 2
+    scratch = [pltpu.VMEM(d.shape, bf16) for d in dense] + [pltpu.VMEM((tokens, units), bf16)] * 2
+    scratch += [pltpu.SemaphoreType.DMA((2, blocks))]
+    return call(
+        body, (), operands, [KEEP] * 6 + [remain] * 2, outs, [KEEP] * 4, scratch=scratch, aliases={2: 0, 3: 1}, limit=24
+    )
+
+
+def far_copies(count, ins, wide, thin, sems):
+    part = ins[0].shape[0]
+    copies = []
+    for n in range(count):
+        for q in range(2):
+            at = slice(q * part, (q + 1) * part)
+            copies.append(pltpu.make_async_copy(ins[4 * n + q], wide.at[n, at], sems.at[4 * n + 2 * q]))
+            copies.append(pltpu.make_async_copy(ins[4 * n + 2 + q], thin.at[n, at], sems.at[4 * n + 2 * q + 1]))
+    for c in copies:
+        c.start()
+    return copies
+
+
+def far_parts(parts, z_ref, gy_ref, copies, wide, thin, received_ref, far_side_ref, rank, base, low_w, low_n, act_ref, grad_ref, sums_ref):
+    count = wide.shape[1] // 2
     total = None
     for n, r in enumerate(parts):
         lanes = slice(r * count, (r + 1) * count)
@@ -550,18 +593,24 @@
         inner = jnp.concatenate(
             [received_ref[base + 2 * rank : base + 3 * rank, lanes], far_side_ref[2 * rank : 3 * rank, lanes]], axis=1
         )
-        for q in range(2):
-            at = slice(q * count, (q + 1) * count)
-            wide[at] = ins[4 * n + q][...]
-            thin[at] = ins[4 * n + 2 + q][...]
-        found = feed_units(z_ref, gy_ref, wide, thin, outer, inner, low_w, low_n, act_ref, grad_ref)
+
+        def ready(b):
+            if b < 2:
+                for c in copies[4 * n + 2 * b : 4 * n + 2 * b + 2]:
+                    c.wait()
+
+        found = feed_units(
+            z_ref, gy_ref, wide.at[n], thin.at[n], outer, inner, low_w, low_n, act_ref, grad_ref, ready
+        )
         sums_ref[n] = found[4]
         total = found[:4] if total is None else [a + b for a, b in zip(total, found[:4])]
     return total
 
 
-def far_scratch(part, features, tokens):
-    return [pltpu.VMEM((2 * part, features), bf16)] * 2 + [pltpu.VMEM((tokens, 2 * part), bf16)] * 2
+def far_scratch(count, part, features, tokens):
+    return [pltpu.VMEM((count, 2 * part, features), bf16)] * 2 + [pltpu.VMEM((tokens, 2 * part), bf16)] * 2 + [
+        pltpu.SemaphoreType.DMA((4 * count,))
+    ]
 
 
 def feed_far(parts, z, gy, branch, second, lows, received, far_side, weights):
@@ -573,9 +622,10 @@
 
     def body(z_ref, gy_ref, branch_in, second_in, lows_in, received_ref, far_side_ref, *refs):
         ins, (branch_ref, second_ref, lows_ref, sums_ref) = refs[:count], refs[count : count + 4]
-        wide, thin, act_ref, grad_ref = refs[count + 4 :]
+        wide, thin, act_ref, grad_ref, sems = refs[count + 4 :]
+        copies = far_copies(len(parts), ins, wide, thin, sems)
         total = far_parts(
-            parts, z_ref, gy_ref, ins, wide, thin, received_ref, far_side_ref, rank, base,
+            parts, z_ref, gy_ref, copies, wide, thin, received_ref, far_side_ref, rank, base,
             lows_in[rank : 2 * rank], lows_in[2 * rank : 3 * rank], act_ref, grad_ref, sums_ref,
         )
         branch_ref[...] = branch_in[...] + total[0]
@@ -592,8 +642,8 @@
         shaped((len(parts), 2 * rank, 2 * part), f32),
     ]
     return call(
-        body, (), operands, [KEEP] * len(operands), outs, [KEEP] * 4,
-        scratch=far_scratch(part, features, tokens), aliases={2: 0, 3: 1},
+        body, (), operands, [KEEP] * 7 + [remain] * count, outs, [KEEP] * 4,
+        scratch=far_scratch(len(parts), part, features, tokens), aliases={2: 0, 3: 1},
     )
 
 
@@ -625,14 +675,15 @@
     tail = lanes_up(width)
     total_lanes = 3 * half + 2 * (2 * units + tail)
 
-    def body(spot_ref, pick_ref, length_ref, hidden_ref, z_ref, gy_ref, branch_in, second_in, lows_ref, near0, near1, far0, far12, c01, c23, wo0, wo1, far_ref, pack_ref, side_ref, far_side_ref, received_ref, oo, wi, no, ca, cb, gain_ref, *refs):
-        hbm, (outa_ref, outb_ref, gh_ref, gc_ref, delta_ref, keep_ref, give_ref) = refs[:4], refs[4:11]
-        wide, thin, act_ref, grad_ref, far3, ga_ref = refs[11:]
+    def body(spot_ref, pick_ref, length_ref, hidden_ref, z_ref, gy_ref, branch_in, second_in, lows_ref, near0, near1, far0, far3, c01, c23, wo0, wo1, far_ref, pack_ref, side_ref, far_side_ref, received_ref, oo, wi, no, ca, cb, gain_ref, *refs):
+        hbm, (out_ref, outb_ref, gh_ref, gc_ref, delta_ref, keep_ref, give_ref) = refs[:8], refs[8:15]
+        wide, thin, act_ref, grad_ref, sems, last, ga_ref = refs[15:]
+        copies = far_copies(len(parts), hbm, wide, thin, sems)
         low_w = lows_ref[rank : 2 * rank]
         low_n = lows_ref[2 * rank : 3 * rank]
         found = far_parts(
-            parts, z_ref, gy_ref, hbm, wide, thin, received_ref, far_side_ref, rank, base,
-            low_w, low_n, act_ref, grad_ref, far3,
+            parts, z_ref, gy_ref, copies, wide, thin, received_ref, far_side_ref, rank, base,
+            low_w, low_n, act_ref, grad_ref, last,
         )
         branch = branch_in[...] + found[0]
         grad_second = second_in[...] + found[1]
@@ -643,7 +694,7 @@
         grad_second = grad_second + tn(halves(grad_low), twice(wi[0]))
         hidden_now = hidden_ref[...]
         output = (hidden_now + mask * branch).astype(bf16)
-        outa_ref[...] = output[:rows]
+        out_ref[0] = output[:rows]
         outb_ref[...] = output[rows:]
         _, unit, scaled = normalize(hidden_now, gain_ref[...], gain_ref[...])
         grad_in = jnp.concatenate([ca[0], cb[...]], axis=0).astype(f32)
@@ -679,7 +730,7 @@
             quarters.append((near[:rank], near[rank:]))
         for q in range(2):
             lanes = slice(q * part, (q + 1) * part)
-            pieces = [far0[0, :, lanes], far12[0, :, lanes], far12[1, :, lanes], far3[0, :, lanes]]
+            pieces = [far0[0, :, lanes], last[0, :, lanes], last[1, :, lanes], far3[0, :, lanes]]
             joined = shuffled(jnp.concatenate(pieces, axis=1), quad)
             quarters.append((joined[:rank], joined[rank:]))
         for i in range(4):
@@ -697,9 +748,9 @@
     specs += [placed_block((1, rank, features), of_mine(n)) for n in (3, 4, 5)]
     operands += [cotangent, cot_side, gain] + weights
     specs += [placed_block((1, rows, features), lambda i, spot, *_: (spot[0], 0, 0))]
-    specs += [whole(cot_side.shape), whole(gain.shape)] + [KEEP] * 4
+    specs += [whole(cot_side.shape), whole(gain.shape)] + [remain] * 8
     outs = [
-        shaped((rows, features), bf16),
+        shaped((2, rows, features), bf16),
         shaped((rows, features), bf16),
         shaped((tokens, features), f32),
         shaped((4, width, tokens), bf16),
@@ -707,38 +758,38 @@
         shaped((rank, total_lanes), f32),
         shaped((rank, total_lanes), f32),
     ]
-    scratch = far_scratch(part, features, tokens)
-    scratch += [pltpu.VMEM((1, 2 * rank, 2 * part), f32), pltpu.VMEM((tokens, features), bf16)]
-    return call(
-        body, (spot, pick, lengths), operands, specs, outs, [whole(o.shape) for o in outs], scratch=scratch
-    )
-
-
-def gather_grads(spot, near, far, z, low, packs, received):
+    scratch = far_scratch(2, part, features, tokens)
+    scratch += [pltpu.VMEM((2, 2 * rank, 2 * part), f32), pltpu.VMEM((tokens, features), bf16)]
+    out_specs = [placed_block((1, rows, features), lambda i, spot, *_: (spot[0], 0, 0))] + [KEEP] * 6
+    return call(body, (spot, pick, lengths), operands, specs, outs, out_specs, scratch=scratch, limit=24)
+
+
+def gather_grads(spot, quarters, z, low, packs, received):
     tokens, features = z.shape
     rank = low.shape[0] // 3
-    width = near[0].shape[1]
+    width = quarters[0][0].shape[0]
     pack, side, far_side = packs
     base = received.shape[0] - 3 * rank
     half = features // 2
     tail = lanes_up(3 * width)
     total_lanes = 3 * half + 2 * tail
 
-    def body(spot_ref, q01, own01, side01, q23, own23, side23, z_ref, low_ref, pack_ref, side_ref, far_side_ref, received_ref, g_ref, gl_ref, keep_ref, give_ref):
-        groups = ((q01, own01, side01), (q23, own23, side23))
+    def body(spot_ref, *refs):
+        groups = [refs[3 * i : 3 * i + 3] for i in range(4)]
+        z_ref, low_ref, pack_ref, side_ref, far_side_ref, received_ref, g_ref, gl_ref, keep_ref, give_ref = refs[12:]
         places = ((pack_ref, 0), (side_ref, 0), (received_ref, base), (far_side_ref, 0))
         lows = [halves(low_ref[n * rank : (n + 1) * rank]) for n in range(3)]
         total = [jnp.zeros((rank, tokens), f32) for _ in range(3)]
         core = spot_ref[3] & 1
         for i in range(4):
-            q, own, other = groups[i // 2]
+            q, own, other = groups[i][0], groups[i][1], groups[i ^ 1][2]
             ref, start = places[i]
             outers = []
             for n in range(3):
                 if n == 0:
-                    g = q[i % 2]
+                    g = q[...]
                 else:
-                    g = (own[i % 2, n - 1] + other[1 - i % 2, n - 1]).astype(bf16)
+                    g = (own[n - 1] + other[n - 1].astype(f32)).astype(bf16)
                 g_ref[i, n] = g
                 lanes = slice(n * width, (n + 1) * width)
                 total[n] = total[n] + nn(ref[start : start + rank, lanes], g)
@@ -750,7 +801,7 @@
             inner = folded(nn(halves(total[n]), z_ref[...]))
             keep_ref[:, n * half : (n + 1) * half], give_ref[:, n * half : (n + 1) * half] = shares(inner, core)
 
-    operands = list(near) + list(far) + [z, low] + list(packs) + [received]
+    operands = [a for q in quarters for a in q] + [z, low] + list(packs) + [received]
     outs = [
         shaped((4, 3, width, tokens), bf16),
         shaped((3 * rank, tokens), f32),
@@ -758,8 +809,7 @@
         shaped((rank, total_lanes), f32),
     ]
     return call(
-        body, (spot,), operands, [whole(o.shape) for o in operands], outs, [whole(o.shape) for o in outs]
-    )
+        body, (spot,), operands, [whole(o.shape) for o in operands], outs, [whole(o.shape) for o in outs], weight=5)
 
 
 def settle(spot, pick, keep, moved, common, with_picks):
@@ -781,51 +831,72 @@
             there_ref[:, common + own :] = line.astype(bf16)
 
     out = shaped((rank, common + own + extra), bf16)
-    return call(body, (spot, pick), [keep, moved], [whole(keep.shape)] * 2, [out, out], [whole(out.shape)] * 2)
-
-
-def combine(picks, arrays, groups, rows_of_table):
+    return call(body, (spot, pick), [keep, moved], [whole(keep.shape)] * 2, [out, out], [whole(out.shape)] * 2, weight=1)
+
+
+def combine(spot, picks, arrays, groups, rows_of_table):
     per, rank = arrays[0].shape[:2]
-
-    def body(pick_ref, *refs):
+    half = groups[0][1]
+
+    def body(spot_ref, pick_ref, *refs):
         ins, outs = refs[: len(arrays)], refs[len(arrays) :]
-        outs = [outs[0].at[n] for n in range(3)] + list(outs[1:])
-        for out in outs:
+        places = [outs[0].at[n] for n in range(3)] + list(outs[4:])
+        for out in places:
             out[...] = jnp.zeros(out.shape, f32)
         for a, ref in enumerate(ins):
             for c in range(per):
-                for (start, count, number), out in zip(groups, outs):
+                for (start, count, number), out in zip(groups, places):
                     row = pick_ref[a * per + c, number]
                     out[row] += ref[c, :, start : start + count].astype(f32)
-
-    outs = [shaped((3, rows_of_table, rank, groups[0][1]), f32)]
+        for n in range(3):
+            outs[1 + n][...] = outs[0][n]
+
+    outs = [shaped((3, rows_of_table, rank, half), f32)] + [shaped((rows_of_table, rank, 2 * half), f32)] * 3
     outs += [shaped((rows_of_table, rank, count), f32) for _, count, _ in groups[3:]]
-    return call(body, (picks,), list(arrays), [whole(a.shape) for a in arrays], outs, [whole(o.shape) for o in outs])
-
-
-def complete(spot, own, moved):
-    _, count, rank, half = own.shape
-
-    def body(spot_ref, own_ref, moved_ref, *outs):
-        core = spot_ref[3] & 1
+    own = placed_block((rows_of_table, rank, half), lambda i, spot, pick: (0, 0, spot[3] & 1))
+    specs = [KEEP] + [own] * 3 + [KEEP] * (len(groups) - 3)
+    return call(body, (spot, picks), list(arrays), [KEEP] * len(arrays), outs, specs, weight=100)
+
+
+def complete(spot, tables, moved):
+    _, count, rank, half = moved.shape
+
+    def body(spot_ref, moved_ref, *refs):
         for n in range(3):
-            mine, theirs = own_ref[n], moved_ref[n]
-            outs[n][:, :, :half] = jnp.where(core == 0, mine, theirs)
-            outs[n][:, :, half:] = jnp.where(core == 0, theirs, mine)
+            refs[3 + n][...] = moved_ref[n]
 
     out = shaped((count, rank, 2 * half), f32)
-    return call(body, (spot,), [own, moved], [whole(own.shape)] * 2, [out] * 3, [whole(out.shape)] * 3)
-
-
-def pair_up(spot, first, second):
-    rows, features = first.shape
-
-    def body(spot_ref, first_ref, second_ref, out_ref):
-        out_ref[spot_ref[0]] = first_ref[...]
-        out_ref[spot_ref[1]] = second_ref[...].astype(first.dtype)
-
-    out = shaped((2, rows, features), first.dtype)
-    return call(body, (spot,), [first, second], [whole(first.shape)] * 2, out, whole(out.shape))
+    theirs = placed_block((count, rank, half), lambda i, spot: (0, 0, 1 - (spot[3] & 1)))
+    return call(
+        body, (spot,), [moved] + list(tables), [KEEP] + [remain] * 3, [out] * 3, [theirs] * 3,
+        aliases={2: 0, 3: 1, 4: 2}, weight=2)
+
+
+def pair_up(spot, array, second):
+    rows, features = second.shape
+
+    def body(spot_ref, array_ref, second_ref, out_ref):
+        out_ref[0] = second_ref[...].astype(array.dtype)
+
+    out_spec = placed_block((1, rows, features), lambda i, spot: (spot[1], 0, 0))
+    return call(
+        body, (spot,), [array, second], [remain, KEEP], shaped(array.shape, array.dtype), out_spec, aliases={1: 0}, weight=1)
+
+
+def join(groups):
+    flat = [a for g in groups for a in g]
+    outs = [shaped((sum(a.shape[0] for a in g),) + g[0].shape[1:], g[0].dtype) for g in groups]
+
+    def body(*refs):
+        at = 0
+        for g, out in zip(groups, refs[len(flat) :]):
+            start = 0
+            for a in g:
+                out[start : start + a.shape[0]] = refs[at][...]
+                start += a.shape[0]
+                at += 1
+
+    return call(body, (), flat, [KEEP] * len(flat), outs, [KEEP] * len(outs), weight=1)
 
 
 def finish(spot, pick, g, gl, inners, weights, far, inputs, received, grad_hidden, gain):
@@ -835,20 +906,22 @@
     rank = gl.shape[0] // 3
 
     def body(spot_ref, pick_ref, g_ref, gl_ref, iq, ik, iv, *refs):
-        ws, (far_ref, xa, xb, gh_ref, gain_ref, grada_ref, gradb_ref) = refs[:6], refs[6:]
+        ws, (far_ref, xa, xb, gh_ref, gain_ref, grad_ref, gradb_ref) = refs[:6], refs[6:]
         low = [halves(gl_ref[n * rank : (n + 1) * rank]) for n in range(3)]
         total = tn(
             jnp.concatenate(low, axis=0),
             jnp.concatenate([twice(iq[0]), twice(ik[0]), twice(iv[0])], axis=0),
         )
         for i in range(4):
-            for n in range(3):
-                weight = ws[3 * i + n][...] if i < 2 else far_ref[i - 2, n]
-                total = total + tn(g_ref[i, n], weight)
+            if i < 2:
+                weight = jnp.concatenate([w[...] for w in ws[3 * i : 3 * i + 3]], axis=0)
+            else:
+                weight = far_ref[i - 2].reshape(3 * width, features)
+            total = total + tn(g_ref[i].reshape(3 * width, tokens), weight)
         states = jnp.concatenate([xa[0], xb[...]], axis=0).astype(f32)
         _, unit, scaled = normalize(states, gain_ref[...], gain_ref[...])
         grad = gh_ref[...] + normalize_back(total, unit, scaled, gain_ref[...])
-        grada_ref[...] = grad[:rows]
+        grad_ref[0] = grad[:rows]
         gradb_ref[...] = grad[rows:].astype(bf16)
 
     operands = [g, gl] + inners + weights + [far, inputs, received, grad_hidden, gain]
@@ -858,10 +931,9 @@
     specs += [placed_block((2, 3, width, features), lambda *_: (0, 0, 0, 0))]
     specs += [placed_block((1, rows, features), lambda i, spot, *_: (spot[0], 0, 0))]
     specs += [placed_block((rows, features), lambda *_: (0, 0)), whole(grad_hidden.shape), whole(gain.shape)]
-    outs = [shaped((rows, features), f32), shaped((rows, features), bf16)]
-    return call(
-        body, (spot, pick), operands, specs, outs, [whole(o.shape) for o in outs],
-    )
+    outs = [shaped((2, rows, features), f32), shaped((rows, features), bf16)]
+    out_specs = [placed_block((1, rows, features), lambda i, spot, *_: (spot[0], 0, 0)), KEEP]
+    return call(body, (spot, pick), operands, specs, outs, out_specs, weight=9)
 
 
 def make_body(dp_size, tensor_size):
@@ -923,81 +995,75 @@
 
         part_heads = stage_heads(spot, heads)
         far0 = across(part_heads)
+        send, pack = stage(after(spot, part_heads), pick, inputs, small)
+        received = across(send)
         near_heads = [beside(w) for w in after(heads, part_heads)]
-        send, pack = stage(after(spot, part_heads), pick, inputs, small)
         side = beside(pack)
-        part_wide, part_thin, cot_send = stage_dense(after(spot, pack), widen_weight, narrow_weight, cotangent)
         near_dense = [beside(w) for w in after(dense, near_heads)]
-        received = across(after(send, far0))
-        far1, far2 = along(far0, 1), along(far0, 2)
+        part_wide, part_thin, part_last, cot_send = stage_dense(
+            after(spot, pack), widen_weight, narrow_weight, cotangent
+        )
+        far1, far2 = along(after(far0, near_dense), 1), along(after(far0, near_dense), 2)
         side0 = beside(after(far0, side, near_dense, part_wide))
-        wide0 = across(after(part_wide, received))
-        far3, far4 = along(far2[:2], 1), along(far1[2:], 2)
-        side1 = beside(far1)
+        wide0 = across(after(part_wide, far0))
         z, low, kv01 = project_near(
-            after(spot, part_wide, far1, far2, side0), pick, inputs, received, gains[0], gains[1], inners, pack, side,
+            spot, pick, inputs, after(received, side0), gains[0], gains[1], inners, pack, side,
             [heads[1], heads[2], near_heads[1], near_heads[2]],
         )
         kv01_side = beside(kv01)
-        side2 = beside(after(far2, kv01, side1))
+        far3, far4 = along(after(far2[:2], kv01), 1), along(after(far1[2:], kv01), 2)
+        side1 = beside(after(far1, kv01))
         q01 = queries_near(after(z, kv01), low, pack, side, [heads[0], near_heads[0]])
-        far_side = beside(after(received[rows:], q01))
-        side3, side4 = beside(after(far3, q01, side2)), beside(after(far4, q01, side2))
-        c01, total01 = attend(after(spot, side2), lengths, q01, kv01, kv01_side)
+        side2 = beside(after(far2, q01, side1))
+        c01, total01 = attend(spot, lengths, q01, kv01, after(kv01_side, side1))
+        far_side = beside(after(received[rows:], c01))
+        side3, side4 = beside(after(far3, c01, side2)), beside(after(far4, c01, side2))
         wide1, wide2 = along(after(wide0, c01), 1), along(after(wide0, c01), 2)
-        cot_side = across(after(cot_send, c01, wide0))
+        cot_side = across(after(cot_send, c01))
         far, kv23 = project_far(
-            after(spot, c01, wide0), z, low, received, far_side,
+            spot, after(z, c01), low, received, far_side,
             [[far0, far1, far2, far3, far4], [side0, side1, side2, side3, side4]],
         )
         kv23_side = beside(kv23)
+        thin0 = across(after(part_thin, kv23))
         q23 = queries_far(after(z, kv23), low, received, far_side, far)
         c23, total23 = attend(spot, lengths, q23, kv23, kv23_side)
-        thin0 = across(after(part_thin, c23))
         packs = [pack, side, far_side]
         outs_w = [heads[3], near_heads[3]]
         hidden, z2, lows = feed_open(
             spot, pick, lengths, [c01, c23], outs_w, far, packs, tables, inputs, received, gains[2], gains[3]
         )
         wide3 = along(after(wide2, lows), 1)
-        wide_sides = [beside(after(w, lows, wide1, wide2)) for w in (wide0, wide1, wide2)]
+        thin3 = across(after(part_last, lows))
+        wide_sides = [beside(after(w, lows)) for w in (wide0, wide1, wide2)]
         gy, branch, second, lows, sums0 = feed_first(
             spot, pick, lengths, z2, lows, tables[2], cotangent, cot_side, pack, dense
         )
-        wide_sides.append(beside(after(wide3, lows)))
         thin1, thin2 = along(after(thin0, lows), 1), along(after(thin0, lows), 2)
         thin_sides = [beside(after(thin0, lows))]
         branch, second, lows, sums1 = feed_near(
-            z2, gy, branch, second, after(lows, wide_sides[:3], thin0, wide3), side, near_dense
-        )
-        thin3 = along(after(thin1, sums1), 2)
-        thin_sides += [beside(after(t, sums1)) for t in (thin1, thin2)]
+            z2, gy, branch, second, after(lows, wide_sides), side, near_dense
+        )
+        wide_sides.append(beside(after(wide3, sums1)))
         branch, second, lows, sums2 = feed_far(
-            (0,), z2, gy, branch, second, after(lows, thin1, thin2), received, far_side,
-            [wide0, wide_sides[0], thin0, thin_sides[0]],
-        )
-        thin_sides.append(beside(after(thin3, sums2)))
+            (0,), z2, gy, branch, second, lows, received, far_side, [wide0, wide_sides[0], thin0, thin_sides[0]]
+        )
+        thin_sides += [beside(after(t, sums2)) for t in (thin1, thin2, thin3)]
         branch, second, lows, sums3 = feed_far(
-            (1, 2), z2, gy, branch, second, after(lows, thin3), received, far_side,
+            (3,), z2, gy, branch, second, lows, received, far_side, [wide3, wide_sides[3], thin3, thin_sides[3]]
+        )
+        output, outb, grad_hidden, grad_context, deltas, keep, give = feed_close(
+            (1, 2), spot, pick, lengths, hidden, z2, gy, branch, second, lows, [sums0, sums1], [sums2, sums3],
+            [c01, c23], outs_w, far, packs, tables, received, cotangent, cot_side, gains[2],
             [wide1, wide_sides[1], thin1, thin_sides[1], wide2, wide_sides[2], thin2, thin_sides[2]],
         )
-        outa, outb, grad_hidden, grad_context, deltas, keep, give = feed_close(
-            (3,), spot, pick, lengths, hidden, z2, gy, branch, second, lows, [sums0, sums1], [sums2, sums3],
-            [c01, c23], outs_w, far, packs, tables, received, cotangent, cot_side, gains[2],
-            [wide3, wide_sides[3], thin3, thin_sides[3]],
-        )
-
-        def crossing(here, other):
-            both = jnp.stack([here, other])
-            return along(both, 4)
 
         def first_turn(here, other, crossed):
-            one = jnp.stack([here, crossed[0]])
-            two = jnp.stack([other, crossed[1]])
+            one, two = join([[here[None], crossed[0][None]], [other[None], crossed[1][None]]])
             return [(one, along(one, 1)), (two, along(two, 2))]
 
         def second_turn(turns):
-            one, two = [jnp.concatenate(t) for t in turns]
+            one, two = join(turns)
             return [one, along(one, 2), two, along(two, 1)]
 
         def whole_sum(table):
@@ -1007,41 +1073,46 @@
                 bits *= 2
             return table
 
+        def back(number, q, kv, kv_side, totals):
+            gq, own, other = attend_back(spot, lengths, q, kv, kv_side, grad_context, totals, deltas, number)
+            return gq, own, other
+
         moved = beside(give)
         here, there = settle(spot, pick, keep, moved, 3 * half, True)
         other = across(there)
-        gq01, own01, other01 = attend_back(
-            after(spot, here), lengths, q01, kv01, kv01_side, grad_context, total01, deltas, 0
-        )
-        side01 = beside(other01)
-        crossed = crossing(here, after(other, gq01))
-        out_side = across(after(outb, other, gq01))
-        gq23, own23, other23 = attend_back(
-            after(spot, gq01, other), lengths, q23, kv23, kv23_side, grad_context, total23, deltas, 1
-        )
-        side23 = beside(other23)
-        turns = first_turn(here, other, after(crossed, gq23))
-        output = pair_up(after(spot, gq23), outa, out_side)
-        g, gl, keep, give = gather_grads(
-            after(spot, output), (gq01, own01, side01), (gq23, own23, side23), z, low, packs, received
-        )
+        crossed = [along(here, 4)]
+        quarters = [back(0, after(q01, here), kv01, kv01_side, total01)]
+        quarters.append(back(1, after(q01, quarters[0][0]), kv01, kv01_side, total01))
+        sides = [beside(after(quarters[0][2], quarters[1][0]))]
+        crossed.append(along(after(other, quarters[0][0]), 4))
+        out_side = across(after(outb, quarters[1][0]))
+        quarters.append(back(2, after(q23, quarters[1][0]), kv23, kv23_side, total23))
+        sides.append(beside(after(quarters[1][2], quarters[2][0], sides[0])))
+        turns = first_turn(here, other, after(crossed, quarters[2][0]))
+        quarters.append(back(3, after(q23, quarters[2][0], turns[0][0]), kv23, kv23_side, total23))
+        sides += [beside(after(quarters[2][2], quarters[3][0], sides[1])), beside(quarters[3][2])]
+        quarters = [(gq, own, sided) for (gq, own, _), sided in zip(quarters, sides)]
+        early = second_turn(after(turns, quarters[3][0]))
+        g, gl, keep, give = gather_grads(spot, quarters, after(z, early[0], early[2]), low, packs, received)
         moved = beside(give)
-        early = second_turn(after(turns, g))
         here, there = settle(spot, pick, keep, moved, 3 * half, False)
         other = across(there)
-        crossed = crossing(here, other)
-        grada, gradb = finish(
-            after(spot, other), pick, g, gl, inners, heads[:3] + near_heads[:3], far, inputs, received, grad_hidden,
+        crossed = [along(here, 4)]
+        crossed.append(along(other, 4))
+        grad, gradb = finish(
+            spot, pick, after(g, other), gl, inners, heads[:3] + near_heads[:3], far, inputs, received, grad_hidden,
             gains[0],
         )
         grad_side = across(after(gradb, crossed))
-        turns = first_turn(here, other, after(crossed, grada))
+        turns = first_turn(here, other, after(crossed, gradb))
+        output = pair_up(spot, output, after(out_side, gradb))
         picks = jnp.concatenate([a[:, 0, -128:-122] for a in early]).astype(jnp.int32)
         adapters = query_inner.shape[0]
         units = widen_weight.shape[1]
         base = 3 * half
         early = combine(
-            after(picks, grada),
+            spot,
+            after(picks, gradb),
             early,
             [
                 (0, half, 4),
@@ -1054,31 +1125,32 @@
             adapters,
         )
         early = [whole_sum(t) for t in early]
-        early_shared = complete(spot, early[0], beside(early[0]))
+        early_shared = complete(spot, early[1:4], beside(early[0]))
         late = second_turn(turns)
-        input_grad = pair_up(spot, grada, grad_side)
+        input_grad = pair_up(spot, grad, grad_side)
         late = combine(
-            picks,
+            spot,
+            after(picks, grad_side),
             late,
             [(n * half, half, n) for n in range(3)] + [(base + n * width, width, n) for n in range(3)],
             adapters,
         )
         late = [whole_sum(t) for t in late]
-        late_shared = complete(spot, late[0], beside(late[0]))
+        late_shared = complete(spot, late[1:4], beside(late[0]))
         return (
             output,
             input_grad,
             flip(late_shared[0]),
-            late[1],
+            late[4],
             flip(late_shared[1]),
-            late[2],
+            late[5],
             flip(late_shared[2]),
-            late[3],
-            flip(early[3]),
+            late[6],
+            flip(early[6]),
             early_shared[1],
             flip(early_shared[0]),
-            early[1],
-            flip(early[2]),
+            early[4],
+            flip(early[5]),
             early_shared[2],
         )
 

time: 321 us -> 282 us (0.88)
  local copies, waits for them, and re-layouts: 34.1 us -> 10.9 us
  waiting for transfers between devices: 70.3 us -> 60.8 us
  Pallas kernels: 166 us -> 160 us
    unnamed x217 -> x203, local copies, waits for them, and re-layouts: 25 us -> 9.02 us
    ppermute x58 -> x62, waiting for transfers between devices: 70.3 us -> 60.8 us  [swap(): return lax.ppermute(array, axis, [(i, i ^ bits) for i in range(size)])]
    pallas_call x27 -> x33, Pallas kernels: 166 us -> 160 us  [call(): pl.pallas_call(body, grid_spec=pltpu.PrefetchScalarGridSpec(num_scalar_pr...]
    concatenate x2 -> x0, local copies, waits for them, and re-layouts: 3.42 us -> none  [second_turn(): one, two = [jnp.concatenate(t) for t in turns]]
    ppermute x58 -> x62, starting transfers between devices: 40.3 us -> 41.9 us  [swap(): return lax.ppermute(array, axis, [(i, i ^ bits) for i in range(size)])]
  transfers between devices with their start and end apart: 58 -> 62, of which waited for: 17 -> 21; matrix products, arithmetic and copies ran while one was open for 3% -> 1% of each run, Pallas kernels for 46% -> 47%
where the time goes in v3:
time: 282 us; the launch traced here: 276 us
  Pallas kernels  160 us (57%)
  waiting for transfers between devices  60.8 us (22%)
  starting transfers between devices  41.9 us (15%)
  local copies, waits for them, and re-layouts  10.9 us (4%)
    pallas_call x33, Pallas kernels, call(): pl.pallas_call(body, grid_spec=pltpu.PrefetchScalarGridSpec(num_scalar_pr...  160 us
    ppermute x62, waiting for transfers between devices, swap(): return lax.ppermute(array, axis, [(i, i ^ bits) for i in range(size)])  60.8 us
    ppermute x62, starting transfers between devices, swap(): return lax.ppermute(array, axis, [(i, i ^ bits) for i in range(size)])  41.9 us
    unnamed x203, local copies, waits for them, and re-layouts  9.02 us
  transfers between devices with their start and end apart: 62, of which 21 were waited for; matrix products, arithmetic and copies ran while one was open for 1% of the time, Pallas kernels for 47%

profile of v3, /device:TPU:0, one launch (start us, length us, event | category | flops | bytes accessed | tf_op | source)
XLA Modules:
  0.0 276.2 jit_solution(4822465274064546648)
XLA Ops:
  0.8 2.8 %shard_map.353 = bf16[4,80,1280]{2,1,0:T(8,128)(2,1)} custom-call(s32[4]{0:T(128)S(1)} %pad_add_fusion.spot_ref, bf16[320,1280]{1,0:T(8,128)(2,1)} %bitcast.4.refs_0_.w0, bf16[320,1280]{1,0:T(8,128)(2,1)} %bitcast.5.refs_1_.refs_0_, bf16[320,1280]{1,0:T(8,128)(2,1)} %bitcast.6.refs_2_.refs_1_, bf16[320,1280]{1,0:T(8,128)(2,1)} %wo0.3), custom_call_target="tpu_custom_call" | custom-call | flops 99999997952 | bytes 100000 | tf_op jit(solution)/shard_map/pallas_call | solution.py:85
  3.6 3.0 %collective-permute-start.1 = (bf16[4,80,1280]{2,1,0:T(8,128)(2,1)}, bf16[4,80,1280]{2,1,0:T(8,128)(2,1)}, u32[]{:S(2)}, u32[]{:S(2)}) collective-permute-start(bf16[4,80,1280]{2,1,0:T(8,128)(2,1)} %shard_map.353), channel_id=1, source_target_pairs={{0,2},{1,3},{2,0},{3,1},{4,6},{5,7},{6,4},{7,5},{8,10},{9,11},{10,... | collective-permute-start | bytes 2457608 | tf_op jit(solution)/shard_map/ppermute | solution.py:23
  16.9 8.3 %collective-permute-done.1.refs_0_ = bf16[4,80,1280]{2,1,0:T(8,128)(2,1)} collective-permute-done((bf16[4,80,1280]{2,1,0:T(8,128)(2,1)}, bf16[4,80,1280]{2,1,0:T(8,128)(2,1)}, u32[]{:S(2)}, u32[]{:S(2)}) %collective-permute-start.1) | collective-permute-done | bytes 819232 | tf_op jit(solution)/shard_map/ppermute | solution.py:23
  34.1 14.7 %collective-permute-done.xb.received_ref.refs_17_.refs_8_ = bf16[304,1280]{1,0:T(8,128)(2,1)S(1)} collective-permute-done((bf16[304,1280]{1,0:T(8,128)(2,1)S(1)}, bf16[304,1280]{1,0:T(8,128)(2,1)S(1)}, u32[]{:S(2)}, u32[]{:S(2)}) %collective-permute-start) | collective-permute-done | bytes 778272 | tf_op jit(solution)/shard_map/ppermute | solution.py:23
  49.7 5.2 %shard_map.356 = (bf16[512,1280]{1,0:T(8,128)(2,1)S(1)}, f32[48,512]{1,0:T(8,128)S(1)}, bf16[2,2,320,512]{3,2,1,0:T(8,128)(2,1)S(1)}) custom-call(s32[4]{0:T(128)S(1)} %pad_add_fusion.spot_ref, s32[2,6]{1,0:T(2,128)S(1)} %copy-done.75, bf16[2,256,1280]{2,1,0:T(8,128)(2,1)S(1)} %copy-done.22, ...), custom_call_target="tpu_custom_call" | custom-call | flops 99999997952 | bytes 100000 | tf_op jit(solution)/shard_map/pallas_call | solution.py:85
  64.6 8.3 %shard_map.358 = (bf16[2,320,512]{2,1,0:T(8,128)(2,1)S(1)}, f32[8,1,512]{2,1,0:T(1,128)S(1)}) custom-call(s32[4]{0:T(128)S(1)} %pad_add_fusion.spot_ref, s32[2]{0:T(128)S(1)} %copy-done.78, bf16[2,320,512]{2,1,0:T(8,128)(2,1)S(1)} %shard_map.357.q_ref, bf16[2,2,320,512]{3,2,1,0:T(8,128)(2,1)S(1)} %get-tuple-element.179.k1.v1, ...), custom_call_target="tpu_custom_call" | custom-call | flops 99999997952 | bytes 100000 | tf_op jit(solution)/shard_map/pallas_call | solution.py:85
  78.3 4.9 %shard_map.359 = (bf16[2,4,320,1280]{3,2,1,0:T(8,128)(2,1)S(1)}, bf16[2,2,320,512]{3,2,1,0:T(8,128)(2,1)S(1)}) custom-call(s32[1]{0:T(128)} %bitcast.2.spot_ref, bf16[512,1280]{1,0:T(8,128)(2,1)S(1)} %get-tuple-element.275.z_ref.refs_12_, f32[48,512]{1,0:T(8,128)S(1)} %get-tuple-element.181.low_ref.refs_13_, bf16[304,1280]{1,0:T(8,128)(2,1)S(1)} %copy-done.1, ...), custom_call_target="tpu_custom_call" | custom-call | flops 99999997952 | bytes 100000 | tf_op jit(solution)/shard_map/pallas_call | solution.py:85
  86.3 8.2 %shard_map.361 = (bf16[2,320,512]{2,1,0:T(8,128)(2,1)S(1)}, f32[8,1,512]{2,1,0:T(1,128)S(1)}) custom-call(s32[4]{0:T(128)S(1)} %copy-done.9, s32[2]{0:T(128)S(1)} %copy-done.79, bf16[2,320,512]{2,1,0:T(8,128)(2,1)S(1)} %shard_map.360.q_ref, bf16[2,2,320,512]{3,2,1,0:T(8,128)(2,1)S(1)} %get-tuple-element.193.k1.v1, ...), custom_call_target="tpu_custom_call" | custom-call | flops 99999997952 | bytes 100000 | tf_op jit(solution)/shard_map/pallas_call | solution.py:85
  94.8 6.1 %shard_map.362 = (f32[512,1280]{1,0:T(8,128)S(1)}, bf16[512,1280]{1,0:T(8,128)(2,1)S(1)}, f32[32,512]{1,0:T(8,128)S(1)}) custom-call(s32[4]{0:T(128)S(1)} %copy-done.9, s32[2,6]{1,0:T(2,128)S(1)} %copy-done.76, s32[2]{0:T(128)S(1)} %copy-done.79, bf16[2,320,512]{2,1,0:T(8,128)(2,1)S(1)} %get-tuple-element.185.c01, ...), custom_call_target="tpu_custom_call" | custom-call | flops 99999997952 | bytes 100000 | tf_op jit(solution)/shard_map/pallas_call | solution.py:85
  102.7 13.4 %shard_map.363 = (bf16[512,1280]{1,0:T(8,128)(2,1)S(1)}, f32[512,1280]{1,0:T(8,128)S(1)}, f32[512,1280]{1,0:T(8,128)S(1)}, f32[80,512]{1,0:T(8,128)S(1)}, f32[32,1280]{1,0:T(8,128)S(1)}) custom-call(s32[4]{0:T(128)S(1)} %copy-done.9, s32[2,6]{1,0:T(2,128)S(1)} %copy-done.76, s32[2]{0:T(128)S(1)} %copy-done.79, ...), custom_call_target="tpu_custom_call" | custom-call | flops 99999997952 | bytes 100000 | tf_op jit(solution)/shard_map/pallas_call | solution.py:85
  119.8 12.1 %shard_map.364 = (f32[512,1280]{1,0:T(8,128)S(1)}, f32[512,1280]{1,0:T(8,128)S(1)}, f32[80,512]{1,0:T(8,128)S(1)}, f32[32,1280]{1,0:T(8,128)S(1)}) custom-call(bf16[512,1280]{1,0:T(8,128)(2,1)S(1)} %get-tuple-element.198.z_ref, bf16[512,1280]{1,0:T(8,128)(2,1)S(1)} %get-tuple-element.202.gy_ref, ...), custom_call_target="tpu_custom_call", output_to_operand_aliasing={{0}: (2, {}), {1}: (3, {})} | custom-call | flops 99999997952 | bytes 100000 | tf_op jit(solution)/shard_map/pallas_call | solution.py:85
  132.0 7.5 %shard_map.365 = (f32[512,1280]{1,0:T(8,128)S(1)}, f32[512,1280]{1,0:T(8,128)S(1)}, f32[80,512]{1,0:T(8,128)S(1)}, f32[1,32,640]{2,1,0:T(8,128)S(1)}) custom-call(bf16[512,1280]{1,0:T(8,128)(2,1)S(1)} %get-tuple-element.198.z_ref, bf16[512,1280]{1,0:T(8,128)(2,1)S(1)} %get-tuple-element.202.gy_ref, ...), custom_call_target="tpu_custom_call", output_to_operand_aliasing={{0}: (2, {}), {1}: (3, {})} | custom-call | flops 99999997952 | bytes 100000 | tf_op jit(solution)/shard_map/pallas_call | solution.py:85
  142.3 7.6 %shard_map.366 = (f32[512,1280]{1,0:T(8,128)S(1)}, f32[512,1280]{1,0:T(8,128)S(1)}, f32[80,512]{1,0:T(8,128)S(1)}, f32[1,32,640]{2,1,0:T(8,128)S(1)}) custom-call(bf16[512,1280]{1,0:T(8,128)(2,1)S(1)} %get-tuple-element.198.z_ref, bf16[512,1280]{1,0:T(8,128)(2,1)S(1)} %get-tuple-element.202.gy_ref, ...), custom_call_target="tpu_custom_call", output_to_operand_aliasing={{0}: (2, {}), {1}: (3, {})} | custom-call | flops 99999997952 | bytes 100000 | tf_op jit(solution)/shard_map/pallas_call | solution.py:85
  150.1 22.6 %shard_map.367 = (bf16[2,256,1280]{2,1,0:T(8,128)(2,1)}, bf16[256,1280]{1,0:T(8,128)(2,1)}, f32[512,1280]{1,0:T(8,128)S(1)}, bf16[4,320,512]{2,1,0:T(8,128)(2,1)...) custom-call(s32[4]{0:T(128)S(1)} %copy-done.10, s32[2,6]{1,0:T(2,128)S(1)} %copy-done.77, ...), custom_call_target="tpu_custom_call" | custom-call | flops 99999997952 | bytes 100000 | tf_op jit(solution)/shard_map/pallas_call | solution.py:85
  178.0 6.8 %shard_map.369 = (bf16[320,512]{1,0:T(8,128)(2,1)S(1)}, f32[2,320,512]{2,1,0:T(8,128)S(1)}, bf16[2,320,512]{2,1,0:T(8,128)(2,1)S(1)}) custom-call(s32[4]{0:T(128)S(1)} %copy-done.10, s32[2]{0:T(128)S(1)} %copy-done.80, bf16[2,320,512]{2,1,0:T(8,128)(2,1)S(1)} %copy-done.87, bf16[2,2,320,512]{3,2,1,0:T(8,128)(2,1)S(1)} %copy-done.26, ...), custom_call_target="tpu_custom_call" | custom-call | flops 8000000000 | bytes 100000 | tf_op jit(solution)/shard_map/pallas_call | solution.py:85
  186.4 6.8 %shard_map.370 = (bf16[320,512]{1,0:T(8,128)(2,1)S(1)}, f32[2,320,512]{2,1,0:T(8,128)S(1)}, bf16[2,320,512]{2,1,0:T(8,128)(2,1)S(1)}) custom-call(s32[4]{0:T(128)S(1)} %copy-done.10, s32[2]{0:T(128)S(1)} %copy-done.80, bf16[2,320,512]{2,1,0:T(8,128)(2,1)S(1)} %copy-done.87, bf16[2,2,320,512]{3,2,1,0:T(8,128)(2,1)S(1)} %copy-done.26, ...), custom_call_target="tpu_custom_call" | custom-call | flops 8000000000 | bytes 100000 | tf_op jit(solution)/shard_map/pallas_call | solution.py:85
  193.7 6.8 %shard_map.371 = (bf16[320,512]{1,0:T(8,128)(2,1)S(1)}, f32[2,320,512]{2,1,0:T(8,128)S(1)}, bf16[2,320,512]{2,1,0:T(8,128)(2,1)S(1)}) custom-call(s32[4]{0:T(128)S(1)} %copy-done.10, s32[2]{0:T(128)S(1)} %copy-done.80, bf16[2,320,512]{2,1,0:T(8,128)(2,1)S(1)} %copy-done.89, bf16[2,2,320,512]{3,2,1,0:T(8,128)(2,1)S(1)} %copy-done.30, ...), custom_call_target="tpu_custom_call" | custom-call | flops 8000000000 | bytes 100000 | tf_op jit(solution)/shard_map/pallas_call | solution.py:85
  200.6 3.6 %collective-permute-done.44 = bf16[16,4992]{1,0:T(8,128)(2,1)S(1)} collective-permute-done((bf16[16,4992]{1,0:T(8,128)(2,1)S(1)}, bf16[16,4992]{1,0:T(8,128)(2,1)S(1)}, u32[]{:S(2)}, u32[]{:S(2)}) %collective-permute-start.44) | collective-permute-done | bytes 159776 | tf_op jit(solution)/shard_map/ppermute | solution.py:23
  204.3 7.0 %shard_map.373 = (bf16[320,512]{1,0:T(8,128)(2,1)S(1)}, f32[2,320,512]{2,1,0:T(8,128)S(1)}, bf16[2,320,512]{2,1,0:T(8,128)(2,1)S(1)}) custom-call(s32[4]{0:T(128)S(1)} %copy-done.10, s32[2]{0:T(128)S(1)} %copy-done.80, bf16[2,320,512]{2,1,0:T(8,128)(2,1)S(1)} %copy-done.89, bf16[2,2,320,512]{3,2,1,0:T(8,128)(2,1)S(1)} %copy-done.30, ...), custom_call_target="tpu_custom_call" | custom-call | flops 8000000000 | bytes 100000 | tf_op jit(solution)/shard_map/pallas_call | solution.py:85
  213.4 8.4 %collective-permute-done.47.refs_1_ = bf16[2,16,4992]{2,1,0:T(8,128)(2,1)S(1)} collective-permute-done((bf16[2,16,4992]{2,1,0:T(8,128)(2,1)S(1)}, bf16[2,16,4992]{2,1,0:T(8,128)(2,1)S(1)}, u32[]{:S(2)}, u32[]{:S(2)}) %collective-permute-start.47) | collective-permute-done | bytes 319520 | tf_op jit(solution)/shard_map/ppermute | solution.py:23
  223.2 3.0 %shard_map.375 = (bf16[4,3,320,512]{3,2,1,0:T(8,128)(2,1)S(1)}, f32[48,512]{1,0:T(8,128)S(1)}, f32[16,3968]{1,0:T(8,128)S(1)}, f32[16,3968]{1,0:T(8,128)S(1)}) custom-call(s32[4]{0:T(128)S(1)} %copy-done.10, bf16[320,512]{1,0:T(8,128)(2,1)S(1)} %get-tuple-element.243.refs_0_, f32[2,320,512]{2,1,0:T(8,128)S(1)} %get-tuple-element.247.refs_1_, ...), custom_call_target="tpu_custom_call" | custom-call | flops 5000000000 | bytes 100000 | tf_op jit(solution)/shard_map/pallas_call | solution.py:85
  234.5 10.4 %shard_map.377 = (f32[2,256,1280]{2,1,0:T(8,128)}, bf16[256,1280]{1,0:T(8,128)(2,1)S(1)}) custom-call(s32[4]{0:T(128)S(1)} %copy-done.10, s32[2,6]{1,0:T(2,128)S(1)} %copy-done.77, bf16[4,3,320,512]{3,2,1,0:T(8,128)(2,1)S(1)} %get-tuple-element.280.g_ref, f32[48,512]{1,0:T(8,128)S(1)} %get-tuple-element.281.gl_ref, bf16[8,16,1280]{2,1,0:T(8,128)(2,1)S(1)} %bitcast.42, ...), custom_call_target="tpu_custom_call" | custom-call | flops 8999999488 | bytes 100000 | tf_op jit(solution)/shard_map/pallas_call | solution.py:85
  244.9 2.7 collective-permute-done.51
  261.1 5.4 %collective-permute-done.53.second_ref = bf16[256,1280]{1,0:T(8,128)(2,1)S(1)} collective-permute-done((bf16[256,1280]{1,0:T(8,128)(2,1)S(1)}, bf16[256,1280]{1,0:T(8,128)(2,1)S(1)}, u32[]{:S(2)}, u32[]{:S(2)}) %collective-permute-start.53) | collective-permute-done | bytes 655392 | tf_op jit(solution)/shard_map/ppermute | solution.py:23
  (350 shorter events, 88.2 us)
Async XLA Ops:
  3.6 21.6 %collective-permute-start.1 = (bf16[4,80,1280]{2,1,0:T(8,128)(2,1)}, bf16[4,80,1280]{2,1,0:T(8,128)(2,1)}, u32[]{:S(2)}, u32[]{:S(2)}) collective-permute-start(bf16[4,80,1280]{2,1,0:T(8,128)(2,1)} %shard_map.353), channel_id=1, source_target_pairs={{0,2},{1,3},{2,0},{3,1},{4,6},{5,7},{6,4},{7,5},{8,10},{9,11},{10,... | collective-permute-start | bytes 2457608 | tf_op jit(solution)/shard_map/ppermute | solution.py:23
  28.6 20.2 %collective-permute-start.9 = (bf16[4,80,1280]{2,1,0:T(8,128)(2,1)}, bf16[4,80,1280]{2,1,0:T(8,128)(2,1)S(1)}, u32[]{:S(2)}, u32[]{:S(2)}) collective-permute-start(bf16[4,80,1280]{2,1,0:T(8,128)(2,1)} %collective-permute-done.1.refs_0_), channel_id=1, source_target_pairs={{0,1},{1,0},{2,3},{3,2},{4,5},{5,4},{6,7},{7,6},{8,9},{9,8},{10,11... | collective-permute-start | bytes 2457608 | tf_op jit(solution)/shard_map/ppermute | solution.py:23
  28.6 20.2 %collective-permute-start = (bf16[304,1280]{1,0:T(8,128)(2,1)S(1)}, bf16[304,1280]{1,0:T(8,128)(2,1)S(1)}, u32[]{:S(2)}, u32[]{:S(2)}) collective-permute-start(bf16[304,1280]{1,0:T(8,128)(2,1)S(1)} %get-tuple-element.166), channel_id=1, source_target_pairs={{0,2},{1,3},{2,0},{3,1},{4,6},{5,7},{6,4},{7,5},{8,10},{9,11},{10,... | collective-permute-start | bytes 2334728 | tf_op jit(solution)/shard_map/ppermute | solution.py:23
  30.4 43.8 %collective-permute-start.22 = (bf16[320,1280]{1,0:T(8,128)(2,1)}, bf16[320,1280]{1,0:T(8,128)(2,1)}, u32[]{:S(2)}, u32[]{:S(2)}) collective-permute-start(bf16[320,1280]{1,0:T(8,128)(2,1)} %get-tuple-element.206), channel_id=1, source_target_pairs={{0,2},{1,3},{2,0},{3,1},{4,6},{5,7},{6,4},{7,5},{8,10},{9,11},{10,... | collective-permute-start | bytes 2457608 | tf_op jit(solution)/shard_map/ppermute | solution.py:23
  30.7 24.4 %collective-permute-start.11 = (bf16[4,80,1280]{2,1,0:T(8,128)(2,1)}, bf16[4,80,1280]{2,1,0:T(8,128)(2,1)S(1)}, u32[]{:S(2)}, u32[]{:S(2)}) collective-permute-start(bf16[4,80,1280]{2,1,0:T(8,128)(2,1)} %collective-permute-done.1.refs_0_), channel_id=1, source_target_pairs={{0,4},{4,0},{8,12},{12,8},{16,20},{20,16},{24,28},{28,24},{1,5},{5... | collective-permute-start | bytes 2457608 | tf_op jit(solution)/shard_map/ppermute | solution.py:23
  32.5 23.1 %collective-permute-start.14 = (bf16[4,80,1280]{2,1,0:T(8,128)(2,1)}, bf16[4,80,1280]{2,1,0:T(8,128)(2,1)S(1)}, u32[]{:S(2)}, u32[]{:S(2)}) collective-permute-start(bf16[4,80,1280]{2,1,0:T(8,128)(2,1)} %collective-permute-done.1.refs_0_), channel_id=1, source_target_pairs={{0,8},{4,12},{8,0},{12,4},{16,24},{20,28},{24,16},{28,20},{1,9},{5... | collective-permute-start | bytes 2457608 | tf_op jit(solution)/shard_map/ppermute | solution.py:23
  56.6 16.3 %collective-permute-start.15 = (bf16[2,80,1280]{2,1,0:T(8,128)(2,1)}, bf16[2,80,1280]{2,1,0:T(8,128)(2,1)}, u32[]{:S(2)}, u32[]{:S(2)}) collective-permute-start(bf16[2,80,1280]{2,1,0:T(8,128)(2,1)} %slice.29), channel_id=1, source_target_pairs={{0,4},{4,0},{8,12},{12,8},{16,20},{20,16},{24,28},{28,24},{1,5},{5... | collective-permute-start | bytes 1228808 | tf_op jit(solution)/shard_map/ppermute | solution.py:23
  74.1 28.0 %collective-permute-start.24 = (bf16[320,1280]{1,0:T(8,128)(2,1)}, bf16[320,1280]{1,0:T(8,128)(2,1)}, u32[]{:S(2)}, u32[]{:S(2)}) collective-permute-start(bf16[320,1280]{1,0:T(8,128)(2,1)} %collective-permute-done.22.refs_0_), channel_id=1, source_target_pairs={{0,4},{4,0},{8,12},{12,8},{16,20},{20,16},{24,28},{28,24},{1,5},{5... | collective-permute-start | bytes 2457608 | tf_op jit(solution)/shard_map/ppermute | solution.py:23
  74.7 26.2 %collective-permute-start.26 = (bf16[320,1280]{1,0:T(8,128)(2,1)}, bf16[320,1280]{1,0:T(8,128)(2,1)}, u32[]{:S(2)}, u32[]{:S(2)}) collective-permute-start(bf16[320,1280]{1,0:T(8,128)(2,1)} %collective-permute-done.22.refs_0_), channel_id=1, source_target_pairs={{0,8},{4,12},{8,0},{12,4},{16,24},{20,28},{24,16},{28,20},{1,9},{5... | collective-permute-start | bytes 2457608 | tf_op jit(solution)/shard_map/ppermute | solution.py:23
  75.6 26.6 %collective-permute-start.21 = (bf16[256,1280]{1,0:T(8,128)(2,1)}, bf16[256,1280]{1,0:T(8,128)(2,1)}, u32[]{:S(2)}, u32[]{:S(2)}) collective-permute-start(bf16[256,1280]{1,0:T(8,128)(2,1)} %get-tuple-element.201), channel_id=1, source_target_pairs={{0,2},{1,3},{2,0},{3,1},{4,6},{5,7},{6,4},{7,5},{8,10},{9,11},{10,... | collective-permute-start | bytes 1966088 | tf_op jit(solution)/shard_map/ppermute | solution.py:23
  83.4 32.8 %collective-permute-start.28 = (bf16[320,1280]{1,0:T(8,128)(2,1)}, bf16[320,1280]{1,0:T(8,128)(2,1)}, u32[]{:S(2)}, u32[]{:S(2)}) collective-permute-start(bf16[320,1280]{1,0:T(8,128)(2,1)} %get-tuple-element.216), channel_id=1, source_target_pairs={{0,2},{1,3},{2,0},{3,1},{4,6},{5,7},{6,4},{7,5},{8,10},{9,11},{10,... | collective-permute-start | bytes 2457608 | tf_op jit(solution)/shard_map/ppermute | solution.py:23
  100.9 18.3 %collective-permute-start.27 = (bf16[320,1280]{1,0:T(8,128)(2,1)}, bf16[320,1280]{1,0:T(8,128)(2,1)S(1)}, u32[]{:S(2)}, u32[]{:S(2)}) collective-permute-start(bf16[320,1280]{1,0:T(8,128)(2,1)} %collective-permute-done.26.refs_4_), channel_id=1, source_target_pairs={{0,1},{1,0},{2,3},{3,2},{4,5},{5,4},{6,7},{7,6},{8,9},{9,8},{10,11... | collective-permute-start | bytes 2457608 | tf_op jit(solution)/shard_map/ppermute | solution.py:23
  101.1 30.8 %collective-permute-start.30 = (bf16[320,1280]{1,0:T(8,128)(2,1)}, bf16[320,1280]{1,0:T(8,128)(2,1)}, u32[]{:S(2)}, u32[]{:S(2)}) collective-permute-start(bf16[320,1280]{1,0:T(8,128)(2,1)} %collective-permute-done.26.refs_4_), channel_id=1, source_target_pairs={{0,4},{4,0},{8,12},{12,8},{16,20},{20,16},{24,28},{28,24},{1,5},{5... | collective-permute-start | bytes 2457608 | tf_op jit(solution)/shard_map/ppermute | solution.py:23
  102.3 15.0 %collective-permute-start.25 = (bf16[320,1280]{1,0:T(8,128)(2,1)}, bf16[320,1280]{1,0:T(8,128)(2,1)S(1)}, u32[]{:S(2)}, u32[]{:S(2)}) collective-permute-start(bf16[320,1280]{1,0:T(8,128)(2,1)} %collective-permute-done.24.refs_0_), channel_id=1, source_target_pairs={{0,1},{1,0},{2,3},{3,2},{4,5},{5,4},{6,7},{7,6},{8,9},{9,8},{10,11... | collective-permute-start | bytes 2457608 | tf_op jit(solution)/shard_map/ppermute | solution.py:23
  116.1 15.8 %collective-permute-start.29 = (bf16[320,1280]{1,0:T(8,128)(2,1)}, bf16[320,1280]{1,0:T(8,128)(2,1)S(1)}, u32[]{:S(2)}, u32[]{:S(2)}) collective-permute-start(bf16[320,1280]{1,0:T(8,128)(2,1)} %collective-permute-done.28.refs_2_), channel_id=1, source_target_pairs={{0,1},{1,0},{2,3},{3,2},{4,5},{5,4},{6,7},{7,6},{8,9},{9,8},{10,11... | collective-permute-start | bytes 2457608 | tf_op jit(solution)/shard_map/ppermute | solution.py:23
  116.3 23.8 %collective-permute-start.34 = (bf16[320,1280]{1,0:T(8,128)(2,1)}, bf16[320,1280]{1,0:T(8,128)(2,1)}, u32[]{:S(2)}, u32[]{:S(2)}) collective-permute-start(bf16[320,1280]{1,0:T(8,128)(2,1)} %collective-permute-done.28.refs_2_), channel_id=1, source_target_pairs={{0,4},{4,0},{8,12},{12,8},{16,20},{20,16},{24,28},{28,24},{1,5},{5... | collective-permute-start | bytes 2457608 | tf_op jit(solution)/shard_map/ppermute | solution.py:23
  118.1 22.0 %collective-permute-start.36 = (bf16[320,1280]{1,0:T(8,128)(2,1)}, bf16[320,1280]{1,0:T(8,128)(2,1)}, u32[]{:S(2)}, u32[]{:S(2)}) collective-permute-start(bf16[320,1280]{1,0:T(8,128)(2,1)} %collective-permute-done.28.refs_2_), channel_id=1, source_target_pairs={{0,8},{4,12},{8,0},{12,4},{16,24},{20,28},{24,16},{28,20},{1,9},{5... | collective-permute-start | bytes 2457608 | tf_op jit(solution)/shard_map/ppermute | solution.py:23
  119.2 20.3 %collective-permute-start.32 = (bf16[320,1280]{1,0:T(8,128)(2,1)}, bf16[320,1280]{1,0:T(8,128)(2,1)}, u32[]{:S(2)}, u32[]{:S(2)}) collective-permute-start(bf16[320,1280]{1,0:T(8,128)(2,1)} %get-tuple-element.224), channel_id=1, source_target_pairs={{0,2},{1,3},{2,0},{3,1},{4,6},{5,7},{6,4},{7,5},{8,10},{9,11},{10,... | collective-permute-start | bytes 2457608 | tf_op jit(solution)/shard_map/ppermute | solution.py:23
  175.3 25.2 %collective-permute-start.42 = (bf16[16,4992]{1,0:T(8,128)(2,1)S(1)}, bf16[16,4992]{1,0:T(8,128)(2,1)S(1)}, u32[]{:S(2)}, u32[]{:S(2)}) collective-permute-start(bf16[16,4992]{1,0:T(8,128)(2,1)S(1)} %get-tuple-element.238), channel_id=1, source_target_pairs={{0,16},{4,20},{8,24},{12,28},{16,0},{20,4},{24,8},{28,12},{1,17},{... | collective-permute-start | bytes 479240 | tf_op jit(solution)/shard_map/ppermute | solution.py:23
  229.0 39.7 %collective-permute-start.39 = (bf16[256,1280]{1,0:T(8,128)(2,1)}, bf16[256,1280]{1,0:T(8,128)(2,1)}, u32[]{:S(2)}, u32[]{:S(2)}) collective-permute-start(bf16[256,1280]{1,0:T(8,128)(2,1)} %get-tuple-element.246), channel_id=1, source_target_pairs={{0,2},{1,3},{2,0},{3,1},{4,6},{5,7},{6,4},{7,5},{8,10},{9,11},{10,... | collective-permute-start | bytes 1966088 | tf_op jit(solution)/shard_map/ppermute | solution.py:23
  230.5 21.4 %collective-permute-start.55 = (bf16[4,16,4992]{2,1,0:T(8,128)(2,1)S(1)}, bf16[4,16,4992]{2,1,0:T(8,128)(2,1)S(1)}, u32[]{:S(2)}, u32[]{:S(2)}) collective-permute-start(bf16[4,16,4992]{2,1,0:T(8,128)(2,1)S(1)} %get-tuple-element.274.refs_2_), channel_id=1, source_target_pairs={{0,4},{4,0},{8,12},{12,8},{16,20},{20,16},{24,28},{28,24},{1,5},{5... | collective-permute-start | bytes 1916936 | tf_op jit(solution)/shard_map/ppermute | solution.py:23
  231.1 20.8 %collective-permute-start.54 = (bf16[4,16,4992]{2,1,0:T(8,128)(2,1)S(1)}, bf16[4,16,4992]{2,1,0:T(8,128)(2,1)S(1)}, u32[]{:S(2)}, u32[]{:S(2)}) collective-permute-start(bf16[4,16,4992]{2,1,0:T(8,128)(2,1)S(1)} %get-tuple-element.273.refs_0_), channel_id=1, source_target_pairs={{0,8},{4,12},{8,0},{12,4},{16,24},{20,28},{24,16},{28,20},{1,9},{5... | collective-permute-start | bytes 1916936 | tf_op jit(solution)/shard_map/ppermute | solution.py:23
  231.5 16.1 %collective-permute-start.51 = (bf16[16,2944]{1,0:T(8,128)(2,1)S(1)}, bf16[16,2944]{1,0:T(8,128)(2,1)S(1)}, u32[]{:S(2)}, u32[]{:S(2)}) collective-permute-start(bf16[16,2944]{1,0:T(8,128)(2,1)S(1)} %get-tuple-element.286), channel_id=1, source_target_pairs={{0,16},{4,20},{8,24},{12,28},{16,0},{20,4},{24,8},{28,12},{1,17},{... | collective-permute-start | bytes 282632 | tf_op jit(solution)/shard_map/ppermute | solution.py:23
  234.1 14.5 %collective-permute-start.52 = (bf16[16,2944]{1,0:T(8,128)(2,1)S(1)}, bf16[16,2944]{1,0:T(8,128)(2,1)S(1)}, u32[]{:S(2)}, u32[]{:S(2)}) collective-permute-start(bf16[16,2944]{1,0:T(8,128)(2,1)S(1)} %collective-permute-done.50), channel_id=1, source_target_pairs={{0,16},{4,20},{8,24},{12,28},{16,0},{20,4},{24,8},{28,12},{1,17},{... | collective-permute-start | bytes 282632 | tf_op jit(solution)/shard_map/ppermute | solution.py:23
  (138 other events, 1441.4 us)

commit v4 on v3

--- a/solution.py
+++ b/solution.py
@@ -17,6 +17,7 @@
 LIMIT = 16
 KEEP = pl.BlockSpec(memory_space=pltpu.VMEM)
 remain = pl.BlockSpec(memory_space=pl.ANY)
+in_hbm = pl.BlockSpec(memory_space=pltpu.HBM)
 
 
 def swap(array, axis, bits, size):
@@ -146,23 +147,6 @@
     return call(body, (spot, pick), [inputs] + factors * 2, specs, outs, [whole(o.shape) for o in outs])
 
 
-def stage_heads(spot, heads):
-    features = heads[0].shape[1]
-    head_rows = heads[0].shape[0] // 4
-
-    def body(spot_ref, *refs):
-        out, sems = refs[4:]
-        at = pl.ds(pl.multiple_of(spot_ref[2] * head_rows, 16), head_rows)
-        copies = [pltpu.make_async_copy(refs[n].at[at], out.at[n], sems.at[n]) for n in range(4)]
-        for c in copies:
-            c.start()
-        for c in copies:
-            c.wait()
-
-    out = shaped((4, head_rows, features), bf16)
-    return call(body, (spot,), heads, [remain] * 4, out, KEEP, scratch=[pltpu.SemaphoreType.DMA((4,))])
-
-
 def stage_dense(spot, wide, thin, cotangent):
     features, units = wide.shape
     part = units // 4
@@ -200,7 +184,10 @@
     rank = inners[0].shape[1]
 
     def body(spot_ref, pick_ref, xa, xb, gain_ref, shift_ref, iq, ik, iv, pack_ref, side_ref, *refs):
-        ws, (z_ref, low_ref, kv_ref) = refs[:4], refs[4:]
+        hbm, (z_ref, low_ref, kv_ref, ws, sems) = refs[:4], refs[4:]
+        copies = [pltpu.make_async_copy(hbm[n], ws.at[n], sems.at[n]) for n in range(4)]
+        for c in copies:
+            c.start()
         states = jnp.concatenate([xa[0], xb[...]], axis=0).astype(f32)
         z_ref[...] = normalize(states, gain_ref[...], shift_ref[...])[0].astype(bf16)
         low = nt(jnp.concatenate([iq[0], ik[0], iv[0]], axis=0), z_ref[...])
@@ -208,8 +195,9 @@
         for i, packs in enumerate((pack_ref, side_ref)):
             for n in (1, 2):
                 outer = packs[:rank, n * width : (n + 1) * width]
+                copies[2 * i + n - 1].wait()
                 kv_ref[i, n - 1] = project_rows(
-                    ws[2 * i + n - 1][...], z_ref[...], outer, low[n * rank : (n + 1) * rank]
+                    ws[2 * i + n - 1], z_ref[...], outer, low[n * rank : (n + 1) * rank]
                 )
 
     specs = [
@@ -219,7 +207,7 @@
         whole((1, features)),
     ]
     specs += [placed_block((1, rank, features), of_mine(n)) for n in range(3)]
-    specs += [whole(pack.shape), whole(side.shape)] + [whole((width, features))] * 4
+    specs += [whole(pack.shape), whole(side.shape)] + [in_hbm] * 4
     outs = [
         shaped((tokens, features), bf16),
         shaped((3 * rank, tokens), f32),
@@ -232,6 +220,7 @@
         specs,
         outs,
         [whole(o.shape) for o in outs],
+        scratch=[pltpu.VMEM((4, width, features), bf16), pltpu.SemaphoreType.DMA((4,))],
     )
 
 
@@ -258,7 +247,7 @@
     flat = [p for group in parts for p in group]
 
     def body(spot_ref, z_ref, low_ref, received_ref, side_ref, *refs):
-        ins, (out_ref, kv_ref, weight_ref, sems) = refs[:10], refs[10:]
+        ins, (out_ref, kv_ref, q_ref, weight_ref, sems) = refs[:10], refs[10:]
         for i in range(2):
             group = ins[5 * i : 5 * i + 5]
             for n in range(4):
@@ -272,37 +261,26 @@
         for c in copies:
             c.start()
         for i, (ref, start) in enumerate(((received_ref, base), (side_ref, 0))):
-            for n in (1, 2):
+            for n in range(3):
                 outer = ref[start : start + rank, n * width : (n + 1) * width]
-                kv_ref[i, n - 1] = project_rows(
-                    weight_ref[i, n], z_ref[...], outer, low_ref[n * rank : (n + 1) * rank]
-                )
+                y = project_rows(weight_ref[i, n], z_ref[...], outer, low_ref[n * rank : (n + 1) * rank])
+                if n == 0:
+                    q_ref[i] = y
+                else:
+                    kv_ref[i, n - 1] = y
         for c in copies:
             c.wait()
 
     operands = [z, low, received, side] + flat
-    outs = [shaped((2, 4, width, features), bf16), shaped((2, 2, width, tokens), bf16)]
+    outs = [
+        shaped((2, 4, width, features), bf16),
+        shaped((2, 2, width, tokens), bf16),
+        shaped((2, width, tokens), bf16),
+    ]
     return call(
-        body, (spot[2:3],), operands, [KEEP] * len(operands), outs, [remain, KEEP],
+        body, (spot[2:3],), operands, [KEEP] * len(operands), outs, [remain, KEEP, KEEP],
         scratch=[pltpu.VMEM((2, 4, width, features), bf16), pltpu.SemaphoreType.DMA((2,))],
     )
-
-
-def queries_far(z, low, received, side, far):
-    tokens, features = z.shape
-    width = far.shape[2]
-    rank = low.shape[0] // 3
-    base = received.shape[0] - 3 * rank
-
-    def body(z_ref, low_ref, received_ref, side_ref, far_ref, q_ref):
-        for i, (ref, start) in enumerate(((received_ref, base), (side_ref, 0))):
-            outer = ref[start : start + rank, :width]
-            q_ref[i] = project_rows(far_ref[i, 0], z_ref[...], outer, low_ref[:rank])
-
-    operands = [z, low, received, side, far]
-    specs = [whole(o.shape) for o in operands[:4]] + [placed_block((2, 1, width, features), lambda *_: (0, 0, 0, 0))]
-    out = shaped((2, width, tokens), bf16)
-    return call(body, (), operands, specs, out, whole(out.shape))
 
 
 def attend(spot, lengths, q, kv, kv_side):
@@ -393,6 +371,8 @@
 
 
 cubic = 0.044715
+BLOCK = 512
+BIG = 20
 root = math.sqrt(2.0 / math.pi)
 
 
@@ -406,19 +386,14 @@
 
 def feed_quarter(z_ref, gy_ref, wide_ref, thin_ref, pack_ref, rank, low_w, low_n, act_ref, grad_ref, sums_ref, ready=None):
     units = wide_ref.shape[1]
-    block = 256
     low_w2, low_n2 = halves(low_w), halves(low_n)
-
-    def step(b, carry):
+    for start in range(0, units, BLOCK):
+        at = slice(start, min(start + BLOCK, units))
         if ready is not None:
-            ready(b)
-        at = pl.ds(pl.multiple_of(b * block, block), block)
+            ready(at)
         widened = nn(z_ref[...], wide_ref[:, at]) + tn(low_w2, twice(pack_ref[rank : 2 * rank, at]))
         grad = nt(gy_ref[...], thin_ref[at, :]) + tn(low_n2, twice(pack_ref[2 * rank : 3 * rank, at]))
         act_ref[:, at], grad_ref[:, at] = bend_of(widened, grad)
-        return carry
-
-    lax.fori_loop(0, units // block, step, 0)
     sums_ref[:rank] = folded(nn(low_w2, grad_ref[...]))
     sums_ref[rank:] = folded(nn(low_n2, act_ref[...]))
     return (
@@ -431,11 +406,10 @@
 
 def feed_units(z_ref, gy_ref, wide_ref, thin_ref, outer, inner, low_w, low_n, act_ref, grad_ref, ready):
     units = wide_ref.shape[0]
-    block = 256
     low_w2, low_n2 = halves(low_w), halves(low_n)
-    for start in range(0, units, block):
-        ready(start // block)
-        at = slice(start, min(start + block, units))
+    for start in range(0, units, BLOCK):
+        at = slice(start, min(start + BLOCK, units))
+        ready(at.stop)
         widened = nt(z_ref[...], wide_ref[at]) + tn(low_w2, twice(outer[:, at]))
         grad = nt(gy_ref[...], thin_ref[at]) + tn(low_n2, twice(inner[:, at]))
         act_ref[:, at], grad_ref[:, at] = bend_of(widened, grad)
@@ -525,29 +499,27 @@
         shaped((2 * rank, units), f32),
     ]
     scratch = [pltpu.VMEM((tokens, units), bf16)] * 2
-    return call(body, (spot, pick, lengths), operands, specs, outs, [KEEP] * 5, scratch=scratch)
+    return call(body, (spot, pick, lengths), operands, specs, outs, [KEEP] * 5, scratch=scratch, limit=BIG)
 
 
 def feed_near(z, gy, branch, second, lows, pack, dense):
     tokens, features = z.shape
     units = dense[0].shape[1]
     rank = lows.shape[0] // 5
-    blocks = units // 256
+    blocks = [slice(n, min(n + BLOCK, units)) for n in range(0, units, BLOCK)]
 
     def body(z_ref, gy_ref, branch_in, second_in, lows_in, pack_ref, wide_hbm, thin_hbm, branch_ref, second_ref, lows_ref, sums_ref, wide, thin, act_ref, grad_ref, sems):
-        def copies(b):
-            at = pl.ds(pl.multiple_of(b * 256, 256), 256)
-            return (
-                pltpu.make_async_copy(wide_hbm.at[:, at], wide.at[:, at], sems.at[0, b]),
-                pltpu.make_async_copy(thin_hbm.at[at], thin.at[at], sems.at[1, b]),
+        copies = {}
+        for n, at in enumerate(blocks):
+            copies[at.start] = (
+                pltpu.make_async_copy(wide_hbm.at[:, at], wide.at[:, at], sems.at[0, n]),
+                pltpu.make_async_copy(thin_hbm.at[at], thin.at[at], sems.at[1, n]),
             )
-
-        for b in range(blocks):
-            for c in copies(b):
+            for c in copies[at.start]:
                 c.start()
 
-        def ready(b):
-            for c in copies(b):
+        def ready(at):
+            for c in copies[at.start]:
                 c.wait()
 
         sums = feed_quarter(
@@ -563,53 +535,54 @@
     operands = [z, gy, branch, second, lows, pack] + dense
     outs = [shaped(branch.shape, f32), shaped(second.shape, f32), shaped(lows.shape, f32), shaped((2 * rank, units), f32)]
     scratch = [pltpu.VMEM(d.shape, bf16) for d in dense] + [pltpu.VMEM((tokens, units), bf16)] * 2
-    scratch += [pltpu.SemaphoreType.DMA((2, blocks))]
+    scratch += [pltpu.SemaphoreType.DMA((2, len(blocks)))]
     return call(
-        body, (), operands, [KEEP] * 6 + [remain] * 2, outs, [KEEP] * 4, scratch=scratch, aliases={2: 0, 3: 1}, limit=24
+        body, (), operands, [KEEP] * 6 + [in_hbm] * 2, outs, [KEEP] * 4, scratch=scratch, aliases={2: 0, 3: 1}, limit=BIG
     )
 
 
-def far_copies(count, ins, wide, thin, sems):
+def far_copies(ins, wide, thin, sems):
     part = ins[0].shape[0]
     copies = []
-    for n in range(count):
+    for n in range(len(ins) // 4):
         for q in range(2):
-            at = slice(q * part, (q + 1) * part)
-            copies.append(pltpu.make_async_copy(ins[4 * n + q], wide.at[n, at], sems.at[4 * n + 2 * q]))
-            copies.append(pltpu.make_async_copy(ins[4 * n + 2 + q], thin.at[n, at], sems.at[4 * n + 2 * q + 1]))
+            k = 2 * n + q
+            at = slice(k * part, (k + 1) * part)
+            copies.append(pltpu.make_async_copy(ins[4 * n + q], wide.at[at], sems.at[2 * k]))
+            copies.append(pltpu.make_async_copy(ins[4 * n + 2 + q], thin.at[at], sems.at[2 * k + 1]))
     for c in copies:
         c.start()
     return copies
 
 
 def far_parts(parts, z_ref, gy_ref, copies, wide, thin, received_ref, far_side_ref, rank, base, low_w, low_n, act_ref, grad_ref, sums_ref):
-    count = wide.shape[1] // 2
-    total = None
-    for n, r in enumerate(parts):
+    count = wide.shape[0] // (2 * len(parts))
+    outer, inner = [], []
+    for r in parts:
         lanes = slice(r * count, (r + 1) * count)
-        outer = jnp.concatenate(
-            [received_ref[base + rank : base + 2 * rank, lanes], far_side_ref[rank : 2 * rank, lanes]], axis=1
-        )
-        inner = jnp.concatenate(
-            [received_ref[base + 2 * rank : base + 3 * rank, lanes], far_side_ref[2 * rank : 3 * rank, lanes]], axis=1
-        )
-
-        def ready(b):
-            if b < 2:
-                for c in copies[4 * n + 2 * b : 4 * n + 2 * b + 2]:
-                    c.wait()
-
-        found = feed_units(
-            z_ref, gy_ref, wide.at[n], thin.at[n], outer, inner, low_w, low_n, act_ref, grad_ref, ready
-        )
-        sums_ref[n] = found[4]
-        total = found[:4] if total is None else [a + b for a, b in zip(total, found[:4])]
+        outer += [received_ref[base + rank : base + 2 * rank, lanes], far_side_ref[rank : 2 * rank, lanes]]
+        inner += [received_ref[base + 2 * rank : base + 3 * rank, lanes], far_side_ref[2 * rank : 3 * rank, lanes]]
+    arrived = []
+
+    def ready(end):
+        while len(arrived) * count < min(end, wide.shape[0]):
+            n = len(arrived)
+            copies[2 * n].wait()
+            copies[2 * n + 1].wait()
+            arrived.append(n)
+
+    *total, sums = feed_units(
+        z_ref, gy_ref, wide, thin, jnp.concatenate(outer, axis=1), jnp.concatenate(inner, axis=1), low_w, low_n,
+        act_ref, grad_ref, ready,
+    )
+    sums_ref[...] = sums
     return total
 
 
-def far_scratch(count, part, features, tokens):
-    return [pltpu.VMEM((count, 2 * part, features), bf16)] * 2 + [pltpu.VMEM((tokens, 2 * part), bf16)] * 2 + [
-        pltpu.SemaphoreType.DMA((4 * count,))
+def far_scratch(parts, part, features, tokens):
+    units = 2 * len(parts) * part
+    return [pltpu.VMEM((units, features), bf16)] * 2 + [pltpu.VMEM((tokens, units), bf16)] * 2 + [
+        pltpu.SemaphoreType.DMA((4 * len(parts),))
     ]
 
 
@@ -623,7 +596,7 @@
     def body(z_ref, gy_ref, branch_in, second_in, lows_in, received_ref, far_side_ref, *refs):
         ins, (branch_ref, second_ref, lows_ref, sums_ref) = refs[:count], refs[count : count + 4]
         wide, thin, act_ref, grad_ref, sems = refs[count + 4 :]
-        copies = far_copies(len(parts), ins, wide, thin, sems)
+        copies = far_copies(ins, wide, thin, sems)
         total = far_parts(
             parts, z_ref, gy_ref, copies, wide, thin, received_ref, far_side_ref, rank, base,
             lows_in[rank : 2 * rank], lows_in[2 * rank : 3 * rank], act_ref, grad_ref, sums_ref,
@@ -639,11 +612,11 @@
         shaped(branch.shape, f32),
         shaped(second.shape, f32),
         shaped(lows.shape, f32),
-        shaped((len(parts), 2 * rank, 2 * part), f32),
+        shaped((2 * rank, 2 * len(parts) * part), f32),
     ]
     return call(
-        body, (), operands, [KEEP] * 7 + [remain] * count, outs, [KEEP] * 4,
-        scratch=far_scratch(len(parts), part, features, tokens), aliases={2: 0, 3: 1},
+        body, (), operands, [KEEP] * 7 + [in_hbm] * count, outs, [KEEP] * 4,
+        scratch=far_scratch(parts, part, features, tokens), aliases={2: 0, 3: 1}, limit=BIG,
     )
 
 
@@ -678,7 +651,7 @@
     def body(spot_ref, pick_ref, length_ref, hidden_ref, z_ref, gy_ref, branch_in, second_in, lows_ref, near0, near1, far0, far3, c01, c23, wo0, wo1, far_ref, pack_ref, side_ref, far_side_ref, received_ref, oo, wi, no, ca, cb, gain_ref, *refs):
         hbm, (out_ref, outb_ref, gh_ref, gc_ref, delta_ref, keep_ref, give_ref) = refs[:8], refs[8:15]
         wide, thin, act_ref, grad_ref, sems, last, ga_ref = refs[15:]
-        copies = far_copies(len(parts), hbm, wide, thin, sems)
+        copies = far_copies(hbm, wide, thin, sems)
         low_w = lows_ref[rank : 2 * rank]
         low_n = lows_ref[2 * rank : 3 * rank]
         found = far_parts(
@@ -730,7 +703,8 @@
             quarters.append((near[:rank], near[rank:]))
         for q in range(2):
             lanes = slice(q * part, (q + 1) * part)
-            pieces = [far0[0, :, lanes], last[0, :, lanes], last[1, :, lanes], far3[0, :, lanes]]
+            later = slice((2 + q) * part, (3 + q) * part)
+            pieces = [far0[:, lanes], last[:, lanes], last[:, later], far3[:, lanes]]
             joined = shuffled(jnp.concatenate(pieces, axis=1), quad)
             quarters.append((joined[:rank], joined[rank:]))
         for i in range(4):
@@ -758,58 +732,67 @@
         shaped((rank, total_lanes), f32),
         shaped((rank, total_lanes), f32),
     ]
-    scratch = far_scratch(2, part, features, tokens)
-    scratch += [pltpu.VMEM((2, 2 * rank, 2 * part), f32), pltpu.VMEM((tokens, features), bf16)]
+    scratch = far_scratch(parts, part, features, tokens)
+    scratch += [pltpu.VMEM((2 * rank, 4 * part), f32), pltpu.VMEM((tokens, features), bf16)]
     out_specs = [placed_block((1, rows, features), lambda i, spot, *_: (spot[0], 0, 0))] + [KEEP] * 6
-    return call(body, (spot, pick, lengths), operands, specs, outs, out_specs, scratch=scratch, limit=24)
-
-
-def gather_grads(spot, quarters, z, low, packs, received):
-    tokens, features = z.shape
+    return call(body, (spot, pick, lengths), operands, specs, outs, out_specs, scratch=scratch, limit=BIG)
+
+
+def gather_pair(quarters, low, factors, before=None):
     rank = low.shape[0] // 3
-    width = quarters[0][0].shape[0]
-    pack, side, far_side = packs
-    base = received.shape[0] - 3 * rank
-    half = features // 2
+    width, tokens = quarters[0][0].shape
     tail = lanes_up(3 * width)
-    total_lanes = 3 * half + 2 * tail
-
-    def body(spot_ref, *refs):
-        groups = [refs[3 * i : 3 * i + 3] for i in range(4)]
-        z_ref, low_ref, pack_ref, side_ref, far_side_ref, received_ref, g_ref, gl_ref, keep_ref, give_ref = refs[12:]
-        places = ((pack_ref, 0), (side_ref, 0), (received_ref, base), (far_side_ref, 0))
+    extra = 0 if before is None else 1
+
+    def body(*refs):
+        groups = [refs[3 * i : 3 * i + 3] for i in range(2)]
+        low_ref, *places = refs[6:9]
+        g_ref, gl_ref, keep_ref, give_ref = refs[9 + extra :]
         lows = [halves(low_ref[n * rank : (n + 1) * rank]) for n in range(3)]
-        total = [jnp.zeros((rank, tokens), f32) for _ in range(3)]
-        core = spot_ref[3] & 1
-        for i in range(4):
-            q, own, other = groups[i][0], groups[i][1], groups[i ^ 1][2]
-            ref, start = places[i]
-            outers = []
-            for n in range(3):
+        for n in range(3):
+            at = slice(n * rank, (n + 1) * rank)
+            total = jnp.zeros((rank, tokens), f32) if before is None else refs[9][at]
+            for i in range(2):
+                q, own, other = groups[i][0], groups[i][1], groups[1 - i][2]
                 if n == 0:
                     g = q[...]
                 else:
                     g = (own[n - 1] + other[n - 1].astype(f32)).astype(bf16)
                 g_ref[i, n] = g
-                lanes = slice(n * width, (n + 1) * width)
-                total[n] = total[n] + nn(ref[start : start + rank, lanes], g)
-                outers.append(folded(nt(lows[n], g)))
-            at = 3 * half + (i // 2) * tail
-            (keep_ref, give_ref)[i % 2][:, at : at + tail] = padded(jnp.concatenate(outers, axis=1), tail)
+                total = total + nn(places[i][:rank, n * width : (n + 1) * width], g)
+                (keep_ref, give_ref)[i][:, n * width : (n + 1) * width] = folded(nt(lows[n], g))
+            gl_ref[at] = total
+        for ref in (keep_ref, give_ref):
+            ref[:, 3 * width :] = jnp.zeros((rank, tail - 3 * width), f32)
+
+    operands = [a for q in quarters for a in q] + [low] + list(factors) + ([] if before is None else [before])
+    outs = [
+        shaped((2, 3, width, tokens), bf16),
+        shaped((3 * rank, tokens), f32),
+        shaped((rank, tail), f32),
+        shaped((rank, tail), f32),
+    ]
+    return call(body, (), operands, [KEEP] * len(operands), outs, [KEEP] * 4, weight=3)
+
+
+def gather_inner(spot, gl, z, first, second):
+    features = z.shape[1]
+    rank = gl.shape[0] // 3
+    half = features // 2
+    tail = first[0].shape[1]
+
+    def body(spot_ref, gl_ref, z_ref, a0, b0, a1, b1, keep_ref, give_ref):
+        core = spot_ref[3] & 1
         for n in range(3):
-            gl_ref[n * rank : (n + 1) * rank] = total[n]
-            inner = folded(nn(halves(total[n]), z_ref[...]))
+            inner = folded(nn(halves(gl_ref[n * rank : (n + 1) * rank]), z_ref[...]))
             keep_ref[:, n * half : (n + 1) * half], give_ref[:, n * half : (n + 1) * half] = shares(inner, core)
-
-    operands = [a for q in quarters for a in q] + [z, low] + list(packs) + [received]
-    outs = [
-        shaped((4, 3, width, tokens), bf16),
-        shaped((3 * rank, tokens), f32),
-        shaped((rank, total_lanes), f32),
-        shaped((rank, total_lanes), f32),
-    ]
-    return call(
-        body, (spot,), operands, [whole(o.shape) for o in operands], outs, [whole(o.shape) for o in outs], weight=5)
+        for ref, pieces in ((keep_ref, (a0, a1)), (give_ref, (b0, b1))):
+            for i in range(2):
+                ref[:, 3 * half + i * tail : 3 * half + (i + 1) * tail] = pieces[i][...]
+
+    out = shaped((rank, 3 * half + 2 * tail), f32)
+    operands = [gl, z] + list(first) + list(second)
+    return call(body, (spot,), operands, [KEEP] * 6, [out, out], [KEEP] * 2, weight=2)
 
 
 def settle(spot, pick, keep, moved, common, with_picks):
@@ -899,15 +882,16 @@
     return call(body, (), flat, [KEEP] * len(flat), outs, [KEEP] * len(outs), weight=1)
 
 
-def finish(spot, pick, g, gl, inners, weights, far, inputs, received, grad_hidden, gain):
-    rows, features = inputs.shape[1:]
-    tokens = 2 * rows
-    width = g.shape[2]
+def finish(spot, pick, g01, g23, gl, inners, weights, far, states, grad_hidden, gain, block):
+    features = gain.shape[1]
+    rows = g01.shape[3] // 2
+    width = g01.shape[2]
     rank = gl.shape[0] // 3
-
-    def body(spot_ref, pick_ref, g_ref, gl_ref, iq, ik, iv, *refs):
-        ws, (far_ref, xa, xb, gh_ref, gain_ref, grad_ref, gradb_ref) = refs[:6], refs[6:]
-        low = [halves(gl_ref[n * rank : (n + 1) * rank]) for n in range(3)]
+    at = slice(block * rows, (block + 1) * rows)
+
+    def body(spot_ref, pick_ref, g01_ref, g23_ref, gl_ref, iq, ik, iv, *refs):
+        ws, (far_ref, x_ref, gh_ref, gain_ref, grad_ref) = refs[:6], refs[6:]
+        low = [halves(gl_ref[n * rank : (n + 1) * rank, at]) for n in range(3)]
         total = tn(
             jnp.concatenate(low, axis=0),
             jnp.concatenate([twice(iq[0]), twice(ik[0]), twice(iv[0])], axis=0),
@@ -917,23 +901,29 @@
                 weight = jnp.concatenate([w[...] for w in ws[3 * i : 3 * i + 3]], axis=0)
             else:
                 weight = far_ref[i - 2].reshape(3 * width, features)
-            total = total + tn(g_ref[i].reshape(3 * width, tokens), weight)
-        states = jnp.concatenate([xa[0], xb[...]], axis=0).astype(f32)
-        _, unit, scaled = normalize(states, gain_ref[...], gain_ref[...])
-        grad = gh_ref[...] + normalize_back(total, unit, scaled, gain_ref[...])
-        grad_ref[0] = grad[:rows]
-        gradb_ref[...] = grad[rows:].astype(bf16)
-
-    operands = [g, gl] + inners + weights + [far, inputs, received, grad_hidden, gain]
-    specs = [whole(g.shape), whole(gl.shape)]
+            g_ref = (g01_ref, g23_ref)[i // 2]
+            total = total + tn(g_ref[i % 2, :, :, at].reshape(3 * width, rows), weight)
+        x = x_ref[0] if block == 0 else x_ref[...]
+        _, unit, scaled = normalize(x.astype(f32), gain_ref[...], gain_ref[...])
+        grad = gh_ref[at] + normalize_back(total, unit, scaled, gain_ref[...])
+        if block == 0:
+            grad_ref[0] = grad
+        else:
+            grad_ref[...] = grad.astype(bf16)
+
+    operands = [g01, g23, gl] + inners + weights + [far, states, grad_hidden, gain]
+    specs = [KEEP] * 3
     specs += [placed_block((1, rank, features), of_mine(n)) for n in range(3)]
-    specs += [whole(w.shape) for w in weights]
+    specs += [KEEP] * 6
     specs += [placed_block((2, 3, width, features), lambda *_: (0, 0, 0, 0))]
-    specs += [placed_block((1, rows, features), lambda i, spot, *_: (spot[0], 0, 0))]
-    specs += [placed_block((rows, features), lambda *_: (0, 0)), whole(grad_hidden.shape), whole(gain.shape)]
-    outs = [shaped((2, rows, features), f32), shaped((rows, features), bf16)]
-    out_specs = [placed_block((1, rows, features), lambda i, spot, *_: (spot[0], 0, 0)), KEEP]
-    return call(body, (spot, pick), operands, specs, outs, out_specs, weight=9)
+    if block == 0:
+        specs += [placed_block((1, rows, features), lambda i, spot, *_: (spot[0], 0, 0))]
+        out, out_spec = shaped((2, rows, features), f32), placed_block((1, rows, features), lambda i, spot, *_: (spot[0], 0, 0))
+    else:
+        specs += [placed_block((rows, features), lambda *_: (0, 0))]
+        out, out_spec = shaped((rows, features), bf16), KEEP
+    specs += [KEEP] * 2
+    return call(body, (spot, pick), operands, specs, out, out_spec, weight=5)
 
 
 def make_body(dp_size, tensor_size):
@@ -993,40 +983,41 @@
         width = query_outer.shape[2]
         half = features // 2
 
-        part_heads = stage_heads(spot, heads)
+        head_rows = heads[0].shape[0] // 4
+        part_heads = jnp.stack([lax.dynamic_slice_in_dim(w, quad * head_rows, head_rows, 0) for w in heads])
         far0 = across(part_heads)
         send, pack = stage(after(spot, part_heads), pick, inputs, small)
-        received = across(send)
         near_heads = [beside(w) for w in after(heads, part_heads)]
+        received = across(after(send, near_heads[:2]))
         side = beside(pack)
-        near_dense = [beside(w) for w in after(dense, near_heads)]
+        near_dense = [beside(after(dense[0], near_heads))]
+        near_dense.append(beside(after(dense[1], near_dense[0])))
         part_wide, part_thin, part_last, cot_send = stage_dense(
             after(spot, pack), widen_weight, narrow_weight, cotangent
         )
-        far1, far2 = along(after(far0, near_dense), 1), along(after(far0, near_dense), 2)
-        side0 = beside(after(far0, side, near_dense, part_wide))
+        far1, far2 = along(far0, 1), along(far0, 2)
         wide0 = across(after(part_wide, far0))
         z, low, kv01 = project_near(
-            spot, pick, inputs, after(received, side0), gains[0], gains[1], inners, pack, side,
-            [heads[1], heads[2], near_heads[1], near_heads[2]],
+            spot, pick, inputs, after(received, part_wide, side, far0, near_dense), gains[0], gains[1], inners, pack,
+            side, [heads[1], heads[2], near_heads[1], near_heads[2]],
         )
         kv01_side = beside(kv01)
+        q01 = queries_near(after(z, kv01), low, pack, side, [heads[0], near_heads[0]])
         far3, far4 = along(after(far2[:2], kv01), 1), along(after(far1[2:], kv01), 2)
-        side1 = beside(after(far1, kv01))
-        q01 = queries_near(after(z, kv01), low, pack, side, [heads[0], near_heads[0]])
-        side2 = beside(after(far2, q01, side1))
+        side0 = beside(after(far0, kv01))
+        side1 = beside(after(far1, kv01, side0))
         c01, total01 = attend(spot, lengths, q01, kv01, after(kv01_side, side1))
+        side2 = beside(after(far2, c01, side1))
         far_side = beside(after(received[rows:], c01))
-        side3, side4 = beside(after(far3, c01, side2)), beside(after(far4, c01, side2))
+        side3, side4 = beside(after(far3, c01)), beside(after(far4, c01))
         wide1, wide2 = along(after(wide0, c01), 1), along(after(wide0, c01), 2)
         cot_side = across(after(cot_send, c01))
-        far, kv23 = project_far(
-            spot, after(z, c01), low, received, far_side,
+        far, kv23, q23 = project_far(
+            spot, after(z, c01, wide0), low, received, far_side,
             [[far0, far1, far2, far3, far4], [side0, side1, side2, side3, side4]],
         )
         kv23_side = beside(kv23)
         thin0 = across(after(part_thin, kv23))
-        q23 = queries_far(after(z, kv23), low, received, far_side, far)
         c23, total23 = attend(spot, lengths, q23, kv23, kv23_side)
         packs = [pack, side, far_side]
         outs_w = [heads[3], near_heads[3]]
@@ -1080,32 +1071,38 @@
         moved = beside(give)
         here, there = settle(spot, pick, keep, moved, 3 * half, True)
         other = across(there)
+        out_side = across(outb)
         crossed = [along(here, 4)]
         quarters = [back(0, after(q01, here), kv01, kv01_side, total01)]
         quarters.append(back(1, after(q01, quarters[0][0]), kv01, kv01_side, total01))
         sides = [beside(after(quarters[0][2], quarters[1][0]))]
-        crossed.append(along(after(other, quarters[0][0]), 4))
-        out_side = across(after(outb, quarters[1][0]))
-        quarters.append(back(2, after(q23, quarters[1][0]), kv23, kv23_side, total23))
+        crossed.append(along(after(other, quarters[1][0]), 4))
+        quarters.append(back(2, after(q23, quarters[1][0], out_side), kv23, kv23_side, total23))
         sides.append(beside(after(quarters[1][2], quarters[2][0], sides[0])))
         turns = first_turn(here, other, after(crossed, quarters[2][0]))
         quarters.append(back(3, after(q23, quarters[2][0], turns[0][0]), kv23, kv23_side, total23))
-        sides += [beside(after(quarters[2][2], quarters[3][0], sides[1])), beside(quarters[3][2])]
-        quarters = [(gq, own, sided) for (gq, own, _), sided in zip(quarters, sides)]
-        early = second_turn(after(turns, quarters[3][0]))
-        g, gl, keep, give = gather_grads(spot, quarters, after(z, early[0], early[2]), low, packs, received)
+        pieces = [(gq, own, sided) for (gq, own, _), sided in zip(quarters, sides)]
+        g01, gl, *first = gather_pair(
+            [pieces[0], (after(pieces[1][0], quarters[3][0]),) + pieces[1][1:]], after(low, turns), [pack, side]
+        )
+        early = second_turn(after(turns, g01))
+        sides += [beside(after(q[2], g01)) for q in quarters[2:]]
+        pieces += [(gq, own, sided) for (gq, own, _), sided in zip(quarters[2:], sides[2:])]
+        far_factors = [received[rows:], far_side]
+        g23, gl, *second = gather_pair(pieces[2:], low, far_factors, gl)
+        keep, give = gather_inner(spot, gl, z, first, second)
         moved = beside(give)
         here, there = settle(spot, pick, keep, moved, 3 * half, False)
         other = across(there)
         crossed = [along(here, 4)]
         crossed.append(along(other, 4))
-        grad, gradb = finish(
-            spot, pick, after(g, other), gl, inners, heads[:3] + near_heads[:3], far, inputs, received, grad_hidden,
-            gains[0],
-        )
-        grad_side = across(after(gradb, crossed))
+        ends = (gl, inners, heads[:3] + near_heads[:3], far)
+        gradb = finish(spot, pick, g01, after(g23, other), *ends, received, grad_hidden, gains[0], 1)
+        grad_side = across(gradb)
+        grad = finish(spot, pick, g01, after(g23, gradb, crossed), *ends, inputs, grad_hidden, gains[0], 0)
         turns = first_turn(here, other, after(crossed, gradb))
-        output = pair_up(spot, output, after(out_side, gradb))
+        output = pair_up(spot, output, after(out_side, grad))
+        early = after(early, gradb, turns[0][0])
         picks = jnp.concatenate([a[:, 0, -128:-122] for a in early]).astype(jnp.int32)
         adapters = query_inner.shape[0]
         units = widen_weight.shape[1]
@@ -1130,7 +1127,7 @@
         input_grad = pair_up(spot, grad, grad_side)
         late = combine(
             spot,
-            after(picks, grad_side),
+            after(picks, grad_side, output),
             late,
             [(n * half, half, n) for n in range(3)] + [(base + n * width, width, n) for n in range(3)],
             adapters,

time: 282 us -> 268 us (0.950); the launches traced: 276 us -> 265 us
  waiting for transfers between devices: 60.8 us -> 45 us
  starting transfers between devices: 41.9 us -> 53.8 us
  Pallas kernels: 160 us -> 151 us
    ppermute x62, waiting for transfers between devices: 60.8 us -> 45 us  [swap(): return lax.ppermute(array, axis, [(i, i ^ bits) for i in range(size)])]
    ppermute x62, starting transfers between devices: 41.9 us -> 53.8 us  [swap(): return lax.ppermute(array, axis, [(i, i ^ bits) for i in range(size)])]
    pallas_call x33 -> x34, Pallas kernels: 160 us -> 151 us  [call(): pl.pallas_call(body, grid_spec=pltpu.PrefetchScalarGridSpec(num_scalar_pr...]
    another operation x0 -> x3, local copies, waits for them, and re-layouts: none -> 3.11 us  [body(): jnp.stack([lax.dynamic_slice_in_dim(w, quad * head_rows, head_rows, 0) fo...]
    unnamed x203 -> x188, local copies, waits for them, and re-layouts: 9.02 us -> 7.62 us
  transfers between devices with their start and end apart: 62 -> 62, of which waited for: 21 -> 22; matrix products, arithmetic and copies ran while one was open for 1% -> 1% of each run, Pallas kernels for 47% -> 45%
where the time goes in v4:
time: 268 us; the launch traced here: 265 us
  Pallas kernels  151 us (56%)
  starting transfers between devices  53.8 us (20%)
  waiting for transfers between devices  45 us (17%)
  local copies, waits for them, and re-layouts  12.4 us (5%)
    pallas_call x34, Pallas kernels, call(): pl.pallas_call(body, grid_spec=pltpu.PrefetchScalarGridSpec(num_scalar_pr...  151 us
    ppermute x62, starting transfers between devices, swap(): return lax.ppermute(array, axis, [(i, i ^ bits) for i in range(size)])  53.8 us
    ppermute x62, waiting for transfers between devices, swap(): return lax.ppermute(array, axis, [(i, i ^ bits) for i in range(size)])  45 us
    unnamed x188, local copies, waits for them, and re-layouts  7.62 us
  transfers between devices with their start and end apart: 62, of which 22 were waited for; matrix products, arithmetic and copies ran while one was open for 1% of the time, Pallas kernels for 45%

profile of v4, /device:TPU:0, one launch (start us, length us, event | category | flops | bytes accessed | tf_op | source)
XLA Modules:
  0.0 265.4 jit_solution(11206741372183308395)
XLA Ops:
  5.9 2.9 %collective-permute-start.4 = (bf16[4,80,1280]{2,1,0:T(8,128)(2,1)}, bf16[4,80,1280]{2,1,0:T(8,128)(2,1)}, u32[]{:S(2)}, u32[]{:S(2)}) collective-permute-start(bf16[4,80,1280]{2,1,0:T(8,128)(2,1)} %pad_maximum_fusion), channel_id=1, source_target_pairs={{0,2},{1,3},{2,0},{3,1},{4,6},{5,7},{6,4},{7,5},{8,10},{9,11},{10,... | collective-permute-start | bytes 2457608 | tf_op jit(solution)/shard_map/ppermute | solution.py:24
  20.4 3.1 %shard_map.354 = (bf16[320,1280]{1,0:T(8,128)(2,1)}, bf16[320,1280]{1,0:T(8,128)(2,1)}, bf16[320,1280]{1,0:T(8,128)(2,1)}, bf16[256,1280]{1,0:T(8,128)(2,1)}) custom-call(s32[4]{0:T(128)S(1)} %pad_add_fusion.spot_ref, bf16[1280,1280]{1,0:T(8,128)(2,1)S(1)} %copy-done.28, bf16[1280,1280]{1,0:T(8,128)(2,1)S(1)} %copy-done.30, ...), custom_call_target="tpu_custom_call" | custom-call | flops 99999997952 | bytes 100000 | tf_op jit(solution)/shard_map/pallas_call | solution.py:86
  23.5 4.6 %collective-permute-done.4.refs_0_ = bf16[4,80,1280]{2,1,0:T(8,128)(2,1)} collective-permute-done((bf16[4,80,1280]{2,1,0:T(8,128)(2,1)}, bf16[4,80,1280]{2,1,0:T(8,128)(2,1)}, u32[]{:S(2)}, u32[]{:S(2)}) %collective-permute-start.4) | collective-permute-done | bytes 819232 | tf_op jit(solution)/shard_map/ppermute | solution.py:24
  31.8 12.3 %collective-permute-done.2.xb.received_ref.refs_7_ = bf16[304,1280]{1,0:T(8,128)(2,1)S(1)} collective-permute-done((bf16[304,1280]{1,0:T(8,128)(2,1)S(1)}, bf16[304,1280]{1,0:T(8,128)(2,1)S(1)}, u32[]{:S(2)}, u32[]{:S(2)}) %collective-permute-start.2) | collective-permute-done | bytes 778272 | tf_op jit(solution)/shard_map/ppermute | solution.py:24
  44.2 4.9 %shard_map.355 = (bf16[512,1280]{1,0:T(8,128)(2,1)S(1)}, f32[48,512]{1,0:T(8,128)S(1)}, bf16[2,2,320,512]{3,2,1,0:T(8,128)(2,1)S(1)}) custom-call(s32[4]{0:T(128)S(1)} %pad_add_fusion.spot_ref, s32[2,6]{1,0:T(2,128)S(1)} %copy-done.27, bf16[2,256,1280]{2,1,0:T(8,128)(2,1)S(1)} %copy-done.5, ...), custom_call_target="tpu_custom_call" | custom-call | flops 99999997952 | bytes 100000 | tf_op jit(solution)/shard_map/pallas_call | solution.py:86
  58.2 8.1 %shard_map.357 = (bf16[2,320,512]{2,1,0:T(8,128)(2,1)S(1)}, f32[8,1,512]{2,1,0:T(1,128)S(1)}) custom-call(s32[4]{0:T(128)S(1)} %pad_add_fusion.spot_ref, s32[2]{0:T(128)S(1)} %copy-done.73, bf16[2,320,512]{2,1,0:T(8,128)(2,1)S(1)} %shard_map.356.q_ref, bf16[2,2,320,512]{3,2,1,0:T(8,128)(2,1)S(1)} %get-tuple-element.188.k1.v1, ...), custom_call_target="tpu_custom_call" | custom-call | flops 99999997952 | bytes 100000 | tf_op jit(solution)/shard_map/pallas_call | solution.py:86
  70.4 5.9 %shard_map.358 = (bf16[2,4,320,1280]{3,2,1,0:T(8,128)(2,1)S(1)}, bf16[2,2,320,512]{3,2,1,0:T(8,128)(2,1)S(1)}, bf16[2,320,512]{2,1,0:T(8,128)(2,1)S(1)}) custom-call(s32[1]{0:T(128)} %bitcast.2.spot_ref, bf16[512,1280]{1,0:T(8,128)(2,1)S(1)} %get-tuple-element.196.z_ref, f32[48,512]{1,0:T(8,128)S(1)} %get-tuple-element.273.low_ref.refs_6_, ...), custom_call_target="tpu_custom_call" | custom-call | flops 99999997952 | bytes 100000 | tf_op jit(solution)/shard_map/pallas_call | solution.py:86
  81.8 8.4 %shard_map.359 = (bf16[2,320,512]{2,1,0:T(8,128)(2,1)S(1)}, f32[8,1,512]{2,1,0:T(1,128)S(1)}) custom-call(s32[4]{0:T(128)S(1)} %pad_add_fusion.spot_ref, s32[2]{0:T(128)S(1)} %copy-done.73, bf16[2,320,512]{2,1,0:T(8,128)(2,1)S(1)} %get-tuple-element.266.q_ref, bf16[2,2,320,512]{3,2,1,0:T(8,128)(2,1)S(1)} %get-tuple-element.204.k1.v1, ...), custom_call_target="tpu_custom_call" | custom-call | flops 99999997952 | bytes 100000 | tf_op jit(solution)/shard_map/pallas_call | solution.py:86
  90.4 6.4 %shard_map.360 = (f32[512,1280]{1,0:T(8,128)S(1)}, bf16[512,1280]{1,0:T(8,128)(2,1)S(1)}, f32[32,512]{1,0:T(8,128)S(1)}) custom-call(s32[4]{0:T(128)S(1)} %pad_add_fusion.spot_ref, s32[2,6]{1,0:T(2,128)S(1)} %copy-done.27, s32[2]{0:T(128)S(1)} %copy-done.73, bf16[2,320,512]{2,1,0:T(8,128)(2,1)S(1)} %get-tuple-element.194.c01, ...), custom_call_target="tpu_custom_call" | custom-call | flops 99999997952 | bytes 100000 | tf_op jit(solution)/shard_map/pallas_call | solution.py:86
  99.8 11.2 %shard_map.361 = (bf16[512,1280]{1,0:T(8,128)(2,1)S(1)}, f32[512,1280]{1,0:T(8,128)S(1)}, f32[512,1280]{1,0:T(8,128)S(1)}, f32[80,512]{1,0:T(8,128)S(1)}, f32[32,1280]{1,0:T(8,128)S(1)}) custom-call(s32[4]{0:T(128)S(1)} %pad_add_fusion.spot_ref, s32[2,6]{1,0:T(2,128)S(1)} %copy-done.27, s32[2]{0:T(128)S(1)} %copy-done.73, ...), custom_call_target="tpu_custom_call" | custom-call | flops 99999997952 | bytes 100000 | tf_op jit(solution)/shard_map/pallas_call | solution.py:86
  111.0 3.1 %collective-permute-done.28.refs_2_ = bf16[320,1280]{1,0:T(8,128)(2,1)} collective-permute-done((bf16[320,1280]{1,0:T(8,128)(2,1)}, bf16[320,1280]{1,0:T(8,128)(2,1)}, u32[]{:S(2)}, u32[]{:S(2)}) %collective-permute-start.28) | collective-permute-done | bytes 819232 | tf_op jit(solution)/shard_map/ppermute | solution.py:24
  118.4 11.4 %shard_map.362 = (f32[512,1280]{1,0:T(8,128)S(1)}, f32[512,1280]{1,0:T(8,128)S(1)}, f32[80,512]{1,0:T(8,128)S(1)}, f32[32,1280]{1,0:T(8,128)S(1)}) custom-call(bf16[512,1280]{1,0:T(8,128)(2,1)S(1)} %get-tuple-element.208.z_ref, bf16[512,1280]{1,0:T(8,128)(2,1)S(1)} %get-tuple-element.212.gy_ref, ...), custom_call_target="tpu_custom_call", output_to_operand_aliasing={{0}: (2, {}), {1}: (3, {})} | custom-call | flops 99999997952 | bytes 100000 | tf_op jit(solution)/shard_map/pallas_call | solution.py:86
  129.9 7.1 %shard_map.363 = (f32[512,1280]{1,0:T(8,128)S(1)}, f32[512,1280]{1,0:T(8,128)S(1)}, f32[80,512]{1,0:T(8,128)S(1)}, f32[32,640]{1,0:T(8,128)S(1)}) custom-call(bf16[512,1280]{1,0:T(8,128)(2,1)S(1)} %get-tuple-element.208.z_ref, bf16[512,1280]{1,0:T(8,128)(2,1)S(1)} %get-tuple-element.212.gy_ref, ...), custom_call_target="tpu_custom_call", output_to_operand_aliasing={{0}: (2, {}), {1}: (3, {})} | custom-call | flops 99999997952 | bytes 100000 | tf_op jit(solution)/shard_map/pallas_call | solution.py:86
  139.9 7.3 %shard_map.364 = (f32[512,1280]{1,0:T(8,128)S(1)}, f32[512,1280]{1,0:T(8,128)S(1)}, f32[80,512]{1,0:T(8,128)S(1)}, f32[32,640]{1,0:T(8,128)S(1)}) custom-call(bf16[512,1280]{1,0:T(8,128)(2,1)S(1)} %get-tuple-element.208.z_ref, bf16[512,1280]{1,0:T(8,128)(2,1)S(1)} %get-tuple-element.212.gy_ref, ...), custom_call_target="tpu_custom_call", output_to_operand_aliasing={{0}: (2, {}), {1}: (3, {})} | custom-call | flops 99999997952 | bytes 100000 | tf_op jit(solution)/shard_map/pallas_call | solution.py:86
  147.3 19.7 %shard_map.365 = (bf16[2,256,1280]{2,1,0:T(8,128)(2,1)}, bf16[256,1280]{1,0:T(8,128)(2,1)S(1)}, f32[512,1280]{1,0:T(8,128)S(1)}, bf16[4,320,512]{2,1,0:T(8,128)(...) custom-call(s32[4]{0:T(128)S(1)} %copy-done.24, s32[2,6]{1,0:T(2,128)S(1)} %copy-done.27, ...), custom_call_target="tpu_custom_call" | custom-call | flops 99999997952 | bytes 100000 | tf_op jit(solution)/shard_map/pallas_call | solution.py:86
  172.4 7.2 %shard_map.367 = (bf16[320,512]{1,0:T(8,128)(2,1)S(1)}, f32[2,320,512]{2,1,0:T(8,128)S(1)}, bf16[2,320,512]{2,1,0:T(8,128)(2,1)S(1)}) custom-call(s32[4]{0:T(128)S(1)} %copy-done.24, s32[2]{0:T(128)S(1)} %copy-done.73, bf16[2,320,512]{2,1,0:T(8,128)(2,1)S(1)} %copy-done.81, bf16[2,2,320,512]{3,2,1,0:T(8,128)(2,1)S(1)} %copy-done.40, ...), custom_call_target="tpu_custom_call" | custom-call | flops 8000000000 | bytes 100000 | tf_op jit(solution)/shard_map/pallas_call | solution.py:86
  181.2 6.8 %shard_map.368 = (bf16[320,512]{1,0:T(8,128)(2,1)S(1)}, f32[2,320,512]{2,1,0:T(8,128)S(1)}, bf16[2,320,512]{2,1,0:T(8,128)(2,1)S(1)}) custom-call(s32[4]{0:T(128)S(1)} %copy-done.24, s32[2]{0:T(128)S(1)} %copy-done.73, bf16[2,320,512]{2,1,0:T(8,128)(2,1)S(1)} %copy-done.81, bf16[2,2,320,512]{3,2,1,0:T(8,128)(2,1)S(1)} %copy-done.40, ...), custom_call_target="tpu_custom_call" | custom-call | flops 8000000000 | bytes 100000 | tf_op jit(solution)/shard_map/pallas_call | solution.py:86
  190.4 6.8 %shard_map.369 = (bf16[320,512]{1,0:T(8,128)(2,1)S(1)}, f32[2,320,512]{2,1,0:T(8,128)S(1)}, bf16[2,320,512]{2,1,0:T(8,128)(2,1)S(1)}) custom-call(s32[4]{0:T(128)S(1)} %copy-done.24, s32[2]{0:T(128)S(1)} %copy-done.73, bf16[2,320,512]{2,1,0:T(8,128)(2,1)S(1)} %copy-done.79, bf16[2,2,320,512]{3,2,1,0:T(8,128)(2,1)S(1)} %copy-done.44, ...), custom_call_target="tpu_custom_call" | custom-call | flops 8000000000 | bytes 100000 | tf_op jit(solution)/shard_map/pallas_call | solution.py:86
  200.7 6.9 %shard_map.371 = (bf16[320,512]{1,0:T(8,128)(2,1)S(1)}, f32[2,320,512]{2,1,0:T(8,128)S(1)}, bf16[2,320,512]{2,1,0:T(8,128)(2,1)S(1)}) custom-call(s32[4]{0:T(128)S(1)} %copy-done.24, s32[2]{0:T(128)S(1)} %copy-done.73, bf16[2,320,512]{2,1,0:T(8,128)(2,1)S(1)} %copy-done.79, bf16[2,2,320,512]{3,2,1,0:T(8,128)(2,1)S(1)} %copy-done.44, ...), custom_call_target="tpu_custom_call" | custom-call | flops 8000000000 | bytes 100000 | tf_op jit(solution)/shard_map/pallas_call | solution.py:86
  220.2 3.4 %collective-permute-start.51 = (bf16[16,2944]{1,0:T(8,128)(2,1)S(1)}, bf16[16,2944]{1,0:T(8,128)(2,1)S(1)}, u32[]{:S(2)}, u32[]{:S(2)}) collective-permute-start(bf16[16,2944]{1,0:T(8,128)(2,1)S(1)} %get-tuple-element.293), channel_id=1, source_target_pairs={{0,16},{4,20},{8,24},{12,28},{16,0},{20,4},{24,8},{28,12},{1,17},{... | collective-permute-start | bytes 282632 | tf_op jit(solution)/shard_map/ppermute | solution.py:24
  224.3 5.6 %shard_map.376 = bf16[256,1280]{1,0:T(8,128)(2,1)S(1)} custom-call(s32[4]{0:T(128)S(1)} %copy-done.24, s32[2,6]{1,0:T(2,128)S(1)} %copy-done.27, bf16[2,3,320,512]{3,2,1,0:T(8,128)(2,1)S(1)} %get-tuple-element.274.g01_ref, bf16[2,3,320,512]{3,2,1,0:T(8,128)(2,1)S(1)} %get-tuple-element.294.g23_ref, f32[48,512]{1,0:T(8,128)S(1)} %get-tuple-element.283.gl_ref, ...), custom_call_target="tpu_custom_call" | custom-call | flops 5000000000 | bytes 100000 | tf_op jit(solution)/shard_map/pallas_call | solution.py:86
  231.7 4.8 %collective-permute-done.51 = bf16[16,2944]{1,0:T(8,128)(2,1)S(1)} collective-permute-done((bf16[16,2944]{1,0:T(8,128)(2,1)S(1)}, bf16[16,2944]{1,0:T(8,128)(2,1)S(1)}, u32[]{:S(2)}, u32[]{:S(2)}) %collective-permute-start.51) | collective-permute-done | bytes 94240 | tf_op jit(solution)/shard_map/ppermute | solution.py:24
  239.0 3.3 %collective-permute-start.57 = (bf16[2,16,2944]{2,1,0:T(8,128)(2,1)S(1)}, bf16[2,16,2944]{2,1,0:T(8,128)(2,1)S(1)}, u32[]{:S(2)}, u32[]{:S(2)}) collective-permute-start(bf16[2,16,2944]{2,1,0:T(8,128)(2,1)S(1)} %get-tuple-element.310.refs_2_), channel_id=1, source_target_pairs={{0,8},{4,12},{8,0},{12,4},{16,24},{20,28},{24,16},{28,20},{1,9},{5... | collective-permute-start | bytes 565256 | tf_op jit(solution)/shard_map/ppermute | solution.py:24
  249.6 6.6 %shard_map.377.array_ref = f32[2,256,1280]{2,1,0:T(8,128)} custom-call(s32[4]{0:T(128)S(1)} %copy-done.24, s32[2,6]{1,0:T(2,128)S(1)} %copy-done.27, bf16[2,3,320,512]{3,2,1,0:T(8,128)(2,1)S(1)} %get-tuple-element.274.g01_ref, bf16[2,3,320,512]{3,2,1,0:T(8,128)(2,1)S(1)} %get-tuple-element.294.g23_ref, f32[48,512]{1,0:T(8,128)S(1)} %get-tuple-element.283.gl_ref, ...), custom_call_target="tpu_custom_call" | custom-call | flops 5000000000 | bytes 100000 | tf_op jit(solution)/shard_map/pallas_call | solution.py:86
  (340 shorter events, 95.4 us)
Async XLA Ops:
  5.9 22.3 %collective-permute-start.4 = (bf16[4,80,1280]{2,1,0:T(8,128)(2,1)}, bf16[4,80,1280]{2,1,0:T(8,128)(2,1)}, u32[]{:S(2)}, u32[]{:S(2)}) collective-permute-start(bf16[4,80,1280]{2,1,0:T(8,128)(2,1)} %pad_maximum_fusion), channel_id=1, source_target_pairs={{0,2},{1,3},{2,0},{3,1},{4,6},{5,7},{6,4},{7,5},{8,10},{9,11},{10,... | collective-permute-start | bytes 2457608 | tf_op jit(solution)/shard_map/ppermute | solution.py:24
  17.4 26.8 %collective-permute-start.2 = (bf16[304,1280]{1,0:T(8,128)(2,1)S(1)}, bf16[304,1280]{1,0:T(8,128)(2,1)S(1)}, u32[]{:S(2)}, u32[]{:S(2)}) collective-permute-start(bf16[304,1280]{1,0:T(8,128)(2,1)S(1)} %get-tuple-element.178), channel_id=1, source_target_pairs={{0,2},{1,3},{2,0},{3,1},{4,6},{5,7},{6,4},{7,5},{8,10},{9,11},{10,... | collective-permute-start | bytes 2334728 | tf_op jit(solution)/shard_map/ppermute | solution.py:24
  20.3 23.9 %collective-permute-start.8 = (bf16[1280,1280]{1,0:T(8,128)(2,1)S(1)}, bf16[1280,1280]{1,0:T(8,128)(2,1)S(1)}, u32[]{:S(2)}, u32[]{:S(2)}) collective-permute-start(bf16[1280,1280]{1,0:T(8,128)(2,1)S(1)} %copy-done.30), channel_id=1, source_target_pairs={{0,1},{1,0},{2,3},{3,2},{4,5},{5,4},{6,7},{7,6},{8,9},{9,8},{10,11... | collective-permute-start | bytes 9830408 | tf_op jit(solution)/shard_map/ppermute | solution.py:24
  28.2 23.7 %collective-permute-start.10 = (bf16[4,80,1280]{2,1,0:T(8,128)(2,1)}, bf16[4,80,1280]{2,1,0:T(8,128)(2,1)S(1)}, u32[]{:S(2)}, u32[]{:S(2)}) collective-permute-start(bf16[4,80,1280]{2,1,0:T(8,128)(2,1)} %collective-permute-done.4.refs_0_), channel_id=1, source_target_pairs={{0,4},{4,0},{8,12},{12,8},{16,20},{20,16},{24,28},{28,24},{1,5},{5... | collective-permute-start | bytes 2457608 | tf_op jit(solution)/shard_map/ppermute | solution.py:24
  30.2 20.8 %collective-permute-start.15 = (bf16[4,80,1280]{2,1,0:T(8,128)(2,1)}, bf16[4,80,1280]{2,1,0:T(8,128)(2,1)S(1)}, u32[]{:S(2)}, u32[]{:S(2)}) collective-permute-start(bf16[4,80,1280]{2,1,0:T(8,128)(2,1)} %collective-permute-done.4.refs_0_), channel_id=1, source_target_pairs={{0,8},{4,12},{8,0},{12,4},{16,24},{20,28},{24,16},{28,20},{1,9},{5... | collective-permute-start | bytes 2457608 | tf_op jit(solution)/shard_map/ppermute | solution.py:24
  49.2 21.0 %collective-permute-start.13 = (bf16[320,1280]{1,0:T(8,128)(2,1)}, bf16[320,1280]{1,0:T(8,128)(2,1)}, u32[]{:S(2)}, u32[]{:S(2)}) collective-permute-start(bf16[320,1280]{1,0:T(8,128)(2,1)} %get-tuple-element.195), channel_id=1, source_target_pairs={{0,2},{1,3},{2,0},{3,1},{4,6},{5,7},{6,4},{7,5},{8,10},{9,11},{10,... | collective-permute-start | bytes 2457608 | tf_op jit(solution)/shard_map/ppermute | solution.py:24
  76.6 22.7 %collective-permute-start.24 = (bf16[320,1280]{1,0:T(8,128)(2,1)}, bf16[320,1280]{1,0:T(8,128)(2,1)}, u32[]{:S(2)}, u32[]{:S(2)}) collective-permute-start(bf16[320,1280]{1,0:T(8,128)(2,1)} %collective-permute-done.13.refs_0_), channel_id=1, source_target_pairs={{0,4},{4,0},{8,12},{12,8},{16,20},{20,16},{24,28},{28,24},{1,5},{5... | collective-permute-start | bytes 2457608 | tf_op jit(solution)/shard_map/ppermute | solution.py:24
  78.2 20.7 %collective-permute-start.26 = (bf16[320,1280]{1,0:T(8,128)(2,1)}, bf16[320,1280]{1,0:T(8,128)(2,1)}, u32[]{:S(2)}, u32[]{:S(2)}) collective-permute-start(bf16[320,1280]{1,0:T(8,128)(2,1)} %collective-permute-done.13.refs_0_), channel_id=1, source_target_pairs={{0,8},{4,12},{8,0},{12,4},{16,24},{20,28},{24,16},{28,20},{1,9},{5... | collective-permute-start | bytes 2457608 | tf_op jit(solution)/shard_map/ppermute | solution.py:24
  79.7 19.7 %collective-permute-start.22 = (bf16[256,1280]{1,0:T(8,128)(2,1)}, bf16[256,1280]{1,0:T(8,128)(2,1)}, u32[]{:S(2)}, u32[]{:S(2)}) collective-permute-start(bf16[256,1280]{1,0:T(8,128)(2,1)} %get-tuple-element.211), channel_id=1, source_target_pairs={{0,2},{1,3},{2,0},{3,1},{4,6},{5,7},{6,4},{7,5},{8,10},{9,11},{10,... | collective-permute-start | bytes 1966088 | tf_op jit(solution)/shard_map/ppermute | solution.py:24
  81.2 32.9 %collective-permute-start.28 = (bf16[320,1280]{1,0:T(8,128)(2,1)}, bf16[320,1280]{1,0:T(8,128)(2,1)}, u32[]{:S(2)}, u32[]{:S(2)}) collective-permute-start(bf16[320,1280]{1,0:T(8,128)(2,1)} %get-tuple-element.225), channel_id=1, source_target_pairs={{0,2},{1,3},{2,0},{3,1},{4,6},{5,7},{6,4},{7,5},{8,10},{9,11},{10,... | collective-permute-start | bytes 2457608 | tf_op jit(solution)/shard_map/ppermute | solution.py:24
  98.8 17.1 %collective-permute-start.27 = (bf16[320,1280]{1,0:T(8,128)(2,1)}, bf16[320,1280]{1,0:T(8,128)(2,1)S(1)}, u32[]{:S(2)}, u32[]{:S(2)}) collective-permute-start(bf16[320,1280]{1,0:T(8,128)(2,1)} %collective-permute-done.26.refs_4_), channel_id=1, source_target_pairs={{0,1},{1,0},{2,3},{3,2},{4,5},{5,4},{6,7},{7,6},{8,9},{9,8},{10,11... | collective-permute-start | bytes 2457608 | tf_op jit(solution)/shard_map/ppermute | solution.py:24
  98.8 31.0 %collective-permute-start.30 = (bf16[320,1280]{1,0:T(8,128)(2,1)}, bf16[320,1280]{1,0:T(8,128)(2,1)}, u32[]{:S(2)}, u32[]{:S(2)}) collective-permute-start(bf16[320,1280]{1,0:T(8,128)(2,1)} %collective-permute-done.26.refs_4_), channel_id=1, source_target_pairs={{0,4},{4,0},{8,12},{12,8},{16,20},{20,16},{24,28},{28,24},{1,5},{5... | collective-permute-start | bytes 2457608 | tf_op jit(solution)/shard_map/ppermute | solution.py:24
  99.3 14.9 %collective-permute-start.23 = (bf16[320,1280]{1,0:T(8,128)(2,1)}, bf16[320,1280]{1,0:T(8,128)(2,1)S(1)}, u32[]{:S(2)}, u32[]{:S(2)}) collective-permute-start(bf16[320,1280]{1,0:T(8,128)(2,1)} %collective-permute-done.13.refs_0_), channel_id=1, source_target_pairs={{0,1},{1,0},{2,3},{3,2},{4,5},{5,4},{6,7},{7,6},{8,9},{9,8},{10,11... | collective-permute-start | bytes 2457608 | tf_op jit(solution)/shard_map/ppermute | solution.py:24
  99.5 15.2 %collective-permute-start.25 = (bf16[320,1280]{1,0:T(8,128)(2,1)}, bf16[320,1280]{1,0:T(8,128)(2,1)S(1)}, u32[]{:S(2)}, u32[]{:S(2)}) collective-permute-start(bf16[320,1280]{1,0:T(8,128)(2,1)} %collective-permute-done.24.refs_0_), channel_id=1, source_target_pairs={{0,1},{1,0},{2,3},{3,2},{4,5},{5,4},{6,7},{7,6},{8,9},{9,8},{10,11... | collective-permute-start | bytes 2457608 | tf_op jit(solution)/shard_map/ppermute | solution.py:24
  114.2 15.7 %collective-permute-start.29 = (bf16[320,1280]{1,0:T(8,128)(2,1)}, bf16[320,1280]{1,0:T(8,128)(2,1)S(1)}, u32[]{:S(2)}, u32[]{:S(2)}) collective-permute-start(bf16[320,1280]{1,0:T(8,128)(2,1)} %collective-permute-done.28.refs_2_), channel_id=1, source_target_pairs={{0,1},{1,0},{2,3},{3,2},{4,5},{5,4},{6,7},{7,6},{8,9},{9,8},{10,11... | collective-permute-start | bytes 2457608 | tf_op jit(solution)/shard_map/ppermute | solution.py:24
  114.2 23.4 %collective-permute-start.34 = (bf16[320,1280]{1,0:T(8,128)(2,1)}, bf16[320,1280]{1,0:T(8,128)(2,1)}, u32[]{:S(2)}, u32[]{:S(2)}) collective-permute-start(bf16[320,1280]{1,0:T(8,128)(2,1)} %collective-permute-done.28.refs_2_), channel_id=1, source_target_pairs={{0,4},{4,0},{8,12},{12,8},{16,20},{20,16},{24,28},{28,24},{1,5},{5... | collective-permute-start | bytes 2457608 | tf_op jit(solution)/shard_map/ppermute | solution.py:24
  115.6 22.2 %collective-permute-start.36 = (bf16[320,1280]{1,0:T(8,128)(2,1)}, bf16[320,1280]{1,0:T(8,128)(2,1)}, u32[]{:S(2)}, u32[]{:S(2)}) collective-permute-start(bf16[320,1280]{1,0:T(8,128)(2,1)} %collective-permute-done.28.refs_2_), channel_id=1, source_target_pairs={{0,8},{4,12},{8,0},{12,4},{16,24},{20,28},{24,16},{28,20},{1,9},{5... | collective-permute-start | bytes 2457608 | tf_op jit(solution)/shard_map/ppermute | solution.py:24
  116.8 20.4 %collective-permute-start.32 = (bf16[320,1280]{1,0:T(8,128)(2,1)}, bf16[320,1280]{1,0:T(8,128)(2,1)}, u32[]{:S(2)}, u32[]{:S(2)}) collective-permute-start(bf16[320,1280]{1,0:T(8,128)(2,1)} %get-tuple-element.233), channel_id=1, source_target_pairs={{0,2},{1,3},{2,0},{3,1},{4,6},{5,7},{6,4},{7,5},{8,10},{9,11},{10,... | collective-permute-start | bytes 2457608 | tf_op jit(solution)/shard_map/ppermute | solution.py:24
  167.5 20.6 %collective-permute-start.38 = (bf16[256,1280]{1,0:T(8,128)(2,1)S(1)}, bf16[256,1280]{1,0:T(8,128)(2,1)S(1)}, u32[]{:S(2)}, u32[]{:S(2)}) collective-permute-start(bf16[256,1280]{1,0:T(8,128)(2,1)S(1)} %get-tuple-element.244), channel_id=1, source_target_pairs={{0,2},{1,3},{2,0},{3,1},{4,6},{5,7},{6,4},{7,5},{8,10},{9,11},{10,... | collective-permute-start | bytes 1966088 | tf_op jit(solution)/shard_map/ppermute | solution.py:24
  169.7 27.6 %collective-permute-start.41 = (bf16[16,4992]{1,0:T(8,128)(2,1)S(1)}, bf16[16,4992]{1,0:T(8,128)(2,1)S(1)}, u32[]{:S(2)}, u32[]{:S(2)}) collective-permute-start(bf16[16,4992]{1,0:T(8,128)(2,1)S(1)} %get-tuple-element.247), channel_id=1, source_target_pairs={{0,16},{4,20},{8,24},{12,28},{16,0},{20,4},{24,8},{28,12},{1,17},{... | collective-permute-start | bytes 479240 | tf_op jit(solution)/shard_map/ppermute | solution.py:24
  218.4 20.5 %collective-permute-start.54 = (bf16[4,16,4992]{2,1,0:T(8,128)(2,1)S(1)}, bf16[4,16,4992]{2,1,0:T(8,128)(2,1)S(1)}, u32[]{:S(2)}, u32[]{:S(2)}) collective-permute-start(bf16[4,16,4992]{2,1,0:T(8,128)(2,1)S(1)} %get-tuple-element.305.refs_0_), channel_id=1, source_target_pairs={{0,8},{4,12},{8,0},{12,4},{16,24},{20,28},{24,16},{28,20},{1,9},{5... | collective-permute-start | bytes 1916936 | tf_op jit(solution)/shard_map/ppermute | solution.py:24
  219.8 19.1 %collective-permute-start.55 = (bf16[4,16,4992]{2,1,0:T(8,128)(2,1)S(1)}, bf16[4,16,4992]{2,1,0:T(8,128)(2,1)S(1)}, u32[]{:S(2)}, u32[]{:S(2)}) collective-permute-start(bf16[4,16,4992]{2,1,0:T(8,128)(2,1)S(1)} %get-tuple-element.307.refs_2_), channel_id=1, source_target_pairs={{0,4},{4,0},{8,12},{12,8},{16,20},{20,16},{24,28},{28,24},{1,5},{5... | collective-permute-start | bytes 1916936 | tf_op jit(solution)/shard_map/ppermute | solution.py:24
  220.2 16.3 %collective-permute-start.51 = (bf16[16,2944]{1,0:T(8,128)(2,1)S(1)}, bf16[16,2944]{1,0:T(8,128)(2,1)S(1)}, u32[]{:S(2)}, u32[]{:S(2)}) collective-permute-start(bf16[16,2944]{1,0:T(8,128)(2,1)S(1)} %get-tuple-element.293), channel_id=1, source_target_pairs={{0,16},{4,20},{8,24},{12,28},{16,0},{20,4},{24,8},{28,12},{1,17},{... | collective-permute-start | bytes 282632 | tf_op jit(solution)/shard_map/ppermute | solution.py:24
  229.9 27.7 %collective-permute-start.53 = (bf16[256,1280]{1,0:T(8,128)(2,1)S(1)}, bf16[256,1280]{1,0:T(8,128)(2,1)S(1)}, u32[]{:S(2)}, u32[]{:S(2)}) collective-permute-start(bf16[256,1280]{1,0:T(8,128)(2,1)S(1)} %shard_map.376), channel_id=1, source_target_pairs={{0,2},{1,3},{2,0},{3,1},{4,6},{5,7},{6,4},{7,5},{8,10},{9,11},{10,... | collective-permute-start | bytes 1966088 | tf_op jit(solution)/shard_map/ppermute | solution.py:24
  (130 other events, 1257.3 us)

commit v5 on v4

--- a/solution.py
+++ b/solution.py
@@ -984,7 +984,8 @@
         half = features // 2
 
         head_rows = heads[0].shape[0] // 4
-        part_heads = jnp.stack([lax.dynamic_slice_in_dim(w, quad * head_rows, head_rows, 0) for w in heads])
+        together = jnp.stack([w.reshape(4, head_rows, features) for w in heads], axis=1)
+        part_heads = lax.dynamic_index_in_dim(together, quad, 0, keepdims=False)
         far0 = across(part_heads)
         send, pack = stage(after(spot, part_heads), pick, inputs, small)
         near_heads = [beside(w) for w in after(heads, part_heads)]
@@ -1003,9 +1004,9 @@
         )
         kv01_side = beside(kv01)
         q01 = queries_near(after(z, kv01), low, pack, side, [heads[0], near_heads[0]])
-        far3, far4 = along(after(far2[:2], kv01), 1), along(after(far1[2:], kv01), 2)
         side0 = beside(after(far0, kv01))
         side1 = beside(after(far1, kv01, side0))
+        far3, far4 = along(after(far2[:2], q01), 1), along(after(far1[2:], q01), 2)
         c01, total01 = attend(spot, lengths, q01, kv01, after(kv01_side, side1))
         side2 = beside(after(far2, c01, side1))
         far_side = beside(after(received[rows:], c01))

time: 268 us -> 266 us (level)
  local copies, waits for them, and re-layouts: 12.4 us -> 7.72 us
    another operation x3 -> x0, local copies, waits for them, and re-layouts: 3.11 us -> none  [body(): jnp.stack([lax.dynamic_slice_in_dim(w, quad * head_rows, head_rows, 0) fo...]
    unnamed x188 -> x186, local copies, waits for them, and re-layouts: 7.62 us -> 7.62 us
  transfers between devices with their start and end apart: 62 -> 62, of which waited for: 22 -> 23; matrix products, arithmetic and copies ran while one was open for 1% -> 0% of each run, Pallas kernels for 45% -> 46%
where the time goes in v5:
time: 266 us; the launch traced here: 263 us
  Pallas kernels  151 us (57%)
  starting transfers between devices  54.4 us (20%)
  waiting for transfers between devices  45.8 us (17%)
  local copies, waits for them, and re-layouts  7.72 us (3%)
    pallas_call x34, Pallas kernels, call(): pl.pallas_call(body, grid_spec=pltpu.PrefetchScalarGridSpec(num_scalar_pr...  151 us
    ppermute x62, starting transfers between devices, swap(): return lax.ppermute(array, axis, [(i, i ^ bits) for i in range(size)])  54.4 us
    ppermute x62, waiting for transfers between devices, swap(): return lax.ppermute(array, axis, [(i, i ^ bits) for i in range(size)])  45.8 us
    unnamed x186, local copies, waits for them, and re-layouts  7.62 us
  transfers between devices with their start and end apart: 62, of which 23 were waited for; matrix products, arithmetic and copies ran while one was open for 0% of the time, Pallas kernels for 46%

profile of v5, /device:TPU:0, one launch (start us, length us, event | category | flops | bytes accessed | tf_op | source)
XLA Modules:
  0.0 263.3 jit_solution(17324330346832596019)
XLA Ops:
  18.6 3.1 %shard_map.354 = (bf16[320,1280]{1,0:T(8,128)(2,1)}, bf16[320,1280]{1,0:T(8,128)(2,1)}, bf16[320,1280]{1,0:T(8,128)(2,1)}, bf16[256,1280]{1,0:T(8,128)(2,1)}) custom-call(s32[4]{0:T(128)S(1)} %pad_add_fusion.spot_ref, bf16[1280,1280]{1,0:T(8,128)(2,1)S(1)} %copy-done.28, bf16[1280,1280]{1,0:T(8,128)(2,1)S(1)} %copy-done.30, ...), custom_call_target="tpu_custom_call" | custom-call | flops 99999997952 | bytes 100000 | tf_op jit(solution)/shard_map/pallas_call | solution.py:86
  21.8 4.6 %collective-permute-done.4.refs_0_ = bf16[4,80,1280]{2,1,0:T(8,128)(2,1)} collective-permute-done((bf16[4,80,1280]{2,1,0:T(8,128)(2,1)}, bf16[4,80,1280]{2,1,0:T(8,128)(2,1)}, u32[]{:S(2)}, u32[]{:S(2)}) %collective-permute-start.4) | collective-permute-done | bytes 819232 | tf_op jit(solution)/shard_map/ppermute | solution.py:24
  30.1 12.3 %collective-permute-done.2.xb.received_ref.refs_7_ = bf16[304,1280]{1,0:T(8,128)(2,1)S(1)} collective-permute-done((bf16[304,1280]{1,0:T(8,128)(2,1)S(1)}, bf16[304,1280]{1,0:T(8,128)(2,1)S(1)}, u32[]{:S(2)}, u32[]{:S(2)}) %collective-permute-start.2) | collective-permute-done | bytes 778272 | tf_op jit(solution)/shard_map/ppermute | solution.py:24
  42.5 4.9 %shard_map.355 = (bf16[512,1280]{1,0:T(8,128)(2,1)S(1)}, f32[48,512]{1,0:T(8,128)S(1)}, bf16[2,2,320,512]{3,2,1,0:T(8,128)(2,1)S(1)}) custom-call(s32[4]{0:T(128)S(1)} %pad_add_fusion.spot_ref, s32[2,6]{1,0:T(2,128)S(1)} %copy-done.27, bf16[2,256,1280]{2,1,0:T(8,128)(2,1)S(1)} %copy-done.5, ...), custom_call_target="tpu_custom_call" | custom-call | flops 99999997952 | bytes 100000 | tf_op jit(solution)/shard_map/pallas_call | solution.py:86
  54.9 8.1 %shard_map.357 = (bf16[2,320,512]{2,1,0:T(8,128)(2,1)S(1)}, f32[8,1,512]{2,1,0:T(1,128)S(1)}) custom-call(s32[4]{0:T(128)S(1)} %pad_add_fusion.spot_ref, s32[2]{0:T(128)S(1)} %copy-done.73, bf16[2,320,512]{2,1,0:T(8,128)(2,1)S(1)} %shard_map.356.q_ref, bf16[2,2,320,512]{3,2,1,0:T(8,128)(2,1)S(1)} %get-tuple-element.188.k1.v1, ...), custom_call_target="tpu_custom_call" | custom-call | flops 99999997952 | bytes 100000 | tf_op jit(solution)/shard_map/pallas_call | solution.py:86
  65.3 3.1 %collective-permute-done.13.refs_0_ = bf16[320,1280]{1,0:T(8,128)(2,1)} collective-permute-done((bf16[320,1280]{1,0:T(8,128)(2,1)}, bf16[320,1280]{1,0:T(8,128)(2,1)}, u32[]{:S(2)}, u32[]{:S(2)}) %collective-permute-start.13) | collective-permute-done | bytes 819232 | tf_op jit(solution)/shard_map/ppermute | solution.py:24
  68.5 5.7 %shard_map.358 = (bf16[2,4,320,1280]{3,2,1,0:T(8,128)(2,1)S(1)}, bf16[2,2,320,512]{3,2,1,0:T(8,128)(2,1)S(1)}, bf16[2,320,512]{2,1,0:T(8,128)(2,1)S(1)}) custom-call(s32[1]{0:T(128)} %bitcast.2.spot_ref, bf16[512,1280]{1,0:T(8,128)(2,1)S(1)} %get-tuple-element.196.z_ref, f32[48,512]{1,0:T(8,128)S(1)} %get-tuple-element.273.low_ref.refs_6_, ...), custom_call_target="tpu_custom_call" | custom-call | flops 99999997952 | bytes 100000 | tf_op jit(solution)/shard_map/pallas_call | solution.py:86
  79.9 8.4 %shard_map.359 = (bf16[2,320,512]{2,1,0:T(8,128)(2,1)S(1)}, f32[8,1,512]{2,1,0:T(1,128)S(1)}) custom-call(s32[4]{0:T(128)S(1)} %pad_add_fusion.spot_ref, s32[2]{0:T(128)S(1)} %copy-done.73, bf16[2,320,512]{2,1,0:T(8,128)(2,1)S(1)} %get-tuple-element.266.q_ref, bf16[2,2,320,512]{3,2,1,0:T(8,128)(2,1)S(1)} %get-tuple-element.204.k1.v1, ...), custom_call_target="tpu_custom_call" | custom-call | flops 99999997952 | bytes 100000 | tf_op jit(solution)/shard_map/pallas_call | solution.py:86
  88.5 6.4 %shard_map.360 = (f32[512,1280]{1,0:T(8,128)S(1)}, bf16[512,1280]{1,0:T(8,128)(2,1)S(1)}, f32[32,512]{1,0:T(8,128)S(1)}) custom-call(s32[4]{0:T(128)S(1)} %pad_add_fusion.spot_ref, s32[2,6]{1,0:T(2,128)S(1)} %copy-done.27, s32[2]{0:T(128)S(1)} %copy-done.73, bf16[2,320,512]{2,1,0:T(8,128)(2,1)S(1)} %get-tuple-element.194.c01, ...), custom_call_target="tpu_custom_call" | custom-call | flops 99999997952 | bytes 100000 | tf_op jit(solution)/shard_map/pallas_call | solution.py:86
  97.8 11.2 %shard_map.361 = (bf16[512,1280]{1,0:T(8,128)(2,1)S(1)}, f32[512,1280]{1,0:T(8,128)S(1)}, f32[512,1280]{1,0:T(8,128)S(1)}, f32[80,512]{1,0:T(8,128)S(1)}, f32[32,1280]{1,0:T(8,128)S(1)}) custom-call(s32[4]{0:T(128)S(1)} %pad_add_fusion.spot_ref, s32[2,6]{1,0:T(2,128)S(1)} %copy-done.27, s32[2]{0:T(128)S(1)} %copy-done.73, ...), custom_call_target="tpu_custom_call" | custom-call | flops 99999997952 | bytes 100000 | tf_op jit(solution)/shard_map/pallas_call | solution.py:86
  109.0 3.2 %collective-permute-done.28.refs_2_ = bf16[320,1280]{1,0:T(8,128)(2,1)} collective-permute-done((bf16[320,1280]{1,0:T(8,128)(2,1)}, bf16[320,1280]{1,0:T(8,128)(2,1)}, u32[]{:S(2)}, u32[]{:S(2)}) %collective-permute-start.28) | collective-permute-done | bytes 819232 | tf_op jit(solution)/shard_map/ppermute | solution.py:24
  116.5 11.4 %shard_map.362 = (f32[512,1280]{1,0:T(8,128)S(1)}, f32[512,1280]{1,0:T(8,128)S(1)}, f32[80,512]{1,0:T(8,128)S(1)}, f32[32,1280]{1,0:T(8,128)S(1)}) custom-call(bf16[512,1280]{1,0:T(8,128)(2,1)S(1)} %get-tuple-element.208.z_ref, bf16[512,1280]{1,0:T(8,128)(2,1)S(1)} %get-tuple-element.212.gy_ref, ...), custom_call_target="tpu_custom_call", output_to_operand_aliasing={{0}: (2, {}), {1}: (3, {})} | custom-call | flops 99999997952 | bytes 100000 | tf_op jit(solution)/shard_map/pallas_call | solution.py:86
  128.0 7.1 %shard_map.363 = (f32[512,1280]{1,0:T(8,128)S(1)}, f32[512,1280]{1,0:T(8,128)S(1)}, f32[80,512]{1,0:T(8,128)S(1)}, f32[32,640]{1,0:T(8,128)S(1)}) custom-call(bf16[512,1280]{1,0:T(8,128)(2,1)S(1)} %get-tuple-element.208.z_ref, bf16[512,1280]{1,0:T(8,128)(2,1)S(1)} %get-tuple-element.212.gy_ref, ...), custom_call_target="tpu_custom_call", output_to_operand_aliasing={{0}: (2, {}), {1}: (3, {})} | custom-call | flops 99999997952 | bytes 100000 | tf_op jit(solution)/shard_map/pallas_call | solution.py:86
  137.9 7.3 %shard_map.364 = (f32[512,1280]{1,0:T(8,128)S(1)}, f32[512,1280]{1,0:T(8,128)S(1)}, f32[80,512]{1,0:T(8,128)S(1)}, f32[32,640]{1,0:T(8,128)S(1)}) custom-call(bf16[512,1280]{1,0:T(8,128)(2,1)S(1)} %get-tuple-element.208.z_ref, bf16[512,1280]{1,0:T(8,128)(2,1)S(1)} %get-tuple-element.212.gy_ref, ...), custom_call_target="tpu_custom_call", output_to_operand_aliasing={{0}: (2, {}), {1}: (3, {})} | custom-call | flops 99999997952 | bytes 100000 | tf_op jit(solution)/shard_map/pallas_call | solution.py:86
  145.4 19.7 %shard_map.365 = (bf16[2,256,1280]{2,1,0:T(8,128)(2,1)}, bf16[256,1280]{1,0:T(8,128)(2,1)S(1)}, f32[512,1280]{1,0:T(8,128)S(1)}, bf16[4,320,512]{2,1,0:T(8,128)(...) custom-call(s32[4]{0:T(128)S(1)} %copy-done.24, s32[2,6]{1,0:T(2,128)S(1)} %copy-done.27, ...), custom_call_target="tpu_custom_call" | custom-call | flops 99999997952 | bytes 100000 | tf_op jit(solution)/shard_map/pallas_call | solution.py:86
  170.5 7.2 %shard_map.367 = (bf16[320,512]{1,0:T(8,128)(2,1)S(1)}, f32[2,320,512]{2,1,0:T(8,128)S(1)}, bf16[2,320,512]{2,1,0:T(8,128)(2,1)S(1)}) custom-call(s32[4]{0:T(128)S(1)} %copy-done.24, s32[2]{0:T(128)S(1)} %copy-done.73, bf16[2,320,512]{2,1,0:T(8,128)(2,1)S(1)} %copy-done.79, bf16[2,2,320,512]{3,2,1,0:T(8,128)(2,1)S(1)} %copy-done.40, ...), custom_call_target="tpu_custom_call" | custom-call | flops 8000000000 | bytes 100000 | tf_op jit(solution)/shard_map/pallas_call | solution.py:86
  179.3 6.8 %shard_map.368 = (bf16[320,512]{1,0:T(8,128)(2,1)S(1)}, f32[2,320,512]{2,1,0:T(8,128)S(1)}, bf16[2,320,512]{2,1,0:T(8,128)(2,1)S(1)}) custom-call(s32[4]{0:T(128)S(1)} %copy-done.24, s32[2]{0:T(128)S(1)} %copy-done.73, bf16[2,320,512]{2,1,0:T(8,128)(2,1)S(1)} %copy-done.79, bf16[2,2,320,512]{3,2,1,0:T(8,128)(2,1)S(1)} %copy-done.40, ...), custom_call_target="tpu_custom_call" | custom-call | flops 8000000000 | bytes 100000 | tf_op jit(solution)/shard_map/pallas_call | solution.py:86
  188.5 6.8 %shard_map.369 = (bf16[320,512]{1,0:T(8,128)(2,1)S(1)}, f32[2,320,512]{2,1,0:T(8,128)S(1)}, bf16[2,320,512]{2,1,0:T(8,128)(2,1)S(1)}) custom-call(s32[4]{0:T(128)S(1)} %copy-done.24, s32[2]{0:T(128)S(1)} %copy-done.73, bf16[2,320,512]{2,1,0:T(8,128)(2,1)S(1)} %copy-done.81, bf16[2,2,320,512]{3,2,1,0:T(8,128)(2,1)S(1)} %copy-done.44, ...), custom_call_target="tpu_custom_call" | custom-call | flops 8000000000 | bytes 100000 | tf_op jit(solution)/shard_map/pallas_call | solution.py:86
  198.7 6.9 %shard_map.371 = (bf16[320,512]{1,0:T(8,128)(2,1)S(1)}, f32[2,320,512]{2,1,0:T(8,128)S(1)}, bf16[2,320,512]{2,1,0:T(8,128)(2,1)S(1)}) custom-call(s32[4]{0:T(128)S(1)} %copy-done.24, s32[2]{0:T(128)S(1)} %copy-done.73, bf16[2,320,512]{2,1,0:T(8,128)(2,1)S(1)} %copy-done.81, bf16[2,2,320,512]{3,2,1,0:T(8,128)(2,1)S(1)} %copy-done.44, ...), custom_call_target="tpu_custom_call" | custom-call | flops 8000000000 | bytes 100000 | tf_op jit(solution)/shard_map/pallas_call | solution.py:86
  218.3 3.4 %collective-permute-start.51 = (bf16[16,2944]{1,0:T(8,128)(2,1)S(1)}, bf16[16,2944]{1,0:T(8,128)(2,1)S(1)}, u32[]{:S(2)}, u32[]{:S(2)}) collective-permute-start(bf16[16,2944]{1,0:T(8,128)(2,1)S(1)} %get-tuple-element.293), channel_id=1, source_target_pairs={{0,16},{4,20},{8,24},{12,28},{16,0},{20,4},{24,8},{28,12},{1,17},{... | collective-permute-start | bytes 282632 | tf_op jit(solution)/shard_map/ppermute | solution.py:24
  222.4 5.6 %shard_map.376 = bf16[256,1280]{1,0:T(8,128)(2,1)S(1)} custom-call(s32[4]{0:T(128)S(1)} %copy-done.24, s32[2,6]{1,0:T(2,128)S(1)} %copy-done.27, bf16[2,3,320,512]{3,2,1,0:T(8,128)(2,1)S(1)} %get-tuple-element.274.g01_ref, bf16[2,3,320,512]{3,2,1,0:T(8,128)(2,1)S(1)} %get-tuple-element.294.g23_ref, f32[48,512]{1,0:T(8,128)S(1)} %get-tuple-element.283.gl_ref, ...), custom_call_target="tpu_custom_call" | custom-call | flops 5000000000 | bytes 100000 | tf_op jit(solution)/shard_map/pallas_call | solution.py:86
  229.7 4.8 %collective-permute-done.51 = bf16[16,2944]{1,0:T(8,128)(2,1)S(1)} collective-permute-done((bf16[16,2944]{1,0:T(8,128)(2,1)S(1)}, bf16[16,2944]{1,0:T(8,128)(2,1)S(1)}, u32[]{:S(2)}, u32[]{:S(2)}) %collective-permute-start.51) | collective-permute-done | bytes 94240 | tf_op jit(solution)/shard_map/ppermute | solution.py:24
  236.9 3.4 %collective-permute-start.57 = (bf16[2,16,2944]{2,1,0:T(8,128)(2,1)S(1)}, bf16[2,16,2944]{2,1,0:T(8,128)(2,1)S(1)}, u32[]{:S(2)}, u32[]{:S(2)}) collective-permute-start(bf16[2,16,2944]{2,1,0:T(8,128)(2,1)S(1)} %get-tuple-element.310.refs_2_), channel_id=1, source_target_pairs={{0,8},{4,12},{8,0},{12,4},{16,24},{20,28},{24,16},{28,20},{1,9},{5... | collective-permute-start | bytes 565256 | tf_op jit(solution)/shard_map/ppermute | solution.py:24
  247.5 6.6 %shard_map.377.array_ref = f32[2,256,1280]{2,1,0:T(8,128)} custom-call(s32[4]{0:T(128)S(1)} %copy-done.24, s32[2,6]{1,0:T(2,128)S(1)} %copy-done.27, bf16[2,3,320,512]{3,2,1,0:T(8,128)(2,1)S(1)} %get-tuple-element.274.g01_ref, bf16[2,3,320,512]{3,2,1,0:T(8,128)(2,1)S(1)} %get-tuple-element.294.g23_ref, f32[48,512]{1,0:T(8,128)S(1)} %get-tuple-element.283.gl_ref, ...), custom_call_target="tpu_custom_call" | custom-call | flops 5000000000 | bytes 100000 | tf_op jit(solution)/shard_map/pallas_call | solution.py:86
  (335 shorter events, 93.3 us)
Async XLA Ops:
  4.1 22.3 %collective-permute-start.4 = (bf16[4,80,1280]{2,1,0:T(8,128)(2,1)}, bf16[4,80,1280]{2,1,0:T(8,128)(2,1)}, u32[]{:S(2)}, u32[]{:S(2)}) collective-permute-start(bf16[4,80,1280]{2,1,0:T(8,128)(2,1)} %fusion.3), channel_id=1, source_target_pairs={{0,2},{1,3},{2,0},{3,1},{4,6},{5,7},{6,4},{7,5},{8,10},{9,11},{10,... | collective-permute-start | bytes 2457608 | tf_op jit(solution)/shard_map/ppermute | solution.py:24
  15.6 26.8 %collective-permute-start.2 = (bf16[304,1280]{1,0:T(8,128)(2,1)S(1)}, bf16[304,1280]{1,0:T(8,128)(2,1)S(1)}, u32[]{:S(2)}, u32[]{:S(2)}) collective-permute-start(bf16[304,1280]{1,0:T(8,128)(2,1)S(1)} %get-tuple-element.178), channel_id=1, source_target_pairs={{0,2},{1,3},{2,0},{3,1},{4,6},{5,7},{6,4},{7,5},{8,10},{9,11},{10,... | collective-permute-start | bytes 2334728 | tf_op jit(solution)/shard_map/ppermute | solution.py:24
  18.5 23.9 %collective-permute-start.8 = (bf16[1280,1280]{1,0:T(8,128)(2,1)S(1)}, bf16[1280,1280]{1,0:T(8,128)(2,1)S(1)}, u32[]{:S(2)}, u32[]{:S(2)}) collective-permute-start(bf16[1280,1280]{1,0:T(8,128)(2,1)S(1)} %copy-done.30), channel_id=1, source_target_pairs={{0,1},{1,0},{2,3},{3,2},{4,5},{5,4},{6,7},{7,6},{8,9},{9,8},{10,11... | collective-permute-start | bytes 9830408 | tf_op jit(solution)/shard_map/ppermute | solution.py:24
  26.4 22.9 %collective-permute-start.10 = (bf16[4,80,1280]{2,1,0:T(8,128)(2,1)}, bf16[4,80,1280]{2,1,0:T(8,128)(2,1)S(1)}, u32[]{:S(2)}, u32[]{:S(2)}) collective-permute-start(bf16[4,80,1280]{2,1,0:T(8,128)(2,1)} %collective-permute-done.4.refs_0_), channel_id=1, source_target_pairs={{0,4},{4,0},{8,12},{12,8},{16,20},{20,16},{24,28},{28,24},{1,5},{5... | collective-permute-start | bytes 2457608 | tf_op jit(solution)/shard_map/ppermute | solution.py:24
  28.5 20.8 %collective-permute-start.15 = (bf16[4,80,1280]{2,1,0:T(8,128)(2,1)}, bf16[4,80,1280]{2,1,0:T(8,128)(2,1)S(1)}, u32[]{:S(2)}, u32[]{:S(2)}) collective-permute-start(bf16[4,80,1280]{2,1,0:T(8,128)(2,1)} %collective-permute-done.4.refs_0_), channel_id=1, source_target_pairs={{0,8},{4,12},{8,0},{12,4},{16,24},{20,28},{24,16},{28,20},{1,9},{5... | collective-permute-start | bytes 2457608 | tf_op jit(solution)/shard_map/ppermute | solution.py:24
  47.5 21.0 %collective-permute-start.13 = (bf16[320,1280]{1,0:T(8,128)(2,1)}, bf16[320,1280]{1,0:T(8,128)(2,1)}, u32[]{:S(2)}, u32[]{:S(2)}) collective-permute-start(bf16[320,1280]{1,0:T(8,128)(2,1)} %get-tuple-element.195), channel_id=1, source_target_pairs={{0,2},{1,3},{2,0},{3,1},{4,6},{5,7},{6,4},{7,5},{8,10},{9,11},{10,... | collective-permute-start | bytes 2457608 | tf_op jit(solution)/shard_map/ppermute | solution.py:24
  74.4 22.9 %collective-permute-start.24 = (bf16[320,1280]{1,0:T(8,128)(2,1)}, bf16[320,1280]{1,0:T(8,128)(2,1)}, u32[]{:S(2)}, u32[]{:S(2)}) collective-permute-start(bf16[320,1280]{1,0:T(8,128)(2,1)} %collective-permute-done.13.refs_0_), channel_id=1, source_target_pairs={{0,4},{4,0},{8,12},{12,8},{16,20},{20,16},{24,28},{28,24},{1,5},{5... | collective-permute-start | bytes 2457608 | tf_op jit(solution)/shard_map/ppermute | solution.py:24
  76.2 20.7 %collective-permute-start.26 = (bf16[320,1280]{1,0:T(8,128)(2,1)}, bf16[320,1280]{1,0:T(8,128)(2,1)}, u32[]{:S(2)}, u32[]{:S(2)}) collective-permute-start(bf16[320,1280]{1,0:T(8,128)(2,1)} %collective-permute-done.13.refs_0_), channel_id=1, source_target_pairs={{0,8},{4,12},{8,0},{12,4},{16,24},{20,28},{24,16},{28,20},{1,9},{5... | collective-permute-start | bytes 2457608 | tf_op jit(solution)/shard_map/ppermute | solution.py:24
  77.8 19.7 %collective-permute-start.22 = (bf16[256,1280]{1,0:T(8,128)(2,1)}, bf16[256,1280]{1,0:T(8,128)(2,1)}, u32[]{:S(2)}, u32[]{:S(2)}) collective-permute-start(bf16[256,1280]{1,0:T(8,128)(2,1)} %get-tuple-element.211), channel_id=1, source_target_pairs={{0,2},{1,3},{2,0},{3,1},{4,6},{5,7},{6,4},{7,5},{8,10},{9,11},{10,... | collective-permute-start | bytes 1966088 | tf_op jit(solution)/shard_map/ppermute | solution.py:24
  79.3 32.9 %collective-permute-start.28 = (bf16[320,1280]{1,0:T(8,128)(2,1)}, bf16[320,1280]{1,0:T(8,128)(2,1)}, u32[]{:S(2)}, u32[]{:S(2)}) collective-permute-start(bf16[320,1280]{1,0:T(8,128)(2,1)} %get-tuple-element.225), channel_id=1, source_target_pairs={{0,2},{1,3},{2,0},{3,1},{4,6},{5,7},{6,4},{7,5},{8,10},{9,11},{10,... | collective-permute-start | bytes 2457608 | tf_op jit(solution)/shard_map/ppermute | solution.py:24
  96.9 17.1 %collective-permute-start.27 = (bf16[320,1280]{1,0:T(8,128)(2,1)}, bf16[320,1280]{1,0:T(8,128)(2,1)S(1)}, u32[]{:S(2)}, u32[]{:S(2)}) collective-permute-start(bf16[320,1280]{1,0:T(8,128)(2,1)} %collective-permute-done.26.refs_4_), channel_id=1, source_target_pairs={{0,1},{1,0},{2,3},{3,2},{4,5},{5,4},{6,7},{7,6},{8,9},{9,8},{10,11... | collective-permute-start | bytes 2457608 | tf_op jit(solution)/shard_map/ppermute | solution.py:24
  96.9 31.0 %collective-permute-start.30 = (bf16[320,1280]{1,0:T(8,128)(2,1)}, bf16[320,1280]{1,0:T(8,128)(2,1)}, u32[]{:S(2)}, u32[]{:S(2)}) collective-permute-start(bf16[320,1280]{1,0:T(8,128)(2,1)} %collective-permute-done.26.refs_4_), channel_id=1, source_target_pairs={{0,4},{4,0},{8,12},{12,8},{16,20},{20,16},{24,28},{28,24},{1,5},{5... | collective-permute-start | bytes 2457608 | tf_op jit(solution)/shard_map/ppermute | solution.py:24
  97.2 15.0 %collective-permute-start.23 = (bf16[320,1280]{1,0:T(8,128)(2,1)}, bf16[320,1280]{1,0:T(8,128)(2,1)S(1)}, u32[]{:S(2)}, u32[]{:S(2)}) collective-permute-start(bf16[320,1280]{1,0:T(8,128)(2,1)} %collective-permute-done.13.refs_0_), channel_id=1, source_target_pairs={{0,1},{1,0},{2,3},{3,2},{4,5},{5,4},{6,7},{7,6},{8,9},{9,8},{10,11... | collective-permute-start | bytes 2457608 | tf_op jit(solution)/shard_map/ppermute | solution.py:24
  97.5 15.2 %collective-permute-start.25 = (bf16[320,1280]{1,0:T(8,128)(2,1)}, bf16[320,1280]{1,0:T(8,128)(2,1)S(1)}, u32[]{:S(2)}, u32[]{:S(2)}) collective-permute-start(bf16[320,1280]{1,0:T(8,128)(2,1)} %collective-permute-done.24.refs_0_), channel_id=1, source_target_pairs={{0,1},{1,0},{2,3},{3,2},{4,5},{5,4},{6,7},{7,6},{8,9},{9,8},{10,11... | collective-permute-start | bytes 2457608 | tf_op jit(solution)/shard_map/ppermute | solution.py:24
  112.2 15.7 %collective-permute-start.29 = (bf16[320,1280]{1,0:T(8,128)(2,1)}, bf16[320,1280]{1,0:T(8,128)(2,1)S(1)}, u32[]{:S(2)}, u32[]{:S(2)}) collective-permute-start(bf16[320,1280]{1,0:T(8,128)(2,1)} %collective-permute-done.28.refs_2_), channel_id=1, source_target_pairs={{0,1},{1,0},{2,3},{3,2},{4,5},{5,4},{6,7},{7,6},{8,9},{9,8},{10,11... | collective-permute-start | bytes 2457608 | tf_op jit(solution)/shard_map/ppermute | solution.py:24
  112.2 23.5 %collective-permute-start.34 = (bf16[320,1280]{1,0:T(8,128)(2,1)}, bf16[320,1280]{1,0:T(8,128)(2,1)}, u32[]{:S(2)}, u32[]{:S(2)}) collective-permute-start(bf16[320,1280]{1,0:T(8,128)(2,1)} %collective-permute-done.28.refs_2_), channel_id=1, source_target_pairs={{0,4},{4,0},{8,12},{12,8},{16,20},{20,16},{24,28},{28,24},{1,5},{5... | collective-permute-start | bytes 2457608 | tf_op jit(solution)/shard_map/ppermute | solution.py:24
  113.6 22.2 %collective-permute-start.36 = (bf16[320,1280]{1,0:T(8,128)(2,1)}, bf16[320,1280]{1,0:T(8,128)(2,1)}, u32[]{:S(2)}, u32[]{:S(2)}) collective-permute-start(bf16[320,1280]{1,0:T(8,128)(2,1)} %collective-permute-done.28.refs_2_), channel_id=1, source_target_pairs={{0,8},{4,12},{8,0},{12,4},{16,24},{20,28},{24,16},{28,20},{1,9},{5... | collective-permute-start | bytes 2457608 | tf_op jit(solution)/shard_map/ppermute | solution.py:24
  114.8 20.4 %collective-permute-start.32 = (bf16[320,1280]{1,0:T(8,128)(2,1)}, bf16[320,1280]{1,0:T(8,128)(2,1)}, u32[]{:S(2)}, u32[]{:S(2)}) collective-permute-start(bf16[320,1280]{1,0:T(8,128)(2,1)} %get-tuple-element.233), channel_id=1, source_target_pairs={{0,2},{1,3},{2,0},{3,1},{4,6},{5,7},{6,4},{7,5},{8,10},{9,11},{10,... | collective-permute-start | bytes 2457608 | tf_op jit(solution)/shard_map/ppermute | solution.py:24
  165.6 20.6 %collective-permute-start.38 = (bf16[256,1280]{1,0:T(8,128)(2,1)S(1)}, bf16[256,1280]{1,0:T(8,128)(2,1)S(1)}, u32[]{:S(2)}, u32[]{:S(2)}) collective-permute-start(bf16[256,1280]{1,0:T(8,128)(2,1)S(1)} %get-tuple-element.244), channel_id=1, source_target_pairs={{0,2},{1,3},{2,0},{3,1},{4,6},{5,7},{6,4},{7,5},{8,10},{9,11},{10,... | collective-permute-start | bytes 1966088 | tf_op jit(solution)/shard_map/ppermute | solution.py:24
  167.7 27.5 %collective-permute-start.41 = (bf16[16,4992]{1,0:T(8,128)(2,1)S(1)}, bf16[16,4992]{1,0:T(8,128)(2,1)S(1)}, u32[]{:S(2)}, u32[]{:S(2)}) collective-permute-start(bf16[16,4992]{1,0:T(8,128)(2,1)S(1)} %get-tuple-element.247), channel_id=1, source_target_pairs={{0,16},{4,20},{8,24},{12,28},{16,0},{20,4},{24,8},{28,12},{1,17},{... | collective-permute-start | bytes 479240 | tf_op jit(solution)/shard_map/ppermute | solution.py:24
  216.4 20.5 %collective-permute-start.54 = (bf16[4,16,4992]{2,1,0:T(8,128)(2,1)S(1)}, bf16[4,16,4992]{2,1,0:T(8,128)(2,1)S(1)}, u32[]{:S(2)}, u32[]{:S(2)}) collective-permute-start(bf16[4,16,4992]{2,1,0:T(8,128)(2,1)S(1)} %get-tuple-element.305.refs_0_), channel_id=1, source_target_pairs={{0,8},{4,12},{8,0},{12,4},{16,24},{20,28},{24,16},{28,20},{1,9},{5... | collective-permute-start | bytes 1916936 | tf_op jit(solution)/shard_map/ppermute | solution.py:24
  217.8 19.1 %collective-permute-start.55 = (bf16[4,16,4992]{2,1,0:T(8,128)(2,1)S(1)}, bf16[4,16,4992]{2,1,0:T(8,128)(2,1)S(1)}, u32[]{:S(2)}, u32[]{:S(2)}) collective-permute-start(bf16[4,16,4992]{2,1,0:T(8,128)(2,1)S(1)} %get-tuple-element.307.refs_2_), channel_id=1, source_target_pairs={{0,4},{4,0},{8,12},{12,8},{16,20},{20,16},{24,28},{28,24},{1,5},{5... | collective-permute-start | bytes 1916936 | tf_op jit(solution)/shard_map/ppermute | solution.py:24
  218.3 16.2 %collective-permute-start.51 = (bf16[16,2944]{1,0:T(8,128)(2,1)S(1)}, bf16[16,2944]{1,0:T(8,128)(2,1)S(1)}, u32[]{:S(2)}, u32[]{:S(2)}) collective-permute-start(bf16[16,2944]{1,0:T(8,128)(2,1)S(1)} %get-tuple-element.293), channel_id=1, source_target_pairs={{0,16},{4,20},{8,24},{12,28},{16,0},{20,4},{24,8},{28,12},{1,17},{... | collective-permute-start | bytes 282632 | tf_op jit(solution)/shard_map/ppermute | solution.py:24
  227.9 27.6 %collective-permute-start.53 = (bf16[256,1280]{1,0:T(8,128)(2,1)S(1)}, bf16[256,1280]{1,0:T(8,128)(2,1)S(1)}, u32[]{:S(2)}, u32[]{:S(2)}) collective-permute-start(bf16[256,1280]{1,0:T(8,128)(2,1)S(1)} %shard_map.376), channel_id=1, source_target_pairs={{0,2},{1,3},{2,0},{3,1},{4,6},{5,7},{6,4},{7,5},{8,10},{9,11},{10,... | collective-permute-start | bytes 1966088 | tf_op jit(solution)/shard_map/ppermute | solution.py:24
  (130 other events, 1241.8 us)

commit v6 on v5

--- a/solution.py
+++ b/solution.py
@@ -866,6 +866,25 @@
         body, (spot,), [array, second], [remain, KEEP], shaped(array.shape, array.dtype), out_spec, aliases={1: 0}, weight=1)
 
 
+def pair_and_complete(spot, array, second, tables, moved):
+    rows, features = second.shape
+    _, count, rank, half = moved.shape
+
+    def body(spot_ref, second_ref, moved_ref, *refs):
+        refs[4][0] = second_ref[...].astype(array.dtype)
+        for n in range(3):
+            refs[5 + n][...] = moved_ref[n]
+
+    table = shaped((count, rank, 2 * half), f32)
+    theirs = placed_block((count, rank, half), lambda i, spot: (0, 0, 1 - (spot[3] & 1)))
+    out_spec = placed_block((1, rows, features), lambda i, spot: (spot[1], 0, 0))
+    return call(
+        body, (spot,), [second, moved, array] + list(tables), [KEEP] * 2 + [remain] * 4,
+        [shaped(array.shape, array.dtype)] + [table] * 3, [out_spec] + [theirs] * 3,
+        aliases={3: 0, 4: 1, 5: 2, 6: 3}, weight=2,
+    )
+
+
 def join(groups):
     flat = [a for g in groups for a in g]
     outs = [shaped((sum(a.shape[0] for a in g),) + g[0].shape[1:], g[0].dtype) for g in groups]
@@ -1090,7 +1109,8 @@
         sides += [beside(after(q[2], g01)) for q in quarters[2:]]
         pieces += [(gq, own, sided) for (gq, own, _), sided in zip(quarters[2:], sides[2:])]
         far_factors = [received[rows:], far_side]
-        g23, gl, *second = gather_pair(pieces[2:], low, far_factors, gl)
+        output = pair_up(spot, output, after(out_side, g01))
+        g23, gl, *second = gather_pair(pieces[2:], low, far_factors, after(gl, output))
         keep, give = gather_inner(spot, gl, z, first, second)
         moved = beside(give)
         here, there = settle(spot, pick, keep, moved, 3 * half, False)
@@ -1102,7 +1122,6 @@
         grad_side = across(gradb)
         grad = finish(spot, pick, g01, after(g23, gradb, crossed), *ends, inputs, grad_hidden, gains[0], 0)
         turns = first_turn(here, other, after(crossed, gradb))
-        output = pair_up(spot, output, after(out_side, grad))
         early = after(early, gradb, turns[0][0])
         picks = jnp.concatenate([a[:, 0, -128:-122] for a in early]).astype(jnp.int32)
         adapters = query_inner.shape[0]
@@ -1123,12 +1142,11 @@
             adapters,
         )
         early = [whole_sum(t) for t in early]
-        early_shared = complete(spot, early[1:4], beside(early[0]))
         late = second_turn(turns)
-        input_grad = pair_up(spot, grad, grad_side)
+        input_grad, *early_shared = pair_and_complete(spot, grad, grad_side, early[1:4], beside(early[0]))
         late = combine(
             spot,
-            after(picks, grad_side, output),
+            after(picks, grad_side, grad),
             late,
             [(n * half, half, n) for n in range(3)] + [(base + n * width, width, n) for n in range(3)],
             adapters,

time: 266 us -> 264 us (level)
    pallas_call x34 -> x33, Pallas kernels: 151 us -> 150 us  [call(): pl.pallas_call(body, grid_spec=pltpu.PrefetchScalarGridSpec(num_scalar_pr...]
  transfers between devices with their start and end apart: 62 -> 62, of which waited for: 23 -> 26; matrix products, arithmetic and copies ran while one was open for 0% -> 0% of each run, Pallas kernels for 46% -> 46%
where the time goes in v6:
time: 264 us; the launch traced here: 261 us
  Pallas kernels  150 us (57%)
  starting transfers between devices  53.9 us (20%)
  waiting for transfers between devices  45.1 us (17%)
  local copies, waits for them, and re-layouts  7.72 us (3%)
    pallas_call x33, Pallas kernels, call(): pl.pallas_call(body, grid_spec=pltpu.PrefetchScalarGridSpec(num_scalar_pr...  150 us
    ppermute x62, starting transfers between devices, swap(): return lax.ppermute(array, axis, [(i, i ^ bits) for i in range(size)])  53.9 us
    ppermute x62, waiting for transfers between devices, swap(): return lax.ppermute(array, axis, [(i, i ^ bits) for i in range(size)])  45.1 us
    unnamed x186, local copies, waits for them, and re-layouts  7.62 us
  transfers between devices with their start and end apart: 62, of which 26 were waited for; matrix products, arithmetic and copies ran while one was open for 0% of the time, Pallas kernels for 46%

profile of v6, /device:TPU:0, one launch (start us, length us, event | category | flops | bytes accessed | tf_op | source)
XLA Modules:
  0.0 261.0 jit_solution(732584617704410567)
XLA Ops:
  18.6 3.1 %shard_map.354 = (bf16[320,1280]{1,0:T(8,128)(2,1)}, bf16[320,1280]{1,0:T(8,128)(2,1)}, bf16[320,1280]{1,0:T(8,128)(2,1)}, bf16[256,1280]{1,0:T(8,128)(2,1)}) custom-call(s32[4]{0:T(128)S(1)} %pad_add_fusion.spot_ref, bf16[1280,1280]{1,0:T(8,128)(2,1)S(1)} %copy-done.28, bf16[1280,1280]{1,0:T(8,128)(2,1)S(1)} %copy-done.30, ...), custom_call_target="tpu_custom_call" | custom-call | flops 99999997952 | bytes 100000 | tf_op jit(solution)/shard_map/pallas_call | solution.py:86
  21.8 4.6 %collective-permute-done.4.refs_0_ = bf16[4,80,1280]{2,1,0:T(8,128)(2,1)} collective-permute-done((bf16[4,80,1280]{2,1,0:T(8,128)(2,1)}, bf16[4,80,1280]{2,1,0:T(8,128)(2,1)}, u32[]{:S(2)}, u32[]{:S(2)}) %collective-permute-start.4) | collective-permute-done | bytes 819232 | tf_op jit(solution)/shard_map/ppermute | solution.py:24
  30.1 12.3 %collective-permute-done.2.xb.received_ref.refs_7_ = bf16[304,1280]{1,0:T(8,128)(2,1)S(1)} collective-permute-done((bf16[304,1280]{1,0:T(8,128)(2,1)S(1)}, bf16[304,1280]{1,0:T(8,128)(2,1)S(1)}, u32[]{:S(2)}, u32[]{:S(2)}) %collective-permute-start.2) | collective-permute-done | bytes 778272 | tf_op jit(solution)/shard_map/ppermute | solution.py:24
  42.5 4.9 %shard_map.355 = (bf16[512,1280]{1,0:T(8,128)(2,1)S(1)}, f32[48,512]{1,0:T(8,128)S(1)}, bf16[2,2,320,512]{3,2,1,0:T(8,128)(2,1)S(1)}) custom-call(s32[4]{0:T(128)S(1)} %pad_add_fusion.spot_ref, s32[2,6]{1,0:T(2,128)S(1)} %copy-done.27, bf16[2,256,1280]{2,1,0:T(8,128)(2,1)S(1)} %copy-done.5, ...), custom_call_target="tpu_custom_call" | custom-call | flops 99999997952 | bytes 100000 | tf_op jit(solution)/shard_map/pallas_call | solution.py:86
  54.8 8.1 %shard_map.357 = (bf16[2,320,512]{2,1,0:T(8,128)(2,1)S(1)}, f32[8,1,512]{2,1,0:T(1,128)S(1)}) custom-call(s32[4]{0:T(128)S(1)} %pad_add_fusion.spot_ref, s32[2]{0:T(128)S(1)} %copy-done.73, bf16[2,320,512]{2,1,0:T(8,128)(2,1)S(1)} %shard_map.356.q_ref, bf16[2,2,320,512]{3,2,1,0:T(8,128)(2,1)S(1)} %get-tuple-element.190.k1.v1, ...), custom_call_target="tpu_custom_call" | custom-call | flops 99999997952 | bytes 100000 | tf_op jit(solution)/shard_map/pallas_call | solution.py:86
  65.3 3.1 %collective-permute-done.13.refs_0_ = bf16[320,1280]{1,0:T(8,128)(2,1)} collective-permute-done((bf16[320,1280]{1,0:T(8,128)(2,1)}, bf16[320,1280]{1,0:T(8,128)(2,1)}, u32[]{:S(2)}, u32[]{:S(2)}) %collective-permute-start.13) | collective-permute-done | bytes 819232 | tf_op jit(solution)/shard_map/ppermute | solution.py:24
  68.5 5.6 %shard_map.358 = (bf16[2,4,320,1280]{3,2,1,0:T(8,128)(2,1)S(1)}, bf16[2,2,320,512]{3,2,1,0:T(8,128)(2,1)S(1)}, bf16[2,320,512]{2,1,0:T(8,128)(2,1)S(1)}) custom-call(s32[1]{0:T(128)} %bitcast.2.spot_ref, bf16[512,1280]{1,0:T(8,128)(2,1)S(1)} %get-tuple-element.198.z_ref, f32[48,512]{1,0:T(8,128)S(1)} %get-tuple-element.275.low_ref.refs_6_, ...), custom_call_target="tpu_custom_call" | custom-call | flops 99999997952 | bytes 100000 | tf_op jit(solution)/shard_map/pallas_call | solution.py:86
  79.9 8.4 %shard_map.359 = (bf16[2,320,512]{2,1,0:T(8,128)(2,1)S(1)}, f32[8,1,512]{2,1,0:T(1,128)S(1)}) custom-call(s32[4]{0:T(128)S(1)} %pad_add_fusion.spot_ref, s32[2]{0:T(128)S(1)} %copy-done.73, bf16[2,320,512]{2,1,0:T(8,128)(2,1)S(1)} %get-tuple-element.268.q_ref, bf16[2,2,320,512]{3,2,1,0:T(8,128)(2,1)S(1)} %get-tuple-element.206.k1.v1, ...), custom_call_target="tpu_custom_call" | custom-call | flops 99999997952 | bytes 100000 | tf_op jit(solution)/shard_map/pallas_call | solution.py:86
  88.5 6.4 %shard_map.360 = (f32[512,1280]{1,0:T(8,128)S(1)}, bf16[512,1280]{1,0:T(8,128)(2,1)S(1)}, f32[32,512]{1,0:T(8,128)S(1)}) custom-call(s32[4]{0:T(128)S(1)} %pad_add_fusion.spot_ref, s32[2,6]{1,0:T(2,128)S(1)} %copy-done.27, s32[2]{0:T(128)S(1)} %copy-done.73, bf16[2,320,512]{2,1,0:T(8,128)(2,1)S(1)} %get-tuple-element.196.c01, ...), custom_call_target="tpu_custom_call" | custom-call | flops 99999997952 | bytes 100000 | tf_op jit(solution)/shard_map/pallas_call | solution.py:86
  97.8 11.2 %shard_map.361 = (bf16[512,1280]{1,0:T(8,128)(2,1)S(1)}, f32[512,1280]{1,0:T(8,128)S(1)}, f32[512,1280]{1,0:T(8,128)S(1)}, f32[80,512]{1,0:T(8,128)S(1)}, f32[32,1280]{1,0:T(8,128)S(1)}) custom-call(s32[4]{0:T(128)S(1)} %pad_add_fusion.spot_ref, s32[2,6]{1,0:T(2,128)S(1)} %copy-done.27, s32[2]{0:T(128)S(1)} %copy-done.73, ...), custom_call_target="tpu_custom_call" | custom-call | flops 99999997952 | bytes 100000 | tf_op jit(solution)/shard_map/pallas_call | solution.py:86
  109.0 3.2 %collective-permute-done.28.refs_2_ = bf16[320,1280]{1,0:T(8,128)(2,1)} collective-permute-done((bf16[320,1280]{1,0:T(8,128)(2,1)}, bf16[320,1280]{1,0:T(8,128)(2,1)}, u32[]{:S(2)}, u32[]{:S(2)}) %collective-permute-start.28) | collective-permute-done | bytes 819232 | tf_op jit(solution)/shard_map/ppermute | solution.py:24
  116.5 11.4 %shard_map.362 = (f32[512,1280]{1,0:T(8,128)S(1)}, f32[512,1280]{1,0:T(8,128)S(1)}, f32[80,512]{1,0:T(8,128)S(1)}, f32[32,1280]{1,0:T(8,128)S(1)}) custom-call(bf16[512,1280]{1,0:T(8,128)(2,1)S(1)} %get-tuple-element.210.z_ref, bf16[512,1280]{1,0:T(8,128)(2,1)S(1)} %get-tuple-element.214.gy_ref, ...), custom_call_target="tpu_custom_call", output_to_operand_aliasing={{0}: (2, {}), {1}: (3, {})} | custom-call | flops 99999997952 | bytes 100000 | tf_op jit(solution)/shard_map/pallas_call | solution.py:86
  128.0 7.1 %shard_map.363 = (f32[512,1280]{1,0:T(8,128)S(1)}, f32[512,1280]{1,0:T(8,128)S(1)}, f32[80,512]{1,0:T(8,128)S(1)}, f32[32,640]{1,0:T(8,128)S(1)}) custom-call(bf16[512,1280]{1,0:T(8,128)(2,1)S(1)} %get-tuple-element.210.z_ref, bf16[512,1280]{1,0:T(8,128)(2,1)S(1)} %get-tuple-element.214.gy_ref, ...), custom_call_target="tpu_custom_call", output_to_operand_aliasing={{0}: (2, {}), {1}: (3, {})} | custom-call | flops 99999997952 | bytes 100000 | tf_op jit(solution)/shard_map/pallas_call | solution.py:86
  137.9 7.3 %shard_map.364 = (f32[512,1280]{1,0:T(8,128)S(1)}, f32[512,1280]{1,0:T(8,128)S(1)}, f32[80,512]{1,0:T(8,128)S(1)}, f32[32,640]{1,0:T(8,128)S(1)}) custom-call(bf16[512,1280]{1,0:T(8,128)(2,1)S(1)} %get-tuple-element.210.z_ref, bf16[512,1280]{1,0:T(8,128)(2,1)S(1)} %get-tuple-element.214.gy_ref, ...), custom_call_target="tpu_custom_call", output_to_operand_aliasing={{0}: (2, {}), {1}: (3, {})} | custom-call | flops 99999997952 | bytes 100000 | tf_op jit(solution)/shard_map/pallas_call | solution.py:86
  145.4 19.7 %shard_map.365 = (bf16[2,256,1280]{2,1,0:T(8,128)(2,1)}, bf16[256,1280]{1,0:T(8,128)(2,1)S(1)}, f32[512,1280]{1,0:T(8,128)S(1)}, bf16[4,320,512]{2,1,0:T(8,128)(...) custom-call(s32[4]{0:T(128)S(1)} %copy-done.26, s32[2,6]{1,0:T(2,128)S(1)} %copy-done.27, ...), custom_call_target="tpu_custom_call" | custom-call | flops 99999997952 | bytes 100000 | tf_op jit(solution)/shard_map/pallas_call | solution.py:86
  170.5 7.2 %shard_map.367 = (bf16[320,512]{1,0:T(8,128)(2,1)S(1)}, f32[2,320,512]{2,1,0:T(8,128)S(1)}, bf16[2,320,512]{2,1,0:T(8,128)(2,1)S(1)}) custom-call(s32[4]{0:T(128)S(1)} %copy-done.26, s32[2]{0:T(128)S(1)} %copy-done.73, bf16[2,320,512]{2,1,0:T(8,128)(2,1)S(1)} %copy-done.79, bf16[2,2,320,512]{3,2,1,0:T(8,128)(2,1)S(1)} %copy-done.40, ...), custom_call_target="tpu_custom_call" | custom-call | flops 8000000000 | bytes 100000 | tf_op jit(solution)/shard_map/pallas_call | solution.py:86
  179.3 6.8 %shard_map.368 = (bf16[320,512]{1,0:T(8,128)(2,1)S(1)}, f32[2,320,512]{2,1,0:T(8,128)S(1)}, bf16[2,320,512]{2,1,0:T(8,128)(2,1)S(1)}) custom-call(s32[4]{0:T(128)S(1)} %copy-done.26, s32[2]{0:T(128)S(1)} %copy-done.73, bf16[2,320,512]{2,1,0:T(8,128)(2,1)S(1)} %copy-done.79, bf16[2,2,320,512]{3,2,1,0:T(8,128)(2,1)S(1)} %copy-done.40, ...), custom_call_target="tpu_custom_call" | custom-call | flops 8000000000 | bytes 100000 | tf_op jit(solution)/shard_map/pallas_call | solution.py:86
  188.5 6.8 %shard_map.369 = (bf16[320,512]{1,0:T(8,128)(2,1)S(1)}, f32[2,320,512]{2,1,0:T(8,128)S(1)}, bf16[2,320,512]{2,1,0:T(8,128)(2,1)S(1)}) custom-call(s32[4]{0:T(128)S(1)} %copy-done.26, s32[2]{0:T(128)S(1)} %copy-done.73, bf16[2,320,512]{2,1,0:T(8,128)(2,1)S(1)} %copy-done.81, bf16[2,2,320,512]{3,2,1,0:T(8,128)(2,1)S(1)} %copy-done.44, ...), custom_call_target="tpu_custom_call" | custom-call | flops 8000000000 | bytes 100000 | tf_op jit(solution)/shard_map/pallas_call | solution.py:86
  198.7 6.9 %shard_map.371 = (bf16[320,512]{1,0:T(8,128)(2,1)S(1)}, f32[2,320,512]{2,1,0:T(8,128)S(1)}, bf16[2,320,512]{2,1,0:T(8,128)(2,1)S(1)}) custom-call(s32[4]{0:T(128)S(1)} %copy-done.26, s32[2]{0:T(128)S(1)} %copy-done.73, bf16[2,320,512]{2,1,0:T(8,128)(2,1)S(1)} %copy-done.81, bf16[2,2,320,512]{3,2,1,0:T(8,128)(2,1)S(1)} %copy-done.44, ...), custom_call_target="tpu_custom_call" | custom-call | flops 8000000000 | bytes 100000 | tf_op jit(solution)/shard_map/pallas_call | solution.py:86
  218.3 3.4 %collective-permute-start.54 = (bf16[16,2944]{1,0:T(8,128)(2,1)S(1)}, bf16[16,2944]{1,0:T(8,128)(2,1)S(1)}, u32[]{:S(2)}, u32[]{:S(2)}) collective-permute-start(bf16[16,2944]{1,0:T(8,128)(2,1)S(1)} %get-tuple-element.303), channel_id=1, source_target_pairs={{0,16},{4,20},{8,24},{12,28},{16,0},{20,4},{24,8},{28,12},{1,17},{... | collective-permute-start | bytes 282632 | tf_op jit(solution)/shard_map/ppermute | solution.py:24
  222.5 5.6 %shard_map.377 = bf16[256,1280]{1,0:T(8,128)(2,1)S(1)} custom-call(s32[4]{0:T(128)S(1)} %copy-done.26, s32[2,6]{1,0:T(2,128)S(1)} %copy-done.27, bf16[2,3,320,512]{3,2,1,0:T(8,128)(2,1)S(1)} %get-tuple-element.276.g01_ref, bf16[2,3,320,512]{3,2,1,0:T(8,128)(2,1)S(1)} %get-tuple-element.313.g23_ref, f32[48,512]{1,0:T(8,128)S(1)} %get-tuple-element.287.gl_ref, ...), custom_call_target="tpu_custom_call" | custom-call | flops 5000000000 | bytes 100000 | tf_op jit(solution)/shard_map/pallas_call | solution.py:86
  229.7 4.8 %collective-permute-done.54 = bf16[16,2944]{1,0:T(8,128)(2,1)S(1)} collective-permute-done((bf16[16,2944]{1,0:T(8,128)(2,1)S(1)}, bf16[16,2944]{1,0:T(8,128)(2,1)S(1)}, u32[]{:S(2)}, u32[]{:S(2)}) %collective-permute-start.54) | collective-permute-done | bytes 94240 | tf_op jit(solution)/shard_map/ppermute | solution.py:24
  237.0 3.4 %collective-permute-start.58 = (bf16[2,16,2944]{2,1,0:T(8,128)(2,1)S(1)}, bf16[2,16,2944]{2,1,0:T(8,128)(2,1)S(1)}, u32[]{:S(2)}, u32[]{:S(2)}) collective-permute-start(bf16[2,16,2944]{2,1,0:T(8,128)(2,1)S(1)} %get-tuple-element.319.refs_2_), channel_id=1, source_target_pairs={{0,8},{4,12},{8,0},{12,4},{16,24},{20,28},{24,16},{28,20},{1,9},{5... | collective-permute-start | bytes 565256 | tf_op jit(solution)/shard_map/ppermute | solution.py:24
  247.6 6.6 %shard_map.381.refs_0_ = f32[2,256,1280]{2,1,0:T(8,128)} custom-call(s32[4]{0:T(128)S(1)} %copy-done.26, s32[2,6]{1,0:T(2,128)S(1)} %copy-done.27, bf16[2,3,320,512]{3,2,1,0:T(8,128)(2,1)S(1)} %get-tuple-element.276.g01_ref, bf16[2,3,320,512]{3,2,1,0:T(8,128)(2,1)S(1)} %get-tuple-element.313.g23_ref, f32[48,512]{1,0:T(8,128)S(1)} %get-tuple-element.287.gl_ref, ...), custom_call_target="tpu_custom_call" | custom-call | flops 5000000000 | bytes 100000 | tf_op jit(solution)/shard_map/pallas_call | solution.py:86
  (334 shorter events, 91.0 us)
Async XLA Ops:
  4.1 22.3 %collective-permute-start.4 = (bf16[4,80,1280]{2,1,0:T(8,128)(2,1)}, bf16[4,80,1280]{2,1,0:T(8,128)(2,1)}, u32[]{:S(2)}, u32[]{:S(2)}) collective-permute-start(bf16[4,80,1280]{2,1,0:T(8,128)(2,1)} %fusion.3), channel_id=1, source_target_pairs={{0,2},{1,3},{2,0},{3,1},{4,6},{5,7},{6,4},{7,5},{8,10},{9,11},{10,... | collective-permute-start | bytes 2457608 | tf_op jit(solution)/shard_map/ppermute | solution.py:24
  15.6 26.8 %collective-permute-start.2 = (bf16[304,1280]{1,0:T(8,128)(2,1)S(1)}, bf16[304,1280]{1,0:T(8,128)(2,1)S(1)}, u32[]{:S(2)}, u32[]{:S(2)}) collective-permute-start(bf16[304,1280]{1,0:T(8,128)(2,1)S(1)} %get-tuple-element.180), channel_id=1, source_target_pairs={{0,2},{1,3},{2,0},{3,1},{4,6},{5,7},{6,4},{7,5},{8,10},{9,11},{10,... | collective-permute-start | bytes 2334728 | tf_op jit(solution)/shard_map/ppermute | solution.py:24
  18.5 23.9 %collective-permute-start.8 = (bf16[1280,1280]{1,0:T(8,128)(2,1)S(1)}, bf16[1280,1280]{1,0:T(8,128)(2,1)S(1)}, u32[]{:S(2)}, u32[]{:S(2)}) collective-permute-start(bf16[1280,1280]{1,0:T(8,128)(2,1)S(1)} %copy-done.30), channel_id=1, source_target_pairs={{0,1},{1,0},{2,3},{3,2},{4,5},{5,4},{6,7},{7,6},{8,9},{9,8},{10,11... | collective-permute-start | bytes 9830408 | tf_op jit(solution)/shard_map/ppermute | solution.py:24
  26.4 22.9 %collective-permute-start.10 = (bf16[4,80,1280]{2,1,0:T(8,128)(2,1)}, bf16[4,80,1280]{2,1,0:T(8,128)(2,1)S(1)}, u32[]{:S(2)}, u32[]{:S(2)}) collective-permute-start(bf16[4,80,1280]{2,1,0:T(8,128)(2,1)} %collective-permute-done.4.refs_0_), channel_id=1, source_target_pairs={{0,4},{4,0},{8,12},{12,8},{16,20},{20,16},{24,28},{28,24},{1,5},{5... | collective-permute-start | bytes 2457608 | tf_op jit(solution)/shard_map/ppermute | solution.py:24
  28.5 20.8 %collective-permute-start.15 = (bf16[4,80,1280]{2,1,0:T(8,128)(2,1)}, bf16[4,80,1280]{2,1,0:T(8,128)(2,1)S(1)}, u32[]{:S(2)}, u32[]{:S(2)}) collective-permute-start(bf16[4,80,1280]{2,1,0:T(8,128)(2,1)} %collective-permute-done.4.refs_0_), channel_id=1, source_target_pairs={{0,8},{4,12},{8,0},{12,4},{16,24},{20,28},{24,16},{28,20},{1,9},{5... | collective-permute-start | bytes 2457608 | tf_op jit(solution)/shard_map/ppermute | solution.py:24
  47.5 21.0 %collective-permute-start.13 = (bf16[320,1280]{1,0:T(8,128)(2,1)}, bf16[320,1280]{1,0:T(8,128)(2,1)}, u32[]{:S(2)}, u32[]{:S(2)}) collective-permute-start(bf16[320,1280]{1,0:T(8,128)(2,1)} %get-tuple-element.197), channel_id=1, source_target_pairs={{0,2},{1,3},{2,0},{3,1},{4,6},{5,7},{6,4},{7,5},{8,10},{9,11},{10,... | collective-permute-start | bytes 2457608 | tf_op jit(solution)/shard_map/ppermute | solution.py:24
  74.4 22.9 %collective-permute-start.24 = (bf16[320,1280]{1,0:T(8,128)(2,1)}, bf16[320,1280]{1,0:T(8,128)(2,1)}, u32[]{:S(2)}, u32[]{:S(2)}) collective-permute-start(bf16[320,1280]{1,0:T(8,128)(2,1)} %collective-permute-done.13.refs_0_), channel_id=1, source_target_pairs={{0,4},{4,0},{8,12},{12,8},{16,20},{20,16},{24,28},{28,24},{1,5},{5... | collective-permute-start | bytes 2457608 | tf_op jit(solution)/shard_map/ppermute | solution.py:24
  76.2 20.7 %collective-permute-start.26 = (bf16[320,1280]{1,0:T(8,128)(2,1)}, bf16[320,1280]{1,0:T(8,128)(2,1)}, u32[]{:S(2)}, u32[]{:S(2)}) collective-permute-start(bf16[320,1280]{1,0:T(8,128)(2,1)} %collective-permute-done.13.refs_0_), channel_id=1, source_target_pairs={{0,8},{4,12},{8,0},{12,4},{16,24},{20,28},{24,16},{28,20},{1,9},{5... | collective-permute-start | bytes 2457608 | tf_op jit(solution)/shard_map/ppermute | solution.py:24
  77.8 19.7 %collective-permute-start.22 = (bf16[256,1280]{1,0:T(8,128)(2,1)}, bf16[256,1280]{1,0:T(8,128)(2,1)}, u32[]{:S(2)}, u32[]{:S(2)}) collective-permute-start(bf16[256,1280]{1,0:T(8,128)(2,1)} %get-tuple-element.213), channel_id=1, source_target_pairs={{0,2},{1,3},{2,0},{3,1},{4,6},{5,7},{6,4},{7,5},{8,10},{9,11},{10,... | collective-permute-start | bytes 1966088 | tf_op jit(solution)/shard_map/ppermute | solution.py:24
  79.3 32.9 %collective-permute-start.28 = (bf16[320,1280]{1,0:T(8,128)(2,1)}, bf16[320,1280]{1,0:T(8,128)(2,1)}, u32[]{:S(2)}, u32[]{:S(2)}) collective-permute-start(bf16[320,1280]{1,0:T(8,128)(2,1)} %get-tuple-element.227), channel_id=1, source_target_pairs={{0,2},{1,3},{2,0},{3,1},{4,6},{5,7},{6,4},{7,5},{8,10},{9,11},{10,... | collective-permute-start | bytes 2457608 | tf_op jit(solution)/shard_map/ppermute | solution.py:24
  96.9 17.1 %collective-permute-start.27 = (bf16[320,1280]{1,0:T(8,128)(2,1)}, bf16[320,1280]{1,0:T(8,128)(2,1)S(1)}, u32[]{:S(2)}, u32[]{:S(2)}) collective-permute-start(bf16[320,1280]{1,0:T(8,128)(2,1)} %collective-permute-done.26.refs_4_), channel_id=1, source_target_pairs={{0,1},{1,0},{2,3},{3,2},{4,5},{5,4},{6,7},{7,6},{8,9},{9,8},{10,11... | collective-permute-start | bytes 2457608 | tf_op jit(solution)/shard_map/ppermute | solution.py:24
  96.9 31.0 %collective-permute-start.30 = (bf16[320,1280]{1,0:T(8,128)(2,1)}, bf16[320,1280]{1,0:T(8,128)(2,1)}, u32[]{:S(2)}, u32[]{:S(2)}) collective-permute-start(bf16[320,1280]{1,0:T(8,128)(2,1)} %collective-permute-done.26.refs_4_), channel_id=1, source_target_pairs={{0,4},{4,0},{8,12},{12,8},{16,20},{20,16},{24,28},{28,24},{1,5},{5... | collective-permute-start | bytes 2457608 | tf_op jit(solution)/shard_map/ppermute | solution.py:24
  97.2 15.0 %collective-permute-start.23 = (bf16[320,1280]{1,0:T(8,128)(2,1)}, bf16[320,1280]{1,0:T(8,128)(2,1)S(1)}, u32[]{:S(2)}, u32[]{:S(2)}) collective-permute-start(bf16[320,1280]{1,0:T(8,128)(2,1)} %collective-permute-done.13.refs_0_), channel_id=1, source_target_pairs={{0,1},{1,0},{2,3},{3,2},{4,5},{5,4},{6,7},{7,6},{8,9},{9,8},{10,11... | collective-permute-start | bytes 2457608 | tf_op jit(solution)/shard_map/ppermute | solution.py:24
  97.5 15.2 %collective-permute-start.25 = (bf16[320,1280]{1,0:T(8,128)(2,1)}, bf16[320,1280]{1,0:T(8,128)(2,1)S(1)}, u32[]{:S(2)}, u32[]{:S(2)}) collective-permute-start(bf16[320,1280]{1,0:T(8,128)(2,1)} %collective-permute-done.24.refs_0_), channel_id=1, source_target_pairs={{0,1},{1,0},{2,3},{3,2},{4,5},{5,4},{6,7},{7,6},{8,9},{9,8},{10,11... | collective-permute-start | bytes 2457608 | tf_op jit(solution)/shard_map/ppermute | solution.py:24
  112.2 15.7 %collective-permute-start.29 = (bf16[320,1280]{1,0:T(8,128)(2,1)}, bf16[320,1280]{1,0:T(8,128)(2,1)S(1)}, u32[]{:S(2)}, u32[]{:S(2)}) collective-permute-start(bf16[320,1280]{1,0:T(8,128)(2,1)} %collective-permute-done.28.refs_2_), channel_id=1, source_target_pairs={{0,1},{1,0},{2,3},{3,2},{4,5},{5,4},{6,7},{7,6},{8,9},{9,8},{10,11... | collective-permute-start | bytes 2457608 | tf_op jit(solution)/shard_map/ppermute | solution.py:24
  112.2 23.5 %collective-permute-start.34 = (bf16[320,1280]{1,0:T(8,128)(2,1)}, bf16[320,1280]{1,0:T(8,128)(2,1)}, u32[]{:S(2)}, u32[]{:S(2)}) collective-permute-start(bf16[320,1280]{1,0:T(8,128)(2,1)} %collective-permute-done.28.refs_2_), channel_id=1, source_target_pairs={{0,4},{4,0},{8,12},{12,8},{16,20},{20,16},{24,28},{28,24},{1,5},{5... | collective-permute-start | bytes 2457608 | tf_op jit(solution)/shard_map/ppermute | solution.py:24
  113.6 22.1 %collective-permute-start.36 = (bf16[320,1280]{1,0:T(8,128)(2,1)}, bf16[320,1280]{1,0:T(8,128)(2,1)}, u32[]{:S(2)}, u32[]{:S(2)}) collective-permute-start(bf16[320,1280]{1,0:T(8,128)(2,1)} %collective-permute-done.28.refs_2_), channel_id=1, source_target_pairs={{0,8},{4,12},{8,0},{12,4},{16,24},{20,28},{24,16},{28,20},{1,9},{5... | collective-permute-start | bytes 2457608 | tf_op jit(solution)/shard_map/ppermute | solution.py:24
  114.8 20.4 %collective-permute-start.32 = (bf16[320,1280]{1,0:T(8,128)(2,1)}, bf16[320,1280]{1,0:T(8,128)(2,1)}, u32[]{:S(2)}, u32[]{:S(2)}) collective-permute-start(bf16[320,1280]{1,0:T(8,128)(2,1)} %get-tuple-element.235), channel_id=1, source_target_pairs={{0,2},{1,3},{2,0},{3,1},{4,6},{5,7},{6,4},{7,5},{8,10},{9,11},{10,... | collective-permute-start | bytes 2457608 | tf_op jit(solution)/shard_map/ppermute | solution.py:24
  165.6 20.5 %collective-permute-start.38 = (bf16[256,1280]{1,0:T(8,128)(2,1)S(1)}, bf16[256,1280]{1,0:T(8,128)(2,1)S(1)}, u32[]{:S(2)}, u32[]{:S(2)}) collective-permute-start(bf16[256,1280]{1,0:T(8,128)(2,1)S(1)} %get-tuple-element.246), channel_id=1, source_target_pairs={{0,2},{1,3},{2,0},{3,1},{4,6},{5,7},{6,4},{7,5},{8,10},{9,11},{10,... | collective-permute-start | bytes 1966088 | tf_op jit(solution)/shard_map/ppermute | solution.py:24
  167.7 27.5 %collective-permute-start.41 = (bf16[16,4992]{1,0:T(8,128)(2,1)S(1)}, bf16[16,4992]{1,0:T(8,128)(2,1)S(1)}, u32[]{:S(2)}, u32[]{:S(2)}) collective-permute-start(bf16[16,4992]{1,0:T(8,128)(2,1)S(1)} %get-tuple-element.249), channel_id=1, source_target_pairs={{0,16},{4,20},{8,24},{12,28},{16,0},{20,4},{24,8},{28,12},{1,17},{... | collective-permute-start | bytes 479240 | tf_op jit(solution)/shard_map/ppermute | solution.py:24
  216.4 20.5 %collective-permute-start.52 = (bf16[4,16,4992]{2,1,0:T(8,128)(2,1)S(1)}, bf16[4,16,4992]{2,1,0:T(8,128)(2,1)S(1)}, u32[]{:S(2)}, u32[]{:S(2)}) collective-permute-start(bf16[4,16,4992]{2,1,0:T(8,128)(2,1)S(1)} %get-tuple-element.307.refs_0_), channel_id=1, source_target_pairs={{0,8},{4,12},{8,0},{12,4},{16,24},{20,28},{24,16},{28,20},{1,9},{5... | collective-permute-start | bytes 1916936 | tf_op jit(solution)/shard_map/ppermute | solution.py:24
  217.8 19.1 %collective-permute-start.53 = (bf16[4,16,4992]{2,1,0:T(8,128)(2,1)S(1)}, bf16[4,16,4992]{2,1,0:T(8,128)(2,1)S(1)}, u32[]{:S(2)}, u32[]{:S(2)}) collective-permute-start(bf16[4,16,4992]{2,1,0:T(8,128)(2,1)S(1)} %get-tuple-element.309.refs_2_), channel_id=1, source_target_pairs={{0,4},{4,0},{8,12},{12,8},{16,20},{20,16},{24,28},{28,24},{1,5},{5... | collective-permute-start | bytes 1916936 | tf_op jit(solution)/shard_map/ppermute | solution.py:24
  218.3 16.2 %collective-permute-start.54 = (bf16[16,2944]{1,0:T(8,128)(2,1)S(1)}, bf16[16,2944]{1,0:T(8,128)(2,1)S(1)}, u32[]{:S(2)}, u32[]{:S(2)}) collective-permute-start(bf16[16,2944]{1,0:T(8,128)(2,1)S(1)} %get-tuple-element.303), channel_id=1, source_target_pairs={{0,16},{4,20},{8,24},{12,28},{16,0},{20,4},{24,8},{28,12},{1,17},{... | collective-permute-start | bytes 282632 | tf_op jit(solution)/shard_map/ppermute | solution.py:24
  228.0 26.2 %collective-permute-start.51 = (bf16[256,1280]{1,0:T(8,128)(2,1)S(1)}, bf16[256,1280]{1,0:T(8,128)(2,1)S(1)}, u32[]{:S(2)}, u32[]{:S(2)}) collective-permute-start(bf16[256,1280]{1,0:T(8,128)(2,1)S(1)} %shard_map.377), channel_id=1, source_target_pairs={{0,2},{1,3},{2,0},{3,1},{4,6},{5,7},{6,4},{7,5},{8,10},{9,11},{10,... | collective-permute-start | bytes 1966088 | tf_op jit(solution)/shard_map/ppermute | solution.py:24
  (130 other events, 1245.3 us)
